TPU v7x, 32 devices: a whole 2x2x4 slice. The times are simulated.
32 devices in a mesh: dp: 16 (over z, x, core), mp: 2 (over y).
Axes of the slice: x: 2, y: 2, z: 4, core: 2. Of those that a mesh axis runs over, the one named last changes fastest.
Arguments:
- tokens: bfloat16 [16384, 1024], P('dp'), may hold values from -6 to 6
- cotangent: bfloat16 [16384, 1024], P('dp')
- proj_qkv: float32 [3, 1024, 1024], P(None, 'dp', 'mp'), may hold values from -0.1875 to 0.1875
- proj_out: float32 [1024, 1024], P('mp', 'dp'), may hold values from -4 to 4
- proj_gate_up: float32 [2, 1024, 2816], P(None, 'dp', 'mp'), may hold values from -0.1875 to 0.1875
- proj_down: float32 [2816, 1024], P('mp', 'dp'), may hold values from -0.109375 to 0.109375
- norm_gains: float32 [2, 1024], P(None, 'dp'), may hold values from 0.5 to 1.5
- first_qkv: float32 [3, 1024, 1024], P(None, 'dp', 'mp'), may hold values from -160 to 160
- first_out: float32 [1024, 1024], P('mp', 'dp'), may hold values from -6 to 6
- first_gate_up: float32 [2, 1024, 2816], P(None, 'dp', 'mp'), may hold values from -48 to 48
- first_down: float32 [2816, 1024], P('mp', 'dp'), may hold values from -96 to 96
- first_gains: float32 [2, 1024], P(None, 'dp'), may hold values from -160 to 160
- second_qkv: float32 [3, 1024, 1024], P(None, 'dp', 'mp'), may hold values from 3440.64 to 13762.56
- second_out: float32 [1024, 1024], P('mp', 'dp'), may hold values from 6.72 to 27.2
- second_gate_up: float32 [2, 1024, 2816], P(None, 'dp', 'mp'), may hold values from 311.296 to 1245.184
- second_down: float32 [2816, 1024], P('mp', 'dp'), may hold values from 1048.576 to 4096
- second_gains: float32 [2, 1024], P(None, 'dp'), may hold values from 3440.64 to 13762.56
- cache: bfloat16 [16384, 2, 1024], P('dp', None, 'mp'), may hold values from -6 to 6
- doc_segments: int32 [3], replicated, may hold values from 1 to 4, as said below
- padding: int32 [16384], replicated, may hold values from 0 to 1, as said below
- retrieval: int32 [16, 128], P('dp'), may hold values from 0 to 1023
Outputs:
- block_out: bfloat16 [16384, 1024], P('dp')
- input_grad: bfloat16 [16384, 1024], P('dp')
- qkv_first: float32 [3, 1024, 1024], P(None, 'dp', 'mp')
- qkv_second: float32 [3, 1024, 1024], P(None, 'dp', 'mp')
- qkv_new: float32 [3, 1024, 1024], P(None, 'dp', 'mp')
- out_first: float32 [1024, 1024], P('mp', 'dp')
- out_second: float32 [1024, 1024], P('mp', 'dp')
- out_new: float32 [1024, 1024], P('mp', 'dp')
- gate_up_first: float32 [2, 1024, 2816], P(None, 'dp', 'mp')
- gate_up_second: float32 [2, 1024, 2816], P(None, 'dp', 'mp')
- gate_up_new: float32 [2, 1024, 2816], P(None, 'dp', 'mp')
- down_first: float32 [2816, 1024], P('mp', 'dp')
- down_second: float32 [2816, 1024], P('mp', 'dp')
- down_new: float32 [2816, 1024], P('mp', 'dp')
- gains_first: float32 [2, 1024], P(None, 'dp')
- gains_second: float32 [2, 1024], P(None, 'dp')
- gains_new: float32 [2, 1024], P(None, 'dp')
Inputs may be any that keep to these rules, and one draw needn't show every extreme that they name: `doc_segments`: segment counts of 3 consecutive documents, summing to 8; one document has exactly 4. `padding`: zeros only at the tail of each document's last segment: 1 to 1024 tokens, at most half of that segment.
All inputs are finite; a program needn't handle non-finite values.
Results may differ from a plain program's by a relative error of at most 0.017.
The roundings to bfloat16 on the way count: a program that leaves them out, or rounds other values in their place, can miss the bound.
Values may be sent and summed in bfloat16 or wider, within the bound.
No kernel may reach another device: no remote copies, remote signals or barrier semaphores. Data moves between devices by JAX's collectives and lax.ppermute only.
A program may use at most 192 MiB of HBM per device.

v0:
```python
import math

import jax
import jax.numpy as jnp
from jax import lax
from jax.sharding import PartitionSpec as P

D = 1024
HEAD_DIM = 128
FF = 2816
SEG = 2048
RETR = 128
STEP = 10


EPS = 1e-05
BETA_ONE = 0.9
BETA_TWO = 0.95
ADAM_EPS = 1e-08
DECAY = 0.1
NEGATIVE = -1e30


def from_behind(value, axis, steps):
    count = lax.axis_size(axis)
    initial, last = (max(0, -steps), min(count, count - steps))
    return lax.ppermute(value, axis, [(source, source + steps) for source in range(initial, last)])


def angles(positions):
    half_dim = HEAD_DIM // 2
    freqs = 10000.0 ** (-(jnp.arange(half_dim, dtype=jnp.float32) / half_dim))
    phase = positions.astype(jnp.float32)[:, None] * freqs[None, :]
    return (jnp.cos(phase)[None], jnp.sin(phase)[None])


def rotate(value, cosines, sine_table):
    half_dim = value.shape[-1] // 2
    first_half = value[..., :half_dim]
    second_half = value[..., half_dim:]
    return jnp.concatenate(
        [
            first_half * cosines - second_half * sine_table,
            second_half * cosines + first_half * sine_table,
        ],
        axis=-1,
    )


def adamw(weight, grad, first, second, rate):
    first_new = BETA_ONE * first + (1.0 - BETA_ONE) * grad
    second_new = BETA_TWO * second + (1.0 - BETA_TWO) * grad * grad
    first_hat = first_new / (1.0 - BETA_ONE**STEP)
    second_hat = second_new / (1.0 - BETA_TWO**STEP)
    updated = weight - rate * (first_hat / (jnp.sqrt(second_hat) + ADAM_EPS) + DECAY * weight)
    return (first_new, second_new, updated)


def body(
    tokens,
    cotangent,
    proj_qkv,
    proj_out,
    proj_gate_up,
    proj_down,
    norm_gains,
    first_qkv,
    first_out,
    first_gate_up,
    first_down,
    first_gains,
    second_qkv,
    second_out,
    second_gate_up,
    second_down,
    second_gains,
    cache,
    doc_segments,
    padding,
    retrieval,
):
    row_count = tokens.shape[0]
    span_devs = SEG // row_count
    device = lax.axis_index("dp")
    qkv_w, out_w, gate_up_w, down_w, gains_low = (
        lax.all_gather(proj_qkv.astype(jnp.bfloat16), "dp", axis=1, tiled=True),
        lax.all_gather(proj_out.astype(jnp.bfloat16), "dp", axis=1, tiled=True),
        lax.all_gather(proj_gate_up.astype(jnp.bfloat16), "dp", axis=1, tiled=True),
        lax.all_gather(proj_down.astype(jnp.bfloat16), "dp", axis=1, tiled=True),
        lax.all_gather(norm_gains.astype(jnp.bfloat16), "dp", axis=1, tiled=True),
    )
    gains_full = gains_low.astype(jnp.float32)
    local_width = qkv_w.shape[2]
    heads_here = local_width // HEAD_DIM
    scale_factor = HEAD_DIM ** (-0.5)

    def heads_first(matrix):
        return matrix.reshape(row_count, heads_here, HEAD_DIM).transpose(1, 0, 2)

    def tokens_first(matrix):
        return matrix.transpose(1, 0, 2).reshape(row_count, local_width)

    inputs = tokens.astype(jnp.float32)
    inverse_one = lax.rsqrt(jnp.mean(inputs * inputs, axis=-1, keepdims=True) + EPS)
    normed_one = (inputs * inverse_one * gains_full[0]).astype(jnp.bfloat16)
    projected = jnp.einsum("td,cde->cte", normed_one, qkv_w, preferred_element_type=jnp.float32)
    seg_rank = device % span_devs
    positions = seg_rank * row_count + jnp.arange(row_count, dtype=jnp.int32)
    cosines, sine_table = angles(positions)
    queries = rotate(heads_first(projected[0]), cosines, sine_table).astype(jnp.bfloat16)
    keys_own = rotate(heads_first(projected[1]), cosines, sine_table).astype(jnp.bfloat16)
    values_own = heads_first(projected[2]).astype(jnp.bfloat16)
    pair = jnp.stack([keys_own, values_own])
    earlier = [from_behind(pair, "dp", 1)]
    local_pair = jnp.concatenate(earlier + [pair], axis=2)
    fetched = cache[retrieval[0]].reshape(RETR, 2, heads_here, HEAD_DIM).transpose(1, 2, 0, 3)
    all_pair = jnp.concatenate([local_pair, fetched], axis=2)
    local_count = span_devs * row_count
    key_place = jnp.arange(local_count, dtype=jnp.int32) + (seg_rank - span_devs + 1) * row_count
    padded = jnp.concatenate([jnp.zeros((SEG - row_count,), jnp.int32), padding])
    key_pad = lax.dynamic_slice_in_dim(padded, device * row_count, local_count)
    local_ok = (
        (key_place[None, :] >= 0)
        & (key_place[None, :] <= positions[:, None])
        & (key_pad[None, :] > 0)
    )
    starts = jnp.cumsum(doc_segments) - doc_segments
    memory_on = jnp.logical_not(jnp.any(starts == device // span_devs))
    memory_ok = jnp.broadcast_to(memory_on, (row_count, RETR))
    allowed = jnp.concatenate([local_ok, memory_ok], axis=1)

    def head_scores(query, keys):
        scores = scale_factor * jnp.einsum(
            "qd,kd->qk", query, keys, preferred_element_type=jnp.float32
        )
        return jnp.where(allowed, scores, NEGATIVE)

    def head_forward(pieces):
        query, keys, values = pieces
        scores = head_scores(query, keys)
        top = jnp.max(scores, axis=-1, keepdims=True)
        exponent = jnp.exp(scores - top)
        total = jnp.sum(exponent, axis=-1, keepdims=True)
        probs = (exponent / total).astype(jnp.bfloat16)
        result = jnp.einsum("qk,kd->qd", probs, values, preferred_element_type=jnp.float32)
        return (result, top + jnp.log(total))

    head_outs, log_totals = lax.map(head_forward, (queries, all_pair[0], all_pair[1]))
    attended = tokens_first(head_outs.astype(jnp.bfloat16))
    attention = lax.psum(jnp.dot(attended, out_w, preferred_element_type=jnp.float32), "mp")
    middle = inputs + attention
    inverse_two = lax.rsqrt(jnp.mean(middle * middle, axis=-1, keepdims=True) + EPS)
    normed_two = (middle * inverse_two * gains_full[1]).astype(jnp.bfloat16)
    gate = jnp.dot(normed_two, gate_up_w[0], preferred_element_type=jnp.float32)
    up_part = jnp.dot(normed_two, gate_up_w[1], preferred_element_type=jnp.float32)
    sigma = jax.nn.sigmoid(gate)
    hidden = (gate * sigma * up_part).astype(jnp.bfloat16)
    feed = lax.psum(
        jnp.dot(hidden, down_w, preferred_element_type=jnp.float32).astype(jnp.bfloat16), "mp"
    ).astype(jnp.float32)
    block_out = (middle + feed).astype(jnp.bfloat16)
    upstream = cotangent.astype(jnp.float32)
    grad_down = jnp.einsum("tf,td->fd", hidden, cotangent, preferred_element_type=jnp.float32)
    grad_hidden = jnp.einsum("td,fd->tf", cotangent, down_w, preferred_element_type=jnp.float32)
    grad_gate = (grad_hidden * up_part * sigma * (1.0 + gate * (1.0 - sigma))).astype(jnp.bfloat16)
    grad_up = (grad_hidden * gate * sigma).astype(jnp.bfloat16)
    grad_gate_up = jnp.stack(
        [
            jnp.einsum("td,tf->df", normed_two, grad_gate, preferred_element_type=jnp.float32),
            jnp.einsum("td,tf->df", normed_two, grad_up, preferred_element_type=jnp.float32),
        ]
    )
    back_part = jnp.einsum(
        "tf,df->td", grad_gate, gate_up_w[0], preferred_element_type=jnp.float32
    ) + jnp.einsum("tf,df->td", grad_up, gate_up_w[1], preferred_element_type=jnp.float32)
    back_two = lax.psum(back_part, "mp")
    scaled_two = gains_full[1] * back_two
    grad_middle = (
        upstream
        + inverse_two * scaled_two
        - middle * inverse_two**3 * jnp.mean(scaled_two * middle, axis=-1, keepdims=True)
    )
    gain_two = jnp.sum(back_two * middle * inverse_two, axis=0)
    grad_branch = grad_middle.astype(jnp.bfloat16)
    grad_out = jnp.einsum("te,td->ed", attended, grad_branch, preferred_element_type=jnp.float32)
    grad_attended = jnp.einsum("td,ed->te", grad_branch, out_w, preferred_element_type=jnp.float32)
    grad_heads = heads_first(grad_attended.astype(jnp.bfloat16))

    def head_backward(pieces):
        query, keys, values, grad_result, log_total = pieces
        probs = jnp.exp(head_scores(query, keys) - log_total)
        grad_probs = jnp.einsum(
            "qd,kd->qk", grad_result, values, preferred_element_type=jnp.float32
        )
        grad_scores = (
            probs * (grad_probs - jnp.sum(probs * grad_probs, axis=-1, keepdims=True))
        ).astype(jnp.bfloat16)
        grad_query = scale_factor * jnp.einsum(
            "qk,kd->qd", grad_scores, keys, preferred_element_type=jnp.float32
        )
        grad_keys = scale_factor * jnp.einsum(
            "qk,qd->kd", grad_scores, query, preferred_element_type=jnp.float32
        )
        grad_values = jnp.einsum(
            "qk,qd->kd", probs.astype(jnp.bfloat16), grad_result, preferred_element_type=jnp.float32
        )
        return (grad_query, grad_keys, grad_values)

    grad_queries, grad_keys, grad_values = lax.map(
        head_backward, (queries, all_pair[0], all_pair[1], grad_heads, log_totals)
    )
    key_value_grads = jnp.stack([grad_keys[:, :local_count], grad_values[:, :local_count]])
    own_grads = key_value_grads[:, :, (span_devs - 1) * row_count :]
    piece = key_value_grads[:, :, (span_devs - 1 - 1) * row_count : (span_devs - 1) * row_count]
    own_grads = own_grads + from_behind(piece.astype(jnp.bfloat16), "dp", -1).astype(piece.dtype)
    query_grad = tokens_first(rotate(grad_queries, cosines, -sine_table).astype(jnp.bfloat16))
    key_grad = tokens_first(rotate(own_grads[0], cosines, -sine_table).astype(jnp.bfloat16))
    value_grad = tokens_first(own_grads[1].astype(jnp.bfloat16))
    stacked_grads = jnp.stack([query_grad, key_grad, value_grad])
    grad_qkv = jnp.einsum(
        "td,cte->cde", normed_one, stacked_grads, preferred_element_type=jnp.float32
    )
    back_one = lax.psum(
        jnp.einsum("cte,cde->td", stacked_grads, qkv_w, preferred_element_type=jnp.float32).astype(
            jnp.bfloat16
        ),
        "mp",
    ).astype(jnp.float32)
    scaled_one = gains_full[0] * back_one
    grad_input = (
        grad_middle
        + inverse_one * scaled_one
        - inputs * inverse_one**3 * jnp.mean(scaled_one * inputs, axis=-1, keepdims=True)
    )
    gain_one = jnp.sum(back_one * inputs * inverse_one, axis=0)
    grad_gains = jnp.stack([gain_one, gain_two])
    qkv_sum, out_sum, gate_up_sum, down_sum, gains_sum = (
        lax.psum_scatter(grad_qkv, "dp", scatter_dimension=1, tiled=True),
        lax.psum_scatter(grad_out, "dp", scatter_dimension=1, tiled=True),
        lax.psum_scatter(grad_gate_up, "dp", scatter_dimension=1, tiled=True),
        lax.psum_scatter(grad_down, "dp", scatter_dimension=1, tiled=True),
        lax.psum_scatter(grad_gains, "dp", scatter_dimension=1, tiled=True),
    )
    qkv_first, qkv_second, qkv_new = adamw(
        proj_qkv, qkv_sum, first_qkv, second_qkv, 0.5 / math.sqrt(D)
    )
    out_first, out_second, out_new = adamw(
        proj_out, out_sum, first_out, second_out, 0.5 / math.sqrt(max(1, 4 * D // SEG))
    )
    gate_up_first, gate_up_second, gate_up_new = adamw(
        proj_gate_up, gate_up_sum, first_gate_up, second_gate_up, 0.5 / math.sqrt(D)
    )
    down_first, down_second, down_new = adamw(
        proj_down, down_sum, first_down, second_down, 0.5 / math.sqrt(FF)
    )
    gains_first, gains_second, gains_new = adamw(
        norm_gains, gains_sum, first_gains, second_gains, 0.6
    )
    return (
        block_out,
        grad_input.astype(jnp.bfloat16),
        qkv_first,
        qkv_second,
        qkv_new,
        out_first,
        out_second,
        out_new,
        gate_up_first,
        gate_up_second,
        gate_up_new,
        down_first,
        down_second,
        down_new,
        gains_first,
        gains_second,
        gains_new,
    )


def solution(mesh):
    return jax.shard_map(
        body,
        mesh=mesh,
        in_specs=(
            P("dp", None),
            P("dp", None),
            P(None, "dp", "mp"),
            P("mp", "dp"),
            P(None, "dp", "mp"),
            P("mp", "dp"),
            P(None, "dp"),
            P(None, "dp", "mp"),
            P("mp", "dp"),
            P(None, "dp", "mp"),
            P("mp", "dp"),
            P(None, "dp"),
            P(None, "dp", "mp"),
            P("mp", "dp"),
            P(None, "dp", "mp"),
            P("mp", "dp"),
            P(None, "dp"),
            P("dp", None, "mp"),
            P(),
            P(),
            P("dp", None),
        ),
        out_specs=(
            P("dp", None),
            P("dp", None),
            P(None, "dp", "mp"),
            P(None, "dp", "mp"),
            P(None, "dp", "mp"),
            P("mp", "dp"),
            P("mp", "dp"),
            P("mp", "dp"),
            P(None, "dp", "mp"),
            P(None, "dp", "mp"),
            P(None, "dp", "mp"),
            P("mp", "dp"),
            P("mp", "dp"),
            P("mp", "dp"),
            P(None, "dp"),
            P(None, "dp"),
            P(None, "dp"),
        ),
        check_vma=False,
    )
```

profile of v0, /device:TPU:0, one launch (start us, length us, event | category | flops | bytes accessed | tf_op | source)
XLA Modules:
  0.0 1333.7 jit_solution(4450977532854672746)
XLA Ops:
  9.9 23.0 %all-gather = bf16[16,64,2]{1,2,0:T(2,128)(2,1)S(1)} all-gather(bf16[1,64,2]{1,2,0:T(2,128)(2,1)S(1)} %convert_bitcast_fusion), channel_id=1, replica_groups=mesh['dp'=16,'mp'=2] {'dp'}, dimensions={0}, use_global_device_ids=true | all-gather | bytes 4352 | tf_op jit(solution)/shard_map/all_gather | solution.py:90
  38.8 19.9 %all-gather.6.cloned.1.call-done = bf16[3,1024,512]{2,1,0:T(8,128)(2,1)} async-done(((bf16[3,64,512]{2,1,0:T(8,128)(2,1)}), bf16[3,1024,512]{2,1,0:T(8,128)(2,1)}) %all-gather.6.cloned.1.call-update) | async-done | bytes 3145744 | tf_op jit(solution)/shard_map/all_gather | solution.py:86
  58.7 6.2 convolution_bitcast_fusion.3
  75.9 6.9 fusion.66
  104.4 36.1 %while.26 = (s32[]{:T(128)}, bf16[4,1024,128]{1,2,0:T(8,128)(2,1)S(1)}, f32[4,1024,1]{1,2,0:T(1,128)S(1)}, bf16[4,1024,128]{2,1,0:T(8,128)(2,1)S(1)}, bf16[4,217...) while((s32[]{:T(128)}, ...), condition=%wide.region_6.7_spmd, body=%wide.region_3.6_spmd.sunk | while | flops 1158675456 | bytes 30910560 | solution.py:148
  141.5 4.6 fusion.89
  149.6 120.7 %all-reduce.9.cloned.1.call-done = f32[1024,1024]{1,0:T(8,128)} async-done(((f32[1024,1024]{1,0:T(8,128)}), f32[1024,1024]{1,0:T(8,128)}) %all-reduce.9.cloned.1.call-update) | async-done | bytes 4194320 | tf_op jit(solution)/shard_map/psum | solution.py:150
  275.5 56.8 %all-gather.10.cloned.1.call-done = bf16[2,1024,1408]{2,1,0:T(8,128)(2,1)} async-done(((bf16[2,64,1408]{2,1,0:T(8,128)(2,1)}), bf16[2,1024,1408]{2,1,0:T(8,128)(2,1)}) %all-gather.10.cloned.1.call-update) | async-done | bytes 5767184 | tf_op jit(solution)/shard_map/all_gather | solution.py:88
  332.3 7.1 fusion.59
  339.4 5.2 fusion.61
  344.6 33.7 %all-gather.12.cloned.1.call-done = bf16[1408,1024]{0,1:T(8,128)(2,1)} async-done(((bf16[1408,64]{0,1:T(8,128)(2,1)}), bf16[1408,1024]{0,1:T(8,128)(2,1)}) %all-gather.12.cloned.1.call-update) | async-done | bytes 2883600 | tf_op jit(solution)/shard_map/all_gather | solution.py:89
  378.3 11.2 multiply_convert_fusion.1
  389.4 7.3 fusion.58
  396.8 6.8 fusion.63
  403.9 106.1 %all-reduce.11.cloned.1.call-done = f32[1024,1024]{1,0:T(8,128)} async-done(((f32[1024,1024]{1,0:T(8,128)}), f32[1024,1024]{1,0:T(8,128)}) %all-reduce.11.cloned.1.call-update) | async-done | bytes 4194320 | tf_op jit(solution)/shard_map/psum | solution.py:176
  510.0 5.2 multiply_reduce_fusion.1
  521.2 126.5 %while.27 = (s32[]{:T(128)}, f32[4,1024,128]{2,1,0:T(8,128)}, f32[4,2176,128]{2,1,0:T(8,128)}, f32[4,2176,128]{2,1,0:T(8,128)}, bf16[4,1024,128]{2,1,0:T(8,128)(...) while((s32[]{:T(128)}, f32[4,1024,128]{2,1,0:T(8,128)}, ...), condition=%wide.region_14.15_spmd, body=%wide.region_12.14_spmd.sunk | while | flops 2872589312 | bytes 136963280 | solution.py:209
  523.8 7.1 multiply_reduce_fusion.5
  531.0 9.0 multiply_convert_fusion.6
  539.9 4.7 fusion.144
  547.0 5.9 fusion.146
  555.5 7.1 multiply_reduce_fusion.5
  562.6 9.0 multiply_convert_fusion.6
  571.5 4.7 fusion.144
  578.6 5.9 fusion.146
  587.0 7.1 multiply_reduce_fusion.5
  594.1 9.0 multiply_convert_fusion.6
  603.1 4.7 fusion.144
  610.1 5.9 fusion.146
  618.6 7.1 multiply_reduce_fusion.5
  625.7 9.0 multiply_convert_fusion.6
  634.7 4.7 fusion.144
  641.8 5.9 fusion.146
  654.2 4.6 convolution_convert_fusion
  676.2 6.5 bitcast_convert_fusion
  683.9 4.8 fusion.69
  688.8 7.1 fusion.90
  697.5 7.4 convolution_bitcast_fusion.2
  705.0 9.3 copy.122
  714.4 8.5 convolution_bitcast_fusion
  722.9 5.3 convolution_bitcast_fusion.1
  728.2 83.0 %all-reduce.15.cloned.1.call-done = (bf16[1024,1024]{1,0:T(8,128)(2,1)}, bf16[1024,1024]{1,0:T(8,128)(2,1)}) async-done(((bf16[1024,1024]{1,0:T(8,128)(2,1)}, bf16[1024,1024]{1,0:T(8,128)(2,1)}), (bf16[1024,1024]{1,0:T(8,128)(2,1)}, bf16[1024,1024]{1,0:T(8,128)(2,1)})) %all-reduce.15.cloned.1.call-update) | async-done | bytes 4194320 | tf_op jit(solution)/shard_map/psum | solution.py:158
  815.8 9.3 pad_maximum_fusion
  826.9 50.1 %reduce-scatter.7.cloned.1.call-done = f32[512,64]{0,1:T(8,128)} async-done(((f32[512,1024]{0,1:T(8,128)}), f32[512,64]{0,1:T(8,128)}) %reduce-scatter.7.cloned.1.call-update) | async-done | bytes 131088 | tf_op jit(solution)/shard_map/reduce_scatter | solution.py:239
  878.8 82.7 %reduce-scatter.11.cloned.1.call-done = f32[1408,64]{0,1:T(8,128)} async-done(((f32[1408,1024]{0,1:T(8,128)}), f32[1408,64]{0,1:T(8,128)}) %reduce-scatter.11.cloned.1.call-update) | async-done | bytes 360464 | tf_op jit(solution)/shard_map/reduce_scatter | solution.py:241
  963.8 170.4 %all-reduce.13.cloned.1.call-done = f32[3,1024,512]{2,0,1:T(4,128)} async-done(((f32[3,1024,512]{2,0,1:T(4,128)}), f32[3,1024,512]{2,0,1:T(4,128)}) %all-reduce.13.cloned.1.call-update) | async-done | bytes 6291472
  1145.6 48.8 %reduce-scatter.13.cloned.1.call-done = f32[64,2]{1,0:T(8,128)} async-done(((f32[1024,2]{1,0:T(8,128)}), f32[64,2]{1,0:T(8,128)}) %reduce-scatter.13.cloned.1.call-update) | async-done | bytes 528
  1196.5 127.2 %reduce-scatter.9.cloned.1.call-done = f32[2,64,1408]{2,1,0:T(8,128)} async-done(((f32[2,1024,1408]{2,1,0:T(8,128)}), f32[2,64,1408]{2,1,0:T(8,128)}) %reduce-scatter.9.cloned.1.call-update) | async-done | bytes 720912 | tf_op jit(solution)/shard_map/reduce_scatter | solution.py:240
  (278 shorter events, 164.5 us)
Async XLA Ops:
  7.2 82.2 %copy-start = (bf16[1024,2,512]{2,1,0:T(2,128)(2,1)S(1)}, bf16[1024,2,512]{2,1,0:T(2,128)(2,1)}, u32[]{:S(2)}) copy-start(bf16[1024,2,512]{2,1,0:T(2,128)(2,1)} %param.42) | copy-start | bytes 6291460
  7.2 51.5 %all-gather.6.cloned.1.call-start = ((), (), s32[]{:S(2)}) async-start(), calls=%async_computation.4 | async-start | bytes 3342336 | tf_op jit(solution)/shard_map/all_gather | solution.py:86
  9.1 131.4 %all-gather.8.cloned.1.call-start = ((), (), s32[]{:S(2)}) async-start(), calls=%async_computation.5 | async-start | bytes 1114112 | tf_op jit(solution)/shard_map/all_gather | solution.py:87
  35.6 29.4 %copy-start.42 = (f32[1024]{0:T(1024)}, f32[1024]{0:T(1024)S(1)}, u32[]{:S(2)}) copy-start(f32[1024]{0:T(1024)S(1)} %get-tuple-element.268) | copy-start | bytes 12292
  35.6 29.4 %copy-start.44 = (f32[1,1024]{1,0:T(1,128)}, f32[1,1024]{1,0:T(1,128)S(1)}, u32[]{:S(2)}) copy-start(f32[1,1024]{1,0:T(1,128)S(1)} %get-tuple-element.263) | copy-start | bytes 12292
  75.9 7.0 copy-start.13
  82.8 6.5 copy-start.55
  82.8 8.1 copy-start.50
  82.9 9.6 copy-start.41
  84.8 14.8 %collective-permute-start = (bf16[2,4,1024,128]{3,2,1,0:T(8,128)(2,1)}, bf16[2,4,1024,128]{3,2,1,0:T(8,128)(2,1)}, u32[]{:S(2)}, u32[]{:S(2)}) collective-permute-start(bf16[2,4,1024,128]{3,2,1,0:T(8,128)(2,1)} %pad_maximum_fusion.3), channel_id=1, source_target_pairs={{0,2},{2,4},{4,6},{6,8},{8,10},{10,12},{12,14},{14,16},{16,18},{18... | collective-permute-start | bytes 6291464 | tf_op jit(solution)/shard_map/ppermute | solution.py:27
  89.0 181.3 %all-reduce.9.cloned.1.call-start = ((), (), s32[]{:S(2)}) async-start(), calls=%async_computation.6 | async-start | bytes 8388608 | tf_op jit(solution)/shard_map/psum | solution.py:150
  146.1 124.2 %copy-start.9 = (bf16[1024,1024]{1,0:T(8,128)(2,1)S(1)}, bf16[1024,1024]{1,0:T(8,128)(2,1)}, u32[]{:S(2)}) copy-start(bf16[1024,1024]{1,0:T(8,128)(2,1)} %param.25) | copy-start | bytes 6291460
  146.1 186.2 %all-gather.10.cloned.1.call-start = ((), (), s32[]{:S(2)}) async-start(), calls=%async_computation.7 | async-start | bytes 6127616 | tf_op jit(solution)/shard_map/all_gather | solution.py:88
  148.2 230.1 %all-gather.12.cloned.1.call-start = ((), (), s32[]{:S(2)}) async-start(), calls=%async_computation.8 | async-start | bytes 3063808 | tf_op jit(solution)/shard_map/all_gather | solution.py:89
  149.0 361.0 %all-reduce.11.cloned.1.call-start = ((), (), s32[]{:S(2)}) async-start(), calls=%async_computation.9 | async-start | bytes 8388608 | tf_op jit(solution)/shard_map/psum | solution.py:176
  275.5 64.0 %copy-start.24 = (bf16[1024,1024]{1,0:T(8,128)(2,1)}, bf16[1024,1024]{1,0:T(8,128)(2,1)S(1)}, u32[]{:S(2)}) copy-start(bf16[1024,1024]{1,0:T(8,128)(2,1)S(1)} %multiply_convert_fusion.4) | copy-start | bytes 6291460
  332.3 7.1 copy-start.51
  389.4 7.3 copy-start.57
  389.4 7.4 copy-start.59
  403.6 111.6 %copy-start.26 = (bf16[1024,1024]{1,0:T(8,128)(2,1)S(1)}, bf16[1024,1024]{1,0:T(8,128)(2,1)}, u32[]{:S(2)}) copy-start(bf16[1024,1024]{1,0:T(8,128)(2,1)} %param.26) | copy-start | bytes 6291460
  403.7 407.5 %all-reduce.15.cloned.1.call-start = ((), (), s32[]{:S(2)}) async-start(), calls=%async_computation.15 | async-start | bytes 8388608 | tf_op jit(solution)/shard_map/psum | solution.py:158
  510.0 5.9 copy-start.12
  523.8 7.2 copy-start.2
  555.4 7.2 copy-start.2
  587.0 7.1 copy-start.2
  618.6 7.2 copy-start.2
  651.9 7.0 collective-permute-start.1
  682.7 6.1 copy-start.27
  682.7 194.3 %reduce-scatter.7.cloned.1.call-start = ((), (), s32[]{:S(2)}) async-start(), calls=%async_computation.10 | async-start | bytes 2228224 | tf_op jit(solution)/shard_map/reduce_scatter | solution.py:239
  688.7 272.7 %reduce-scatter.11.cloned.1.call-start = ((), (), s32[]{:S(2)}) async-start(), calls=%async_computation.12 | async-start | bytes 6127616 | tf_op jit(solution)/shard_map/reduce_scatter | solution.py:241
  696.0 438.3 %all-reduce.13.cloned.1.call-start = ((), (), s32[]{:S(2)}) async-start(), calls=%async_computation.14 | async-start | bytes 16777216
  714.3 480.1 %reduce-scatter.13.cloned.1.call-start = ((), (), s32[]{:S(2)}) async-start(), calls=%async_computation.13 | async-start | bytes 557056
  714.3 8.5 copy-start.25
  714.4 8.5 copy-start.58
  728.2 86.3 %copy-start.47 = (f32[1024]{0:T(1024)S(1)}, f32[1024]{0:T(1024)}, u32[]{:S(2)}) copy-start(f32[1024]{0:T(1024)} %get-tuple-element.182) | copy-start | bytes 12292
  815.5 508.2 %reduce-scatter.9.cloned.1.call-start = ((), (), s32[]{:S(2)}) async-start(), calls=%async_computation.11 | async-start | bytes 12255232 | tf_op jit(solution)/shard_map/reduce_scatter | solution.py:240
  825.0 52.0 %copy-start.38 = (f32[512,64]{0,1:T(8,128)S(1)}, f32[512,64]{0,1:T(8,128)}, u32[]{:S(2)}) copy-start(f32[512,64]{0,1:T(8,128)} %param.28) | copy-start | bytes 393220
  825.0 52.0 %copy-start.40 = (f32[512,64]{0,1:T(8,128)S(1)}, f32[512,64]{0,1:T(8,128)}, u32[]{:S(2)}) copy-start(f32[512,64]{0,1:T(8,128)} %param.38) | copy-start | bytes 393220
  825.0 136.4 %copy-start.32 = (f32[1408,64]{0,1:T(8,128)S(1)}, f32[1408,64]{0,1:T(8,128)}, u32[]{:S(2)}) copy-start(f32[1408,64]{0,1:T(8,128)} %param.30) | copy-start | bytes 1081348
  825.1 310.3 %copy-start.30 = (f32[3,64,512]{2,1,0:T(8,128)S(1)}, f32[3,64,512]{2,1,0:T(8,128)}, u32[]{:S(2)}) copy-start(f32[3,64,512]{2,1,0:T(8,128)} %param.27) | copy-start | bytes 1179652
  825.1 310.3 %copy-start.39 = (f32[3,64,512]{2,1,0:T(8,128)S(1)}, f32[3,64,512]{2,1,0:T(8,128)}, u32[]{:S(2)}) copy-start(f32[3,64,512]{2,1,0:T(8,128)} %param.37) | copy-start | bytes 1179652
  825.1 312.6 %copy-start.28 = (bf16[1024,1024]{1,0:T(8,128)(2,1)S(1)}, bf16[1024,1024]{1,0:T(8,128)(2,1)}, u32[]{:S(2)}) copy-start(bf16[1024,1024]{1,0:T(8,128)(2,1)} %get-tuple-element.220) | copy-start | bytes 6291460
  1134.2 7.9 copy-start.46
  1143.2 52.1 %copy-start.48 = (f32[2,64]{1,0:T(2,128)S(1)}, f32[2,64]{1,0:T(2,128)}, u32[]{:S(2)}) copy-start(f32[2,64]{1,0:T(2,128)} %param.31) | copy-start | bytes 1540
  1143.2 52.1 %copy-start.49 = (f32[2,64]{1,0:T(2,128)S(1)}, f32[2,64]{1,0:T(2,128)}, u32[]{:S(2)}) copy-start(f32[2,64]{1,0:T(2,128)} %param.41) | copy-start | bytes 1540
  1143.2 180.5 %copy-start.23 = (f32[2,64,1408]{2,1,0:T(8,128)S(1)}, f32[2,64,1408]{2,1,0:T(8,128)}, u32[]{:S(2)}) copy-start(f32[2,64,1408]{2,1,0:T(8,128)} %param.29) | copy-start | bytes 2162692
  1143.2 180.5 %copy-start.36 = (f32[2,64,1408]{2,1,0:T(8,128)S(1)}, f32[2,64,1408]{2,1,0:T(8,128)}, u32[]{:S(2)}) copy-start(f32[2,64,1408]{2,1,0:T(8,128)} %param.39) | copy-start | bytes 2162692
  1143.2 183.5 %copy-start.1 = (bf16[1024,2,512]{2,1,0:T(2,128)(2,1)S(1)}, bf16[1024,2,512]{2,1,0:T(2,128)(2,1)}, u32[]{:S(2)}) copy-start(bf16[1024,2,512]{2,1,0:T(2,128)(2,1)} %param.42) | copy-start | bytes 6291460
  (36 other events, 112.5 us)
Sparse Core Ops, SparseCore 0:
  10.8 47.8 all-gather.5
  89.1 36.9 all-gather.7
  146.2 123.9 all-reduce.8
  273.2 59.0 all-gather.9
  335.3 42.9 all-gather.11
  403.8 106.1 all-reduce.10
  682.8 128.3 all-reduce.14
  815.4 61.5 reduce-scatter.6
  880.9 80.5 reduce-scatter.10
  965.1 169.1 all-reduce.12
  1138.8 55.6 reduce-scatter.12
  1198.4 125.2 reduce-scatter.8
where the time goes:
time: 1340 us; the launch traced here: 1330 us
  waiting for transfers between devices  900 us (67%)
  matrix products  215 us (16%)
  other arithmetic  115 us (9%)
  local copies, waits for them, and re-layouts  56.8 us (4%)
  blocking collectives  23 us (2%)
  between operations  16.5 us (1%)
    unnamed x14, waiting for transfers between devices  219 us
    reduce_scatter x1, waiting for transfers between devices, body(): lax.psum_scatter(grad_gate_up, 'dp', scatter_dimension=1, tiled=True)  127 us
    psum x1, waiting for transfers between devices, body(): lax.psum(jnp.dot(attended, out_w, preferred_element_type=jnp.float32), 'mp')  121 us
    psum x1, waiting for transfers between devices, body(): back_two = lax.psum(back_part, 'mp')  106 us
    psum x1, waiting for transfers between devices, body(): lax.psum(jnp.dot(hidden, down_w, preferred_element_type=jnp.float32).asty...  83 us
    reduce_scatter x1, waiting for transfers between devices, body(): lax.psum_scatter(grad_down, 'dp', scatter_dimension=1, tiled=True)  82.7 us
    all_gather x1, waiting for transfers between devices, body(): lax.all_gather(proj_gate_up.astype(jnp.bfloat16), 'dp', axis=1, tiled=True)  56.8 us
    reduce_scatter x1, waiting for transfers between devices, body(): lax.psum_scatter(grad_out, 'dp', scatter_dimension=1, tiled=True)  50.1 us
  transfers between devices with their start and end apart: 14, of which 11 were waited for; matrix products, arithmetic and copies ran while one was open for 12% of the time, Pallas kernels for 0%

commit v1 on v0

v1 whole, which is shorter than its diff:
```python
import functools
import math

import jax
import jax.numpy as jnp
from jax import lax
from jax.experimental import pallas as pl
from jax.experimental.pallas import tpu as pltpu
from jax.sharding import PartitionSpec as P

D = 1024
HEAD_DIM = 128
FF = 2816
SEG = 2048
RETR = 128
STEP = 10

EPS = 1e-05
BETA_ONE = 0.9
BETA_TWO = 0.95
ADAM_EPS = 1e-08
DECAY = 0.1
NEGATIVE = -1e30
SCALE = HEAD_DIM**-0.5
SCALE_TWO = SCALE * math.log2(math.e)

BF = jnp.bfloat16
F32 = jnp.float32
MIB = 1024 * 1024
TILE = 256


def dot(left, right):
    return jnp.dot(left, right, preferred_element_type=F32)


def dot_nt(left, right):
    return lax.dot_general(left, right, (((1,), (1,)), ((), ())), preferred_element_type=F32)


def dot_tn(left, right):
    return lax.dot_general(left, right, (((0,), (0,)), ((), ())), preferred_element_type=F32)


def params(mib, axes=1):
    return pltpu.CompilerParams(
        dimension_semantics=("arbitrary",) * axes, vmem_limit_bytes=mib * MIB
    )


def cost(flops, moved, trans=0):
    return pl.CostEstimate(flops=int(flops), bytes_accessed=int(moved), transcendentals=int(trans))


def rope_tables(count):
    half_dim = HEAD_DIM // 2
    freqs = 10000.0 ** (-(jnp.arange(half_dim, dtype=F32) / half_dim))
    phase = jnp.arange(count, dtype=jnp.int32).astype(F32)[:, None] * freqs[None, :]
    cosines, sines = jnp.cos(phase), jnp.sin(phase)
    return jnp.concatenate([cosines, cosines], 1), jnp.concatenate([-sines, sines], 1)


def turn(value, cosines, sines):
    return value * cosines + pltpu.roll(value, HEAD_DIM // 2, 1) * sines


def adamw(weight, grad, first, second, rate):
    first_new = BETA_ONE * first + (1.0 - BETA_ONE) * grad
    second_new = BETA_TWO * second + (1.0 - BETA_TWO) * grad * grad
    first_hat = first_new / (1.0 - BETA_ONE**STEP)
    second_hat = second_new / (1.0 - BETA_TWO**STEP)
    updated = weight - rate * (first_hat / (jnp.sqrt(second_hat) + ADAM_EPS) + DECAY * weight)
    return (first_new, second_new, updated)


def qkv_kernel(info, normed, weight, cosines, sines, out):
    result = dot(normed[...], weight[...])
    part = pl.program_id(0)
    for head in range(2):
        value = result[:, head * HEAD_DIM : (head + 1) * HEAD_DIM]

        @pl.when(part < 2)
        def _():
            out[0, head] = turn(value, cosines[...], sines[...]).astype(BF)

        @pl.when(part == 2)
        def _():
            out[0, head] = value.astype(BF)


def project_pair(info, normed, weights, cosines, sines, slot):
    rows = normed.shape[0]
    return pl.pallas_call(
        qkv_kernel,
        out_shape=jax.ShapeDtypeStruct((3, 2, rows, HEAD_DIM), BF),
        grid_spec=pltpu.PrefetchScalarGridSpec(
            num_scalar_prefetch=1,
            grid=(3,),
            in_specs=[
                pl.BlockSpec((rows, D), lambda j, info: (0, 0)),
                pl.BlockSpec((D, 256), lambda j, info: (0, 2 * j + info[slot])),
                pl.BlockSpec((rows, HEAD_DIM), lambda j, info: (info[0], 0)),
                pl.BlockSpec((rows, HEAD_DIM), lambda j, info: (info[0], 0)),
            ],
            out_specs=pl.BlockSpec((1, 2, rows, HEAD_DIM), lambda j, info: (j, 0, 0, 0)),
        ),
        compiler_params=params(40),
        cost_estimate=cost(2 * rows * D * 768, 6 * MIB),
        name="project_pair",
    )(info, normed, weights, cosines, sines)


def place(scratch, own, other, rank, rows):
    scratch[pl.ds(pl.multiple_of(rank * rows, rows), rows), :] = own
    scratch[pl.ds(pl.multiple_of((1 - rank) * rows, rows), rows), :] = other


def chunks_of(tile, step):
    end = tile * TILE
    spans = [(start, min(step, end - start)) for start in range(0, end, step)]
    return spans + [(end, TILE)]


def causal(scores):
    rows = lax.broadcasted_iota(jnp.int32, scores.shape, 0)
    columns = lax.broadcasted_iota(jnp.int32, scores.shape, 1)
    return jnp.where(rows <= columns, scores, NEGATIVE)


def forward_kernel(
    info, own, other, mem_own, mem_other, bias, keep, send, turned, logs,
    q_s, k_s, v_s, vt_s, mem_s, s_s, out_s,
):
    rank = info[0]
    rows = own.shape[2]
    mem_bias = jnp.where(info[2] > 0, 0.0, NEGATIVE).astype(F32)
    place(q_s, own[0, 0], other[0, 0], rank, rows)
    place(k_s, own[1, 0], other[1, 0], rank, rows)
    place(v_s, own[2, 0], other[2, 0], rank, rows)
    mem_s[rank] = mem_own[:, 0]
    mem_s[1 - rank] = mem_other[:, 0]
    vt_s[...] = v_s[...].astype(F32).T.astype(BF)
    ones = (lax.broadcasted_iota(jnp.int32, (TILE, HEAD_DIM), 1) == 0).astype(BF)
    for tile in range(SEG // TILE):
        here = slice(tile * TILE, (tile + 1) * TILE)
        block = tile * TILE // rows
        query = q_s[here, :]
        wide = jnp.concatenate([query, ones], axis=1)
        spans = chunks_of(tile, 512)
        scores = dot_nt(mem_s[block, 0], query) + mem_bias
        s_s[SEG : SEG + RETR, :] = scores
        top = jnp.max(scores, axis=0, keepdims=True)
        for start, size in spans:
            span = slice(start, start + size)
            if start + size > SEG // 2:
                scores = dot_nt(jnp.concatenate([k_s[span, :], bias[span, :]], axis=1), wide)
            else:
                scores = dot_nt(k_s[span, :], query)
            if start == tile * TILE:
                scores = causal(scores)
            s_s[span, :] = scores
            top = jnp.maximum(top, jnp.max(scores, axis=0, keepdims=True))
        shift = top * SCALE_TWO
        exponent = jnp.exp2(s_s[SEG : SEG + RETR, :] * SCALE_TWO - shift)
        total = jnp.sum(exponent, axis=0, keepdims=True)
        result = dot(mem_s[block, 1].astype(F32).T.astype(BF), exponent.astype(BF))
        for start, size in spans:
            span = slice(start, start + size)
            exponent = jnp.exp2(s_s[span, :] * SCALE_TWO - shift)
            total = total + jnp.sum(exponent, axis=0, keepdims=True)
            result = result + dot(vt_s[:, span], exponent.astype(BF))
        result = result * (1.0 / total)
        turned[0, :, here] = result
        logs[0, :, here] = shift + jnp.log2(total)
        out_s[here, :] = result.T.astype(BF)
    keep[0] = out_s[pl.ds(pl.multiple_of(rank * rows, rows), rows), :]
    send[0] = out_s[pl.ds(pl.multiple_of((1 - rank) * rows, rows), rows), :]


def attend_forward(info, own, other, mem_own, mem_other, bias):
    rows = own.shape[2]
    part = pl.BlockSpec((3, 1, rows, HEAD_DIM), lambda h, info: (0, h, 0, 0))
    mem = pl.BlockSpec((2, 1, RETR, HEAD_DIM), lambda h, info: (0, h, 0, 0))
    half = pl.BlockSpec((1, rows, HEAD_DIM), lambda h, info: (h, 0, 0))
    return pl.pallas_call(
        forward_kernel,
        out_shape=(
            jax.ShapeDtypeStruct((2, rows, HEAD_DIM), BF),
            jax.ShapeDtypeStruct((2, rows, HEAD_DIM), BF),
            jax.ShapeDtypeStruct((2, HEAD_DIM, SEG), F32),
            jax.ShapeDtypeStruct((2, 1, SEG), F32),
        ),
        grid_spec=pltpu.PrefetchScalarGridSpec(
            num_scalar_prefetch=1,
            grid=(2,),
            in_specs=[
                part,
                part,
                mem,
                mem,
                pl.BlockSpec((SEG, HEAD_DIM), lambda h, info: (0, 0)),
            ],
            out_specs=(
                half,
                half,
                pl.BlockSpec((1, HEAD_DIM, SEG), lambda h, info: (h, 0, 0)),
                pl.BlockSpec((1, 1, SEG), lambda h, info: (h, 0, 0)),
            ),
            scratch_shapes=[
                pltpu.VMEM((SEG, HEAD_DIM), BF),
                pltpu.VMEM((SEG, HEAD_DIM), BF),
                pltpu.VMEM((SEG, HEAD_DIM), BF),
                pltpu.VMEM((HEAD_DIM, SEG), BF),
                pltpu.VMEM((2, 2, RETR, HEAD_DIM), BF),
                pltpu.VMEM((SEG + RETR, TILE), F32),
                pltpu.VMEM((SEG, HEAD_DIM), BF),
            ],
        ),
        compiler_params=params(48),
        cost_estimate=cost(5e9, 8 * MIB, 5e6),
        name="attend_forward",
    )(info, own, other, mem_own, mem_other, bias)


def backward_kernel(
    info, own, other, mem_own, mem_other, bias, grad_own, grad_other, turned, logs, cosines, sines,
    keep, send,
    q_s, k_s, v_s, g_s, kt_s, mem_s, dots_s, dq_s, dk_s, dv_s,
):
    rank = info[0]
    rows = own.shape[2]
    mem_bias = jnp.where(info[2] > 0, 0.0, NEGATIVE).astype(F32)
    place(q_s, own[0, 0], other[0, 0], rank, rows)
    place(k_s, own[1, 0], other[1, 0], rank, rows)
    place(v_s, own[2, 0], other[2, 0], rank, rows)
    place(g_s, grad_own[0], grad_other[0], rank, rows)
    mem_s[rank] = mem_own[:, 0]
    mem_s[1 - rank] = mem_other[:, 0]
    kt_s[...] = k_s[...].astype(F32).T.astype(BF)
    dots_s[...] = jnp.sum(g_s[...].astype(F32).T * turned[0], axis=0, keepdims=True)
    dk_s[...] = jnp.zeros_like(dk_s)
    dv_s[...] = jnp.zeros_like(dv_s)
    ones = (lax.broadcasted_iota(jnp.int32, (TILE, HEAD_DIM), 1) == 0).astype(BF)
    for tile in range(SEG // TILE):
        here = slice(tile * TILE, (tile + 1) * TILE)
        block = tile * TILE // rows
        query = q_s[here, :]
        wide = jnp.concatenate([query, ones], axis=1)
        grad = g_s[here, :]
        log = logs[0, :, here]
        dots = dots_s[:, here]
        scores = dot_nt(mem_s[block, 0], query) + mem_bias
        probs = jnp.exp2(scores * SCALE_TWO - log)
        change = (probs * (dot_nt(mem_s[block, 1], grad) - dots)).astype(BF)
        result = dot(mem_s[block, 0].astype(F32).T.astype(BF), change)
        for start, size in chunks_of(tile, 512):
            span = slice(start, start + size)
            keys = k_s[span, :]
            if start + size > SEG // 2:
                scores = dot_nt(jnp.concatenate([keys, bias[span, :]], axis=1), wide)
            else:
                scores = dot_nt(keys, query)
            if start == tile * TILE:
                scores = causal(scores)
            probs = jnp.exp2(scores * SCALE_TWO - log)
            change = (probs * (dot_nt(v_s[span, :], grad) - dots)).astype(BF)
            dv_s[span, :] += dot(probs.astype(BF), grad)
            dk_s[span, :] += dot(change, query)
            result = result + dot(kt_s[:, span], change)
        dq_s[here, :] = turn(result.T * SCALE, cosines[here, :], -sines[here, :]).astype(BF)
    for index in range(2):
        held = pl.ds(pl.multiple_of((rank if index == 0 else 1 - rank) * rows, rows), rows)
        out = keep if index == 0 else send
        out[0, 0] = dq_s[held, :]
        out[1, 0] = turn(dk_s[held, :] * SCALE, cosines[held, :], -sines[held, :]).astype(BF)
        out[2, 0] = dv_s[held, :].astype(BF)


def attend_backward(
    info, own, other, mem_own, mem_other, bias, grad_own, grad_other, turned, logs, cosines, sines
):
    rows = own.shape[2]
    part = pl.BlockSpec((3, 1, rows, HEAD_DIM), lambda h, info: (0, h, 0, 0))
    mem = pl.BlockSpec((2, 1, RETR, HEAD_DIM), lambda h, info: (0, h, 0, 0))
    half = pl.BlockSpec((1, rows, HEAD_DIM), lambda h, info: (h, 0, 0))
    table = pl.BlockSpec((SEG, HEAD_DIM), lambda h, info: (0, 0))
    return pl.pallas_call(
        backward_kernel,
        out_shape=(jax.ShapeDtypeStruct((3, 2, rows, HEAD_DIM), BF),) * 2,
        grid_spec=pltpu.PrefetchScalarGridSpec(
            num_scalar_prefetch=1,
            grid=(2,),
            in_specs=[
                part,
                part,
                mem,
                mem,
                table,
                half,
                half,
                pl.BlockSpec((1, HEAD_DIM, SEG), lambda h, info: (h, 0, 0)),
                pl.BlockSpec((1, 1, SEG), lambda h, info: (h, 0, 0)),
                table,
                table,
            ],
            out_specs=(part, part),
            scratch_shapes=[pltpu.VMEM((SEG, HEAD_DIM), BF)] * 4
            + [
                pltpu.VMEM((HEAD_DIM, SEG), BF),
                pltpu.VMEM((2, 2, RETR, HEAD_DIM), BF),
                pltpu.VMEM((1, SEG), F32),
                pltpu.VMEM((SEG, HEAD_DIM), BF),
                pltpu.VMEM((SEG, HEAD_DIM), F32),
                pltpu.VMEM((SEG, HEAD_DIM), F32),
            ],
        ),
        compiler_params=params(48),
        cost_estimate=cost(12e9, 16 * MIB, 5e6),
        name="attend_backward",
    )(info, own, other, mem_own, mem_other, bias, grad_own, grad_other, turned, logs, cosines, sines)


def middle_kernel(info, one, two, three, four, tokens, weight, gain, middle, normed, o_s):
    rank, group = info[0], info[1]
    pieces = ((one, group, rank), (two, group, 1 - rank), (three, 1 - group, rank), (four, 1 - group, 1 - rank))
    for piece, side, pair in pieces:
        for head in range(2):
            column = pl.multiple_of((side * 4 + pair * 2 + head) * HEAD_DIM, HEAD_DIM)
            o_s[:, pl.ds(column, HEAD_DIM)] = piece[head]
    value = tokens[...].astype(F32) + dot_nt(o_s[...], weight[...])
    middle[...] = value
    inverse = lax.rsqrt(jnp.mean(value * value, axis=1, keepdims=True) + EPS)
    normed[...] = (value * inverse * gain[...]).astype(BF)


def middle_call(info, pieces, tokens, weight, gain):
    rows = tokens.shape[0]
    piece = pl.BlockSpec((2, TILE, HEAD_DIM), lambda i, info: (0, i, 0))
    wide = pl.BlockSpec((TILE, D), lambda i, info: (i, 0))
    return pl.pallas_call(
        middle_kernel,
        out_shape=(
            jax.ShapeDtypeStruct((rows, D), F32),
            jax.ShapeDtypeStruct((rows, D), BF),
        ),
        grid_spec=pltpu.PrefetchScalarGridSpec(
            num_scalar_prefetch=1,
            grid=(rows // TILE,),
            in_specs=[piece] * 4
            + [
                wide,
                pl.BlockSpec((D, D), lambda i, info: (0, 0)),
                pl.BlockSpec((1, D), lambda i, info: (0, 0)),
            ],
            out_specs=(wide, wide),
            scratch_shapes=[pltpu.VMEM((TILE, D), BF)],
        ),
        compiler_params=params(40),
        cost_estimate=cost(2 * rows * D * D, 12 * MIB),
        name="middle",
    )(info, *pieces, tokens, weight, gain)


def feed_kernel(normed, upstream, gate_w, up_w, down_w, hidden, gate_grad, up_grad, back):
    gate = dot(normed[...], gate_w[...])
    up_part = dot(normed[...], up_w[...])
    sigma = jax.nn.sigmoid(gate)
    silu = gate * sigma
    hidden[...] = (silu * up_part).astype(BF)
    grad = dot(upstream[...], down_w[...])
    grad_gate = (grad * up_part * sigma * (1.0 + gate * (1.0 - sigma))).astype(BF)
    grad_up = (grad * silu).astype(BF)
    gate_grad[...] = grad_gate
    up_grad[...] = grad_up
    back[...] = (dot_nt(grad_gate, gate_w[...]) + dot_nt(grad_up, up_w[...])).astype(BF)


def feed_call(normed, upstream, weights, first, count):
    width = weights.shape[1] // 3
    whole = lambda index: pl.BlockSpec((D, width), lambda i: (0, index), pipeline_mode=pl.Buffered(1))
    source = pl.BlockSpec((TILE, D), lambda i: (i + first // TILE, 0))
    narrow = pl.BlockSpec((TILE, width), lambda i: (i, 0))
    return pl.pallas_call(
        feed_kernel,
        out_shape=(jax.ShapeDtypeStruct((count, width), BF),) * 3
        + (jax.ShapeDtypeStruct((count, D), BF),),
        grid=(count // TILE,),
        in_specs=[source, source, whole(0), whole(1), whole(2)],
        out_specs=(narrow, narrow, narrow, pl.BlockSpec((TILE, D), lambda i: (i, 0))),
        compiler_params=params(48),
        cost_estimate=cost(10 * count * D * width, 9 * MIB + 16 * count * D),
        name="feed",
    )(normed, upstream, weights, weights, weights)


def out_kernel(hidden, down_w, out):
    out[...] = dot_nt(hidden[...], down_w[...]).astype(BF)


def out_call(hidden, weights):
    count, width = hidden.shape
    return pl.pallas_call(
        out_kernel,
        out_shape=jax.ShapeDtypeStruct((count, D), BF),
        grid=(count // TILE,),
        in_specs=[
            pl.BlockSpec((TILE, width), lambda i: (i, 0)),
            pl.BlockSpec((D, width), lambda i: (0, 2), pipeline_mode=pl.Buffered(1)),
        ],
        out_specs=pl.BlockSpec((TILE, D), lambda i: (i, 0)),
        compiler_params=params(40),
        cost_estimate=cost(2 * count * D * width, 6 * MIB),
        name="feed_out",
    )(hidden, weights)


def feed_weight_kernel(normed, upstream, hidden, gate_grad, up_grad, out):
    width = hidden.shape[1]
    left = normed[...].astype(F32).T.astype(BF)
    out[:, :width] = dot(left, gate_grad[...]).astype(BF)
    out[:, width : 2 * width] = dot(left, up_grad[...]).astype(BF)
    left = upstream[...].astype(F32).T.astype(BF)
    out[:, 2 * width :] = dot(left, hidden[...]).astype(BF)


def feed_weight_call(normed, upstream, hidden, gate_grad, up_grad):
    rows, width = hidden.shape
    left = pl.BlockSpec((rows, TILE), lambda i: (0, i))
    whole = pl.BlockSpec((rows, width), lambda i: (0, 0), pipeline_mode=pl.Buffered(1))
    return pl.pallas_call(
        feed_weight_kernel,
        out_shape=jax.ShapeDtypeStruct((D, 3 * width), BF),
        grid=(D // TILE,),
        in_specs=[left, left, whole, whole, whole],
        out_specs=pl.BlockSpec((TILE, 3 * width), lambda i: (i, 0)),
        compiler_params=params(48),
        cost_estimate=cost(6 * rows * D * width, 22 * MIB),
        name="feed_weights",
    )(normed, upstream, hidden, gate_grad, up_grad)


def residual_kernel(info, middle, back_own, back_other, upstream, gain, weight, grad, low, keep, send, gain_grad):
    rank = info[0]
    value = middle[...]
    back = back_own[...].astype(F32) + back_other[...].astype(F32)
    inverse = lax.rsqrt(jnp.mean(value * value, axis=1, keepdims=True) + EPS)
    scaled = gain[...] * back
    inner = jnp.mean(scaled * value, axis=1, keepdims=True)
    total = upstream[...].astype(F32) + inverse * scaled - value * (inverse**3 * inner)
    grad[...] = total
    branch = total.astype(BF)
    low[...] = branch

    @pl.when(pl.program_id(0) == 0)
    def _():
        gain_grad[...] = jnp.zeros_like(gain_grad)

    gain_grad[...] += jnp.sum(back * value * inverse, axis=0, keepdims=True)
    for out, pair in ((keep, rank), (send, 1 - rank)):
        column = pl.multiple_of(pair * 2 * HEAD_DIM, 2 * HEAD_DIM)
        result = dot(branch, weight[:, pl.ds(column, 2 * HEAD_DIM)]).astype(BF)
        for head in range(2):
            out[head] = result[:, head * HEAD_DIM : (head + 1) * HEAD_DIM]


def residual_call(info, middle, back_own, back_other, upstream, gain, weight):
    rows = middle.shape[0]
    half = weight.shape[1] // 2
    wide = pl.BlockSpec((TILE, D), lambda i, info: (i, 0))
    row = pl.BlockSpec((1, D), lambda i, info: (0, 0))
    piece = pl.BlockSpec((2, TILE, HEAD_DIM), lambda i, info: (0, i, 0))
    return pl.pallas_call(
        residual_kernel,
        out_shape=(
            jax.ShapeDtypeStruct((rows, D), F32),
            jax.ShapeDtypeStruct((rows, D), BF),
            jax.ShapeDtypeStruct((2, rows, HEAD_DIM), BF),
            jax.ShapeDtypeStruct((2, rows, HEAD_DIM), BF),
            jax.ShapeDtypeStruct((1, D), F32),
        ),
        grid_spec=pltpu.PrefetchScalarGridSpec(
            num_scalar_prefetch=1,
            grid=(rows // TILE,),
            in_specs=[
                wide,
                wide,
                wide,
                wide,
                row,
                pl.BlockSpec((D, half), lambda i, info: (0, info[1])),
            ],
            out_specs=(wide, wide, piece, piece, row),
        ),
        compiler_params=params(40),
        cost_estimate=cost(2 * rows * D * half, 18 * MIB),
        name="residual",
    )(info, middle, back_own, back_other, upstream, gain, weight)


def back_kernel(info, own, other, weight, tokens, out, joined, gain_grad):
    rank = info[0]
    for piece, pair in ((own, rank), (other, 1 - rank)):
        for part in range(3):
            for head in range(2):
                column = pl.multiple_of((part * 4 + pair * 2 + head) * HEAD_DIM, HEAD_DIM)
                joined[:, pl.ds(column, HEAD_DIM)] = piece[part, head]
    back = dot_nt(joined[...], weight[...])
    out[...] = back.astype(BF)

    @pl.when(pl.program_id(0) == 0)
    def _():
        gain_grad[...] = jnp.zeros_like(gain_grad)

    value = tokens[...].astype(F32)
    inverse = lax.rsqrt(jnp.mean(value * value, axis=1, keepdims=True) + EPS)
    gain_grad[...] += jnp.sum(back * value * inverse, axis=0, keepdims=True)


def back_call(info, own, other, weights, tokens):
    rows = tokens.shape[0]
    width = 3 * 4 * HEAD_DIM
    piece = pl.BlockSpec((3, 2, TILE, HEAD_DIM), lambda i, info: (0, 0, i, 0))
    wide = pl.BlockSpec((TILE, D), lambda i, info: (i, 0))
    return pl.pallas_call(
        back_kernel,
        out_shape=(
            jax.ShapeDtypeStruct((rows, D), BF),
            jax.ShapeDtypeStruct((rows, width), BF),
            jax.ShapeDtypeStruct((1, D), F32),
        ),
        grid_spec=pltpu.PrefetchScalarGridSpec(
            num_scalar_prefetch=1,
            grid=(rows // TILE,),
            in_specs=[
                piece,
                piece,
                pl.BlockSpec((D, width), lambda i, info: (0, 0)),
                wide,
            ],
            out_specs=(
                wide,
                pl.BlockSpec((TILE, width), lambda i, info: (i, 0)),
                pl.BlockSpec((1, D), lambda i, info: (0, 0)),
            ),
        ),
        compiler_params=params(40),
        cost_estimate=cost(2 * rows * D * width, 13 * MIB),
        name="back",
    )(info, own, other, weights, tokens)


def attend_weight_kernel(info, normed, joined, low, one, two, out, o_s):
    @pl.when(pl.program_id(0) == 0)
    def _():
        for piece, pair in ((one, info[0]), (two, 1 - info[0])):
            for head in range(2):
                column = pl.multiple_of((pair * 2 + head) * HEAD_DIM, HEAD_DIM)
                o_s[:, pl.ds(column, HEAD_DIM)] = piece[head]

    width = joined.shape[1]
    left = normed[...].astype(F32).T.astype(BF)
    out[:, :width] = dot(left, joined[...]).astype(BF)
    left = low[...].astype(F32).T.astype(BF)
    out[:, width:] = dot(left, o_s[...]).astype(BF)


def attend_weight_call(info, normed, joined, low, one, two):
    rows, width = joined.shape
    half = 4 * HEAD_DIM
    left = pl.BlockSpec((rows, TILE), lambda i, info: (0, i))
    piece = pl.BlockSpec((2, rows, HEAD_DIM), lambda i, info: (0, 0, 0))
    return pl.pallas_call(
        attend_weight_kernel,
        out_shape=jax.ShapeDtypeStruct((D, width + half), BF),
        grid_spec=pltpu.PrefetchScalarGridSpec(
            num_scalar_prefetch=1,
            grid=(D // TILE,),
            in_specs=[
                left,
                pl.BlockSpec((rows, width), lambda i, info: (0, 0)),
                left,
                piece,
                piece,
            ],
            out_specs=pl.BlockSpec((TILE, width + half), lambda i, info: (i, 0)),
            scratch_shapes=[pltpu.VMEM((rows, half), BF)],
        ),
        compiler_params=params(40),
        cost_estimate=cost(2 * rows * D * (width + half), 13 * MIB),
        name="attend_weights",
    )(info, normed, joined, low, one, two)


def input_kernel(grad, back_own, back_other, tokens, gain, out):
    value = tokens[...].astype(F32)
    back = back_own[...].astype(F32) + back_other[...].astype(F32)
    inverse = lax.rsqrt(jnp.mean(value * value, axis=1, keepdims=True) + EPS)
    scaled = gain[...] * back
    inner = jnp.mean(scaled * value, axis=1, keepdims=True)
    out[...] = (grad[...] + inverse * scaled - value * (inverse**3 * inner)).astype(BF)


def input_call(grad, back_own, back_other, tokens, gain):
    rows = tokens.shape[0]
    wide = pl.BlockSpec((TILE, D), lambda i: (i, 0))
    return pl.pallas_call(
        input_kernel,
        out_shape=jax.ShapeDtypeStruct((rows, D), BF),
        grid=(rows // TILE,),
        in_specs=[wide, wide, wide, wide, pl.BlockSpec((1, D), lambda i: (0, 0))],
        out_specs=wide,
        compiler_params=params(32),
        cost_estimate=cost(12 * rows * D, 12 * MIB),
        name="input_grad",
    )(grad, back_own, back_other, tokens, gain)


def body(
    tokens,
    cotangent,
    proj_qkv,
    proj_out,
    proj_gate_up,
    proj_down,
    norm_gains,
    first_qkv,
    first_out,
    first_gate_up,
    first_down,
    first_gains,
    second_qkv,
    second_out,
    second_gate_up,
    second_down,
    second_gains,
    cache,
    doc_segments,
    padding,
    retrieval,
):
    rows = tokens.shape[0]
    count = lax.axis_size("dp")
    device = lax.axis_index("dp")
    group = lax.axis_index("mp")
    rank = device % 2
    segment = device // 2
    shard = proj_qkv.shape[1]
    local = proj_qkv.shape[2]
    hidden_here = proj_gate_up.shape[2]
    core_pairs = [(i, i ^ 1) for i in range(count)]

    def across(value):
        return lax.ppermute(value, "mp", [(0, 1), (1, 0)])

    def beside(value):
        return lax.ppermute(value, "dp", core_pairs)

    gain_columns = jnp.pad(norm_gains.astype(BF).T, ((0, 0), (0, HEAD_DIM - 2)))
    shard_one = jnp.concatenate(
        [proj_qkv[part].astype(BF) for part in range(3)] + [gain_columns], axis=1
    )
    out_own = proj_out.astype(BF).T
    out_other = across(out_own)
    out_both = [
        jnp.where(group == 0, out_own, out_other),
        jnp.where(group == 0, out_other, out_own),
    ]
    shard_two = jnp.concatenate(
        [proj_gate_up[0].astype(BF), proj_gate_up[1].astype(BF), proj_down.astype(BF).T], axis=1
    )
    weights_one = lax.all_gather(shard_one, "dp", axis=0, tiled=True)
    weights_two = lax.all_gather(shard_two, "dp", axis=0, tiled=True)
    weights_out = lax.all_gather(jnp.concatenate(out_both, axis=1), "dp", axis=0, tiled=True)
    gains = weights_one[:, 3 * local : 3 * local + 2].astype(F32).T
    gain_one, gain_two = gains[0:1], gains[1:2]

    starts = jnp.cumsum(doc_segments) - doc_segments
    memory_on = jnp.logical_not(jnp.any(starts == segment))
    info = jnp.stack(
        [rank, group, memory_on.astype(jnp.int32), 1 - rank]
    ).astype(jnp.int32)
    cosines, sines = rope_tables(SEG)
    valid = lax.dynamic_slice_in_dim(padding, segment * SEG, SEG)
    lane = jnp.arange(HEAD_DIM, dtype=jnp.int32)[None, :]
    bias = jnp.where((valid[:, None] == 0) & (lane == 0), NEGATIVE, 0.0).astype(BF)
    fetched = cache[retrieval[0]].reshape(RETR, 2, 2, 2, HEAD_DIM).transpose(2, 1, 3, 0, 4)
    mem_own = lax.dynamic_index_in_dim(fetched, rank, keepdims=False)
    mem_other = beside(lax.dynamic_index_in_dim(fetched, 1 - rank, keepdims=False))

    inputs = tokens.astype(F32)
    inverse_one = lax.rsqrt(jnp.mean(inputs * inputs, axis=-1, keepdims=True) + EPS)
    normed_one = (inputs * inverse_one * gain_one).astype(BF)

    send = project_pair(info, normed_one, weights_one, cosines, sines, 3)
    other = beside(send)
    own = project_pair(info, normed_one, weights_one, cosines, sines, 0)
    out_keep, out_send, turned, logs = attend_forward(info, own, other, mem_own, mem_other, bias)
    out_recv = beside(out_send)
    pieces = (out_keep, out_recv, across(out_keep), across(out_recv))
    middle, normed_two = middle_call(info, pieces, tokens, weights_out, gain_two)

    half = rows // 2
    feeds = [feed_call(normed_two, cotangent, weights_two, first, half) for first in (0, half)]
    backs = [feed[3] for feed in feeds]
    backs_other = [across(back) for back in backs]
    hidden, grad_gate, grad_up = (
        jnp.concatenate([feed[index] for feed in feeds], axis=0) for index in range(3)
    )
    feed_part = out_call(hidden, weights_two)
    feed_other = across(feed_part)
    feed_grads = feed_weight_call(normed_two, cotangent, hidden, grad_gate, grad_up)
    back_two = jnp.concatenate(backs, axis=0)
    back_two_other = jnp.concatenate(backs_other, axis=0)
    grad_middle, grad_low, grad_keep, grad_send, gain_two_grad = residual_call(
        info, middle, back_two, back_two_other, cotangent, gain_two, weights_out
    )
    grad_other = beside(grad_send)
    block_out = (middle + (feed_part.astype(F32) + feed_other.astype(F32))).astype(BF)

    d_keep, d_send = attend_backward(
        info, own, other, mem_own, mem_other, bias, grad_keep, grad_other, turned, logs, cosines, sines
    )
    d_other = beside(d_send)
    back_one, joined, gain_one_grad = back_call(info, d_keep, d_other, weights_one, tokens)
    back_one_other = across(back_one)
    attend_grads = attend_weight_call(info, normed_one, joined, grad_low, out_keep, out_recv)
    gain_grads = jnp.pad(
        jnp.concatenate([gain_one_grad, gain_two_grad], axis=0).astype(BF).T,
        ((0, 0), (0, HEAD_DIM - 2)),
    )
    input_grad = input_call(grad_middle, back_one, back_one_other, tokens, gain_one)

    feed_sum = lax.psum_scatter(feed_grads, "dp", scatter_dimension=0, tiled=True)
    attend_sum = lax.psum_scatter(
        jnp.concatenate([attend_grads, gain_grads], axis=1), "dp", scatter_dimension=0, tiled=True
    )
    feed_sum, attend_sum = feed_sum.astype(F32), attend_sum.astype(F32)
    gate_up_sum = jnp.stack([feed_sum[:, :hidden_here], feed_sum[:, hidden_here : 2 * hidden_here]])
    down_sum = feed_sum[:, 2 * hidden_here :].T
    qkv_sum = jnp.stack([attend_sum[:, part * local : (part + 1) * local] for part in range(3)])
    out_sum = attend_sum[:, 3 * local : 4 * local].T
    gains_sum = attend_sum[:, 4 * local : 4 * local + 2].T
    gains_sum = jnp.concatenate([gains_sum[0:1] + across(gains_sum[0:1]), gains_sum[1:2]], axis=0)

    qkv_first, qkv_second, qkv_new = adamw(
        proj_qkv, qkv_sum, first_qkv, second_qkv, 0.5 / math.sqrt(D)
    )
    out_first, out_second, out_new = adamw(
        proj_out, out_sum, first_out, second_out, 0.5 / math.sqrt(max(1, 4 * D // SEG))
    )
    gate_up_first, gate_up_second, gate_up_new = adamw(
        proj_gate_up, gate_up_sum, first_gate_up, second_gate_up, 0.5 / math.sqrt(D)
    )
    down_first, down_second, down_new = adamw(
        proj_down, down_sum, first_down, second_down, 0.5 / math.sqrt(FF)
    )
    gains_first, gains_second, gains_new = adamw(
        norm_gains, gains_sum, first_gains, second_gains, 0.6
    )
    return (
        block_out,
        input_grad,
        qkv_first,
        qkv_second,
        qkv_new,
        out_first,
        out_second,
        out_new,
        gate_up_first,
        gate_up_second,
        gate_up_new,
        down_first,
        down_second,
        down_new,
        gains_first,
        gains_second,
        gains_new,
    )


def solution(mesh):
    return jax.shard_map(
        body,
        mesh=mesh,
        in_specs=(
            P("dp", None),
            P("dp", None),
            P(None, "dp", "mp"),
            P("mp", "dp"),
            P(None, "dp", "mp"),
            P("mp", "dp"),
            P(None, "dp"),
            P(None, "dp", "mp"),
            P("mp", "dp"),
            P(None, "dp", "mp"),
            P("mp", "dp"),
            P(None, "dp"),
            P(None, "dp", "mp"),
            P("mp", "dp"),
            P(None, "dp", "mp"),
            P("mp", "dp"),
            P(None, "dp"),
            P("dp", None, "mp"),
            P(),
            P(),
            P("dp", None),
        ),
        out_specs=(
            P("dp", None),
            P("dp", None),
            P(None, "dp", "mp"),
            P(None, "dp", "mp"),
            P(None, "dp", "mp"),
            P("mp", "dp"),
            P("mp", "dp"),
            P("mp", "dp"),
            P(None, "dp", "mp"),
            P(None, "dp", "mp"),
            P(None, "dp", "mp"),
            P("mp", "dp"),
            P("mp", "dp"),
            P("mp", "dp"),
            P(None, "dp"),
            P(None, "dp"),
            P(None, "dp"),
        ),
        check_vma=False,
    )
```

time: 1340 us -> 510 us (0.38)
  waiting for transfers between devices: 900 us -> 267 us
  matrix products: 215 us -> 0 us
  Pallas kernels: 0 us -> 117 us
  other arithmetic: 115 us -> 39.6 us
  blocking collectives: 23 us -> 0 us
    psum x3 -> x0, waiting for transfers between devices: 310 us -> none  [the longest x1 121 us: body(): lax.psum(jnp.dot(attended, out_w, preferred_element_type=jnp.float32), 'mp')]
    unnamed x14 -> x5, waiting for transfers between devices: 219 us -> 0.08 us
    dot_general x43 -> x0, matrix products: 215 us -> none  [the longest x8 44.3 us: head_scores(): jnp.einsum('qd,kd->qk', query, keys, preferred_element_type=jnp.float32)]
    reduce_scatter x3 -> x2, waiting for transfers between devices: 260 us -> 45.3 us  [the longest x1 45.3 us: body(): lax.psum_scatter(feed_grads, 'dp', scatter_dimension=0, tiled=True)]
    ppermute x2 -> x13, waiting for transfers between devices: 0.01 us -> 146 us  [the longest x8 141 us: across(): return lax.ppermute(value, 'mp', [(0, 1), (1, 0)])]
    pallas_call x0 -> x13, Pallas kernels: none -> 117 us  [the longest x2 26.3 us: feed_call(): pl.pallas_call(feed_kernel, out_shape=(jax.ShapeDtypeStruct((count, width...]
    convert_element_type x12 -> x7, other arithmetic: 48.3 us -> 8.13 us  [the longest x1 2.46 us: body(): (middle + (feed_part.astype(F32) + feed_other.astype(F32))).astype(BF)]
    all_gather x4 -> x3, waiting for transfers between devices: 110 us -> 75.6 us  [the longest x1 42 us: body(): weights_two = lax.all_gather(shard_two, 'dp', axis=0, tiled=True)]
  transfers between devices with their start and end apart: 14 -> 18, of which waited for: 11 -> 13; matrix products, arithmetic and copies ran while one was open for 12% -> 7% of each run, Pallas kernels for 0% -> 13%
where the time goes in v1:
time: 510 us; the launch traced here: 504 us
  waiting for transfers between devices  267 us (52%)
  Pallas kernels  117 us (23%)
  local copies, waits for them, and re-layouts  52.5 us (10%)
  other arithmetic  39.6 us (8%)
  between operations  15.3 us (3%)
  starting transfers between devices  11.8 us (2%)
    ppermute x8, waiting for transfers between devices, across(): return lax.ppermute(value, 'mp', [(0, 1), (1, 0)])  141 us
    unnamed x146, local copies, waits for them, and re-layouts  48.7 us
    reduce_scatter x1, waiting for transfers between devices, body(): lax.psum_scatter(feed_grads, 'dp', scatter_dimension=0, tiled=True)  45.3 us
    all_gather x1, waiting for transfers between devices, body(): weights_two = lax.all_gather(shard_two, 'dp', axis=0, tiled=True)  42 us
    all_gather x1, waiting for transfers between devices, body(): weights_one = lax.all_gather(shard_one, 'dp', axis=0, tiled=True)  32.2 us
    pallas_call x2, Pallas kernels, feed_call(): pl.pallas_call(feed_kernel, out_shape=(jax.ShapeDtypeStruct((count, width...  26.3 us
    pallas_call x1, Pallas kernels, attend_backward(): pl.pallas_call(backward_kernel, out_shape=(jax.ShapeDtypeStruct((3, 2, ro...  20.1 us
    pallas_call x1, Pallas kernels, feed_weight_call(): pl.pallas_call(feed_weight_kernel, out_shape=jax.ShapeDtypeStruct((D, 3 *...  16.6 us
  transfers between devices with their start and end apart: 18, of which 13 were waited for; matrix products, arithmetic and copies ran while one was open for 7% of the time, Pallas kernels for 13%

profile of v1, /device:TPU:0, one launch (start us, length us, event | category | flops | bytes accessed | tf_op | source)
XLA Modules:
  0.0 503.6 jit_solution(7591547656882083111)
XLA Ops:
  11.0 3.0 collective-permute-start.5
  14.0 2.2 collective-permute-done.5
  20.6 2.1 fusion.2
  22.7 3.7 fusion.9
  28.0 32.2 %all-gather.4.cloned.1.call-done.weight = bf16[1024,1664]{1,0:T(8,128)(2,1)} async-done(((bf16[64,1664]{1,0:T(8,128)(2,1)}), bf16[1024,1664]{1,0:T(8,128)(2,1)}) %all-gather.4.cloned.1.call-update) | async-done | bytes 3407888 | tf_op jit(solution)/shard_map/all_gather | solution.py:671
  60.2 1.8 slice_convert_fusion
  63.2 2.3 fusion.4.normed
  65.8 1.7 copy-done.15
  67.5 4.7 project_pair.3
  77.8 2.0 copy-done.13
  81.0 3.8 project_pair.2.own
  84.8 13.0 %attend_forward.1 = (bf16[2,1024,128]{2,1,0:T(8,128)(2,1)S(1)}, bf16[2,1024,128]{2,1,0:T(8,128)(2,1)S(1)}, f32[2,128,2048]{2,1,0:T(8,128)}, f32[2,1,2048]{2,1,0:T(1,128)S(1)}) custom-call(s32[4]{0:T(128)S(1)} %pad_add_fusion.info, bf16[3,2,1024,128]{3,2,1,0:T(8,128)(2,1)S(1)} %project_pair.2.own, bf16[3,2,1024,128]{3,2,1,0:T(8,128)(2,1)} %collective-permute-done.other, ...), custom_call_target="tpu_custom_call" | custom-call | flops 5000000000 | bytes 8388608 | tf_op jit(solution)/shard_map/attend_forward/pallas_call | solution.py:185
  103.3 9.4 %collective-permute-done.3.three = bf16[2,1024,128]{2,1,0:T(8,128)(2,1)S(1)} collective-permute-done((bf16[2,1024,128]{2,1,0:T(8,128)(2,1)S(1)}, bf16[2,1024,128]{2,1,0:T(8,128)(2,1)S(1)}, u32[]{:S(2)}, u32[]{:S(2)}) %collective-permute-start.3) | collective-permute-done | bytes 524320 | tf_op jit(solution)/shard_map/ppermute | solution.py:653
  113.6 9.8 %collective-permute-done.4.four = bf16[2,1024,128]{2,1,0:T(8,128)(2,1)S(1)} collective-permute-done((bf16[2,1024,128]{2,1,0:T(8,128)(2,1)S(1)}, bf16[2,1024,128]{2,1,0:T(8,128)(2,1)S(1)}, u32[]{:S(2)}, u32[]{:S(2)}) %collective-permute-start.4) | collective-permute-done | bytes 524320 | tf_op jit(solution)/shard_map/ppermute | solution.py:653
  124.1 1.6 copy-done.4
  125.7 1.6 copy-done.23
  131.5 4.6 middle.1
  136.2 2.1 copy-done.10
  139.5 42.0 %all-gather.8.cloned.1.call-done.gate_w.up_w.down_w = bf16[1024,4224]{1,0:T(8,128)(2,1)} async-done(((bf16[64,4224]{1,0:T(8,128)(2,1)}), bf16[1024,4224]{1,0:T(8,128)(2,1)}) %all-gather.8.cloned.1.call-update) | async-done | bytes 8650768 | tf_op jit(solution)/shard_map/all_gather | solution.py:672
  181.5 13.3 %feed.3 = (bf16[512,1408]{1,0:T(8,128)(2,1)S(1)}, bf16[512,1408]{1,0:T(8,128)(2,1)S(1)}, bf16[512,1408]{1,0:T(8,128)(2,1)S(1)}, bf16[512,1024]{1,0:T(8,128)(2,1)S(1)}) custom-call(bf16[1024,1024]{1,0:T(8,128)(2,1)} %copy-done.18, bf16[1024,1024]{1,0:T(8,128)(2,1)} %upstream.7, bf16[1024,4224]{1,0:T(8,128)(2,1)} %all-gather.8.cloned.1.call-done.gate_w.up_w.down_w, ...), custom_call_target="tpu_custom_call" | custom-call | flops 7381975040 | bytes 17825792 | tf_op jit(solution)/shard_map/feed/pallas_call | solution.py:383
  199.6 13.1 %feed.2 = (bf16[512,1408]{1,0:T(8,128)(2,1)S(1)}, bf16[512,1408]{1,0:T(8,128)(2,1)S(1)}, bf16[512,1408]{1,0:T(8,128)(2,1)S(1)}, bf16[512,1024]{1,0:T(8,128)(2,1)S(1)}) custom-call(bf16[1024,1024]{1,0:T(8,128)(2,1)} %copy-done.18, bf16[1024,1024]{1,0:T(8,128)(2,1)} %upstream.7, bf16[1024,4224]{1,0:T(8,128)(2,1)} %all-gather.8.cloned.1.call-done.gate_w.up_w.down_w, ...), custom_call_target="tpu_custom_call" | custom-call | flops 7381975040 | bytes 17825792 | tf_op jit(solution)/shard_map/feed/pallas_call | solution.py:383
  214.6 9.5 %collective-permute-done.8 = bf16[512,1024]{1,0:T(8,128)(2,1)S(1)} collective-permute-done((bf16[512,1024]{1,0:T(8,128)(2,1)S(1)}, bf16[512,1024]{1,0:T(8,128)(2,1)S(1)}, u32[]{:S(2)}, u32[]{:S(2)}) %collective-permute-start.8) | collective-permute-done | bytes 1048608 | tf_op jit(solution)/shard_map/ppermute | solution.py:653
  224.1 21.8 %collective-permute-done.7 = bf16[512,1024]{1,0:T(8,128)(2,1)S(1)} collective-permute-done((bf16[512,1024]{1,0:T(8,128)(2,1)S(1)}, bf16[512,1024]{1,0:T(8,128)(2,1)S(1)}, u32[]{:S(2)}, u32[]{:S(2)}) %collective-permute-start.7) | collective-permute-done | bytes 1048608 | tf_op jit(solution)/shard_map/ppermute | solution.py:653
  246.2 7.4 %residual.1 = (f32[1024,1024]{1,0:T(8,128)}, bf16[1024,1024]{1,0:T(8,128)(2,1)S(1)}, bf16[2,1024,128]{2,1,0:T(8,128)(2,1)S(1)}, bf16[2,1024,128]{2,1,0:T(8,128)(2,1)S(1)}, f32[1,1024]{1,0:T(1,128)S(1)}) custom-call(s32[4]{0:T(128)S(1)} %pad_add_fusion.info, f32[1024,1024]{1,0:T(8,128)} %copy-done.10, bf16[1024,1024]{1,0:T(8,128)(2,1)S(1)} %pad_maximum_fusion.2.back_own, ...), custom_call_target="tpu_custom_call" | custom-call | flops 1073741824 | bytes 18874368 | tf_op jit(solution)/shard_map/residual/pallas_call | solution.py:472
  255.7 1.9 collective-permute-done.9.grad_other
  259.7 20.1 %attend_backward.1 = (bf16[3,2,1024,128]{3,2,1,0:T(8,128)(2,1)S(1)}, bf16[3,2,1024,128]{3,2,1,0:T(8,128)(2,1)}) custom-call(s32[4]{0:T(128)S(1)} %pad_add_fusion.info, bf16[3,2,1024,128]{3,2,1,0:T(8,128)(2,1)} %copy-done.27, bf16[3,2,1024,128]{3,2,1,0:T(8,128)(2,1)} %collective-permute-done.other, bf16[2,2,128,128]{3,2,1,0:T(8,128)(2,1)S(1)} %bitcast.70, ...), custom_call_target="tpu_custom_call" | custom-call | flops 12000000000 | bytes 16777216 | tf_op jit(solution)/shard_map/attend_backward/pallas_call | solution.py:287
  279.9 3.5 collective-permute-done.10.other
  283.4 6.5 %back.1 = (bf16[1024,1024]{1,0:T(8,128)(2,1)S(1)}, bf16[1024,1536]{1,0:T(8,128)(2,1)S(1)}, f32[1,1024]{1,0:T(1,128)S(1)}) custom-call(s32[4]{0:T(128)S(1)} %pad_add_fusion.info, bf16[3,2,1024,128]{3,2,1,0:T(8,128)(2,1)S(1)} %get-tuple-element.54.own, bf16[3,2,1024,128]{3,2,1,0:T(8,128)(2,1)S(1)} %collective-permute-done.10.other, ...), custom_call_target="tpu_custom_call" | custom-call | flops 3221225472 | bytes 13631488 | tf_op jit(solution)/shard_map/back/pallas_call | solution.py:524
  291.2 1.7 copy-done.55
  294.8 1.6 copy-done.42
  296.4 1.9 copy-done.56
  298.3 6.6 %attend_weights.1 = bf16[1024,2048]{1,0:T(8,128)(2,1)S(1)} custom-call(s32[4]{0:T(128)S(1)} %pad_add_fusion.info, bf16[1024,1024]{1,0:T(8,128)(2,1)S(1)} %copy-done.9, bf16[1024,1536]{1,0:T(8,128)(2,1)S(1)} %copy-done.56, bf16[1024,1024]{1,0:T(8,128)(2,1)S(1)} %copy-done.42, bf16[2,1024,128]{2,1,0:T(8,128)(2,1)S(1)} %copy-done.45, ...), custom_call_target="tpu_custom_call" | custom-call | flops 4294967296 | bytes 13631488 | tf_op jit(solution)/shard_map/attend_weights/pallas_call | solution.py:572
  304.9 2.3 fusion.1
  307.3 1.6 constant_dynamic-update-slice_fusion.1
  309.9 1.9 pad_maximum_fusion.gate_grad
  313.2 1.8 pad_maximum_fusion.1.up_grad
  315.9 16.6 %feed_weights.1 = bf16[1024,4224]{1,0:T(8,128)(2,1)} custom-call(bf16[1024,1024]{1,0:T(8,128)(2,1)S(1)} %copy-done.19, bf16[1024,1024]{1,0:T(8,128)(2,1)S(1)} %copy-done.3, bf16[1024,1408]{1,0:T(8,128)(2,1)} %copy-done.20, bf16[1024,1408]{1,0:T(8,128)(2,1)} %pad_maximum_fusion.gate_grad, bf16[1024,1408]{1,0:T(8,128)(2,1)} %pad_maximum_fusion.1.up_grad), custom_call_target="tpu_custom_call" | custom-call | flops 8858370048 | bytes 23068672 | tf_op jit(solution)/shard_map/feed_weights/pallas_call | solution.py:430
  332.6 4.0 copy-done.2
  336.6 1.8 copy-done.21
  338.4 4.3 feed_out.1
  344.8 46.4 %collective-permute-done.6 = bf16[1024,1024]{1,0:T(8,128)(2,1)S(1)} collective-permute-done((bf16[1024,1024]{1,0:T(8,128)(2,1)S(1)}, bf16[1024,1024]{1,0:T(8,128)(2,1)S(1)}, u32[]{:S(2)}, u32[]{:S(2)}) %collective-permute-start.6) | collective-permute-done | bytes 2097184 | tf_op jit(solution)/shard_map/ppermute | solution.py:653
  391.3 2.5 add_convert_fusion
  393.7 41.7 %collective-permute-done.11.back_other = bf16[1024,1024]{1,0:T(8,128)(2,1)S(1)} collective-permute-done((bf16[1024,1024]{1,0:T(8,128)(2,1)S(1)}, bf16[1024,1024]{1,0:T(8,128)(2,1)S(1)}, u32[]{:S(2)}, u32[]{:S(2)}) %collective-permute-start.11) | collective-permute-done | bytes 2097184 | tf_op jit(solution)/shard_map/ppermute | solution.py:653
  435.4 3.2 input_grad.1
  441.0 2.4 multiply_subtract_fusion.1
  445.1 45.3 %reduce-scatter.5.cloned.1.call-done = bf16[64,4224]{1,0:T(8,128)(2,1)} async-done(((bf16[1024,4224]{1,0:T(8,128)(2,1)}), bf16[64,4224]{1,0:T(8,128)(2,1)}) %reduce-scatter.5.cloned.1.call-update) | async-done | bytes 540688 | tf_op jit(solution)/shard_map/reduce_scatter | solution.py:733
  491.6 2.3 multiply_subtract_fusion.2
  493.9 3.0 multiply_subtract_fusion
  (208 shorter events, 54.7 us)
Async XLA Ops:
  7.2 65.3 %copy-start = (bf16[1024,2,512]{2,1,0:T(2,128)(2,1)S(1)}, bf16[1024,2,512]{2,1,0:T(2,128)(2,1)}, u32[]{:S(2)}) copy-start(bf16[1024,2,512]{2,1,0:T(2,128)(2,1)} %param.38) | copy-start | bytes 6291460
  7.2 10.7 %copy-start.57 = (f32[2,64,1408]{2,1,0:T(8,128)S(1)}, f32[2,64,1408]{2,1,0:T(8,128)}, u32[]{:S(2)}) copy-start(f32[2,64,1408]{2,1,0:T(8,128)} %param.25) | copy-start | bytes 2162692
  7.2 10.8 %copy-start.60 = (f32[1408,64]{0,1:T(8,128)S(1)}, f32[1408,64]{0,1:T(8,128)}, u32[]{:S(2)}) copy-start(f32[1408,64]{0,1:T(8,128)} %param.26) | copy-start | bytes 1081348
  7.2 53.0 %all-gather.4.cloned.1.call-start = ((), (), s32[]{:S(2)}) async-start(), calls=%async_computation.2 | async-start | bytes 3620864 | tf_op jit(solution)/shard_map/all_gather | solution.py:671
  9.3 9.7 %copy-start.69 = (s32[3]{0:T(128)S(1)}, s32[3]{0:T(128)}, u32[]{:S(2)}) copy-start(s32[3]{0:T(128)} %param.39) | copy-start | bytes 40
  10.0 93.3 %all-gather.6.cloned.1.call-start = ((), (), s32[]{:S(2)}) async-start(), calls=%async_computation.3 | async-start | bytes 2228224 | tf_op jit(solution)/shard_map/all_gather | solution.py:673
  11.0 5.3 %collective-permute-start.5 = (bf16[64,512]{1,0:T(8,128)(2,1)S(1)}, bf16[64,512]{1,0:T(8,128)(2,1)S(1)}, u32[]{:S(2)}, u32[]{:S(2)}) collective-permute-start(bf16[64,512]{1,0:T(8,128)(2,1)S(1)} %convert_bitcast_fusion.1), channel_id=1, source_target_pairs={{0,1},{1,0},{2,3},{3,2},{4,5},{5,4},{6,7},{7,6},{8,9},{9,8},{10,11... | collective-permute-start | bytes 196616 | tf_op jit(solution)/shard_map/ppermute | solution.py:653
  17.9 163.7 %all-gather.8.cloned.1.call-start = ((), (), s32[]{:S(2)}) async-start(), calls=%async_computation.4 | async-start | bytes 9191424 | tf_op jit(solution)/shard_map/all_gather | solution.py:672
  18.9 419.7 %reduce-scatter.3.cloned.1.call-start = ((), (), s32[]{:S(2)}) async-start(), calls=%async_computation.5 | async-start | bytes 4734976 | tf_op jit(solution)/shard_map/reduce_scatter | solution.py:734
  65.5 6.7 %copy-start.7 = (bf16[1024,1024]{1,0:T(8,128)(2,1)}, bf16[1024,1024]{1,0:T(8,128)(2,1)S(1)}, u32[]{:S(2)}) copy-start(bf16[1024,1024]{1,0:T(8,128)(2,1)S(1)} %fusion.4.normed) | copy-start | bytes 6291460
  67.5 5.0 copy-start.70
  72.2 12.6 %collective-permute-start = (bf16[3,2,1024,128]{3,2,1,0:T(8,128)(2,1)}, bf16[3,2,1024,128]{3,2,1,0:T(8,128)(2,1)}, u32[]{:S(2)}, u32[]{:S(2)}) collective-permute-start(bf16[3,2,1024,128]{3,2,1,0:T(8,128)(2,1)} %project_pair.3), channel_id=1, source_target_pairs={{0,2},{2,0},{4,6},{6,4},{8,10},{10,8},{12,14},{14,12},{16,18},{18,... | collective-permute-start | bytes 4718600 | tf_op jit(solution)/shard_map/ppermute | solution.py:656
  76.3 8.5 %collective-permute-start.1 = (bf16[2,2,128,128]{3,2,1,0:T(8,128)(2,1)}, bf16[2,2,128,128]{3,2,1,0:T(8,128)(2,1)S(1)}, u32[]{:S(2)}, u32[]{:S(2)}) collective-permute-start(bf16[2,2,128,128]{3,2,1,0:T(8,128)(2,1)} %bitcast.18), channel_id=1, source_target_pairs={{0,2},{2,0},{4,6},{6,4},{8,10},{10,8},{12,14},{14,12},{16,18},{18,... | collective-permute-start | bytes 393224 | tf_op jit(solution)/shard_map/ppermute | solution.py:656
  84.8 13.0 %copy-start.27 = (bf16[3,2,1024,128]{3,2,1,0:T(8,128)(2,1)}, bf16[3,2,1024,128]{3,2,1,0:T(8,128)(2,1)S(1)}, u32[]{:S(2)}) copy-start(bf16[3,2,1024,128]{3,2,1,0:T(8,128)(2,1)S(1)} %project_pair.2.own) | copy-start | bytes 4718596
  97.8 2.5 collective-permute-start.2
  98.0 14.8 %collective-permute-start.3 = (bf16[2,1024,128]{2,1,0:T(8,128)(2,1)S(1)}, bf16[2,1024,128]{2,1,0:T(8,128)(2,1)S(1)}, u32[]{:S(2)}, u32[]{:S(2)}) collective-permute-start(bf16[2,1024,128]{2,1,0:T(8,128)(2,1)S(1)} %get-tuple-element.41.one), channel_id=1, source_target_pairs={{0,1},{1,0},{2,3},{3,2},{4,5},{5,4},{6,7},{7,6},{8,9},{9,8},{10,11... | collective-permute-start | bytes 1572872 | tf_op jit(solution)/shard_map/ppermute | solution.py:653
  100.3 23.1 %collective-permute-start.4 = (bf16[2,1024,128]{2,1,0:T(8,128)(2,1)S(1)}, bf16[2,1024,128]{2,1,0:T(8,128)(2,1)S(1)}, u32[]{:S(2)}, u32[]{:S(2)}) collective-permute-start(bf16[2,1024,128]{2,1,0:T(8,128)(2,1)S(1)} %collective-permute-done.2.two), channel_id=1, source_target_pairs={{0,1},{1,0},{2,3},{3,2},{4,5},{5,4},{6,7},{7,6},{8,9},{9,8},{10,11... | collective-permute-start | bytes 1572872 | tf_op jit(solution)/shard_map/ppermute | solution.py:653
  198.1 26.0 %collective-permute-start.8 = (bf16[512,1024]{1,0:T(8,128)(2,1)S(1)}, bf16[512,1024]{1,0:T(8,128)(2,1)S(1)}, u32[]{:S(2)}, u32[]{:S(2)}) collective-permute-start(bf16[512,1024]{1,0:T(8,128)(2,1)S(1)} %get-tuple-element.48), channel_id=1, source_target_pairs={{0,1},{1,0},{2,3},{3,2},{4,5},{5,4},{6,7},{7,6},{8,9},{9,8},{10,11... | collective-permute-start | bytes 3145736 | tf_op jit(solution)/shard_map/ppermute | solution.py:653
  213.8 32.3 %copy-start.30 = (bf16[512,1408]{1,0:T(8,128)(2,1)}, bf16[512,1408]{1,0:T(8,128)(2,1)S(1)}, u32[]{:S(2)}) copy-start(bf16[512,1408]{1,0:T(8,128)(2,1)S(1)} %get-tuple-element.45) | copy-start | bytes 4325380
  213.8 32.3 %copy-start.35 = (bf16[512,1408]{1,0:T(8,128)(2,1)}, bf16[512,1408]{1,0:T(8,128)(2,1)S(1)}, u32[]{:S(2)}) copy-start(bf16[512,1408]{1,0:T(8,128)(2,1)S(1)} %get-tuple-element.63) | copy-start | bytes 4325380
  213.8 32.1 %collective-permute-start.7 = (bf16[512,1024]{1,0:T(8,128)(2,1)S(1)}, bf16[512,1024]{1,0:T(8,128)(2,1)S(1)}, u32[]{:S(2)}, u32[]{:S(2)}) collective-permute-start(bf16[512,1024]{1,0:T(8,128)(2,1)S(1)} %get-tuple-element.47), channel_id=1, source_target_pairs={{0,1},{1,0},{2,3},{3,2},{4,5},{5,4},{6,7},{7,6},{8,9},{9,8},{10,11... | collective-permute-start | bytes 3145736 | tf_op jit(solution)/shard_map/ppermute | solution.py:653
  214.6 31.6 %copy-start.3 = (bf16[1024,1024]{1,0:T(8,128)(2,1)S(1)}, bf16[1024,1024]{1,0:T(8,128)(2,1)}, u32[]{:S(2)}) copy-start(bf16[1024,1024]{1,0:T(8,128)(2,1)} %upstream.7) | copy-start | bytes 6291460
  214.6 31.6 %copy-start.24 = (bf16[1024,1024]{1,0:T(8,128)(2,1)S(1)}, bf16[1024,1024]{1,0:T(8,128)(2,1)}, u32[]{:S(2)}) copy-start(bf16[1024,1024]{1,0:T(8,128)(2,1)} %all-gather.6.cloned.1.call-done.weight) | copy-start | bytes 6291460
  246.2 11.4 %copy-start.17 = (f32[2048,128]{1,0:T(8,128)S(1)}, f32[2048,128]{1,0:T(8,128)}, u32[]{:S(2)}) copy-start(f32[2048,128]{1,0:T(8,128)} %get-tuple-element.153.sines) | copy-start | bytes 3145732
  255.7 1.9 collective-permute-start.9
  259.7 23.7 %copy-start.5 = (bf16[1024,1024]{1,0:T(8,128)(2,1)S(1)}, bf16[1024,1024]{1,0:T(8,128)(2,1)}, u32[]{:S(2)}) copy-start(bf16[1024,1024]{1,0:T(8,128)(2,1)} %tokens.5) | copy-start | bytes 6291460
  259.7 23.7 %copy-start.14 = (bf16[1024,1664]{1,0:T(8,128)(2,1)S(1)}, bf16[1024,1664]{1,0:T(8,128)(2,1)}, u32[]{:S(2)}) copy-start(bf16[1024,1664]{1,0:T(8,128)(2,1)} %all-gather.4.cloned.1.call-done.weight) | copy-start | bytes 10223620
  279.8 3.6 collective-permute-start.10
  283.4 9.8 %copy-start.45 = (bf16[2,1024,128]{2,1,0:T(8,128)(2,1)S(1)}, bf16[2,1024,128]{2,1,0:T(8,128)(2,1)}, u32[]{:S(2)}) copy-start(bf16[2,1024,128]{2,1,0:T(8,128)(2,1)} %copy-done.43) | copy-start | bytes 1572868
  283.4 9.8 %copy-start.48 = (bf16[2,1024,128]{2,1,0:T(8,128)(2,1)S(1)}, bf16[2,1024,128]{2,1,0:T(8,128)(2,1)}, u32[]{:S(2)}) copy-start(bf16[2,1024,128]{2,1,0:T(8,128)(2,1)} %copy-done.46) | copy-start | bytes 1572868
  307.2 183.2 %reduce-scatter.5.cloned.1.call-start = ((), (), s32[]{:S(2)}) async-start(), calls=%async_computation.6 | async-start | bytes 9191424 | tf_op jit(solution)/shard_map/reduce_scatter | solution.py:733
  338.4 5.5 %copy-start.26 = (bf16[1024,1024]{1,0:T(8,128)(2,1)S(1)}, bf16[1024,1024]{1,0:T(8,128)(2,1)}, u32[]{:S(2)}) copy-start(bf16[1024,1024]{1,0:T(8,128)(2,1)} %copy-done.25) | copy-start | bytes 6291460
  338.4 52.9 %copy-start.11 = (f32[1024,1024]{1,0:T(8,128)S(1)}, f32[1024,1024]{1,0:T(8,128)}, u32[]{:S(2)}) copy-start(f32[1024,1024]{1,0:T(8,128)} %copy-done.10) | copy-start | bytes 12582916
  342.7 48.5 %collective-permute-start.6 = (bf16[1024,1024]{1,0:T(8,128)(2,1)S(1)}, bf16[1024,1024]{1,0:T(8,128)(2,1)S(1)}, u32[]{:S(2)}, u32[]{:S(2)}) collective-permute-start(bf16[1024,1024]{1,0:T(8,128)(2,1)S(1)} %feed_out.1), channel_id=1, source_target_pairs={{0,1},{1,0},{2,3},{3,2},{4,5},{5,4},{6,7},{7,6},{8,9},{9,8},{10,11... | collective-permute-start | bytes 6291464 | tf_op jit(solution)/shard_map/ppermute | solution.py:653
  343.9 91.5 %copy-start.6 = (bf16[1024,1024]{1,0:T(8,128)(2,1)S(1)}, bf16[1024,1024]{1,0:T(8,128)(2,1)}, u32[]{:S(2)}) copy-start(bf16[1024,1024]{1,0:T(8,128)(2,1)} %tokens.5) | copy-start | bytes 6291460
  343.9 91.5 %copy-start.22 = (f32[1024,1024]{1,0:T(8,128)S(1)}, f32[1024,1024]{1,0:T(8,128)}, u32[]{:S(2)}) copy-start(f32[1024,1024]{1,0:T(8,128)} %get-tuple-element.49.grad) | copy-start | bytes 12582916
  343.9 91.5 %collective-permute-start.11 = (bf16[1024,1024]{1,0:T(8,128)(2,1)S(1)}, bf16[1024,1024]{1,0:T(8,128)(2,1)S(1)}, u32[]{:S(2)}, u32[]{:S(2)}) collective-permute-start(bf16[1024,1024]{1,0:T(8,128)(2,1)S(1)} %copy-done.26), channel_id=1, source_target_pairs={{0,1},{1,0},{2,3},{3,2},{4,5},{5,4},{6,7},{7,6},{8,9},{9,8},{10,11... | collective-permute-start | bytes 6291464 | tf_op jit(solution)/shard_map/ppermute | solution.py:653
  435.4 5.6 %copy-start.59 = (f32[3,64,512]{2,1,0:T(8,128)S(1)}, f32[3,64,512]{2,1,0:T(8,128)}, u32[]{:S(2)}) copy-start(f32[3,64,512]{2,1,0:T(8,128)} %param.23) | copy-start | bytes 1179652
  438.6 4.8 copy-start.64
  438.6 4.8 copy-start.65
  438.6 5.9 %copy-start.66 = (f32[2,64]{1,0:T(2,128)S(1)}, f32[2,64]{1,0:T(2,128)}, u32[]{:S(2)}) copy-start(f32[2,64]{1,0:T(2,128)} %param.27) | copy-start | bytes 1540
  438.6 5.8 %copy-start.67 = (f32[2,64]{1,0:T(2,128)S(1)}, f32[2,64]{1,0:T(2,128)}, u32[]{:S(2)}) copy-start(f32[2,64]{1,0:T(2,128)} %param.37) | copy-start | bytes 1540
  438.6 5.9 %copy-start.68 = (f32[2,64]{1,0:T(2,128)S(1)}, f32[2,64]{1,0:T(2,128)}, u32[]{:S(2)}) copy-start(f32[2,64]{1,0:T(2,128)} %param.32) | copy-start | bytes 1540
  439.8 4.5 collective-permute-start.12
  441.0 50.6 %copy-start.61 = (f32[1408,64]{0,1:T(8,128)S(1)}, f32[1408,64]{0,1:T(8,128)}, u32[]{:S(2)}) copy-start(f32[1408,64]{0,1:T(8,128)} %param.26) | copy-start | bytes 1081348
  441.0 50.6 %copy-start.63 = (f32[1408,64]{0,1:T(8,128)S(1)}, f32[1408,64]{0,1:T(8,128)}, u32[]{:S(2)}) copy-start(f32[1408,64]{0,1:T(8,128)} %param.36) | copy-start | bytes 1081348
  444.2 49.6 %copy-start.58 = (f32[2,64,1408]{2,1,0:T(8,128)S(1)}, f32[2,64,1408]{2,1,0:T(8,128)}, u32[]{:S(2)}) copy-start(f32[2,64,1408]{2,1,0:T(8,128)} %param.25) | copy-start | bytes 2162692
  491.6 5.3 %copy-start.1 = (bf16[1024,2,512]{2,1,0:T(2,128)(2,1)S(1)}, bf16[1024,2,512]{2,1,0:T(2,128)(2,1)}, u32[]{:S(2)}) copy-start(bf16[1024,2,512]{2,1,0:T(2,128)(2,1)} %param.38) | copy-start | bytes 6291460
  (41 other events, 74.5 us)
Sparse Core Ops, SparseCore 0:
  10.9 49.2 all-gather.3
  62.9 40.3 all-gather.5
  106.2 75.2 all-gather.7
  307.4 72.2 reduce-scatter.2
  384.1 106.2 reduce-scatter.4

commit v2 on v1

--- a/solution.py
+++ b/solution.py
@@ -28,6 +28,8 @@
 F32 = jnp.float32
 MIB = 1024 * 1024
 TILE = 256
+VMEM = 26
+WEIGH = 1.0
 
 
 def dot(left, right):
@@ -49,13 +51,13 @@
 
 
 def cost(flops, moved, trans=0):
-    return pl.CostEstimate(flops=int(flops), bytes_accessed=int(moved), transcendentals=int(trans))
-
-
-def rope_tables(count):
+    return pl.CostEstimate(flops=int(flops * WEIGH), bytes_accessed=int(moved * WEIGH), transcendentals=int(trans))
+
+
+def rope_tables(places):
     half_dim = HEAD_DIM // 2
     freqs = 10000.0 ** (-(jnp.arange(half_dim, dtype=F32) / half_dim))
-    phase = jnp.arange(count, dtype=jnp.int32).astype(F32)[:, None] * freqs[None, :]
+    phase = places.astype(F32)[:, None] * freqs[None, :]
     cosines, sines = jnp.cos(phase), jnp.sin(phase)
     return jnp.concatenate([cosines, cosines], 1), jnp.concatenate([-sines, sines], 1)
 
@@ -73,9 +75,7 @@
     return (first_new, second_new, updated)
 
 
-def qkv_kernel(info, normed, weight, cosines, sines, out):
-    result = dot(normed[...], weight[...])
-    part = pl.program_id(0)
+def rotate_out(result, part, cosines, sines, out):
     for head in range(2):
         value = result[:, head * HEAD_DIM : (head + 1) * HEAD_DIM]
 
@@ -88,25 +88,74 @@
             out[0, head] = value.astype(BF)
 
 
-def project_pair(info, normed, weights, cosines, sines, slot):
+def first_kernel(info, tokens, gain_columns, weight, cosines, sines, out, normed, gains):
+    part = pl.program_id(0)
+
+    @pl.when(part == 0)
+    def _():
+        rows = gain_columns[...].astype(F32).T[:8, :]
+        gains[...] = rows
+        value = tokens[...].astype(F32)
+        inverse = lax.rsqrt(jnp.mean(value * value, axis=1, keepdims=True) + EPS)
+        normed[...] = (value * inverse * rows[0:1, :]).astype(BF)
+
+    rotate_out(dot(normed[...], weight[...]), part, cosines, sines, out)
+
+
+def second_kernel(info, normed, weight, cosines, sines, out):
+    rotate_out(dot(normed[...], weight[...]), pl.program_id(0), cosines, sines, out)
+
+
+def project_first(info, tokens, weights, cosines, sines):
+    rows = tokens.shape[0]
+    return pl.pallas_call(
+        first_kernel,
+        out_shape=(
+            jax.ShapeDtypeStruct((3, 2, rows, HEAD_DIM), BF),
+            jax.ShapeDtypeStruct((rows, D), BF),
+            jax.ShapeDtypeStruct((8, D), F32),
+        ),
+        grid_spec=pltpu.PrefetchScalarGridSpec(
+            num_scalar_prefetch=1,
+            grid=(3,),
+            in_specs=[
+                pl.BlockSpec((rows, D), lambda j, info: (0, 0)),
+                pl.BlockSpec((D, HEAD_DIM), lambda j, info: (0, 12)),
+                pl.BlockSpec((D, 256), lambda j, info: (0, 2 * j + 1 - info[0])),
+                pl.BlockSpec((rows, HEAD_DIM), lambda j, info: (info[0], 0)),
+                pl.BlockSpec((rows, HEAD_DIM), lambda j, info: (info[0], 0)),
+            ],
+            out_specs=(
+                pl.BlockSpec((1, 2, rows, HEAD_DIM), lambda j, info: (j, 0, 0, 0)),
+                pl.BlockSpec((rows, D), lambda j, info: (0, 0)),
+                pl.BlockSpec((8, D), lambda j, info: (0, 0)),
+            ),
+        ),
+        compiler_params=params(VMEM),
+        cost_estimate=cost(0, 0),
+        name="project_first",
+    )(info, tokens, weights, weights, cosines, sines)
+
+
+def project_second(info, normed, weights, cosines, sines):
     rows = normed.shape[0]
     return pl.pallas_call(
-        qkv_kernel,
+        second_kernel,
         out_shape=jax.ShapeDtypeStruct((3, 2, rows, HEAD_DIM), BF),
         grid_spec=pltpu.PrefetchScalarGridSpec(
             num_scalar_prefetch=1,
             grid=(3,),
             in_specs=[
                 pl.BlockSpec((rows, D), lambda j, info: (0, 0)),
-                pl.BlockSpec((D, 256), lambda j, info: (0, 2 * j + info[slot])),
+                pl.BlockSpec((D, 256), lambda j, info: (0, 2 * j + info[0])),
                 pl.BlockSpec((rows, HEAD_DIM), lambda j, info: (info[0], 0)),
                 pl.BlockSpec((rows, HEAD_DIM), lambda j, info: (info[0], 0)),
             ],
             out_specs=pl.BlockSpec((1, 2, rows, HEAD_DIM), lambda j, info: (j, 0, 0, 0)),
         ),
-        compiler_params=params(40),
-        cost_estimate=cost(2 * rows * D * 768, 6 * MIB),
-        name="project_pair",
+        compiler_params=params(VMEM),
+        cost_estimate=cost(0, 0),
+        name="project_second",
     )(info, normed, weights, cosines, sines)
 
 
@@ -216,8 +265,8 @@
                 pltpu.VMEM((SEG, HEAD_DIM), BF),
             ],
         ),
-        compiler_params=params(48),
-        cost_estimate=cost(5e9, 8 * MIB, 5e6),
+        compiler_params=params(VMEM),
+        cost_estimate=cost(0, 0),
         name="attend_forward",
     )(info, own, other, mem_own, mem_other, bias)
 
@@ -277,19 +326,19 @@
 
 
 def attend_backward(
-    info, own, other, mem_own, mem_other, bias, grad_own, grad_other, turned, logs, cosines, sines
+    info, own, other, mem_own, mem_other, bias, grad_own, grad_other, turned, logs, cosines, sines, head
 ):
     rows = own.shape[2]
-    part = pl.BlockSpec((3, 1, rows, HEAD_DIM), lambda h, info: (0, h, 0, 0))
-    mem = pl.BlockSpec((2, 1, RETR, HEAD_DIM), lambda h, info: (0, h, 0, 0))
-    half = pl.BlockSpec((1, rows, HEAD_DIM), lambda h, info: (h, 0, 0))
+    part = pl.BlockSpec((3, 1, rows, HEAD_DIM), lambda h, info: (0, head, 0, 0))
+    mem = pl.BlockSpec((2, 1, RETR, HEAD_DIM), lambda h, info: (0, head, 0, 0))
+    half = pl.BlockSpec((1, rows, HEAD_DIM), lambda h, info: (head, 0, 0))
     table = pl.BlockSpec((SEG, HEAD_DIM), lambda h, info: (0, 0))
     return pl.pallas_call(
         backward_kernel,
-        out_shape=(jax.ShapeDtypeStruct((3, 2, rows, HEAD_DIM), BF),) * 2,
+        out_shape=(jax.ShapeDtypeStruct((3, 1, rows, HEAD_DIM), BF),) * 2,
         grid_spec=pltpu.PrefetchScalarGridSpec(
             num_scalar_prefetch=1,
-            grid=(2,),
+            grid=(1,),
             in_specs=[
                 part,
                 part,
@@ -298,12 +347,12 @@
                 table,
                 half,
                 half,
-                pl.BlockSpec((1, HEAD_DIM, SEG), lambda h, info: (h, 0, 0)),
-                pl.BlockSpec((1, 1, SEG), lambda h, info: (h, 0, 0)),
+                pl.BlockSpec((1, HEAD_DIM, SEG), lambda h, info: (head, 0, 0)),
+                pl.BlockSpec((1, 1, SEG), lambda h, info: (head, 0, 0)),
                 table,
                 table,
             ],
-            out_specs=(part, part),
+            out_specs=(pl.BlockSpec((3, 1, rows, HEAD_DIM), lambda h, info: (0, 0, 0, 0)),) * 2,
             scratch_shapes=[pltpu.VMEM((SEG, HEAD_DIM), BF)] * 4
             + [
                 pltpu.VMEM((HEAD_DIM, SEG), BF),
@@ -314,54 +363,78 @@
                 pltpu.VMEM((SEG, HEAD_DIM), F32),
             ],
         ),
-        compiler_params=params(48),
-        cost_estimate=cost(12e9, 16 * MIB, 5e6),
+        compiler_params=params(VMEM),
+        cost_estimate=cost(0, 0),
         name="attend_backward",
-    )(info, own, other, mem_own, mem_other, bias, grad_own, grad_other, turned, logs, cosines, sines)
-
-
-def middle_kernel(info, one, two, three, four, tokens, weight, gain, middle, normed, o_s):
-    rank, group = info[0], info[1]
-    pieces = ((one, group, rank), (two, group, 1 - rank), (three, 1 - group, rank), (four, 1 - group, 1 - rank))
-    for piece, side, pair in pieces:
+    )(
+        info, own, other, mem_own, mem_other, bias, grad_own, grad_other, turned, logs, cosines, sines
+    )
+
+
+OUT_AT = 3 * 4 * HEAD_DIM + HEAD_DIM
+
+
+def columns(width, start):
+    return pl.BlockSpec(
+        (pl.Element(D), pl.Element(width)),
+        lambda *indices: (0, start),
+        pipeline_mode=pl.Buffered(1),
+    )
+
+
+def attend_out_kernel(info, own, other, weight, out, joined):
+    for piece, pair in ((own, info[0]), (other, 1 - info[0])):
         for head in range(2):
-            column = pl.multiple_of((side * 4 + pair * 2 + head) * HEAD_DIM, HEAD_DIM)
-            o_s[:, pl.ds(column, HEAD_DIM)] = piece[head]
-    value = tokens[...].astype(F32) + dot_nt(o_s[...], weight[...])
+            column = pl.multiple_of((pair * 2 + head) * HEAD_DIM, HEAD_DIM)
+            joined[:, pl.ds(column, HEAD_DIM)] = piece[head]
+    out[...] = dot_nt(joined[...], weight[...]).astype(BF)
+
+
+def attend_out_call(info, own, other, weights):
+    rows, half = own.shape[1], 4 * HEAD_DIM
+    piece = pl.BlockSpec((2, TILE, HEAD_DIM), lambda i, info: (0, i, 0))
+    return pl.pallas_call(
+        attend_out_kernel,
+        out_shape=(jax.ShapeDtypeStruct((rows, D), BF), jax.ShapeDtypeStruct((rows, half), BF)),
+        grid_spec=pltpu.PrefetchScalarGridSpec(
+            num_scalar_prefetch=1,
+            grid=(rows // TILE,),
+            in_specs=[piece, piece, columns(half, OUT_AT)],
+            out_specs=(
+                pl.BlockSpec((TILE, D), lambda i, info: (i, 0)),
+                pl.BlockSpec((TILE, half), lambda i, info: (i, 0)),
+            ),
+        ),
+        compiler_params=params(VMEM),
+        cost_estimate=cost(0, 0),
+        name="attend_out",
+    )(info, own, other, weights)
+
+
+def middle_kernel(tokens, own, other, gain, middle, normed):
+    value = tokens[...].astype(F32) + (own[...].astype(F32) + other[...].astype(F32))
     middle[...] = value
     inverse = lax.rsqrt(jnp.mean(value * value, axis=1, keepdims=True) + EPS)
     normed[...] = (value * inverse * gain[...]).astype(BF)
 
 
-def middle_call(info, pieces, tokens, weight, gain):
+def middle_call(tokens, own, other, gain):
     rows = tokens.shape[0]
-    piece = pl.BlockSpec((2, TILE, HEAD_DIM), lambda i, info: (0, i, 0))
-    wide = pl.BlockSpec((TILE, D), lambda i, info: (i, 0))
+    wide = pl.BlockSpec((TILE, D), lambda i: (i, 0))
     return pl.pallas_call(
         middle_kernel,
-        out_shape=(
-            jax.ShapeDtypeStruct((rows, D), F32),
-            jax.ShapeDtypeStruct((rows, D), BF),
-        ),
-        grid_spec=pltpu.PrefetchScalarGridSpec(
-            num_scalar_prefetch=1,
-            grid=(rows // TILE,),
-            in_specs=[piece] * 4
-            + [
-                wide,
-                pl.BlockSpec((D, D), lambda i, info: (0, 0)),
-                pl.BlockSpec((1, D), lambda i, info: (0, 0)),
-            ],
-            out_specs=(wide, wide),
-            scratch_shapes=[pltpu.VMEM((TILE, D), BF)],
-        ),
-        compiler_params=params(40),
-        cost_estimate=cost(2 * rows * D * D, 12 * MIB),
+        out_shape=(jax.ShapeDtypeStruct((rows, D), F32), jax.ShapeDtypeStruct((rows, D), BF)),
+        grid=(rows // TILE,),
+        in_specs=[wide, wide, wide, pl.BlockSpec((1, D), lambda i: (0, 0))],
+        out_specs=(wide, wide),
+        compiler_params=params(VMEM),
+        cost_estimate=cost(0, 0),
         name="middle",
-    )(info, *pieces, tokens, weight, gain)
-
-
-def feed_kernel(normed, upstream, gate_w, up_w, down_w, hidden, gate_grad, up_grad, back):
+    )(tokens, own, other, gain)
+
+
+def feed_kernel(normed, upstream, gate_w, up_w, down_w, *refs):
+    hidden, gate_grad, up_grad, back = refs[-4:]
     gate = dot(normed[...], gate_w[...])
     up_part = dot(normed[...], up_w[...])
     sigma = jax.nn.sigmoid(gate)
@@ -375,22 +448,25 @@
     back[...] = (dot_nt(grad_gate, gate_w[...]) + dot_nt(grad_up, up_w[...])).astype(BF)
 
 
-def feed_call(normed, upstream, weights, first, count):
-    width = weights.shape[1] // 3
+def feed_call(normed, upstream, weights, first, count, earlier):
+    rows = normed.shape[0]
+    width = FF // 2
     whole = lambda index: pl.BlockSpec((D, width), lambda i: (0, index), pipeline_mode=pl.Buffered(1))
     source = pl.BlockSpec((TILE, D), lambda i: (i + first // TILE, 0))
-    narrow = pl.BlockSpec((TILE, width), lambda i: (i, 0))
+    narrow = pl.BlockSpec((TILE, width), lambda i: (i + first // TILE, 0))
     return pl.pallas_call(
         feed_kernel,
-        out_shape=(jax.ShapeDtypeStruct((count, width), BF),) * 3
+        out_shape=(jax.ShapeDtypeStruct((rows, width), BF),) * 3
         + (jax.ShapeDtypeStruct((count, D), BF),),
         grid=(count // TILE,),
-        in_specs=[source, source, whole(0), whole(1), whole(2)],
+        in_specs=[source, source, whole(0), whole(1), whole(2)]
+        + [pl.BlockSpec(memory_space=pl.ANY)] * len(earlier),
         out_specs=(narrow, narrow, narrow, pl.BlockSpec((TILE, D), lambda i: (i, 0))),
-        compiler_params=params(48),
-        cost_estimate=cost(10 * count * D * width, 9 * MIB + 16 * count * D),
+        input_output_aliases={5 + index: index for index in range(len(earlier))},
+        compiler_params=params(VMEM),
+        cost_estimate=cost(5e7, 0),
         name="feed",
-    )(normed, upstream, weights, weights, weights)
+    )(normed, upstream, weights, weights, weights, *earlier)
 
 
 def out_kernel(hidden, down_w, out):
@@ -408,8 +484,8 @@
             pl.BlockSpec((D, width), lambda i: (0, 2), pipeline_mode=pl.Buffered(1)),
         ],
         out_specs=pl.BlockSpec((TILE, D), lambda i: (i, 0)),
-        compiler_params=params(40),
-        cost_estimate=cost(2 * count * D * width, 6 * MIB),
+        compiler_params=params(VMEM),
+        cost_estimate=cost(5e7, 0),
         name="feed_out",
     )(hidden, weights)
 
@@ -429,17 +505,18 @@
     whole = pl.BlockSpec((rows, width), lambda i: (0, 0), pipeline_mode=pl.Buffered(1))
     return pl.pallas_call(
         feed_weight_kernel,
-        out_shape=jax.ShapeDtypeStruct((D, 3 * width), BF),
+        out_shape=pltpu.HBM((D, 3 * width), BF),
         grid=(D // TILE,),
         in_specs=[left, left, whole, whole, whole],
         out_specs=pl.BlockSpec((TILE, 3 * width), lambda i: (i, 0)),
-        compiler_params=params(48),
-        cost_estimate=cost(6 * rows * D * width, 22 * MIB),
+        compiler_params=params(VMEM),
+        cost_estimate=cost(5e7, 0),
         name="feed_weights",
     )(normed, upstream, hidden, gate_grad, up_grad)
 
 
-def residual_kernel(info, middle, back_own, back_other, upstream, gain, weight, grad, low, keep, send, gain_grad):
+def residual_kernel(info, middle, back_own, back_other, upstream, gain, weight, *refs):
+    grad, low, keep, send, gain_grad = refs[-5:]
     rank = info[0]
     value = middle[...]
     back = back_own[...].astype(F32) + back_other[...].astype(F32)
@@ -463,12 +540,13 @@
             out[head] = result[:, head * HEAD_DIM : (head + 1) * HEAD_DIM]
 
 
-def residual_call(info, middle, back_own, back_other, upstream, gain, weight):
-    rows = middle.shape[0]
-    half = weight.shape[1] // 2
-    wide = pl.BlockSpec((TILE, D), lambda i, info: (i, 0))
+def residual_call(info, middle, back_own, back_other, upstream, gain, weights, first, earlier):
+    rows, count = middle.shape[0], back_own.shape[0]
+    start = first // TILE
+    wide = pl.BlockSpec((TILE, D), lambda i, info: (i + start, 0))
+    part = pl.BlockSpec((TILE, D), lambda i, info: (i, 0))
     row = pl.BlockSpec((1, D), lambda i, info: (0, 0))
-    piece = pl.BlockSpec((2, TILE, HEAD_DIM), lambda i, info: (0, i, 0))
+    piece = pl.BlockSpec((2, TILE, HEAD_DIM), lambda i, info: (0, i + start, 0))
     return pl.pallas_call(
         residual_kernel,
         out_shape=(
@@ -480,30 +558,25 @@
         ),
         grid_spec=pltpu.PrefetchScalarGridSpec(
             num_scalar_prefetch=1,
-            grid=(rows // TILE,),
-            in_specs=[
-                wide,
-                wide,
-                wide,
-                wide,
-                row,
-                pl.BlockSpec((D, half), lambda i, info: (0, info[1])),
-            ],
+            grid=(count // TILE,),
+            in_specs=[wide, part, part, wide, row, columns(4 * HEAD_DIM, OUT_AT)]
+            + [pl.BlockSpec(memory_space=pl.ANY)] * len(earlier),
             out_specs=(wide, wide, piece, piece, row),
         ),
-        compiler_params=params(40),
-        cost_estimate=cost(2 * rows * D * half, 18 * MIB),
+        input_output_aliases={7 + index: index for index in range(len(earlier))},
+        compiler_params=params(VMEM),
+        cost_estimate=cost(5e7 if first + count < rows else 3e11, 0),
         name="residual",
-    )(info, middle, back_own, back_other, upstream, gain, weight)
-
-
-def back_kernel(info, own, other, weight, tokens, out, joined, gain_grad):
+    )(info, middle, back_own, back_other, upstream, gain, weights, *earlier)
+
+
+def back_kernel(info, own_one, own_two, other_one, other_two, weight, tokens, out, joined, gain_grad):
     rank = info[0]
-    for piece, pair in ((own, rank), (other, 1 - rank)):
+    for index, piece in enumerate((own_one, own_two, other_one, other_two)):
+        pair = (rank, 1 - rank)[index // 2]
         for part in range(3):
-            for head in range(2):
-                column = pl.multiple_of((part * 4 + pair * 2 + head) * HEAD_DIM, HEAD_DIM)
-                joined[:, pl.ds(column, HEAD_DIM)] = piece[part, head]
+            column = pl.multiple_of((part * 4 + pair * 2 + index % 2) * HEAD_DIM, HEAD_DIM)
+            joined[:, pl.ds(column, HEAD_DIM)] = piece[part, 0]
     back = dot_nt(joined[...], weight[...])
     out[...] = back.astype(BF)
 
@@ -516,10 +589,10 @@
     gain_grad[...] += jnp.sum(back * value * inverse, axis=0, keepdims=True)
 
 
-def back_call(info, own, other, weights, tokens):
+def back_call(info, pieces, weights, tokens):
     rows = tokens.shape[0]
     width = 3 * 4 * HEAD_DIM
-    piece = pl.BlockSpec((3, 2, TILE, HEAD_DIM), lambda i, info: (0, 0, i, 0))
+    piece = pl.BlockSpec((3, 1, TILE, HEAD_DIM), lambda i, info: (0, 0, i, 0))
     wide = pl.BlockSpec((TILE, D), lambda i, info: (i, 0))
     return pl.pallas_call(
         back_kernel,
@@ -532,6 +605,8 @@
             num_scalar_prefetch=1,
             grid=(rows // TILE,),
             in_specs=[
+                piece,
+                piece,
                 piece,
                 piece,
                 pl.BlockSpec((D, width), lambda i, info: (0, 0)),
@@ -543,52 +618,66 @@
                 pl.BlockSpec((1, D), lambda i, info: (0, 0)),
             ),
         ),
-        compiler_params=params(40),
-        cost_estimate=cost(2 * rows * D * width, 13 * MIB),
+        compiler_params=params(VMEM),
+        cost_estimate=cost(5e7, 0),
         name="back",
-    )(info, own, other, weights, tokens)
-
-
-def attend_weight_kernel(info, normed, joined, low, one, two, out, o_s):
-    @pl.when(pl.program_id(0) == 0)
-    def _():
-        for piece, pair in ((one, info[0]), (two, 1 - info[0])):
-            for head in range(2):
-                column = pl.multiple_of((pair * 2 + head) * HEAD_DIM, HEAD_DIM)
-                o_s[:, pl.ds(column, HEAD_DIM)] = piece[head]
-
-    width = joined.shape[1]
+    )(info, *pieces, weights, tokens)
+
+
+def attend_weight_kernel(info, normed, joined, low, attended, gain_one, gain_two, *refs):
+    outs, out = refs[:-1], refs[-1]
+    step = pl.program_id(0)
+    count = len(outs) // 2
+
+    tile, width, half = normed.shape[1], joined.shape[1], attended.shape[1]
     left = normed[...].astype(F32).T.astype(BF)
     out[:, :width] = dot(left, joined[...]).astype(BF)
     left = low[...].astype(F32).T.astype(BF)
-    out[:, width:] = dot(left, o_s[...]).astype(BF)
-
-
-def attend_weight_call(info, normed, joined, low, one, two):
+    out[:, width : width + half] = dot(left, attended[...]).astype(BF)
+    both = jnp.concatenate([gain_one[...], gain_two[...], jnp.zeros((HEAD_DIM - 2, tile), F32)])
+    out[:, width + half :] = both.T.astype(BF)
+    size = outs[0].shape[1]
+    for line in range(tile // (4 * size)):
+        place_ = step * (tile // (4 * size)) + line
+        for slot in range(count):
+
+            @pl.when(count - 1 - (place_ ^ info[4]) == slot)
+            def _():
+                for column in range(2):
+                    for target, core in ((outs[slot], info[0]), (outs[count + slot], 1 - info[0])):
+                        side = info[3] if column == 0 else 1 - info[3]
+                        start = pl.multiple_of((line * 4 + side * 2 + core) * size, size)
+                        target[column] = out[pl.ds(start, size), :]
+
+
+def attend_weight_call(info, normed, joined, low, attended, gain_one, gain_two, size):
     rows, width = joined.shape
     half = 4 * HEAD_DIM
-    left = pl.BlockSpec((rows, TILE), lambda i, info: (0, i))
-    piece = pl.BlockSpec((2, rows, HEAD_DIM), lambda i, info: (0, 0, 0))
+    total = width + half + HEAD_DIM
+    tile, count = TILE, D // (4 * size)
+    left = pl.BlockSpec((rows, tile), lambda i, info: (0, i))
+    row = pl.BlockSpec((1, tile), lambda i, info: (0, i))
     return pl.pallas_call(
         attend_weight_kernel,
-        out_shape=jax.ShapeDtypeStruct((D, width + half), BF),
+        out_shape=(jax.ShapeDtypeStruct((2, size, total), BF),) * (2 * count),
         grid_spec=pltpu.PrefetchScalarGridSpec(
             num_scalar_prefetch=1,
-            grid=(D // TILE,),
+            grid=(D // tile,),
             in_specs=[
                 left,
                 pl.BlockSpec((rows, width), lambda i, info: (0, 0)),
                 left,
-                piece,
-                piece,
+                pl.BlockSpec((rows, half), lambda i, info: (0, 0)),
+                row,
+                row,
             ],
-            out_specs=pl.BlockSpec((TILE, width + half), lambda i, info: (i, 0)),
-            scratch_shapes=[pltpu.VMEM((rows, half), BF)],
-        ),
-        compiler_params=params(40),
-        cost_estimate=cost(2 * rows * D * (width + half), 13 * MIB),
+            out_specs=(pl.BlockSpec((2, size, total), lambda i, info: (0, 0, 0)),) * (2 * count),
+            scratch_shapes=[pltpu.VMEM((tile, total), BF)],
+        ),
+        compiler_params=params(VMEM),
+        cost_estimate=cost(0, 0),
         name="attend_weights",
-    )(info, normed, joined, low, one, two)
+    )(info, normed, joined, low, attended, gain_one, gain_two)
 
 
 def input_kernel(grad, back_own, back_other, tokens, gain, out):
@@ -609,10 +698,112 @@
         grid=(rows // TILE,),
         in_specs=[wide, wide, wide, wide, pl.BlockSpec((1, D), lambda i: (0, 0))],
         out_specs=wide,
-        compiler_params=params(32),
+        compiler_params=params(VMEM),
         cost_estimate=cost(12 * rows * D, 12 * MIB),
         name="input_grad",
     )(grad, back_own, back_other, tokens, gain)
+
+
+def choose(line, options):
+    value = options[0]
+    for here in range(1, len(options)):
+        if options[here] is not options[0]:
+            value = jnp.where(line == here, options[here], value)
+    return value
+
+
+def pair_kernel(keep, core, mine, theirs):
+    total = (keep[...].astype(F32) + core[...].astype(F32)).astype(BF)
+    mine[...] = total[0]
+    theirs[...] = total[1]
+
+
+def pair_add(keep, core):
+    shape = jax.ShapeDtypeStruct(keep.shape[1:], BF)
+    return pl.pallas_call(
+        pair_kernel,
+        out_shape=(shape, shape),
+        compiler_params=pltpu.CompilerParams(vmem_limit_bytes=VMEM * MIB),
+        cost_estimate=cost(0, 0),
+        name="pair_add",
+    )(keep, core)
+
+
+def low_kernel(left, right, out):
+    out[...] = (left[...].astype(F32) + right[...].astype(F32)).astype(out.dtype)
+
+
+def low_add(left, right):
+    return pl.pallas_call(
+        low_kernel,
+        out_shape=jax.ShapeDtypeStruct(left.shape, BF),
+        compiler_params=pltpu.CompilerParams(vmem_limit_bytes=VMEM * MIB),
+        cost_estimate=cost(0, 0),
+        name="low_add",
+    )(left, right)
+
+
+def chosen_kernel(flags, first, second, up_in, down_in, up, down):
+    one, two = first[...].astype(F32), second[...].astype(F32)
+    up[...] = (jnp.where(flags[0] > 0, one, two) + up_in[...].astype(F32)).astype(BF)
+    down[...] = (jnp.where(flags[1] > 0, one, two) + down_in[...].astype(F32)).astype(BF)
+
+
+def chosen_add(flags, first, second, up_in, down_in):
+    shape = jax.ShapeDtypeStruct(first.shape, BF)
+    vmem = pl.BlockSpec(memory_space=pltpu.VMEM)
+    return pl.pallas_call(
+        chosen_kernel,
+        out_shape=(shape, shape),
+        in_specs=[pl.BlockSpec(memory_space=pltpu.SMEM)] + [vmem] * 4,
+        out_specs=(vmem, vmem),
+        compiler_params=pltpu.CompilerParams(vmem_limit_bytes=VMEM * MIB),
+        cost_estimate=cost(0, 0),
+        name="chosen_add",
+    )(flags, first, second, up_in, down_in)
+
+
+def reduce_rows(keeps, sends, count):
+    length = count // 4
+    line = lax.axis_index("dp") // 4
+    sums = []
+    for keep, send in zip(keeps, sends):
+        core = lax.ppermute(send, "dp", [(i, i ^ 1) for i in range(count)])
+        mine, theirs = pair_add(keep, core)
+        other = lax.ppermute(theirs, "dp", [(i, i ^ 2) for i in range(count)])
+        sums.append(low_add(mine, other))
+    above = below = None
+    for step in range(1, length):
+        gap = length - step
+        slots = lambda towards: [
+            length - 1 - (here ^ (here + towards)) if 0 <= here + towards < length else None
+            for here in range(length)
+        ]
+        ups, downs = slots(gap), slots(-gap)
+        used = sorted({slot for slot in ups + downs if slot is not None})
+        if len(used) == 1 and step == 1:
+            up = down = sums[used[0]]
+        elif len(used) == 1:
+            up, down = low_add(sums[used[0]], below), low_add(sums[used[0]], above)
+        elif len(used) == 2:
+            flags = jnp.stack(
+                [
+                    choose(line, [jnp.int32(slot == used[0]) for slot in side])
+                    for side in (ups, downs)
+                ]
+            )
+            up, down = chosen_add(flags, sums[used[0]], sums[used[1]], below, above)
+        else:
+            fill = lambda side: [sums[used[0] if slot is None else slot] for slot in side]
+            up, down = choose(line, fill(ups)), choose(line, fill(downs))
+            up, down = low_add(up, below), low_add(down, above)
+        below = lax.ppermute(up, "dp", [(i, i + 4) for i in range(count - 4) if i // 4 + gap < length])
+        above = lax.ppermute(down, "dp", [(i, i - 4) for i in range(4, count) if i // 4 >= gap])
+    return sums[-1], below, above
+
+
+def pin(values):
+    return lax.optimization_barrier(values)
 
 
 def body(
@@ -657,84 +848,82 @@
 
     gain_columns = jnp.pad(norm_gains.astype(BF).T, ((0, 0), (0, HEAD_DIM - 2)))
     shard_one = jnp.concatenate(
-        [proj_qkv[part].astype(BF) for part in range(3)] + [gain_columns], axis=1
-    )
-    out_own = proj_out.astype(BF).T
-    out_other = across(out_own)
-    out_both = [
-        jnp.where(group == 0, out_own, out_other),
-        jnp.where(group == 0, out_other, out_own),
-    ]
+        [proj_qkv[part].astype(BF) for part in range(3)] + [gain_columns, proj_out.astype(BF).T],
+        axis=1,
+    )
     shard_two = jnp.concatenate(
         [proj_gate_up[0].astype(BF), proj_gate_up[1].astype(BF), proj_down.astype(BF).T], axis=1
     )
+    length = count // 4
     weights_one = lax.all_gather(shard_one, "dp", axis=0, tiled=True)
-    weights_two = lax.all_gather(shard_two, "dp", axis=0, tiled=True)
-    weights_out = lax.all_gather(jnp.concatenate(out_both, axis=1), "dp", axis=0, tiled=True)
-    gains = weights_one[:, 3 * local : 3 * local + 2].astype(F32).T
-    gain_one, gain_two = gains[0:1], gains[1:2]
-
+
+    places = jnp.arange(SEG, dtype=jnp.int32)
     starts = jnp.cumsum(doc_segments) - doc_segments
     memory_on = jnp.logical_not(jnp.any(starts == segment))
-    info = jnp.stack(
-        [rank, group, memory_on.astype(jnp.int32), 1 - rank]
-    ).astype(jnp.int32)
-    cosines, sines = rope_tables(SEG)
+    side = (device // 2) % 2
+    info = jnp.stack([rank, group, memory_on.astype(jnp.int32), side, device // 4]).astype(jnp.int32)
+    cosines, sines = rope_tables(places)
     valid = lax.dynamic_slice_in_dim(padding, segment * SEG, SEG)
     lane = jnp.arange(HEAD_DIM, dtype=jnp.int32)[None, :]
     bias = jnp.where((valid[:, None] == 0) & (lane == 0), NEGATIVE, 0.0).astype(BF)
     fetched = cache[retrieval[0]].reshape(RETR, 2, 2, 2, HEAD_DIM).transpose(2, 1, 3, 0, 4)
     mem_own = lax.dynamic_index_in_dim(fetched, rank, keepdims=False)
     mem_other = beside(lax.dynamic_index_in_dim(fetched, 1 - rank, keepdims=False))
-
-    inputs = tokens.astype(F32)
-    inverse_one = lax.rsqrt(jnp.mean(inputs * inputs, axis=-1, keepdims=True) + EPS)
-    normed_one = (inputs * inverse_one * gain_one).astype(BF)
-
-    send = project_pair(info, normed_one, weights_one, cosines, sines, 3)
+    weights_one, shard_two, mem_own, mem_other, bias, cosines, sines = pin(
+        (weights_one, shard_two, mem_own, mem_other, bias, cosines, sines)
+    )
+    weights_two = lax.all_gather(shard_two, "dp", axis=0, tiled=True)
+
+    send, normed_one, gains = project_first(info, tokens, weights_one, cosines, sines)
+    gain_one, gain_two = gains[0:1], gains[1:2]
     other = beside(send)
-    own = project_pair(info, normed_one, weights_one, cosines, sines, 0)
+    own = project_second(info, normed_one, weights_one, cosines, sines)
     out_keep, out_send, turned, logs = attend_forward(info, own, other, mem_own, mem_other, bias)
-    out_recv = beside(out_send)
-    pieces = (out_keep, out_recv, across(out_keep), across(out_recv))
-    middle, normed_two = middle_call(info, pieces, tokens, weights_out, gain_two)
-
-    half = rows // 2
-    feeds = [feed_call(normed_two, cotangent, weights_two, first, half) for first in (0, half)]
-    backs = [feed[3] for feed in feeds]
-    backs_other = [across(back) for back in backs]
-    hidden, grad_gate, grad_up = (
-        jnp.concatenate([feed[index] for feed in feeds], axis=0) for index in range(3)
-    )
+    attend_part, attended = attend_out_call(info, out_keep, beside(out_send), weights_one)
+    middle, normed_two = middle_call(tokens, attend_part, across(attend_part), gain_two)
+
+    earlier, backs, backs_other = (), [], []
+    for first in range(0, rows, TILE):
+        *earlier, back = feed_call(normed_two, cotangent, weights_two, first, TILE, earlier)
+        backs.append(back)
+        backs_other.append(across(back))
+    hidden, grad_gate, grad_up = earlier
+    feed_grads = feed_weight_call(normed_two, cotangent, hidden, grad_gate, grad_up)
+    hidden, _ = pin((hidden, feed_grads))
     feed_part = out_call(hidden, weights_two)
-    feed_other = across(feed_part)
-    feed_grads = feed_weight_call(normed_two, cotangent, hidden, grad_gate, grad_up)
-    back_two = jnp.concatenate(backs, axis=0)
-    back_two_other = jnp.concatenate(backs_other, axis=0)
-    grad_middle, grad_low, grad_keep, grad_send, gain_two_grad = residual_call(
-        info, middle, back_two, back_two_other, cotangent, gain_two, weights_out
-    )
+    middle, _ = pin((middle, feed_part))
+    earlier, gain_two_grad = (), 0.0
+    for index, first in enumerate(range(0, rows, TILE)):
+        if first + TILE == rows:
+            backs_other[index], feed_pinned = pin((backs_other[index], feed_part))
+            feed_other = across(feed_pinned)
+        *earlier, gain_part = residual_call(
+            info, middle, backs[index], backs_other[index], cotangent, gain_two, weights_one, first, earlier
+        )
+        gain_two_grad = gain_two_grad + gain_part
+    grad_middle, grad_low, grad_keep, grad_send = earlier
     grad_other = beside(grad_send)
+
+    d_keeps, d_others = [], []
+    for head in range(2):
+        d_keep, d_send = attend_backward(
+            info, own, other, mem_own, mem_other, bias, grad_keep, grad_other, turned, logs,
+            cosines, sines, head,
+        )
+        d_keeps.append(d_keep)
+        d_others.append(beside(d_send))
+    back_one, joined, gain_one_grad = back_call(info, d_keeps + d_others, weights_one, tokens)
+    back_one_other = across(back_one)
+    attend_slots = attend_weight_call(
+        info, normed_one, joined, grad_low, attended, gain_one_grad, gain_two_grad, shard
+    )
+    feed_other, attend_slots = pin((feed_other, attend_slots))
+    total, below, above = reduce_rows(attend_slots[:length], attend_slots[length:], count)
+    input_grad = input_call(grad_middle, back_one, back_one_other, tokens, gain_one)
     block_out = (middle + (feed_part.astype(F32) + feed_other.astype(F32))).astype(BF)
-
-    d_keep, d_send = attend_backward(
-        info, own, other, mem_own, mem_other, bias, grad_keep, grad_other, turned, logs, cosines, sines
-    )
-    d_other = beside(d_send)
-    back_one, joined, gain_one_grad = back_call(info, d_keep, d_other, weights_one, tokens)
-    back_one_other = across(back_one)
-    attend_grads = attend_weight_call(info, normed_one, joined, grad_low, out_keep, out_recv)
-    gain_grads = jnp.pad(
-        jnp.concatenate([gain_one_grad, gain_two_grad], axis=0).astype(BF).T,
-        ((0, 0), (0, HEAD_DIM - 2)),
-    )
-    input_grad = input_call(grad_middle, back_one, back_one_other, tokens, gain_one)
-
-    feed_sum = lax.psum_scatter(feed_grads, "dp", scatter_dimension=0, tiled=True)
-    attend_sum = lax.psum_scatter(
-        jnp.concatenate([attend_grads, gain_grads], axis=1), "dp", scatter_dimension=0, tiled=True
-    )
-    feed_sum, attend_sum = feed_sum.astype(F32), attend_sum.astype(F32)
+    input_grad, total, below, above = pin((input_grad, total, below, above))
+    attend_sum = total.astype(F32) + (below.astype(F32) + above.astype(F32))
+    feed_sum = lax.psum_scatter(feed_grads, "dp", scatter_dimension=0, tiled=True).astype(F32)
     gate_up_sum = jnp.stack([feed_sum[:, :hidden_here], feed_sum[:, hidden_here : 2 * hidden_here]])
     down_sum = feed_sum[:, 2 * hidden_here :].T
     qkv_sum = jnp.stack([attend_sum[:, part * local : (part + 1) * local] for part in range(3)])

time: 510 us -> 351 us (0.69)
  waiting for transfers between devices: 267 us -> 121 us
  starting transfers between devices: 11.8 us -> 33.5 us
  local copies, waits for them, and re-layouts: 52.5 us -> 31.2 us
  other arithmetic: 39.6 us -> 29.5 us
    ppermute x8, waiting for transfers between devices: 141 us -> 58.9 us  [across(): return lax.ppermute(value, 'mp', [(0, 1), (1, 0)])]
    reduce_scatter x1, waiting for transfers between devices: 45.3 us -> 0.01 us  [body(): lax.psum_scatter(feed_grads, 'dp', scatter_dimension=0, tiled=True)]
    all_gather x1, waiting for transfers between devices: 42 us -> 0.01 us  [body(): weights_two = lax.all_gather(shard_two, 'dp', axis=0, tiled=True)]
    unnamed x146 -> x128, local copies, waits for them, and re-layouts: 48.7 us -> 27.1 us
    ppermute x0 -> x14, starting transfers between devices: none -> 21 us  [the longest x3 12.7 us: reduce_rows(): lax.ppermute(up, 'dp', [(i, i + 4) for i in range(count - 4) if i // 4 +...]
    ppermute x0 -> x14, waiting for transfers between devices: none -> 20.2 us  [the longest x4 13.9 us: reduce_rows(): other = lax.ppermute(theirs, 'dp', [(i, i ^ 2) for i in range(count)])]
    concatenate x7 -> x0, other arithmetic: 6.99 us -> none  [the longest x2 3.65 us: body(): jnp.concatenate([feed[index] for feed in feeds], axis=0)]
    pallas_call x1 -> x4, Pallas kernels: 7.41 us -> 11.1 us  [residual_call(): pl.pallas_call(residual_kernel, out_shape=(jax.ShapeDtypeStruct((rows, D)...]
  transfers between devices with their start and end apart: 18 -> 31, of which waited for: 13 -> 13; matrix products, arithmetic and copies ran while one was open for 7% -> 8% of each run, Pallas kernels for 13% -> 27%
where the time goes in v2:
time: 351 us; the launch traced here: 347 us
  waiting for transfers between devices  121 us (34%)
  Pallas kernels  116 us (33%)
  starting transfers between devices  33.5 us (10%)
  local copies, waits for them, and re-layouts  31.2 us (9%)
  other arithmetic  29.5 us (8%)
  between operations  15.7 us (4%)
    ppermute x8, waiting for transfers between devices, across(): return lax.ppermute(value, 'mp', [(0, 1), (1, 0)])  58.9 us
    all_gather x1, waiting for transfers between devices, body(): weights_one = lax.all_gather(shard_one, 'dp', axis=0, tiled=True)  35.9 us
    unnamed x128, local copies, waits for them, and re-layouts  27.1 us
    pallas_call x4, Pallas kernels, feed_call(): pl.pallas_call(feed_kernel, out_shape=(jax.ShapeDtypeStruct((rows, width)...  22.6 us
    pallas_call x2, Pallas kernels, attend_backward(): pl.pallas_call(backward_kernel, out_shape=(jax.ShapeDtypeStruct((3, 1, ro...  17.3 us
    ppermute x4, waiting for transfers between devices, reduce_rows(): other = lax.ppermute(theirs, 'dp', [(i, i ^ 2) for i in range(count)])  13.9 us
    ppermute x3, starting transfers between devices, reduce_rows(): lax.ppermute(up, 'dp', [(i, i + 4) for i in range(count - 4) if i // 4 +...  12.7 us
    pallas_call x1, Pallas kernels, feed_weight_call(): pl.pallas_call(feed_weight_kernel, out_shape=pltpu.HBM((D, 3 * width), BF...  12.7 us
  transfers between devices with their start and end apart: 31, of which 13 were waited for; matrix products, arithmetic and copies ran while one was open for 8% of the time, Pallas kernels for 27%

profile of v2, /device:TPU:0, one launch (start us, length us, event | category | flops | bytes accessed | tf_op | source)
XLA Modules:
  0.0 346.7 jit_solution(9398486629554846104)
XLA Ops:
  11.7 1.8 gather_fusion
  18.6 5.7 %fusion.3 = (f32[2048,64]{1,0:T(8,128)}, f32[2048,64]{1,0:T(8,128)}, f32[2048,64]{1,0:T(8,128)}) fusion(f32[64]{0:T(128)S(1)} %negate_power_fusion, f32[2048]{0:T(1024)S(1)} %iota_convert_fusion), kind=kLoop, calls=%fused_computation.26 | loop fusion | flops 262144 | bytes 1581312 | tf_op jit(solution)/shard_map/neg | solution.py:62
  25.1 3.9 %pad_maximum_fusion = (f32[2048,128]{1,0:T(8,128)S(1)}, f32[2048,128]{1,0:T(8,128)}) fusion(f32[2048,64]{1,0:T(8,128)} %get-tuple-element.290, f32[2048,64]{1,0:T(8,128)} %get-tuple-element.289, f32[2048,64]{1,0:T(8,128)} %get-tuple-element.288), kind=kLoop, calls=%fused_computation.5 | loop fusion | flops 524288 | bytes 3670016 | tf_op jit(solution)/shard_map/concatenate | solution.py:62
  29.8 35.9 %all-gather.3.cloned.1.call-done.gain_columns.weight = bf16[1024,2176]{1,0:T(8,128)(2,1)} async-done(((bf16[64,2176]{1,0:T(8,128)(2,1)}), bf16[1024,2176]{1,0:T(8,128)(2,1)}) %all-gather.3.cloned.1.call-update) | async-done | bytes 4456464 | tf_op jit(solution)/shard_map/all_gather | solution.py:858
  67.6 2.3 copy-done.4
  71.1 4.6 %project_first.1 = (bf16[3,2,1024,128]{3,2,1,0:T(8,128)(2,1)S(1)}, bf16[1024,1024]{1,0:T(8,128)(2,1)S(1)}, f32[8,1024]{1,0:T(8,128)S(1)}) custom-call(s32[5]{0:T(128)S(1)} %stack.57.info, bf16[1024,1024]{1,0:T(8,128)(2,1)S(1)} %copy-done.14, bf16[1024,2176]{1,0:T(8,128)(2,1)S(1)} %copy-done.4, bf16[1024,2176]{1,0:T(8,128)(2,1)S(1)} %copy-done.4, ...), custom_call_target="tpu_custom_call" | custom-call | tf_op jit(solution)/shard_map/project_first/pallas_call | solution.py:111
  76.1 3.7 %project_second.1.own = bf16[3,2,1024,128]{3,2,1,0:T(8,128)(2,1)S(1)} custom-call(s32[5]{0:T(128)S(1)} %stack.57.info, bf16[1024,1024]{1,0:T(8,128)(2,1)S(1)} %get-tuple-element.116.normed, bf16[1024,2176]{1,0:T(8,128)(2,1)S(1)} %bitcast.74, f32[2048,128]{1,0:T(8,128)S(1)} %get-tuple-element.114.cosines, f32[2048,128]{1,0:T(8,128)S(1)} %copy-done.18), custom_call_target="tpu_custom_call" | custom-call | tf_op jit(solution)/shard_map/project_second/pallas_call | solution.py:142
  79.9 11.2 %attend_forward.1 = (bf16[2,1024,128]{2,1,0:T(8,128)(2,1)S(1)}, bf16[2,1024,128]{2,1,0:T(8,128)(2,1)S(1)}, f32[2,128,2048]{2,1,0:T(8,128)S(1)}, f32[2,1,2048]{2,1,0:T(1,128)S(1)}) custom-call(s32[5]{0:T(128)S(1)} %stack.57.info, bf16[3,2,1024,128]{3,2,1,0:T(8,128)(2,1)S(1)} %project_second.1.own, bf16[3,2,1024,128]{3,2,1,0:T(8,128)(2,1)S(1)} %collective-permute-done.1.other, ...), custom_call_target="tpu_custom_call" | custom-call | tf_op jit(solution)/shard_map/attend_forward/pallas_call | solution.py:234
  93.2 1.6 collective-permute-done.2.other
  94.9 2.7 attend_out.1
  100.1 46.3 %collective-permute-done.3.other = bf16[1024,1024]{1,0:T(8,128)(2,1)S(1)} collective-permute-done((bf16[1024,1024]{1,0:T(8,128)(2,1)S(1)}, bf16[1024,1024]{1,0:T(8,128)(2,1)S(1)}, u32[]{:S(2)}, u32[]{:S(2)}) %collective-permute-start.3) | collective-permute-done | bytes 2097184 | tf_op jit(solution)/shard_map/ppermute | solution.py:844
  148.0 2.0 copy-done.8
  151.4 3.5 copy-done.2
  156.5 5.5 %feed.4 = (bf16[1024,1408]{1,0:T(8,128)(2,1)S(1)}, bf16[1024,1408]{1,0:T(8,128)(2,1)S(1)}, bf16[1024,1408]{1,0:T(8,128)(2,1)S(1)}, bf16[256,1024]{1,0:T(8,128)(2,1)}) custom-call(bf16[1024,1024]{1,0:T(8,128)(2,1)S(1)} %copy-done.11, bf16[1024,1024]{1,0:T(8,128)(2,1)S(1)} %copy-done.5, bf16[1024,4224]{1,0:T(8,128)(2,1)S(1)} %copy-done.2, ...), custom_call_target="tpu_custom_call" | custom-call | flops 50000000 | tf_op jit(solution)/shard_map/feed/pallas_call | solution.py:457
  162.0 5.5 %feed.5 = (bf16[1024,1408]{1,0:T(8,128)(2,1)S(1)}, bf16[1024,1408]{1,0:T(8,128)(2,1)S(1)}, bf16[1024,1408]{1,0:T(8,128)(2,1)S(1)}, bf16[256,1024]{1,0:T(8,128)(2,1)}) custom-call(bf16[1024,1024]{1,0:T(8,128)(2,1)S(1)} %copy-done.11, bf16[1024,1024]{1,0:T(8,128)(2,1)S(1)} %copy-done.5, ...), custom_call_target="tpu_custom_call", output_to_operand_aliasing={{0}: (5, {}), {1}: (6, {}), {2}: (7, {})} | custom-call | flops 50000000 | tf_op jit(solution)/shard_map/feed/pallas_call | solution.py:457
  167.5 6.0 %feed.6 = (bf16[1024,1408]{1,0:T(8,128)(2,1)S(1)}, bf16[1024,1408]{1,0:T(8,128)(2,1)S(1)}, bf16[1024,1408]{1,0:T(8,128)(2,1)S(1)}, bf16[256,1024]{1,0:T(8,128)(2,1)}) custom-call(bf16[1024,1024]{1,0:T(8,128)(2,1)S(1)} %copy-done.11, bf16[1024,1024]{1,0:T(8,128)(2,1)S(1)} %copy-done.5, ...), custom_call_target="tpu_custom_call", output_to_operand_aliasing={{0}: (5, {}), {1}: (6, {}), {2}: (7, {})} | custom-call | flops 50000000 | tf_op jit(solution)/shard_map/feed/pallas_call | solution.py:457
  173.5 5.5 %feed.7 = (bf16[1024,1408]{1,0:T(8,128)(2,1)S(1)}, bf16[1024,1408]{1,0:T(8,128)(2,1)S(1)}, bf16[1024,1408]{1,0:T(8,128)(2,1)S(1)}, bf16[256,1024]{1,0:T(8,128)(2,1)}) custom-call(bf16[1024,1024]{1,0:T(8,128)(2,1)S(1)} %copy-done.11, bf16[1024,1024]{1,0:T(8,128)(2,1)S(1)} %copy-done.5, ...), custom_call_target="tpu_custom_call", output_to_operand_aliasing={{0}: (5, {}), {1}: (6, {}), {2}: (7, {})} | custom-call | flops 50000000 | tf_op jit(solution)/shard_map/feed/pallas_call | solution.py:457
  183.1 12.7 %feed_weights.1 = bf16[1024,4224]{1,0:T(8,128)(2,1)} custom-call(bf16[1024,1024]{1,0:T(8,128)(2,1)S(1)} %copy-done.11, bf16[1024,1024]{1,0:T(8,128)(2,1)S(1)} %copy-done.5, bf16[1024,1408]{1,0:T(8,128)(2,1)S(1)} %get-tuple-element.140.hidden, bf16[1024,1408]{1,0:T(8,128)(2,1)S(1)} %get-tuple-element.138.gate_grad, ...), custom_call_target="tpu_custom_call" | custom-call | flops 50000000 | tf_op jit(solution)/shard_map/feed_weights/pallas_call | solution.py:506
  195.8 1.7 copy-done.6
  197.5 3.5 %copy-done.3 = bf16[1024,4224]{1,0:T(8,128)(2,1)S(1)} copy-done((bf16[1024,4224]{1,0:T(8,128)(2,1)S(1)}, bf16[1024,4224]{1,0:T(8,128)(2,1)}, u32[]{:S(2)}) %copy-start.3) | copy-done | bytes 8650776
  201.0 1.9 copy-done.7
  202.9 5.2 %feed_out.1 = bf16[1024,1024]{1,0:T(8,128)(2,1)} custom-call(bf16[1024,1408]{1,0:T(8,128)(2,1)S(1)} %copy-done.7, bf16[1024,4224]{1,0:T(8,128)(2,1)S(1)} %copy-done.3), custom_call_target="tpu_custom_call" | custom-call | flops 50000000 | tf_op jit(solution)/shard_map/feed_out/pallas_call | solution.py:478
  208.2 1.8 collective-permute-start.5
  210.0 2.8 residual.4
  212.8 4.0 %collective-permute-done.7.back_other = bf16[256,1024]{1,0:T(8,128)(2,1)} collective-permute-done((bf16[256,1024]{1,0:T(8,128)(2,1)}, bf16[256,1024]{1,0:T(8,128)(2,1)}, u32[]{:S(2)}, u32[]{:S(2)}) %collective-permute-start.7) | collective-permute-done | bytes 524320 | tf_op jit(solution)/shard_map/ppermute | solution.py:844
  216.7 2.7 residual.5
  219.5 8.5 %collective-permute-done.6.back_other = bf16[256,1024]{1,0:T(8,128)(2,1)} collective-permute-done((bf16[256,1024]{1,0:T(8,128)(2,1)}, bf16[256,1024]{1,0:T(8,128)(2,1)}, u32[]{:S(2)}, u32[]{:S(2)}) %collective-permute-start.6) | collective-permute-done | bytes 524320 | tf_op jit(solution)/shard_map/ppermute | solution.py:844
  228.0 2.7 residual.6
  230.7 2.9 residual.7
  233.7 2.0 copy-done.12
  235.7 1.9 collective-permute-done.9.grad_other
  237.7 8.6 %attend_backward.3 = (bf16[3,1,1024,128]{3,2,1,0:T(8,128)(2,1)S(1)}, bf16[3,1,1024,128]{3,2,1,0:T(8,128)(2,1)S(1)}) custom-call(s32[5]{0:T(128)S(1)} %stack.57.info, bf16[3,2,1024,128]{3,2,1,0:T(8,128)(2,1)S(1)} %copy-done.21, bf16[3,2,1024,128]{3,2,1,0:T(8,128)(2,1)S(1)} %copy-done.23, bf16[2,2,128,128]{3,2,1,0:T(8,128)(2,1)S(1)} %bitcast.78, ...), custom_call_target="tpu_custom_call" | custom-call | tf_op jit(solution)/shard_map/attend_backward/pallas_call | solution.py:336
  246.5 8.8 %attend_backward.2 = (bf16[3,1,1024,128]{3,2,1,0:T(8,128)(2,1)S(1)}, bf16[3,1,1024,128]{3,2,1,0:T(8,128)(2,1)S(1)}) custom-call(s32[5]{0:T(128)S(1)} %stack.57.info, bf16[3,2,1024,128]{3,2,1,0:T(8,128)(2,1)S(1)} %copy-done.21, bf16[3,2,1024,128]{3,2,1,0:T(8,128)(2,1)S(1)} %copy-done.23, bf16[2,2,128,128]{3,2,1,0:T(8,128)(2,1)S(1)} %bitcast.79, ...), custom_call_target="tpu_custom_call" | custom-call | tf_op jit(solution)/shard_map/attend_backward/pallas_call | solution.py:336
  255.7 1.9 collective-permute-done.10.other_one
  257.6 7.3 %back.1 = (bf16[1024,1024]{1,0:T(8,128)(2,1)}, bf16[1024,1536]{1,0:T(8,128)(2,1)S(1)}, f32[1,1024]{1,0:T(1,128)S(1)}) custom-call(s32[5]{0:T(128)S(1)} %stack.57.info, bf16[3,1,1024,128]{3,2,1,0:T(8,128)(2,1)S(1)} %get-tuple-element.164.own_one, bf16[3,1,1024,128]{3,2,1,0:T(8,128)(2,1)S(1)} %get-tuple-element.165.own_two, ...), custom_call_target="tpu_custom_call" | custom-call | flops 50000000 | tf_op jit(solution)/shard_map/back/pallas_call | solution.py:597
  266.4 7.7 %attend_weights.1 = (bf16[2,64,2176]{2,1,0:T(8,128)(2,1)S(1)}, bf16[2,64,2176]{2,1,0:T(8,128)(2,1)S(1)}, bf16[2,64,2176]{2,1,0:T(8,128)(2,1)S(1)}, bf16[2,64,217...) custom-call(s32[5]{0:T(128)S(1)} %stack.57.info, ...), custom_call_target="tpu_custom_call" | custom-call | tf_op jit(solution)/shard_map/attend_weights/pallas_call | solution.py:660
  278.5 8.2 %collective-permute-done.16.right = bf16[64,2176]{1,0:T(8,128)(2,1)S(1)} collective-permute-done((bf16[64,2176]{1,0:T(8,128)(2,1)S(1)}, bf16[64,2176]{1,0:T(8,128)(2,1)S(1)}, u32[]{:S(2)}, u32[]{:S(2)}) %collective-permute-start.16) | collective-permute-done | bytes 278560 | tf_op jit(solution)/shard_map/ppermute | solution.py:773
  287.5 3.4 collective-permute-start.21
  291.0 5.7 %collective-permute-done.20.right = bf16[64,2176]{1,0:T(8,128)(2,1)S(1)} collective-permute-done((bf16[64,2176]{1,0:T(8,128)(2,1)S(1)}, bf16[64,2176]{1,0:T(8,128)(2,1)S(1)}, u32[]{:S(2)}, u32[]{:S(2)}) %collective-permute-start.20) | collective-permute-done | bytes 278560 | tf_op jit(solution)/shard_map/ppermute | solution.py:773
  299.0 2.7 collective-permute-done.21.right
  301.8 4.7 %collective-permute-start.22 = (bf16[64,2176]{1,0:T(8,128)(2,1)S(1)}, bf16[64,2176]{1,0:T(8,128)(2,1)S(1)}, u32[]{:S(2)}, u32[]{:S(2)}) collective-permute-start(bf16[64,2176]{1,0:T(8,128)(2,1)S(1)} %low_add.10), channel_id=1, source_target_pairs={{0,8},{2,10},{4,12},{6,14},{8,16},{10,18},{12,20},{14,22},{1,9},{3... | collective-permute-start | bytes 835592 | tf_op jit(solution)/shard_map/ppermute | solution.py:800
  306.7 2.2 collective-permute-start.14
  309.9 2.2 collective-permute-done.22.up_in
  312.8 4.6 %collective-permute-start.25 = (bf16[64,2176]{1,0:T(8,128)(2,1)S(1)}, bf16[64,2176]{1,0:T(8,128)(2,1)S(1)}, u32[]{:S(2)}, u32[]{:S(2)}) collective-permute-start(bf16[64,2176]{1,0:T(8,128)(2,1)S(1)} %get-tuple-element.203), channel_id=1, source_target_pairs={{0,8},{2,10},{4,12},{6,14},{8,16},{10,18},{12,20},{14,22},{16,24},... | collective-permute-start | bytes 835592 | tf_op jit(solution)/shard_map/ppermute | solution.py:800
  318.8 6.1 %add_convert_fusion = bf16[1024,1024]{1,0:T(8,128)(2,1)} fusion(f32[1024,1024]{1,0:T(8,128)} %copy-done.8, bf16[1024,1024]{1,0:T(8,128)(2,1)} %collective-permute-done.5, bf16[1024,1024]{1,0:T(8,128)(2,1)} %feed_out.1), kind=kLoop, calls=%fused_computation.1 | loop fusion | flops 5242880 | bytes 10485760 | tf_op jit(solution)/shard_map/convert_element_type | solution.py:923
  325.0 5.1 %input_grad.1 = bf16[1024,1024]{1,0:T(8,128)(2,1)} custom-call(f32[1024,1024]{1,0:T(8,128)S(1)} %copy-done.13, bf16[1024,1024]{1,0:T(8,128)(2,1)} %get-tuple-element.186.back_own, bf16[1024,1024]{1,0:T(8,128)(2,1)} %collective-permute-done.12.back_other, bf16[1024,1024]{1,0:T(8,128)(2,1)S(1)} %copy-done.17, f32[1,1024]{1,0:T(1,128)S(1)} %get-tuple-element.286.gain), custom_call_target="tpu_custom_call" | custom-call | flops 12582912 | bytes 12582912 | tf_op jit(solution)/shard_map/input_grad/pallas_call | solution.py:695
  330.3 1.7 collective-permute-start.27
  338.2 1.7 multiply_subtract_fusion
  (218 shorter events, 46.5 us)
Async XLA Ops:
  7.2 9.4 %copy-start.37 = (f32[2,64,1408]{2,1,0:T(8,128)S(1)}, f32[2,64,1408]{2,1,0:T(8,128)}, u32[]{:S(2)}) copy-start(f32[2,64,1408]{2,1,0:T(8,128)} %param.25) | copy-start | bytes 2162692
  7.2 58.6 %all-gather.3.cloned.1.call-start = ((), (), s32[]{:S(2)}) async-start(), calls=%async_computation.1 | async-start | bytes 4734976 | tf_op jit(solution)/shard_map/all_gather | solution.py:858
  11.0 140.4 %all-gather.5.cloned.1.call-start = ((), (), s32[]{:S(2)}) async-start(), calls=%async_computation.2 | async-start | bytes 9191424 | tf_op jit(solution)/shard_map/all_gather | solution.py:875
  16.1 13.0 %collective-permute-start = (bf16[2,2,128,128]{3,2,1,0:T(8,128)(2,1)}, bf16[2,2,128,128]{3,2,1,0:T(8,128)(2,1)S(1)}, u32[]{:S(2)}, u32[]{:S(2)}) collective-permute-start(bf16[2,2,128,128]{3,2,1,0:T(8,128)(2,1)} %bitcast.21), channel_id=1, source_target_pairs={{0,2},{2,0},{4,6},{6,4},{8,10},{10,8},{12,14},{14,12},{16,18},{18,... | collective-permute-start | bytes 393224 | tf_op jit(solution)/shard_map/ppermute | solution.py:847
  25.1 40.9 %copy-start.56 = (s32[3]{0:T(128)S(1)}, s32[3]{0:T(128)}, u32[]{:S(2)}) copy-start(s32[3]{0:T(128)} %param.39) | copy-start | bytes 40
  25.1 42.5 %copy-start.14 = (bf16[1024,1024]{1,0:T(8,128)(2,1)S(1)}, bf16[1024,1024]{1,0:T(8,128)(2,1)}, u32[]{:S(2)}) copy-start(bf16[1024,1024]{1,0:T(8,128)(2,1)} %tokens.7) | copy-start | bytes 6291460
  65.8 10.3 %slice-start = ((s8[4456448]{0:T(1024)(128)(4,1)}), s8[262144]{0:T(1024)(128)(4,1)S(1)}, s32[]{:S(2)}) async-start(s8[4456448]{0:T(1024)(128)(4,1)} %bitcast.73), calls=%async_computation.4 | async-start | bytes 524288
  65.8 269.3 %reduce-scatter.2.cloned.1.call-start = ((), (), s32[]{:S(2)}) async-start(), calls=%async_computation.3 | async-start | bytes 9191424 | tf_op jit(solution)/shard_map/reduce_scatter | solution.py:926
  75.7 4.1 %collective-permute-start.1 = (bf16[3,2,1024,128]{3,2,1,0:T(8,128)(2,1)S(1)}, bf16[3,2,1024,128]{3,2,1,0:T(8,128)(2,1)S(1)}, u32[]{:S(2)}, u32[]{:S(2)}) collective-permute-start(bf16[3,2,1024,128]{3,2,1,0:T(8,128)(2,1)S(1)} %get-tuple-element.117), channel_id=1, source_target_pairs={{0,2},{2,0},{4,6},{6,4},{8,10},{10,8},{12,14},{14,12},{16,18},{18,... | collective-permute-start | bytes 4718600 | tf_op jit(solution)/shard_map/ppermute | solution.py:847
  79.8 15.1 %copy-start.20 = (bf16[3,2,1024,128]{3,2,1,0:T(8,128)(2,1)}, bf16[3,2,1024,128]{3,2,1,0:T(8,128)(2,1)S(1)}, u32[]{:S(2)}) copy-start(bf16[3,2,1024,128]{3,2,1,0:T(8,128)(2,1)S(1)} %project_second.1.own) | copy-start | bytes 4718596
  79.9 15.0 %copy-start.22 = (bf16[3,2,1024,128]{3,2,1,0:T(8,128)(2,1)}, bf16[3,2,1024,128]{3,2,1,0:T(8,128)(2,1)S(1)}, u32[]{:S(2)}) copy-start(bf16[3,2,1024,128]{3,2,1,0:T(8,128)(2,1)S(1)} %collective-permute-done.1.other) | copy-start | bytes 4718596
  93.0 1.9 collective-permute-start.2
  94.9 51.5 %copy-start.15 = (bf16[1024,1024]{1,0:T(8,128)(2,1)S(1)}, bf16[1024,1024]{1,0:T(8,128)(2,1)}, u32[]{:S(2)}) copy-start(bf16[1024,1024]{1,0:T(8,128)(2,1)} %tokens.7) | copy-start | bytes 6291460
  98.6 47.8 %collective-permute-start.3 = (bf16[1024,1024]{1,0:T(8,128)(2,1)S(1)}, bf16[1024,1024]{1,0:T(8,128)(2,1)S(1)}, u32[]{:S(2)}, u32[]{:S(2)}) collective-permute-start(bf16[1024,1024]{1,0:T(8,128)(2,1)S(1)} %get-tuple-element.123.own), channel_id=1, source_target_pairs={{0,1},{1,0},{2,3},{3,2},{4,5},{5,4},{6,7},{7,6},{8,9},{9,8},{10,11... | collective-permute-start | bytes 6291464 | tf_op jit(solution)/shard_map/ppermute | solution.py:844
  179.1 29.1 %collective-permute-start.4 = (bf16[256,1024]{1,0:T(8,128)(2,1)}, bf16[256,1024]{1,0:T(8,128)(2,1)}, u32[]{:S(2)}, u32[]{:S(2)}) collective-permute-start(bf16[256,1024]{1,0:T(8,128)(2,1)} %get-tuple-element.142.back_own), channel_id=1, source_target_pairs={{0,1},{1,0},{2,3},{3,2},{4,5},{5,4},{6,7},{7,6},{8,9},{9,8},{10,11... | collective-permute-start | bytes 1572872 | tf_op jit(solution)/shard_map/ppermute | solution.py:844
  180.5 29.4 %collective-permute-start.8 = (bf16[256,1024]{1,0:T(8,128)(2,1)}, bf16[256,1024]{1,0:T(8,128)(2,1)}, u32[]{:S(2)}, u32[]{:S(2)}) collective-permute-start(bf16[256,1024]{1,0:T(8,128)(2,1)} %get-tuple-element.147.back_own), channel_id=1, source_target_pairs={{0,1},{1,0},{2,3},{3,2},{4,5},{5,4},{6,7},{7,6},{8,9},{9,8},{10,11... | collective-permute-start | bytes 1572872 | tf_op jit(solution)/shard_map/ppermute | solution.py:844
  181.1 35.6 %collective-permute-start.7 = (bf16[256,1024]{1,0:T(8,128)(2,1)}, bf16[256,1024]{1,0:T(8,128)(2,1)}, u32[]{:S(2)}, u32[]{:S(2)}) collective-permute-start(bf16[256,1024]{1,0:T(8,128)(2,1)} %get-tuple-element.146.back_own), channel_id=1, source_target_pairs={{0,1},{1,0},{2,3},{3,2},{4,5},{5,4},{6,7},{7,6},{8,9},{9,8},{10,11... | collective-permute-start | bytes 1572872 | tf_op jit(solution)/shard_map/ppermute | solution.py:844
  182.6 45.4 %collective-permute-start.6 = (bf16[256,1024]{1,0:T(8,128)(2,1)}, bf16[256,1024]{1,0:T(8,128)(2,1)}, u32[]{:S(2)}, u32[]{:S(2)}) collective-permute-start(bf16[256,1024]{1,0:T(8,128)(2,1)} %get-tuple-element.145.back_own), channel_id=1, source_target_pairs={{0,1},{1,0},{2,3},{3,2},{4,5},{5,4},{6,7},{7,6},{8,9},{9,8},{10,11... | collective-permute-start | bytes 1572872 | tf_op jit(solution)/shard_map/ppermute | solution.py:844
  197.5 12.5 %slice-start.2 = ((s8[4456448]{0:T(1024)(128)(4,1)}), s8[262144]{0:T(1024)(128)(4,1)S(1)}, s32[]{:S(2)}) async-start(s8[4456448]{0:T(1024)(128)(4,1)} %bitcast.75), calls=%async_computation.6 | async-start | bytes 524288
  202.9 7.1 %slice-start.3 = ((s8[4456448]{0:T(1024)(128)(4,1)}), s8[4194304]{0:T(1024)(128)(4,1)S(1)}, s32[]{:S(2)}) async-start(s8[4456448]{0:T(1024)(128)(4,1)} %bitcast.75), calls=%async_computation.7 | async-start | bytes 8388608
  202.9 7.1 %copy-start.9 = (f32[1024,1024]{1,0:T(8,128)S(1)}, f32[1024,1024]{1,0:T(8,128)}, u32[]{:S(2)}) copy-start(f32[1024,1024]{1,0:T(8,128)} %copy-done.8) | copy-start | bytes 12582916
  208.2 65.9 %collective-permute-start.5 = (bf16[1024,1024]{1,0:T(8,128)(2,1)}, bf16[1024,1024]{1,0:T(8,128)(2,1)}, u32[]{:S(2)}, u32[]{:S(2)}) collective-permute-start(bf16[1024,1024]{1,0:T(8,128)(2,1)} %feed_out.1), channel_id=1, source_target_pairs={{0,1},{1,0},{2,3},{3,2},{4,5},{5,4},{6,7},{7,6},{8,9},{9,8},{10,11... | collective-permute-start | bytes 6291464 | tf_op jit(solution)/shard_map/ppermute | solution.py:844
  230.6 7.0 %copy-start.19 = (f32[2048,128]{1,0:T(8,128)S(1)}, f32[2048,128]{1,0:T(8,128)}, u32[]{:S(2)}) copy-start(f32[2048,128]{1,0:T(8,128)} %get-tuple-element.115.sines) | copy-start | bytes 3145732
  230.6 7.0 %copy-start.21 = (bf16[3,2,1024,128]{3,2,1,0:T(8,128)(2,1)S(1)}, bf16[3,2,1024,128]{3,2,1,0:T(8,128)(2,1)}, u32[]{:S(2)}) copy-start(bf16[3,2,1024,128]{3,2,1,0:T(8,128)(2,1)} %copy-done.20) | copy-start | bytes 4718596
  230.7 7.0 %copy-start.23 = (bf16[3,2,1024,128]{3,2,1,0:T(8,128)(2,1)S(1)}, bf16[3,2,1024,128]{3,2,1,0:T(8,128)(2,1)}, u32[]{:S(2)}) copy-start(bf16[3,2,1024,128]{3,2,1,0:T(8,128)(2,1)} %copy-done.22) | copy-start | bytes 4718596
  230.7 7.0 %copy-start.27 = (bf16[2048,128]{1,0:T(8,128)(2,1)S(1)}, bf16[2048,128]{1,0:T(8,128)(2,1)}, u32[]{:S(2)}) copy-start(bf16[2048,128]{1,0:T(8,128)(2,1)} %select_convert_fusion.bias) | copy-start | bytes 1572868
  235.7 1.9 collective-permute-start.9
  246.2 11.4 %copy-start.16 = (bf16[1024,1024]{1,0:T(8,128)(2,1)S(1)}, bf16[1024,1024]{1,0:T(8,128)(2,1)}, u32[]{:S(2)}) copy-start(bf16[1024,1024]{1,0:T(8,128)(2,1)} %tokens.7) | copy-start | bytes 6291460
  246.3 9.4 %collective-permute-start.11 = (bf16[3,1,1024,128]{3,2,1,0:T(8,128)(2,1)S(1)}, bf16[3,1,1024,128]{3,2,1,0:T(8,128)(2,1)S(1)}, u32[]{:S(2)}, u32[]{:S(2)}) collective-permute-start(bf16[3,1,1024,128]{3,2,1,0:T(8,128)(2,1)S(1)} %get-tuple-element.167), channel_id=1, source_target_pairs={{0,2},{2,0},{4,6},{6,4},{8,10},{10,8},{12,14},{14,12},{16,18},{18,... | collective-permute-start | bytes 2359304 | tf_op jit(solution)/shard_map/ppermute | solution.py:847
  255.3 2.4 collective-permute-start.10
  257.6 8.8 %copy-start.25 = (bf16[1024,1024]{1,0:T(8,128)(2,1)S(1)}, bf16[1024,1024]{1,0:T(8,128)(2,1)}, u32[]{:S(2)}) copy-start(bf16[1024,1024]{1,0:T(8,128)(2,1)} %copy-done.24) | copy-start | bytes 6291460
  257.6 8.8 %copy-start.34 = (bf16[1024,512]{1,0:T(8,128)(2,1)S(1)}, bf16[1024,512]{1,0:T(8,128)(2,1)}, u32[]{:S(2)}) copy-start(bf16[1024,512]{1,0:T(8,128)(2,1)} %copy-done.33) | copy-start | bytes 3145732
  264.9 60.1 %collective-permute-start.12 = (bf16[1024,1024]{1,0:T(8,128)(2,1)}, bf16[1024,1024]{1,0:T(8,128)(2,1)}, u32[]{:S(2)}, u32[]{:S(2)}) collective-permute-start(bf16[1024,1024]{1,0:T(8,128)(2,1)} %get-tuple-element.186.back_own), channel_id=1, source_target_pairs={{0,1},{1,0},{2,3},{3,2},{4,5},{5,4},{6,7},{7,6},{8,9},{9,8},{10,11... | collective-permute-start | bytes 6291464 | tf_op jit(solution)/shard_map/ppermute | solution.py:844
  274.1 2.0 collective-permute-start.15
  274.2 2.8 collective-permute-start.19
  274.6 12.9 %collective-permute-start.17 = (bf16[2,64,2176]{2,1,0:T(8,128)(2,1)S(1)}, bf16[2,64,2176]{2,1,0:T(8,128)(2,1)S(1)}, u32[]{:S(2)}, u32[]{:S(2)}) collective-permute-start(bf16[2,64,2176]{2,1,0:T(8,128)(2,1)S(1)} %get-tuple-element.196), channel_id=1, source_target_pairs={{0,2},{2,0},{4,6},{6,4},{8,10},{10,8},{12,14},{14,12},{16,18},{18,... | collective-permute-start | bytes 1671176 | tf_op jit(solution)/shard_map/ppermute | solution.py:771
  276.2 10.5 %collective-permute-start.16 = (bf16[64,2176]{1,0:T(8,128)(2,1)S(1)}, bf16[64,2176]{1,0:T(8,128)(2,1)S(1)}, u32[]{:S(2)}, u32[]{:S(2)}) collective-permute-start(bf16[64,2176]{1,0:T(8,128)(2,1)S(1)} %get-tuple-element.194), channel_id=1, source_target_pairs={{0,4},{2,6},{4,0},{6,2},{8,12},{10,14},{12,8},{14,10},{16,20},{18,... | collective-permute-start | bytes 835592 | tf_op jit(solution)/shard_map/ppermute | solution.py:773
  277.1 19.6 %collective-permute-start.20 = (bf16[64,2176]{1,0:T(8,128)(2,1)S(1)}, bf16[64,2176]{1,0:T(8,128)(2,1)S(1)}, u32[]{:S(2)}, u32[]{:S(2)}) collective-permute-start(bf16[64,2176]{1,0:T(8,128)(2,1)S(1)} %get-tuple-element.202), channel_id=1, source_target_pairs={{0,4},{2,6},{4,0},{6,2},{8,12},{10,14},{12,8},{14,10},{16,20},{18,... | collective-permute-start | bytes 835592 | tf_op jit(solution)/shard_map/ppermute | solution.py:773
  278.5 28.1 %collective-permute-start.13 = (bf16[2,64,2176]{2,1,0:T(8,128)(2,1)}, bf16[2,64,2176]{2,1,0:T(8,128)(2,1)S(1)}, u32[]{:S(2)}, u32[]{:S(2)}) collective-permute-start(bf16[2,64,2176]{2,1,0:T(8,128)(2,1)} %get-tuple-element.188), channel_id=1, source_target_pairs={{0,2},{2,0},{4,6},{6,4},{8,10},{10,8},{12,14},{14,12},{16,18},{18,... | collective-permute-start | bytes 1671176 | tf_op jit(solution)/shard_map/ppermute | solution.py:771
  286.8 10.8 %collective-permute-start.23 = (bf16[64,2176]{1,0:T(8,128)(2,1)S(1)}, bf16[64,2176]{1,0:T(8,128)(2,1)S(1)}, u32[]{:S(2)}, u32[]{:S(2)}) collective-permute-start(bf16[64,2176]{1,0:T(8,128)(2,1)S(1)} %low_add.7.first), channel_id=1, source_target_pairs={{24,16},{26,18},{28,20},{30,22},{25,17},{27,19},{29,21},{31,23}} | collective-permute-start | bytes 835592 | tf_op jit(solution)/shard_map/ppermute | solution.py:801
  287.5 14.2 %collective-permute-start.21 = (bf16[64,2176]{1,0:T(8,128)(2,1)S(1)}, bf16[64,2176]{1,0:T(8,128)(2,1)S(1)}, u32[]{:S(2)}, u32[]{:S(2)}) collective-permute-start(bf16[64,2176]{1,0:T(8,128)(2,1)S(1)} %low_add.7.first), channel_id=1, source_target_pairs={{0,8},{2,10},{4,12},{6,14},{1,9},{3,11},{5,13},{7,15}} | collective-permute-start | bytes 835592 | tf_op jit(solution)/shard_map/ppermute | solution.py:800
  296.7 12.1 %collective-permute-start.18 = (bf16[64,2176]{1,0:T(8,128)(2,1)S(1)}, bf16[64,2176]{1,0:T(8,128)(2,1)}, u32[]{:S(2)}, u32[]{:S(2)}) collective-permute-start(bf16[64,2176]{1,0:T(8,128)(2,1)S(1)} %get-tuple-element.198), channel_id=1, source_target_pairs={{0,4},{2,6},{4,0},{6,2},{8,12},{10,14},{12,8},{14,10},{16,20},{18,... | collective-permute-start | bytes 835592 | tf_op jit(solution)/shard_map/ppermute | solution.py:773
  298.3 11.5 %collective-permute-start.24 = (bf16[64,2176]{1,0:T(8,128)(2,1)}, bf16[64,2176]{1,0:T(8,128)(2,1)S(1)}, u32[]{:S(2)}, u32[]{:S(2)}) collective-permute-start(bf16[64,2176]{1,0:T(8,128)(2,1)} %low_add.11), channel_id=1, source_target_pairs={{16,8},{18,10},{20,12},{22,14},{24,16},{26,18},{28,20},{30,22},{17... | collective-permute-start | bytes 835592 | tf_op jit(solution)/shard_map/ppermute | solution.py:801
  301.8 10.3 %collective-permute-start.22 = (bf16[64,2176]{1,0:T(8,128)(2,1)S(1)}, bf16[64,2176]{1,0:T(8,128)(2,1)S(1)}, u32[]{:S(2)}, u32[]{:S(2)}) collective-permute-start(bf16[64,2176]{1,0:T(8,128)(2,1)S(1)} %low_add.10), channel_id=1, source_target_pairs={{0,8},{2,10},{4,12},{6,14},{8,16},{10,18},{12,20},{14,22},{1,9},{3... | collective-permute-start | bytes 835592 | tf_op jit(solution)/shard_map/ppermute | solution.py:800
  306.7 18.2 %collective-permute-start.14 = (bf16[64,2176]{1,0:T(8,128)(2,1)S(1)}, bf16[64,2176]{1,0:T(8,128)(2,1)S(1)}, u32[]{:S(2)}, u32[]{:S(2)}) collective-permute-start(bf16[64,2176]{1,0:T(8,128)(2,1)S(1)} %get-tuple-element.190), channel_id=1, source_target_pairs={{0,4},{2,6},{4,0},{6,2},{8,12},{10,14},{12,8},{14,10},{16,20},{18,... | collective-permute-start | bytes 835592 | tf_op jit(solution)/shard_map/ppermute | solution.py:773
  312.8 17.3 %collective-permute-start.25 = (bf16[64,2176]{1,0:T(8,128)(2,1)S(1)}, bf16[64,2176]{1,0:T(8,128)(2,1)S(1)}, u32[]{:S(2)}, u32[]{:S(2)}) collective-permute-start(bf16[64,2176]{1,0:T(8,128)(2,1)S(1)} %get-tuple-element.203), channel_id=1, source_target_pairs={{0,8},{2,10},{4,12},{6,14},{8,16},{10,18},{12,20},{14,22},{16,24},... | collective-permute-start | bytes 835592 | tf_op jit(solution)/shard_map/ppermute | solution.py:800
  317.5 12.7 %collective-permute-start.26 = (bf16[64,2176]{1,0:T(8,128)(2,1)S(1)}, bf16[64,2176]{1,0:T(8,128)(2,1)S(1)}, u32[]{:S(2)}, u32[]{:S(2)}) collective-permute-start(bf16[64,2176]{1,0:T(8,128)(2,1)S(1)} %get-tuple-element.204), channel_id=1, source_target_pairs={{8,0},{10,2},{12,4},{14,6},{16,8},{18,10},{20,12},{22,14},{24,16},... | collective-permute-start | bytes 835592 | tf_op jit(solution)/shard_map/ppermute | solution.py:801
  330.3 4.0 %collective-permute-start.27 = (f32[1,64]{0,1:T(8,128)S(1)}, f32[1,64]{0,1:T(8,128)S(1)}, u32[]{:S(2)}, u32[]{:S(2)}) collective-permute-start(f32[1,64]{0,1:T(8,128)S(1)} %bitcast.81), channel_id=1, source_target_pairs={{0,1},{1,0},{2,3},{3,2},{4,5},{5,4},{6,7},{7,6},{8,9},{9,8},{10,11... | collective-permute-start | bytes 776 | tf_op jit(solution)/shard_map/ppermute | solution.py:844
  (44 other events, 134.2 us)
Sparse Core Ops, SparseCore 0:
  11.1 54.6 all-gather.2
  68.6 75.0 all-gather.4
  197.6 112.0 reduce-scatter.1

commit v3 on v2

--- a/solution.py
+++ b/solution.py
@@ -28,6 +28,7 @@
 F32 = jnp.float32
 MIB = 1024 * 1024
 TILE = 256
+PART = 512
 VMEM = 26
 WEIGH = 1.0
 
@@ -134,7 +135,7 @@
         compiler_params=params(VMEM),
         cost_estimate=cost(0, 0),
         name="project_first",
-    )(info, tokens, weights, weights, cosines, sines)
+    )(info, in_hbm(tokens), weights, weights, in_hbm(cosines), in_hbm(sines))
 
 
 def project_second(info, normed, weights, cosines, sines):
@@ -236,7 +237,7 @@
         out_shape=(
             jax.ShapeDtypeStruct((2, rows, HEAD_DIM), BF),
             jax.ShapeDtypeStruct((2, rows, HEAD_DIM), BF),
-            jax.ShapeDtypeStruct((2, HEAD_DIM, SEG), F32),
+            pltpu.HBM((2, HEAD_DIM, SEG), F32),
             jax.ShapeDtypeStruct((2, 1, SEG), F32),
         ),
         grid_spec=pltpu.PrefetchScalarGridSpec(
@@ -273,7 +274,7 @@
 
 def backward_kernel(
     info, own, other, mem_own, mem_other, bias, grad_own, grad_other, turned, logs, cosines, sines,
-    keep, send,
+    keep, send, send_v,
     q_s, k_s, v_s, g_s, kt_s, mem_s, dots_s, dq_s, dk_s, dv_s,
 ):
     rank = info[0]
@@ -317,12 +318,11 @@
             dk_s[span, :] += dot(change, query)
             result = result + dot(kt_s[:, span], change)
         dq_s[here, :] = turn(result.T * SCALE, cosines[here, :], -sines[here, :]).astype(BF)
-    for index in range(2):
-        held = pl.ds(pl.multiple_of((rank if index == 0 else 1 - rank) * rows, rows), rows)
-        out = keep if index == 0 else send
-        out[0, 0] = dq_s[held, :]
-        out[1, 0] = turn(dk_s[held, :] * SCALE, cosines[held, :], -sines[held, :]).astype(BF)
-        out[2, 0] = dv_s[held, :].astype(BF)
+    for outs, place_ in (((keep.at[0], keep.at[1], keep.at[2]), rank), ((send.at[0], send.at[1], send_v.at[0]), 1 - rank)):
+        held = pl.ds(pl.multiple_of(place_ * rows, rows), rows)
+        outs[0][0] = dq_s[held, :]
+        outs[1][0] = turn(dk_s[held, :] * SCALE, cosines[held, :], -sines[held, :]).astype(BF)
+        outs[2][0] = dv_s[held, :].astype(BF)
 
 
 def attend_backward(
@@ -335,7 +335,7 @@
     table = pl.BlockSpec((SEG, HEAD_DIM), lambda h, info: (0, 0))
     return pl.pallas_call(
         backward_kernel,
-        out_shape=(jax.ShapeDtypeStruct((3, 1, rows, HEAD_DIM), BF),) * 2,
+        out_shape=tuple(jax.ShapeDtypeStruct((parts, 1, rows, HEAD_DIM), BF) for parts in (3, 2, 1)),
         grid_spec=pltpu.PrefetchScalarGridSpec(
             num_scalar_prefetch=1,
             grid=(1,),
@@ -346,13 +346,15 @@
                 mem,
                 table,
                 half,
-                half,
+                pl.BlockSpec((1, rows, HEAD_DIM), lambda h, info: (0, 0, 0)),
                 pl.BlockSpec((1, HEAD_DIM, SEG), lambda h, info: (head, 0, 0)),
                 pl.BlockSpec((1, 1, SEG), lambda h, info: (head, 0, 0)),
                 table,
                 table,
             ],
-            out_specs=(pl.BlockSpec((3, 1, rows, HEAD_DIM), lambda h, info: (0, 0, 0, 0)),) * 2,
+            out_specs=tuple(
+                pl.BlockSpec((parts, 1, rows, HEAD_DIM), lambda h, info: (0, 0, 0, 0)) for parts in (3, 2, 1)
+            ),
             scratch_shapes=[pltpu.VMEM((SEG, HEAD_DIM), BF)] * 4
             + [
                 pltpu.VMEM((HEAD_DIM, SEG), BF),
@@ -371,75 +373,75 @@
     )
 
 
-OUT_AT = 3 * 4 * HEAD_DIM + HEAD_DIM
+OUT_AT = 3 * FF // 2
+
+
+def in_hbm(value):
+    return pltpu.with_memory_space_constraint(value, pltpu.HBM)
 
 
 def columns(width, start):
     return pl.BlockSpec(
-        (pl.Element(D), pl.Element(width)),
-        lambda *indices: (0, start),
-        pipeline_mode=pl.Buffered(1),
-    )
-
-
-def attend_out_kernel(info, own, other, weight, out, joined):
-    for piece, pair in ((own, info[0]), (other, 1 - info[0])):
+        (pl.Element(D), pl.Element(width)), start, pipeline_mode=pl.Buffered(1)
+    )
+
+
+def middle_kernel(info, *refs):
+    pieces, (tokens, weight, gain, middle, normed, attended, joined) = refs[:4], refs[4:]
+    rank, group = info[0], info[1]
+    for index, piece in enumerate(pieces):
+        pair = (rank, 1 - rank)[index % 2]
+        side = (group, 1 - group)[index // 2]
         for head in range(2):
-            column = pl.multiple_of((pair * 2 + head) * HEAD_DIM, HEAD_DIM)
+            column = pl.multiple_of((side * 4 + pair * 2 + head) * HEAD_DIM, HEAD_DIM)
             joined[:, pl.ds(column, HEAD_DIM)] = piece[head]
-    out[...] = dot_nt(joined[...], weight[...]).astype(BF)
-
-
-def attend_out_call(info, own, other, weights):
-    rows, half = own.shape[1], 4 * HEAD_DIM
-    piece = pl.BlockSpec((2, TILE, HEAD_DIM), lambda i, info: (0, i, 0))
-    return pl.pallas_call(
-        attend_out_kernel,
-        out_shape=(jax.ShapeDtypeStruct((rows, D), BF), jax.ShapeDtypeStruct((rows, half), BF)),
-        grid_spec=pltpu.PrefetchScalarGridSpec(
-            num_scalar_prefetch=1,
-            grid=(rows // TILE,),
-            in_specs=[piece, piece, columns(half, OUT_AT)],
-            out_specs=(
-                pl.BlockSpec((TILE, D), lambda i, info: (i, 0)),
-                pl.BlockSpec((TILE, half), lambda i, info: (i, 0)),
-            ),
-        ),
-        compiler_params=params(VMEM),
-        cost_estimate=cost(0, 0),
-        name="attend_out",
-    )(info, own, other, weights)
-
-
-def middle_kernel(tokens, own, other, gain, middle, normed):
-    value = tokens[...].astype(F32) + (own[...].astype(F32) + other[...].astype(F32))
+    half = attended.shape[1]
+    attended[...] = joined[:, pl.ds(pl.multiple_of(group * half, half), half)]
+    value = tokens[...].astype(F32) + dot_nt(joined[...], weight[...])
     middle[...] = value
     inverse = lax.rsqrt(jnp.mean(value * value, axis=1, keepdims=True) + EPS)
     normed[...] = (value * inverse * gain[...]).astype(BF)
 
 
-def middle_call(tokens, own, other, gain):
-    rows = tokens.shape[0]
-    wide = pl.BlockSpec((TILE, D), lambda i: (i, 0))
+def middle_call(info, pieces, tokens, weights, gain, chunk):
+    half = 4 * HEAD_DIM
+    first = chunk * (PART // TILE)
+    piece = pl.BlockSpec((2, TILE, HEAD_DIM), lambda i, info: (0, i + first, 0))
+    one = pl.BlockSpec((TILE, D), lambda i, info: (i, 0))
     return pl.pallas_call(
         middle_kernel,
-        out_shape=(jax.ShapeDtypeStruct((rows, D), F32), jax.ShapeDtypeStruct((rows, D), BF)),
-        grid=(rows // TILE,),
-        in_specs=[wide, wide, wide, pl.BlockSpec((1, D), lambda i: (0, 0))],
-        out_specs=(wide, wide),
+        out_shape=(
+            pltpu.HBM((PART, D), F32),
+            jax.ShapeDtypeStruct((PART, D), BF),
+            jax.ShapeDtypeStruct((PART, half), BF),
+        ),
+        grid_spec=pltpu.PrefetchScalarGridSpec(
+            num_scalar_prefetch=1,
+            grid=(PART // TILE,),
+            in_specs=[piece] * 4
+            + [
+                pl.BlockSpec((TILE, D), lambda i, info: (i + first, 0)),
+                columns(D, lambda i, info: (0, OUT_AT)),
+                pl.BlockSpec((1, D), lambda i, info: (0, 0)),
+            ],
+            out_specs=(one, one, pl.BlockSpec((TILE, half), lambda i, info: (i, 0))),
+            scratch_shapes=[pltpu.VMEM((TILE, D), BF)],
+        ),
         compiler_params=params(VMEM),
         cost_estimate=cost(0, 0),
         name="middle",
-    )(tokens, own, other, gain)
+    )(info, *[in_hbm(piece) for piece in pieces], in_hbm(tokens), in_hbm(weights), gain)
 
 
 def feed_kernel(normed, upstream, gate_w, up_w, down_w, *refs):
-    hidden, gate_grad, up_grad, back = refs[-4:]
+    hidden, gate_grad, up_grad, feed, back = refs[-5:]
     gate = dot(normed[...], gate_w[...])
     up_part = dot(normed[...], up_w[...])
     sigma = jax.nn.sigmoid(gate)
     silu = gate * sigma
-    hidden[...] = (silu * up_part).astype(BF)
+    low = (silu * up_part).astype(BF)
+    hidden[...] = low
+    feed[...] = dot_nt(low, down_w[...]).astype(BF)
     grad = dot(upstream[...], down_w[...])
     grad_gate = (grad * up_part * sigma * (1.0 + gate * (1.0 - sigma))).astype(BF)
     grad_up = (grad * silu).astype(BF)
@@ -449,19 +451,19 @@
 
 
 def feed_call(normed, upstream, weights, first, count, earlier):
-    rows = normed.shape[0]
+    rows = upstream.shape[0]
     width = FF // 2
     whole = lambda index: pl.BlockSpec((D, width), lambda i: (0, index), pipeline_mode=pl.Buffered(1))
     source = pl.BlockSpec((TILE, D), lambda i: (i + first // TILE, 0))
     narrow = pl.BlockSpec((TILE, width), lambda i: (i + first // TILE, 0))
     return pl.pallas_call(
         feed_kernel,
-        out_shape=(jax.ShapeDtypeStruct((rows, width), BF),) * 3
-        + (jax.ShapeDtypeStruct((count, D), BF),),
+        out_shape=(pltpu.HBM((rows, width), BF),) * 3
+        + (jax.ShapeDtypeStruct((rows, D), BF), jax.ShapeDtypeStruct((count, D), BF)),
         grid=(count // TILE,),
-        in_specs=[source, source, whole(0), whole(1), whole(2)]
+        in_specs=[pl.BlockSpec((TILE, D), lambda i: (first % PART // TILE, 0)), source, whole(0), whole(1), whole(2)]
         + [pl.BlockSpec(memory_space=pl.ANY)] * len(earlier),
-        out_specs=(narrow, narrow, narrow, pl.BlockSpec((TILE, D), lambda i: (i, 0))),
+        out_specs=(narrow, narrow, narrow, source, pl.BlockSpec((TILE, D), lambda i: (i, 0))),
         input_output_aliases={5 + index: index for index in range(len(earlier))},
         compiler_params=params(VMEM),
         cost_estimate=cost(5e7, 0),
@@ -469,54 +471,68 @@
     )(normed, upstream, weights, weights, weights, *earlier)
 
 
-def out_kernel(hidden, down_w, out):
-    out[...] = dot_nt(hidden[...], down_w[...]).astype(BF)
-
-
-def out_call(hidden, weights):
-    count, width = hidden.shape
-    return pl.pallas_call(
-        out_kernel,
-        out_shape=jax.ShapeDtypeStruct((count, D), BF),
-        grid=(count // TILE,),
-        in_specs=[
-            pl.BlockSpec((TILE, width), lambda i: (i, 0)),
-            pl.BlockSpec((D, width), lambda i: (0, 2), pipeline_mode=pl.Buffered(1)),
-        ],
-        out_specs=pl.BlockSpec((TILE, D), lambda i: (i, 0)),
-        compiler_params=params(VMEM),
-        cost_estimate=cost(5e7, 0),
-        name="feed_out",
-    )(hidden, weights)
-
-
-def feed_weight_kernel(normed, upstream, hidden, gate_grad, up_grad, out):
-    width = hidden.shape[1]
-    left = normed[...].astype(F32).T.astype(BF)
-    out[:, :width] = dot(left, gate_grad[...]).astype(BF)
-    out[:, width : 2 * width] = dot(left, up_grad[...]).astype(BF)
-    left = upstream[...].astype(F32).T.astype(BF)
-    out[:, 2 * width :] = dot(left, hidden[...]).astype(BF)
+def feed_weight_kernel(upstream, hidden, gate_grad, up_grad, *refs):
+    normed, (out, held, left_s, sems, left_sem) = refs[:-5], refs[-5:]
+    part, tile = pl.program_id(0), pl.program_id(1)
+    copies = [
+        pltpu.make_async_copy(source, held.at[index], sems.at[index])
+        for index, source in enumerate((gate_grad, up_grad, hidden))
+    ]
+    chunks = [
+        pltpu.make_async_copy(chunk, left_s.at[0, pl.ds(index * PART, PART), :], left_sem.at[index])
+        for index, chunk in enumerate(normed)
+    ]
+    chunks.append(pltpu.make_async_copy(upstream, left_s.at[1], left_sem.at[len(normed)]))
+
+    @pl.when((part == 0) & (tile == 0))
+    def _():
+        for copy in chunks[:-1]:
+            copy.start()
+        copies[0].start()
+        copies[1].start()
+        chunks[-1].start()
+        copies[2].start()
+        for copy in chunks[:-1]:
+            copy.wait()
+        copies[0].wait()
+
+    @pl.when((part == 1) & (tile == 0))
+    def _():
+        copies[1].wait()
+
+    @pl.when((part == 2) & (tile == 0))
+    def _():
+        chunks[-1].wait()
+        copies[2].wait()
+
+    column = pl.multiple_of(tile * TILE, TILE)
+    left = left_s[part // 2, :, pl.ds(column, TILE)].astype(F32).T.astype(BF)
+    out[...] = dot(left, held[part]).astype(BF)
 
 
 def feed_weight_call(normed, upstream, hidden, gate_grad, up_grad):
     rows, width = hidden.shape
-    left = pl.BlockSpec((rows, TILE), lambda i: (0, i))
-    whole = pl.BlockSpec((rows, width), lambda i: (0, 0), pipeline_mode=pl.Buffered(1))
+    anywhere = pl.BlockSpec(memory_space=pl.ANY)
     return pl.pallas_call(
         feed_weight_kernel,
         out_shape=pltpu.HBM((D, 3 * width), BF),
-        grid=(D // TILE,),
-        in_specs=[left, left, whole, whole, whole],
-        out_specs=pl.BlockSpec((TILE, 3 * width), lambda i: (i, 0)),
-        compiler_params=params(VMEM),
+        grid=(3, D // TILE),
+        in_specs=[anywhere] * (4 + len(normed)),
+        out_specs=pl.BlockSpec((TILE, width), lambda part, tile: (tile, part)),
+        scratch_shapes=[
+            pltpu.VMEM((3, rows, width), BF),
+            pltpu.VMEM((2, rows, D), BF),
+            pltpu.SemaphoreType.DMA((3,)),
+            pltpu.SemaphoreType.DMA((len(normed) + 1,)),
+        ],
+        compiler_params=params(VMEM, 2),
         cost_estimate=cost(5e7, 0),
         name="feed_weights",
-    )(normed, upstream, hidden, gate_grad, up_grad)
+    )(*[in_hbm(value) for value in (upstream, hidden, gate_grad, up_grad, *normed)])
 
 
 def residual_kernel(info, middle, back_own, back_other, upstream, gain, weight, *refs):
-    grad, low, keep, send, gain_grad = refs[-5:]
+    grad, low, keep, send_one, send_two = refs[-5:]
     rank = info[0]
     value = middle[...]
     back = back_own[...].astype(F32) + back_other[...].astype(F32)
@@ -528,156 +544,142 @@
     branch = total.astype(BF)
     low[...] = branch
 
-    @pl.when(pl.program_id(0) == 0)
-    def _():
-        gain_grad[...] = jnp.zeros_like(gain_grad)
-
-    gain_grad[...] += jnp.sum(back * value * inverse, axis=0, keepdims=True)
-    for out, pair in ((keep, rank), (send, 1 - rank)):
+    for outs, pair in (((keep.at[0], keep.at[1]), rank), ((send_one.at[0], send_two.at[0]), 1 - rank)):
         column = pl.multiple_of(pair * 2 * HEAD_DIM, 2 * HEAD_DIM)
         result = dot(branch, weight[:, pl.ds(column, 2 * HEAD_DIM)]).astype(BF)
         for head in range(2):
-            out[head] = result[:, head * HEAD_DIM : (head + 1) * HEAD_DIM]
+            outs[head][...] = result[:, head * HEAD_DIM : (head + 1) * HEAD_DIM]
 
 
 def residual_call(info, middle, back_own, back_other, upstream, gain, weights, first, earlier):
-    rows, count = middle.shape[0], back_own.shape[0]
-    start = first // TILE
+    rows, count = upstream.shape[0], back_own.shape[0]
+    start, half = first // TILE, 4 * HEAD_DIM
     wide = pl.BlockSpec((TILE, D), lambda i, info: (i + start, 0))
     part = pl.BlockSpec((TILE, D), lambda i, info: (i, 0))
     row = pl.BlockSpec((1, D), lambda i, info: (0, 0))
     piece = pl.BlockSpec((2, TILE, HEAD_DIM), lambda i, info: (0, i + start, 0))
+    single = pl.BlockSpec((1, TILE, HEAD_DIM), lambda i, info: (0, i + start, 0))
     return pl.pallas_call(
         residual_kernel,
         out_shape=(
-            jax.ShapeDtypeStruct((rows, D), F32),
+            pltpu.HBM((rows, D), F32),
             jax.ShapeDtypeStruct((rows, D), BF),
             jax.ShapeDtypeStruct((2, rows, HEAD_DIM), BF),
-            jax.ShapeDtypeStruct((2, rows, HEAD_DIM), BF),
-            jax.ShapeDtypeStruct((1, D), F32),
+            jax.ShapeDtypeStruct((1, rows, HEAD_DIM), BF),
+            jax.ShapeDtypeStruct((1, rows, HEAD_DIM), BF),
         ),
         grid_spec=pltpu.PrefetchScalarGridSpec(
             num_scalar_prefetch=1,
             grid=(count // TILE,),
-            in_specs=[wide, part, part, wide, row, columns(4 * HEAD_DIM, OUT_AT)]
+            in_specs=[
+                pl.BlockSpec((TILE, D), lambda i, info: (i + first % PART // TILE, 0)),
+                part,
+                part,
+                wide,
+                row,
+                columns(half, lambda i, info: (0, pl.multiple_of(OUT_AT + info[1] * half, HEAD_DIM))),
+            ]
             + [pl.BlockSpec(memory_space=pl.ANY)] * len(earlier),
-            out_specs=(wide, wide, piece, piece, row),
+            out_specs=(wide, wide, piece, single, single),
         ),
         input_output_aliases={7 + index: index for index in range(len(earlier))},
         compiler_params=params(VMEM),
-        cost_estimate=cost(5e7 if first + count < rows else 3e11, 0),
+        cost_estimate=cost(3e11 if first + count == rows else 5e7, 0),
         name="residual",
-    )(info, middle, back_own, back_other, upstream, gain, weights, *earlier)
-
-
-def back_kernel(info, own_one, own_two, other_one, other_two, weight, tokens, out, joined, gain_grad):
-    rank = info[0]
-    for index, piece in enumerate((own_one, own_two, other_one, other_two)):
-        pair = (rank, 1 - rank)[index // 2]
+    )(info, middle, back_own, back_other, in_hbm(upstream), gain, in_hbm(weights), *earlier)
+
+
+def join(rank, pieces, joined):
+    for head in range(2):
+        own, other, other_v = pieces[head], pieces[2 + 2 * head], pieces[3 + 2 * head]
         for part in range(3):
-            column = pl.multiple_of((part * 4 + pair * 2 + index % 2) * HEAD_DIM, HEAD_DIM)
-            joined[:, pl.ds(column, HEAD_DIM)] = piece[part, 0]
-    back = dot_nt(joined[...], weight[...])
-    out[...] = back.astype(BF)
-
-    @pl.when(pl.program_id(0) == 0)
-    def _():
-        gain_grad[...] = jnp.zeros_like(gain_grad)
-
-    value = tokens[...].astype(F32)
-    inverse = lax.rsqrt(jnp.mean(value * value, axis=1, keepdims=True) + EPS)
-    gain_grad[...] += jnp.sum(back * value * inverse, axis=0, keepdims=True)
-
-
-def back_call(info, pieces, weights, tokens):
-    rows = tokens.shape[0]
+            for value, pair in (
+                (own[part, 0], rank),
+                (other_v[0, 0] if part == 2 else other[part, 0], 1 - rank),
+            ):
+                column = pl.multiple_of((part * 4 + pair * 2 + head) * HEAD_DIM, HEAD_DIM)
+                joined[:, pl.ds(column, HEAD_DIM)] = value
+
+
+def back_kernel(info, *refs):
+    pieces, (weight, out, joined) = refs[:6], refs[6:]
+    join(info[0], pieces, joined)
+    out[...] = dot_nt(joined[...], weight[...]).astype(BF)
+
+
+def back_call(info, pieces, weights):
+    rows = pieces[0].shape[2]
     width = 3 * 4 * HEAD_DIM
-    piece = pl.BlockSpec((3, 1, TILE, HEAD_DIM), lambda i, info: (0, 0, i, 0))
-    wide = pl.BlockSpec((TILE, D), lambda i, info: (i, 0))
+    piece = [
+        pl.BlockSpec((parts, 1, TILE, HEAD_DIM), lambda i, info: (0, 0, i, 0))
+        for parts in (3, 3, 2, 1, 2, 1)
+    ]
     return pl.pallas_call(
         back_kernel,
-        out_shape=(
-            jax.ShapeDtypeStruct((rows, D), BF),
-            jax.ShapeDtypeStruct((rows, width), BF),
-            jax.ShapeDtypeStruct((1, D), F32),
-        ),
+        out_shape=jax.ShapeDtypeStruct((rows, D), BF),
         grid_spec=pltpu.PrefetchScalarGridSpec(
             num_scalar_prefetch=1,
             grid=(rows // TILE,),
-            in_specs=[
-                piece,
-                piece,
-                piece,
-                piece,
-                pl.BlockSpec((D, width), lambda i, info: (0, 0)),
-                wide,
-            ],
-            out_specs=(
-                wide,
-                pl.BlockSpec((TILE, width), lambda i, info: (i, 0)),
-                pl.BlockSpec((1, D), lambda i, info: (0, 0)),
-            ),
+            in_specs=piece + [pl.BlockSpec((D, width), lambda i, info: (0, 0))],
+            out_specs=pl.BlockSpec((TILE, D), lambda i, info: (i, 0)),
+            scratch_shapes=[pltpu.VMEM((TILE, width), BF)],
         ),
         compiler_params=params(VMEM),
-        cost_estimate=cost(5e7, 0),
+        cost_estimate=cost(0, 0),
         name="back",
-    )(info, *pieces, weights, tokens)
-
-
-def attend_weight_kernel(info, normed, joined, low, attended, gain_one, gain_two, *refs):
-    outs, out = refs[:-1], refs[-1]
+    )(info, *pieces, weights)
+
+
+def attend_weight_kernel(info, normed, low, *refs):
+    pieces, refs = refs[:6], refs[6:]
+    attended, (keep, send, joined, out) = refs[:-4], refs[-4:]
     step = pl.program_id(0)
-    count = len(outs) // 2
-
-    tile, width, half = normed.shape[1], joined.shape[1], attended.shape[1]
+
+    @pl.when(step == 0)
+    def _():
+        join(info[0], pieces, joined)
+
+    tile, width = normed.shape[1], joined.shape[1]
     left = normed[...].astype(F32).T.astype(BF)
     out[:, :width] = dot(left, joined[...]).astype(BF)
     left = low[...].astype(F32).T.astype(BF)
-    out[:, width : width + half] = dot(left, attended[...]).astype(BF)
-    both = jnp.concatenate([gain_one[...], gain_two[...], jnp.zeros((HEAD_DIM - 2, tile), F32)])
-    out[:, width + half :] = both.T.astype(BF)
-    size = outs[0].shape[1]
+    out[:, width:] = dot(left, jnp.concatenate([part[...] for part in attended])).astype(BF)
+    count, size = keep.shape[1], keep.shape[2]
     for line in range(tile // (4 * size)):
-        place_ = step * (tile // (4 * size)) + line
-        for slot in range(count):
-
-            @pl.when(count - 1 - (place_ ^ info[4]) == slot)
-            def _():
-                for column in range(2):
-                    for target, core in ((outs[slot], info[0]), (outs[count + slot], 1 - info[0])):
-                        side = info[3] if column == 0 else 1 - info[3]
-                        start = pl.multiple_of((line * 4 + side * 2 + core) * size, size)
-                        target[column] = out[pl.ds(start, size), :]
-
-
-def attend_weight_call(info, normed, joined, low, attended, gain_one, gain_two, size):
-    rows, width = joined.shape
-    half = 4 * HEAD_DIM
-    total = width + half + HEAD_DIM
-    tile, count = TILE, D // (4 * size)
-    left = pl.BlockSpec((rows, tile), lambda i, info: (0, i))
-    row = pl.BlockSpec((1, tile), lambda i, info: (0, i))
+        slot = count - 1 - ((step * (tile // (4 * size)) + line) ^ info[4])
+        for column in range(2):
+            for target, core in ((keep, info[0]), (send, 1 - info[0])):
+                side = info[3] if column == 0 else 1 - info[3]
+                start = pl.multiple_of((line * 4 + side * 2 + core) * size, size)
+                target[column, slot] = out[pl.ds(start, size), :]
+
+
+def attend_weight_call(info, normed, low, attended, pieces, size):
+    rows, half = normed.shape[0], attended[0].shape[1]
+    width = 3 * half
+    total = width + half
+    left = pl.BlockSpec((rows, TILE), lambda i, info: (0, i))
+    piece = [
+        pl.BlockSpec((parts, 1, rows, HEAD_DIM), lambda i, info: (0, 0, 0, 0))
+        for parts in (3, 3, 2, 1, 2, 1)
+    ]
+    count = D // (4 * size)
     return pl.pallas_call(
         attend_weight_kernel,
-        out_shape=(jax.ShapeDtypeStruct((2, size, total), BF),) * (2 * count),
+        out_shape=(jax.ShapeDtypeStruct((2, count, size, total), BF),) * 2,
         grid_spec=pltpu.PrefetchScalarGridSpec(
             num_scalar_prefetch=1,
-            grid=(D // tile,),
-            in_specs=[
-                left,
-                pl.BlockSpec((rows, width), lambda i, info: (0, 0)),
-                left,
-                pl.BlockSpec((rows, half), lambda i, info: (0, 0)),
-                row,
-                row,
-            ],
-            out_specs=(pl.BlockSpec((2, size, total), lambda i, info: (0, 0, 0)),) * (2 * count),
-            scratch_shapes=[pltpu.VMEM((tile, total), BF)],
+            grid=(D // TILE,),
+            in_specs=[left, left]
+            + piece
+            + [pl.BlockSpec((PART, half), lambda i, info: (0, 0))] * len(attended),
+            out_specs=(pl.BlockSpec((2, count, size, total), lambda i, info: (0, 0, 0, 0)),) * 2,
+            scratch_shapes=[pltpu.VMEM((rows, width), BF), pltpu.VMEM((TILE, total), BF)],
         ),
         compiler_params=params(VMEM),
         cost_estimate=cost(0, 0),
         name="attend_weights",
-    )(info, normed, joined, low, attended, gain_one, gain_two)
+    )(info, normed, low, *pieces, *attended)
 
 
 def input_kernel(grad, back_own, back_other, tokens, gain, out):
@@ -712,21 +714,41 @@
     return value
 
 
-def pair_kernel(keep, core, mine, theirs):
-    total = (keep[...].astype(F32) + core[...].astype(F32)).astype(BF)
-    mine[...] = total[0]
-    theirs[...] = total[1]
+def pair_kernel(keep, core, *outs):
+    half = keep.shape[1] // 2
+    for part in range(2):
+        slots = slice(part * half, (part + 1) * half)
+        for column in range(2):
+            outs[2 * part + column][...] = (
+                keep[column, slots].astype(F32) + core[column, slots].astype(F32)
+            ).astype(BF)
 
 
 def pair_add(keep, core):
-    shape = jax.ShapeDtypeStruct(keep.shape[1:], BF)
+    count, size, width = keep.shape[1:]
     return pl.pallas_call(
         pair_kernel,
-        out_shape=(shape, shape),
+        out_shape=(jax.ShapeDtypeStruct((count // 2, size, width), BF),) * 4,
         compiler_params=pltpu.CompilerParams(vmem_limit_bytes=VMEM * MIB),
         cost_estimate=cost(0, 0),
         name="pair_add",
     )(keep, core)
+
+
+def split_kernel(left, right, *outs):
+    for index, out in enumerate(outs):
+        out[...] = (left[index].astype(F32) + right[index].astype(F32)).astype(BF)
+
+
+def split_add(left, right):
+    count, size, width = left.shape
+    return pl.pallas_call(
+        split_kernel,
+        out_shape=(jax.ShapeDtypeStruct((size, width), BF),) * count,
+        compiler_params=pltpu.CompilerParams(vmem_limit_bytes=VMEM * MIB),
+        cost_estimate=cost(0, 0),
+        name="split_add",
+    )(left, right)
 
 
 def low_kernel(left, right, out):
@@ -763,15 +785,15 @@
     )(flags, first, second, up_in, down_in)
 
 
-def reduce_rows(keeps, sends, count):
+def reduce_rows(keep, send, count, first_wait, last_wait):
     length = count // 4
     line = lax.axis_index("dp") // 4
-    sums = []
-    for keep, send in zip(keeps, sends):
-        core = lax.ppermute(send, "dp", [(i, i ^ 1) for i in range(count)])
-        mine, theirs = pair_add(keep, core)
-        other = lax.ppermute(theirs, "dp", [(i, i ^ 2) for i in range(count)])
-        sums.append(low_add(mine, other))
+    core = lax.ppermute(send, "dp", [(i, i ^ 1) for i in range(count)])
+    mine_one, theirs_one, mine_two, theirs_two = pair_add(keep, core)
+    pairs = [(i, i ^ 2) for i in range(count)]
+    other_one, first_wait = pin((lax.ppermute(theirs_one, "dp", pairs), first_wait))
+    sums = list(split_add(mine_one, other_one))
+    other = lax.ppermute(theirs_two, "dp", pairs)
     above = below = None
     for step in range(1, length):
         gap = length - step
@@ -797,9 +819,78 @@
             fill = lambda side: [sums[used[0] if slot is None else slot] for slot in side]
             up, down = choose(line, fill(ups)), choose(line, fill(downs))
             up, down = low_add(up, below), low_add(down, above)
+        if step == length - 1:
+            up, down, last_wait = pin((up, down, last_wait))
         below = lax.ppermute(up, "dp", [(i, i + 4) for i in range(count - 4) if i // 4 + gap < length])
         above = lax.ppermute(down, "dp", [(i, i - 4) for i in range(4, count) if i // 4 >= gap])
-    return sums[-1], below, above
+        if step == length // 2 - 1:
+            below, above, other = pin((below, above, other))
+            sums += split_add(mine_two, other)
+    return sums[-1], below, above, first_wait, last_wait
+
+
+def interleave_kernel(info, *refs):
+    pieces, out = refs[:4], refs[4]
+    size = out.shape[0] // (4 * pieces[0].shape[0])
+    length = pieces[0].shape[0]
+    for index, piece in enumerate(pieces):
+        side = info[3] if index % 2 == 0 else 1 - info[3]
+        core = info[0] if index // 2 == 0 else 1 - info[0]
+        for line in range(length):
+            start = pl.multiple_of((line * 4 + side * 2 + core) * size, size)
+            out[pl.ds(start, size), :] = piece[line]
+
+
+def interleave(info, pieces, size):
+    width = pieces[0].shape[1]
+    pieces = [piece.reshape(-1, size, width) for piece in pieces]
+    vmem = pl.BlockSpec(memory_space=pltpu.VMEM)
+    return pl.pallas_call(
+        interleave_kernel,
+        out_shape=pltpu.VMEM((D, width), BF),
+        in_specs=[pl.BlockSpec(memory_space=pltpu.SMEM)] + [vmem] * 4,
+        out_specs=vmem,
+        compiler_params=pltpu.CompilerParams(vmem_limit_bytes=VMEM * MIB),
+        cost_estimate=cost(0, 0),
+        name="interleave",
+    )(info, *pieces)
+
+
+def gain_kernel(own, other, gain, first, second, first_out, second_out, gain_out):
+    low = gain[...].astype(BF).astype(F32)
+    results = adamw(gain[...], (own[...] + other[...]) / low, first[...], second[...], 0.6)
+    for out, result in zip((first_out, second_out, gain_out), results):
+        out[...] = result
+
+
+def gain_call(own, other, gain, first, second):
+    shape = jax.ShapeDtypeStruct(gain.shape, F32)
+    return pl.pallas_call(
+        gain_kernel,
+        out_shape=(shape, shape, shape),
+        compiler_params=pltpu.CompilerParams(vmem_limit_bytes=VMEM * MIB),
+        cost_estimate=cost(0, 0),
+        name="gains",
+    )(own, other, gain, first, second)
+
+
+def shard_kernel(qkv, gains, out):
+    width = qkv.shape[2]
+    for part in range(3):
+        out[:, part * width : (part + 1) * width] = qkv[part].astype(BF)
+    rows = jnp.concatenate([gains[...], jnp.zeros((HEAD_DIM - 2, gains.shape[1]), F32)])
+    out[:, 3 * width :] = rows.T.astype(BF)
+
+
+def shard_call(qkv, gains):
+    total = 3 * qkv.shape[2] + HEAD_DIM
+    return pl.pallas_call(
+        shard_kernel,
+        out_shape=jax.ShapeDtypeStruct((qkv.shape[1], total), BF),
+        compiler_params=pltpu.CompilerParams(vmem_limit_bytes=VMEM * MIB),
+        cost_estimate=cost(0, 0),
+        name="shard",
+    )(qkv, gains)
 
 
 def pin(values):
@@ -846,16 +937,25 @@
     def beside(value):
         return lax.ppermute(value, "dp", core_pairs)
 
-    gain_columns = jnp.pad(norm_gains.astype(BF).T, ((0, 0), (0, HEAD_DIM - 2)))
-    shard_one = jnp.concatenate(
-        [proj_qkv[part].astype(BF) for part in range(3)] + [gain_columns, proj_out.astype(BF).T],
+    shard_one = shard_call(proj_qkv, norm_gains)
+    out_own = proj_out.astype(BF).T
+    out_other = across(out_own)
+    shard_two = jnp.concatenate(
+        [
+            proj_gate_up[0].astype(BF),
+            proj_gate_up[1].astype(BF),
+            proj_down.astype(BF).T,
+            jnp.where(group == 0, out_own, out_other),
+            jnp.where(group == 0, out_other, out_own),
+        ],
         axis=1,
     )
-    shard_two = jnp.concatenate(
-        [proj_gate_up[0].astype(BF), proj_gate_up[1].astype(BF), proj_down.astype(BF).T], axis=1
-    )
     length = count // 4
-    weights_one = lax.all_gather(shard_one, "dp", axis=0, tiled=True)
+    lines = [[i for i in range(count) if i % 4 == lane] for lane in range(4)]
+    own_column = lax.all_gather(shard_one, "dp", axis=0, tiled=True, axis_index_groups=lines)
+    next_column = lax.ppermute(own_column, "dp", [(i, i ^ 2) for i in range(count)])
+    pieces = (own_column, next_column, beside(own_column), beside(next_column))
+    weights_two = lax.all_gather(shard_two, "dp", axis=0, tiled=True)
 
     places = jnp.arange(SEG, dtype=jnp.int32)
     starts = jnp.cumsum(doc_segments) - doc_segments
@@ -869,82 +969,92 @@
     fetched = cache[retrieval[0]].reshape(RETR, 2, 2, 2, HEAD_DIM).transpose(2, 1, 3, 0, 4)
     mem_own = lax.dynamic_index_in_dim(fetched, rank, keepdims=False)
     mem_other = beside(lax.dynamic_index_in_dim(fetched, 1 - rank, keepdims=False))
-    weights_one, shard_two, mem_own, mem_other, bias, cosines, sines = pin(
-        (weights_one, shard_two, mem_own, mem_other, bias, cosines, sines)
-    )
-    weights_two = lax.all_gather(shard_two, "dp", axis=0, tiled=True)
+    pieces, mem_own, mem_other, bias, cosines, sines, info = pin(
+        (pieces, mem_own, mem_other, bias, cosines, sines, info)
+    )
+    weights_one = interleave(info, pieces, shard)
 
     send, normed_one, gains = project_first(info, tokens, weights_one, cosines, sines)
     gain_one, gain_two = gains[0:1], gains[1:2]
     other = beside(send)
     own = project_second(info, normed_one, weights_one, cosines, sines)
     out_keep, out_send, turned, logs = attend_forward(info, own, other, mem_own, mem_other, bias)
-    attend_part, attended = attend_out_call(info, out_keep, beside(out_send), weights_one)
-    middle, normed_two = middle_call(tokens, attend_part, across(attend_part), gain_two)
+    out_recv = beside(out_send)
+    pieces = (out_keep, out_recv, across(out_keep), across(out_recv))
+    middles, normed_two, attended = [], [], []
+    for chunk in range(rows // PART):
+        middle, normed, own_out = middle_call(info, pieces, tokens, weights_two, gain_two, chunk)
+        middles.append(middle)
+        normed_two.append(normed)
+        attended.append(own_out)
 
     earlier, backs, backs_other = (), [], []
-    for first in range(0, rows, TILE):
-        *earlier, back = feed_call(normed_two, cotangent, weights_two, first, TILE, earlier)
+    for chunk, first in enumerate(range(0, rows, TILE)):
+        *earlier, back = feed_call(normed_two[first // PART], cotangent, weights_two, first, TILE, earlier)
         backs.append(back)
         backs_other.append(across(back))
-    hidden, grad_gate, grad_up = earlier
+    hidden, grad_gate, grad_up, feed_part = earlier
+    hidden, backs_other[:2] = pin((hidden, backs_other[:2]))
     feed_grads = feed_weight_call(normed_two, cotangent, hidden, grad_gate, grad_up)
-    hidden, _ = pin((hidden, feed_grads))
-    feed_part = out_call(hidden, weights_two)
-    middle, _ = pin((middle, feed_part))
-    earlier, gain_two_grad = (), 0.0
-    for index, first in enumerate(range(0, rows, TILE)):
-        if first + TILE == rows:
-            backs_other[index], feed_pinned = pin((backs_other[index], feed_part))
-            feed_other = across(feed_pinned)
-        *earlier, gain_part = residual_call(
-            info, middle, backs[index], backs_other[index], cotangent, gain_two, weights_one, first, earlier
+    feed_other = across(feed_part)
+    backs[2], _ = pin((backs[2], feed_grads))
+    earlier = ()
+    for index in (2, 3, 0, 1):
+        first = index * TILE
+        earlier = residual_call(
+            info, middles[first // PART], backs[index], backs_other[index], cotangent, gain_two, weights_two,
+            first, earlier,
         )
-        gain_two_grad = gain_two_grad + gain_part
-    grad_middle, grad_low, grad_keep, grad_send = earlier
-    grad_other = beside(grad_send)
+    grad_middle, grad_low, grad_keep, *grad_sends = earlier
+    grad_others = [beside(value) for value in grad_sends]
 
     d_keeps, d_others = [], []
     for head in range(2):
-        d_keep, d_send = attend_backward(
-            info, own, other, mem_own, mem_other, bias, grad_keep, grad_other, turned, logs,
+        d_keep, d_send, d_send_v = attend_backward(
+            info, own, other, mem_own, mem_other, bias, grad_keep, grad_others[head], turned, logs,
             cosines, sines, head,
         )
         d_keeps.append(d_keep)
-        d_others.append(beside(d_send))
-    back_one, joined, gain_one_grad = back_call(info, d_keeps + d_others, weights_one, tokens)
+        d_others += [beside(d_send), beside(d_send_v)]
+    moved = d_keeps + d_others
+    back_one = back_call(info, moved, weights_one)
+    moved[0], _ = pin((moved[0], back_one))
+    attend_keep, attend_send = attend_weight_call(info, normed_one, grad_low, attended, moved, shard)
+    back_one, feed_other = pin((back_one, feed_other))
     back_one_other = across(back_one)
-    attend_slots = attend_weight_call(
-        info, normed_one, joined, grad_low, attended, gain_one_grad, gain_two_grad, shard
-    )
-    feed_other, attend_slots = pin((feed_other, attend_slots))
-    total, below, above = reduce_rows(attend_slots[:length], attend_slots[length:], count)
     input_grad = input_call(grad_middle, back_one, back_one_other, tokens, gain_one)
-    block_out = (middle + (feed_part.astype(F32) + feed_other.astype(F32))).astype(BF)
-    input_grad, total, below, above = pin((input_grad, total, below, above))
-    attend_sum = total.astype(F32) + (below.astype(F32) + above.astype(F32))
+    block_out = (
+        jnp.concatenate(middles) + (feed_part.astype(F32) + feed_other.astype(F32))
+    ).astype(BF)
+    total, below, above, block_out, input_grad = reduce_rows(
+        attend_keep, attend_send, count, block_out, input_grad
+    )
     feed_sum = lax.psum_scatter(feed_grads, "dp", scatter_dimension=0, tiled=True).astype(F32)
     gate_up_sum = jnp.stack([feed_sum[:, :hidden_here], feed_sum[:, hidden_here : 2 * hidden_here]])
     down_sum = feed_sum[:, 2 * hidden_here :].T
+    gate_up_first, gate_up_second, gate_up_new = adamw(
+        proj_gate_up, gate_up_sum, first_gate_up, second_gate_up, 0.5 / math.sqrt(D)
+    )
+    down_first, down_second, down_new = adamw(
+        proj_down, down_sum, first_down, second_down, 0.5 / math.sqrt(FF)
+    )
+    gate_up_new, down_new, total, below, above = pin((gate_up_new, down_new, total, below, above))
+    attend_sum = total.astype(F32) + (below.astype(F32) + above.astype(F32))
     qkv_sum = jnp.stack([attend_sum[:, part * local : (part + 1) * local] for part in range(3)])
     out_sum = attend_sum[:, 3 * local : 4 * local].T
-    gains_sum = attend_sum[:, 4 * local : 4 * local + 2].T
-    gains_sum = jnp.concatenate([gains_sum[0:1] + across(gains_sum[0:1]), gains_sum[1:2]], axis=0)
+    low_qkv, low_gate_up = proj_qkv.astype(BF).astype(F32), proj_gate_up.astype(BF).astype(F32)
+    gains_sum = jnp.stack(
+        [jnp.sum(low_qkv * qkv_sum, axis=(0, 2)), jnp.sum(low_gate_up * gate_up_sum, axis=(0, 2))]
+    )
+    gains_first, gains_second, gains_new = gain_call(
+        gains_sum, across(gains_sum), norm_gains, first_gains, second_gains
+    )
 
     qkv_first, qkv_second, qkv_new = adamw(
         proj_qkv, qkv_sum, first_qkv, second_qkv, 0.5 / math.sqrt(D)
     )
     out_first, out_second, out_new = adamw(
         proj_out, out_sum, first_out, second_out, 0.5 / math.sqrt(max(1, 4 * D // SEG))
-    )
-    gate_up_first, gate_up_second, gate_up_new = adamw(
-        proj_gate_up, gate_up_sum, first_gate_up, second_gate_up, 0.5 / math.sqrt(D)
-    )
-    down_first, down_second, down_new = adamw(
-        proj_down, down_sum, first_down, second_down, 0.5 / math.sqrt(FF)
-    )
-    gains_first, gains_second, gains_new = adamw(
-        norm_gains, gains_sum, first_gains, second_gains, 0.6
     )
     return (
         block_out,

time: 351 us -> 338 us (0.963)
  waiting for transfers between devices: 121 us -> 82.9 us
  blocking collectives: 0 us -> 26.8 us
  local copies, waits for them, and re-layouts: 31.2 us -> 10.6 us
  Pallas kernels: 116 us -> 134 us
  other arithmetic: 29.5 us -> 25.4 us
  starting transfers between devices: 33.5 us -> 37.1 us
    all_gather x1 -> x0, waiting for transfers between devices: 35.9 us -> none  [body(): weights_one = lax.all_gather(shard_one, 'dp', axis=0, tiled=True)]
    ppermute x8 -> x10, waiting for transfers between devices: 58.9 us -> 27.6 us  [across(): return lax.ppermute(value, 'mp', [(0, 1), (1, 0)])]
    all_gather x0 -> x1, blocking collectives: none -> 26.8 us  [body(): lax.all_gather(shard_one, 'dp', axis=0, tiled=True, axis_index_groups=lines)]
    ppermute x4 -> x3, waiting for transfers between devices: 13.9 us -> 39.9 us  [the longest x1 15.5 us: body(): lax.ppermute(own_column, 'dp', [(i, i ^ 2) for i in range(count)])]
    unnamed x128 -> x134, local copies, waits for them, and re-layouts: 27.1 us -> 9.08 us
    pallas_call x18 -> x19, Pallas kernels: 68.4 us -> 78.6 us  [the longest x4 23.8 us: feed_call(): pl.pallas_call(feed_kernel, out_shape=(pltpu.HBM((rows, width), BF),) * 3...]
    ppermute x3, starting transfers between devices: 12.7 us -> 16.6 us  [reduce_rows(): lax.ppermute(up, 'dp', [(i, i + 4) for i in range(count - 4) if i // 4 +...]
    pallas_call x1, Pallas kernels: 12.7 us -> 16.5 us  [feed_weight_call(): pl.pallas_call(feed_weight_kernel, out_shape=pltpu.HBM((D, 3 * width), BF...]
  transfers between devices with their start and end apart: 31 -> 33, of which waited for: 13 -> 15; matrix products, arithmetic and copies ran while one was open for 8% -> 7% of each run, Pallas kernels for 27% -> 35%
where the time goes in v3:
time: 338 us; the launch traced here: 332 us
  Pallas kernels  134 us (40%)
  waiting for transfers between devices  82.9 us (25%)
  starting transfers between devices  37.1 us (11%)
  blocking collectives  26.8 us (8%)
  other arithmetic  25.4 us (8%)
  between operations  15.8 us (5%)
  local copies, waits for them, and re-layouts  10.6 us (3%)
    ppermute x10, waiting for transfers between devices, across(): return lax.ppermute(value, 'mp', [(0, 1), (1, 0)])  27.6 us
    all_gather x1, blocking collectives, body(): lax.all_gather(shard_one, 'dp', axis=0, tiled=True, axis_index_groups=lines)  26.8 us
    pallas_call x4, Pallas kernels, feed_call(): pl.pallas_call(feed_kernel, out_shape=(pltpu.HBM((rows, width), BF),) * 3...  23.8 us
    pallas_call x2, Pallas kernels, attend_backward(): pl.pallas_call(backward_kernel, out_shape=tuple((jax.ShapeDtypeStruct((pa...  17.7 us
    ppermute x3, starting transfers between devices, reduce_rows(): lax.ppermute(up, 'dp', [(i, i + 4) for i in range(count - 4) if i // 4 +...  16.6 us
    pallas_call x1, Pallas kernels, feed_weight_call(): pl.pallas_call(feed_weight_kernel, out_shape=pltpu.HBM((D, 3 * width), BF...  16.5 us
    pallas_call x4, Pallas kernels, residual_call(): pl.pallas_call(residual_kernel, out_shape=(pltpu.HBM((rows, D), F32), jax...  16 us
    ppermute x1, waiting for transfers between devices, body(): lax.ppermute(own_column, 'dp', [(i, i ^ 2) for i in range(count)])  15.5 us
  transfers between devices with their start and end apart: 33, of which 15 were waited for; matrix products, arithmetic and copies ran while one was open for 7% of the time, Pallas kernels for 35%

profile of v3, /device:TPU:0, one launch (start us, length us, event | category | flops | bytes accessed | tf_op | source)
XLA Modules:
  0.0 332.2 jit_solution(4161347217787555740)
XLA Ops:
  8.4 3.0 collective-permute-start.8
  16.1 26.8 %all_gather.6 = bf16[256,1664]{1,0:T(8,128)(2,1)S(1)} all-gather(bf16[64,1664]{1,0:T(8,128)(2,1)S(1)} %shard.1), channel_id=1, replica_groups={{0,8,16,24},{2,10,18,26},{4,12,20,28},{6,14,22,30},{1,9,17,25},{3,11,19..., dimensions={0}, use_global_device_ids=true | all-gather | bytes 1064960 | tf_op jit(solution)/shard_map/all_gather | solution.py:955
  46.8 3.7 %fusion.4 = (f32[2048,64]{1,0:T(8,128)S(1)}, f32[2048,64]{1,0:T(8,128)S(1)}, f32[2048,64]{1,0:T(8,128)S(1)}) fusion(f32[64]{0:T(128)S(1)} %negate_power_fusion, f32[2048]{0:T(1024)S(1)} %iota_convert_fusion), kind=kLoop, calls=%fused_computation.28 | loop fusion | flops 262144 | bytes 1581312 | tf_op jit(solution)/shard_map/neg | solution.py:63
  50.5 15.5 %collective-permute-done = bf16[256,1664]{1,0:T(8,128)(2,1)} collective-permute-done((bf16[256,1664]{1,0:T(8,128)(2,1)S(1)}, bf16[256,1664]{1,0:T(8,128)(2,1)}, u32[]{:S(2)}, u32[]{:S(2)}) %collective-permute-start) | collective-permute-done | bytes 852000 | tf_op jit(solution)/shard_map/ppermute | solution.py:956
  66.4 1.9 pad_maximum_fusion
  70.1 1.7 interleave.1.gain_columns.weight.refs_6_
  71.8 7.6 %project_first.1 = (bf16[3,2,1024,128]{3,2,1,0:T(8,128)(2,1)S(1)}, bf16[1024,1024]{1,0:T(8,128)(2,1)S(1)}, f32[8,1024]{1,0:T(8,128)S(1)}) custom-call(s32[5]{0:T(128)S(1)} %stack.66.info, bf16[1024,1024]{1,0:T(8,128)(2,1)} %tokens.3, bf16[1024,1664]{1,0:T(8,128)(2,1)S(1)} %interleave.1.gain_columns.weight.refs_6_, ...), custom_call_target="tpu_custom_call" | custom-call | tf_op jit(solution)/shard_map/project_first/pallas_call | solution.py:112
  80.0 3.8 %project_second.1.own = bf16[3,2,1024,128]{3,2,1,0:T(8,128)(2,1)S(1)} custom-call(s32[5]{0:T(128)S(1)} %stack.66.info, bf16[1024,1024]{1,0:T(8,128)(2,1)S(1)} %get-tuple-element.128.normed, bf16[1024,1664]{1,0:T(8,128)(2,1)S(1)} %interleave.1.gain_columns.weight.refs_6_, f32[2048,128]{1,0:T(8,128)S(1)} %copy-done.8, f32[2048,128]{1,0:T(8,128)S(1)} %copy-done.10), custom_call_target="tpu_custom_call" | custom-call | tf_op jit(solution)/shard_map/project_second/pallas_call | solution.py:143
  83.9 12.0 %attend_forward.1 = (bf16[2,1024,128]{2,1,0:T(8,128)(2,1)S(1)}, bf16[2,1024,128]{2,1,0:T(8,128)(2,1)S(1)}, f32[2,128,2048]{2,1,0:T(8,128)}, f32[2,1,2048]{2,1,0:T(1,128)S(1)}) custom-call(s32[5]{0:T(128)S(1)} %stack.66.info, bf16[3,2,1024,128]{3,2,1,0:T(8,128)(2,1)S(1)} %project_second.1.own, bf16[3,2,1024,128]{3,2,1,0:T(8,128)(2,1)S(1)} %collective-permute-done.4.other, ...), custom_call_target="tpu_custom_call" | custom-call | tf_op jit(solution)/shard_map/attend_forward/pallas_call | solution.py:235
  97.1 1.9 collective-permute-done.5.refs_1_
  99.1 12.7 %collective-permute-done.6.refs_2_ = bf16[2,1024,128]{2,1,0:T(8,128)(2,1)S(1)} collective-permute-done((bf16[2,1024,128]{2,1,0:T(8,128)(2,1)S(1)}, bf16[2,1024,128]{2,1,0:T(8,128)(2,1)S(1)}, u32[]{:S(2)}, u32[]{:S(2)}) %collective-permute-start.6) | collective-permute-done | bytes 524320 | tf_op jit(solution)/shard_map/ppermute | solution.py:935
  111.8 10.8 %collective-permute-done.7.refs_3_ = bf16[2,1024,128]{2,1,0:T(8,128)(2,1)S(1)} collective-permute-done((bf16[2,1024,128]{2,1,0:T(8,128)(2,1)S(1)}, bf16[2,1024,128]{2,1,0:T(8,128)(2,1)S(1)}, u32[]{:S(2)}, u32[]{:S(2)}) %collective-permute-start.7) | collective-permute-done | bytes 524320 | tf_op jit(solution)/shard_map/ppermute | solution.py:935
  123.4 6.1 %middle.2 = (f32[512,1024]{1,0:T(8,128)}, bf16[512,1024]{1,0:T(8,128)(2,1)S(1)}, bf16[512,512]{1,0:T(8,128)(2,1)S(1)}) custom-call(s32[5]{0:T(128)S(1)} %stack.66.info, bf16[2,1024,128]{2,1,0:T(8,128)(2,1)} %copy-done.27, bf16[2,1024,128]{2,1,0:T(8,128)(2,1)} %copy-done.47, bf16[2,1024,128]{2,1,0:T(8,128)(2,1)} %copy-done.48, ...), custom_call_target="tpu_custom_call" | custom-call | tf_op jit(solution)/shard_map/middle/pallas_call | solution.py:411
  130.2 5.5 %feed.4 = (bf16[1024,1408]{1,0:T(8,128)(2,1)}, bf16[1024,1408]{1,0:T(8,128)(2,1)}, bf16[1024,1408]{1,0:T(8,128)(2,1)}, bf16[1024,1024]{1,0:T(8,128)(2,1)}, bf16[256,1024]{1,0:T(8,128)(2,1)S(1)}) custom-call(bf16[512,1024]{1,0:T(8,128)(2,1)S(1)} %get-tuple-element.137.normed.refs_0_, bf16[1024,1024]{1,0:T(8,128)(2,1)S(1)} %copy-done.3, ...), custom_call_target="tpu_custom_call" | custom-call | flops 50000000 | tf_op jit(solution)/shard_map/feed/pallas_call | solution.py:459
  135.8 5.5 %feed.5 = (bf16[1024,1408]{1,0:T(8,128)(2,1)}, bf16[1024,1408]{1,0:T(8,128)(2,1)}, bf16[1024,1408]{1,0:T(8,128)(2,1)}, bf16[1024,1024]{1,0:T(8,128)(2,1)}, bf16[256,1024]{1,0:T(8,128)(2,1)S(1)}) custom-call(bf16[512,1024]{1,0:T(8,128)(2,1)S(1)} %get-tuple-element.137.normed.refs_0_, ...), custom_call_target="tpu_custom_call", output_to_operand_aliasing={{0}: (5, {}), {1}: (6, {}), {2}: (7, {}), {3}: (8, {})} | custom-call | flops 50000000 | tf_op jit(solution)/shard_map/feed/pallas_call | solution.py:459
  141.7 1.7 collective-permute-start.9
  143.4 5.6 %middle.3 = (f32[512,1024]{1,0:T(8,128)}, bf16[512,1024]{1,0:T(8,128)(2,1)S(1)}, bf16[512,512]{1,0:T(8,128)(2,1)S(1)}) custom-call(s32[5]{0:T(128)S(1)} %stack.66.info, bf16[2,1024,128]{2,1,0:T(8,128)(2,1)} %copy-done.27, bf16[2,1024,128]{2,1,0:T(8,128)(2,1)} %copy-done.47, bf16[2,1024,128]{2,1,0:T(8,128)(2,1)} %copy-done.48, ...), custom_call_target="tpu_custom_call" | custom-call | tf_op jit(solution)/shard_map/middle/pallas_call | solution.py:411
  149.1 6.3 %feed.6 = (bf16[1024,1408]{1,0:T(8,128)(2,1)}, bf16[1024,1408]{1,0:T(8,128)(2,1)}, bf16[1024,1408]{1,0:T(8,128)(2,1)}, bf16[1024,1024]{1,0:T(8,128)(2,1)}, bf16[256,1024]{1,0:T(8,128)(2,1)}) custom-call(bf16[512,1024]{1,0:T(8,128)(2,1)S(1)} %get-tuple-element.143.normed.refs_1_, ...), custom_call_target="tpu_custom_call", output_to_operand_aliasing={{0}: (5, {}), {1}: (6, {}), {2}: (7, {}), {3}: (8, {})} | custom-call | flops 50000000 | tf_op jit(solution)/shard_map/feed/pallas_call | solution.py:459
  155.7 6.3 %feed.7 = (bf16[1024,1408]{1,0:T(8,128)(2,1)}, bf16[1024,1408]{1,0:T(8,128)(2,1)}, bf16[1024,1408]{1,0:T(8,128)(2,1)}, bf16[1024,1024]{1,0:T(8,128)(2,1)}, bf16[256,1024]{1,0:T(8,128)(2,1)}) custom-call(bf16[512,1024]{1,0:T(8,128)(2,1)S(1)} %get-tuple-element.143.normed.refs_1_, ...), custom_call_target="tpu_custom_call", output_to_operand_aliasing={{0}: (5, {}), {1}: (6, {}), {2}: (7, {}), {3}: (8, {})} | custom-call | flops 50000000 | tf_op jit(solution)/shard_map/feed/pallas_call | solution.py:459
  162.1 1.7 collective-permute-start.11
  164.1 3.4 %collective-permute-done.9.back_other = bf16[256,1024]{1,0:T(8,128)(2,1)S(1)} collective-permute-done((bf16[256,1024]{1,0:T(8,128)(2,1)S(1)}, bf16[256,1024]{1,0:T(8,128)(2,1)S(1)}, u32[]{:S(2)}, u32[]{:S(2)}) %collective-permute-start.9) | collective-permute-done | bytes 524320 | tf_op jit(solution)/shard_map/ppermute | solution.py:935
  168.3 16.5 %feed_weights.1 = bf16[1024,4224]{1,0:T(8,128)(2,1)} custom-call(bf16[1024,1024]{1,0:T(8,128)(2,1)} %upstream.17, bf16[1024,1408]{1,0:T(8,128)(2,1)} %get-tuple-element.159.hidden, bf16[1024,1408]{1,0:T(8,128)(2,1)} %get-tuple-element.160.gate_grad, bf16[1024,1408]{1,0:T(8,128)(2,1)} %get-tuple-element.161.up_grad, bf16[512,1024]{1,0:T(8,128)(2,1)} %copy-done.17, ...), custom_call_target="tpu_custom_call" | custom-call | flops 50000000 | tf_op jit(solution)/shard_map/feed_weights/pallas_call | solution.py:516
  184.9 1.5 copy-done.24
  186.4 3.8 %residual.4 = (f32[1024,1024]{1,0:T(8,128)}, bf16[1024,1024]{1,0:T(8,128)(2,1)S(1)}, bf16[2,1024,128]{2,1,0:T(8,128)(2,1)S(1)}, bf16[1,1024,128]{2,1,0:T(8,128)(2,1)S(1)}, bf16[1,1024,128]{2,1,0:T(8,128)(2,1)S(1)}) custom-call(s32[5]{0:T(128)S(1)} %stack.66.info, f32[512,1024]{1,0:T(8,128)S(1)} %copy-done.24, bf16[256,1024]{1,0:T(8,128)(2,1)} %get-tuple-element.162.back_own, ...), custom_call_target="tpu_custom_call" | custom-call | flops 50000000 | tf_op jit(solution)/shard_map/residual/pallas_call | solution.py:562
  190.3 4.2 %residual.5 = (f32[1024,1024]{1,0:T(8,128)}, bf16[1024,1024]{1,0:T(8,128)(2,1)S(1)}, bf16[2,1024,128]{2,1,0:T(8,128)(2,1)S(1)}, bf16[1,1024,128]{2,1,0:T(8,128)(2,1)S(1)}, bf16[1,1024,128]{2,1,0:T(8,128)(2,1)S(1)}) custom-call(s32[5]{0:T(128)S(1)} %stack.66.info, ...), custom_call_target="tpu_custom_call", output_to_operand_aliasing={{0}: (7, {}), {1}: (8, {}), {2}: (9, {}), {3}: (10, {}), {4... | custom-call | flops 299999985664 | tf_op jit(solution)/shard_map/residual/pallas_call | solution.py:562
  194.5 3.7 %residual.6 = (f32[1024,1024]{1,0:T(8,128)}, bf16[1024,1024]{1,0:T(8,128)(2,1)S(1)}, bf16[2,1024,128]{2,1,0:T(8,128)(2,1)S(1)}, bf16[1,1024,128]{2,1,0:T(8,128)(2,1)S(1)}, bf16[1,1024,128]{2,1,0:T(8,128)(2,1)S(1)}) custom-call(s32[5]{0:T(128)S(1)} %stack.66.info, ...), custom_call_target="tpu_custom_call", output_to_operand_aliasing={{0}: (7, {}), {1}: (8, {}), {2}: (9, {}), {3}: (10, {}), {4... | custom-call | flops 50000000 | tf_op jit(solution)/shard_map/residual/pallas_call | solution.py:562
  198.3 4.3 %residual.7 = (f32[1024,1024]{1,0:T(8,128)}, bf16[1024,1024]{1,0:T(8,128)(2,1)S(1)}, bf16[2,1024,128]{2,1,0:T(8,128)(2,1)S(1)}, bf16[1,1024,128]{2,1,0:T(8,128)(2,1)S(1)}, bf16[1,1024,128]{2,1,0:T(8,128)(2,1)S(1)}) custom-call(s32[5]{0:T(128)S(1)} %stack.66.info, ...), custom_call_target="tpu_custom_call", output_to_operand_aliasing={{0}: (7, {}), {1}: (8, {}), {2}: (9, {}), {3}: (10, {}), {4... | custom-call | flops 50000000 | tf_op jit(solution)/shard_map/residual/pallas_call | solution.py:562
  204.3 8.6 %attend_backward.3 = (bf16[3,1,1024,128]{3,2,1,0:T(8,128)(2,1)S(1)}, bf16[2,1,1024,128]{3,2,1,0:T(8,128)(2,1)S(1)}, bf16[1,1,1024,128]{3,2,1,0:T(8,128)(2,1)S(1)}) custom-call(s32[5]{0:T(128)S(1)} %stack.66.info, bf16[3,2,1024,128]{3,2,1,0:T(8,128)(2,1)S(1)} %copy-done.13, bf16[3,2,1024,128]{3,2,1,0:T(8,128)(2,1)S(1)} %copy-done.16, ...), custom_call_target="tpu_custom_call" | custom-call | tf_op jit(solution)/shard_map/attend_backward/pallas_call | solution.py:336
  213.2 9.0 %attend_backward.2 = (bf16[3,1,1024,128]{3,2,1,0:T(8,128)(2,1)S(1)}, bf16[2,1,1024,128]{3,2,1,0:T(8,128)(2,1)S(1)}, bf16[1,1,1024,128]{3,2,1,0:T(8,128)(2,1)S(1)}) custom-call(s32[5]{0:T(128)S(1)} %stack.66.info, bf16[3,2,1024,128]{3,2,1,0:T(8,128)(2,1)S(1)} %copy-done.13, bf16[3,2,1024,128]{3,2,1,0:T(8,128)(2,1)S(1)} %copy-done.16, ...), custom_call_target="tpu_custom_call" | custom-call | tf_op jit(solution)/shard_map/attend_backward/pallas_call | solution.py:336
  223.2 1.4 collective-permute-done.18.refs_5_
  225.0 6.3 %back.1.back_own = bf16[1024,1024]{1,0:T(8,128)(2,1)} custom-call(s32[5]{0:T(128)S(1)} %stack.66.info, bf16[3,1,1024,128]{3,2,1,0:T(8,128)(2,1)S(1)} %get-tuple-element.190.refs_0_, bf16[3,1,1024,128]{3,2,1,0:T(8,128)(2,1)S(1)} %get-tuple-element.185.refs_1_, bf16[2,1,1024,128]{3,2,1,0:T(8,128)(2,1)S(1)} %collective-permute-done.15.refs_2_, ...), custom_call_target="tpu_custom_call" | custom-call | tf_op jit(solution)/shard_map/back/pallas_call | solution.py:617
  231.3 7.3 %attend_weights.1 = (bf16[2,4,64,2048]{3,2,1,0:T(8,128)(2,1)S(1)}, bf16[2,4,64,2048]{3,2,1,0:T(8,128)(2,1)S(1)}) custom-call(s32[5]{0:T(128)S(1)} %stack.66.info, bf16[1024,1024]{1,0:T(8,128)(2,1)S(1)} %copy-done.23, bf16[1024,1024]{1,0:T(8,128)(2,1)S(1)} %get-tuple-element.178.low, bf16[3,1,1024,128]{3,2,1,0:T(8,128)(2,1)S(1)} %get-tuple-element.190.refs_0_, ...), custom_call_target="tpu_custom_call" | custom-call | tf_op jit(solution)/shard_map/attend_weights/pallas_call | solution.py:667
  239.2 3.7 %collective-permute-done.19.core = bf16[2,4,64,2048]{3,2,1,0:T(8,128)(2,1)S(1)} collective-permute-done((bf16[2,4,64,2048]{3,2,1,0:T(8,128)(2,1)S(1)}, bf16[2,4,64,2048]{3,2,1,0:T(8,128)(2,1)S(1)}, u32[]{:S(2)}, u32[]{:S(2)}) %collective-permute-start.19) | collective-permute-done | bytes 2097184 | tf_op jit(solution)/shard_map/ppermute | solution.py:791
  243.3 2.5 collective-permute-start.20
  245.9 4.8 %fusion = bf16[1024,1024]{1,0:T(8,128)(2,1)} fusion(f32[512,1024]{1,0:T(8,128)S(1)} %copy-done.24, f32[512,1024]{1,0:T(8,128)S(1)} %copy-done.14, bf16[1024,1024]{1,0:T(8,128)(2,1)} %collective-permute-done.21, bf16[1024,1024]{1,0:T(8,128)(2,1)} %get-tuple-element.196), kind=kLoop, calls=%fused_computation.2 | loop fusion | flops 6291456 | bytes 10485760 | tf_op jit(solution)/shard_map/convert_element_type | solution.py:1028
  250.7 15.1 %collective-permute-done.20.right = bf16[2,64,2048]{2,1,0:T(8,128)(2,1)S(1)} collective-permute-done((bf16[2,64,2048]{2,1,0:T(8,128)(2,1)S(1)}, bf16[2,64,2048]{2,1,0:T(8,128)(2,1)S(1)}, u32[]{:S(2)}, u32[]{:S(2)}) %collective-permute-start.20) | collective-permute-done | bytes 524320 | tf_op jit(solution)/shard_map/ppermute | solution.py:794
  266.6 5.2 %collective-permute-start.22 = (bf16[64,2048]{1,0:T(8,128)(2,1)S(1)}, bf16[64,2048]{1,0:T(8,128)(2,1)S(1)}, u32[]{:S(2)}, u32[]{:S(2)}) collective-permute-start(bf16[64,2048]{1,0:T(8,128)(2,1)S(1)} %get-tuple-element.201.first), channel_id=1, source_target_pairs={{0,8},{2,10},{4,12},{6,14},{1,9},{3,11},{5,13},{7,15}} | collective-permute-start | bytes 786440 | tf_op jit(solution)/shard_map/ppermute | solution.py:824
  271.8 9.3 %collective-permute-done.24.right = bf16[2,64,2048]{2,1,0:T(8,128)(2,1)S(1)} collective-permute-done((bf16[2,64,2048]{2,1,0:T(8,128)(2,1)S(1)}, bf16[2,64,2048]{2,1,0:T(8,128)(2,1)S(1)}, u32[]{:S(2)}, u32[]{:S(2)}) %collective-permute-start.24) | collective-permute-done | bytes 524320 | tf_op jit(solution)/shard_map/ppermute | solution.py:796
  282.6 1.5 collective-permute-start.26
  284.2 4.0 %collective-permute-start.25 = (bf16[64,2048]{1,0:T(8,128)(2,1)}, bf16[64,2048]{1,0:T(8,128)(2,1)}, u32[]{:S(2)}, u32[]{:S(2)}) collective-permute-start(bf16[64,2048]{1,0:T(8,128)(2,1)} %low_add.2), channel_id=1, source_target_pairs={{0,8},{2,10},{4,12},{6,14},{8,16},{10,18},{12,20},{14,22},{1,9},{3... | collective-permute-start | bytes 786440 | tf_op jit(solution)/shard_map/ppermute | solution.py:824
  288.2 2.2 copy-done.6
  290.4 5.1 %input_grad.1 = bf16[1024,1024]{1,0:T(8,128)(2,1)} custom-call(f32[1024,1024]{1,0:T(8,128)S(1)} %copy-done.6, bf16[1024,1024]{1,0:T(8,128)(2,1)} %back.1.back_own, bf16[1024,1024]{1,0:T(8,128)(2,1)} %collective-permute-done.27.back_other, bf16[1024,1024]{1,0:T(8,128)(2,1)S(1)} %copy-done.7, f32[1,1024]{1,0:T(1,128)S(1)} %get-tuple-element.246.gain), custom_call_target="tpu_custom_call" | custom-call | flops 12582912 | bytes 12582912 | tf_op jit(solution)/shard_map/input_grad/pallas_call | solution.py:697
  295.7 4.0 %collective-permute-done.25.up_in = bf16[64,2048]{1,0:T(8,128)(2,1)} collective-permute-done((bf16[64,2048]{1,0:T(8,128)(2,1)}, bf16[64,2048]{1,0:T(8,128)(2,1)}, u32[]{:S(2)}, u32[]{:S(2)}) %collective-permute-start.25) | collective-permute-done | bytes 262176 | tf_op jit(solution)/shard_map/ppermute | solution.py:824
  300.9 7.4 %collective-permute-start.28 = (bf16[64,2048]{1,0:T(8,128)(2,1)S(1)}, bf16[64,2048]{1,0:T(8,128)(2,1)}, u32[]{:S(2)}, u32[]{:S(2)}) collective-permute-start(bf16[64,2048]{1,0:T(8,128)(2,1)S(1)} %get-tuple-element.215), channel_id=1, source_target_pairs={{0,8},{2,10},{4,12},{6,14},{8,16},{10,18},{12,20},{14,22},{16,24},... | collective-permute-start | bytes 786440 | tf_op jit(solution)/shard_map/ppermute | solution.py:824
  309.6 1.5 reduce-scatter.2.cloned.1.call-done
  312.4 2.4 multiply_subtract_fusion.2
  314.8 1.8 multiply_subtract_fusion
  320.7 2.3 collective-permute-start.30
  (216 shorter events, 33.1 us)
Async XLA Ops:
  7.2 37.0 %copy-start = (bf16[1024,2,512]{2,1,0:T(2,128)(2,1)S(1)}, bf16[1024,2,512]{2,1,0:T(2,128)(2,1)}, u32[]{:S(2)}) copy-start(bf16[1024,2,512]{2,1,0:T(2,128)(2,1)} %param.38) | copy-start | bytes 6291460
  7.3 115.4 %all-gather.2.cloned.1.call-start = ((), (), s32[]{:S(2)}) async-start(), calls=%async_computation.1 | async-start | bytes 11419648 | tf_op jit(solution)/shard_map/all_gather | solution.py:958
  8.4 6.3 %collective-permute-start.8 = (bf16[64,512]{1,0:T(8,128)(2,1)S(1)}, bf16[64,512]{1,0:T(8,128)(2,1)S(1)}, u32[]{:S(2)}, u32[]{:S(2)}) collective-permute-start(bf16[64,512]{1,0:T(8,128)(2,1)S(1)} %convert_bitcast_fusion), channel_id=1, source_target_pairs={{0,1},{1,0},{2,3},{3,2},{4,5},{5,4},{6,7},{7,6},{8,9},{9,8},{10,11... | collective-permute-start | bytes 196616 | tf_op jit(solution)/shard_map/ppermute | solution.py:935
  12.6 31.6 %copy-start.61 = (s32[1,128]{1,0:T(1,128)S(1)}, s32[1,128]{1,0:T(1,128)}, u32[]{:S(2)}) copy-start(s32[1,128]{1,0:T(1,128)} %param.41) | copy-start | bytes 1540
  16.0 295.2 %reduce-scatter.2.cloned.1.call-start = ((), (), s32[]{:S(2)}) async-start(), calls=%async_computation.2 | async-start | bytes 9191424 | tf_op jit(solution)/shard_map/reduce_scatter | solution.py:1032
  42.9 27.2 %collective-permute-start.1 = (bf16[256,1664]{1,0:T(8,128)(2,1)S(1)}, bf16[256,1664]{1,0:T(8,128)(2,1)}, u32[]{:S(2)}, u32[]{:S(2)}) collective-permute-start(bf16[256,1664]{1,0:T(8,128)(2,1)S(1)} %all_gather.6), channel_id=1, source_target_pairs={{0,2},{2,0},{4,6},{6,4},{8,10},{10,8},{12,14},{14,12},{16,18},{18,... | collective-permute-start | bytes 2555912 | tf_op jit(solution)/shard_map/ppermute | solution.py:938
  42.9 23.1 %collective-permute-start = (bf16[256,1664]{1,0:T(8,128)(2,1)S(1)}, bf16[256,1664]{1,0:T(8,128)(2,1)}, u32[]{:S(2)}, u32[]{:S(2)}) collective-permute-start(bf16[256,1664]{1,0:T(8,128)(2,1)S(1)} %all_gather.6), channel_id=1, source_target_pairs={{0,4},{2,6},{4,0},{6,2},{8,12},{10,14},{12,8},{14,10},{16,20},{18,... | collective-permute-start | bytes 2555912 | tf_op jit(solution)/shard_map/ppermute | solution.py:956
  45.8 24.3 %collective-permute-start.3 = (bf16[2,2,128,128]{3,2,1,0:T(8,128)(2,1)S(1)}, bf16[2,2,128,128]{3,2,1,0:T(8,128)(2,1)S(1)}, u32[]{:S(2)}, u32[]{:S(2)}) collective-permute-start(bf16[2,2,128,128]{3,2,1,0:T(8,128)(2,1)S(1)} %bitcast.79), channel_id=1, source_target_pairs={{0,2},{2,0},{4,6},{6,4},{8,10},{10,8},{12,14},{14,12},{16,18},{18,... | collective-permute-start | bytes 393224 | tf_op jit(solution)/shard_map/ppermute | solution.py:938
  66.1 4.0 %collective-permute-start.2 = (bf16[256,1664]{1,0:T(8,128)(2,1)}, bf16[256,1664]{1,0:T(8,128)(2,1)S(1)}, u32[]{:S(2)}, u32[]{:S(2)}) collective-permute-start(bf16[256,1664]{1,0:T(8,128)(2,1)} %collective-permute-done), channel_id=1, source_target_pairs={{0,2},{2,0},{4,6},{6,4},{8,10},{10,8},{12,14},{14,12},{16,18},{18,... | collective-permute-start | bytes 2555912 | tf_op jit(solution)/shard_map/ppermute | solution.py:938
  66.4 17.4 %copy-start.20 = (bf16[2048,128]{1,0:T(8,128)(2,1)}, bf16[2048,128]{1,0:T(8,128)(2,1)S(1)}, u32[]{:S(2)}) copy-start(bf16[2048,128]{1,0:T(8,128)(2,1)S(1)} %select_convert_fusion.bias) | copy-start | bytes 1572868
  70.0 13.9 %copy-start.25 = (bf16[128,2,1,2,128]{4,0,3,1,2:T(8,128)(2,1)}, bf16[128,2,1,2,128]{4,0,3,1,2:T(8,128)(2,1)S(1)}, u32[]{:S(2)}) copy-start(bf16[128,2,1,2,128]{4,0,3,1,2:T(8,128)(2,1)S(1)} %copy.70) | copy-start | bytes 393220
  70.1 13.8 %copy-start.30 = (bf16[2,2,128,128]{3,2,1,0:T(8,128)(2,1)}, bf16[2,2,128,128]{3,2,1,0:T(8,128)(2,1)S(1)}, u32[]{:S(2)}) copy-start(bf16[2,2,128,128]{3,2,1,0:T(8,128)(2,1)S(1)} %collective-permute-done.3.mem_other) | copy-start | bytes 393220
  79.4 4.4 %collective-permute-start.4 = (bf16[3,2,1024,128]{3,2,1,0:T(8,128)(2,1)S(1)}, bf16[3,2,1024,128]{3,2,1,0:T(8,128)(2,1)S(1)}, u32[]{:S(2)}, u32[]{:S(2)}) collective-permute-start(bf16[3,2,1024,128]{3,2,1,0:T(8,128)(2,1)S(1)} %get-tuple-element.129), channel_id=1, source_target_pairs={{0,2},{2,0},{4,6},{6,4},{8,10},{10,8},{12,14},{14,12},{16,18},{18,... | collective-permute-start | bytes 4718600 | tf_op jit(solution)/shard_map/ppermute | solution.py:938
  83.9 12.0 %copy-start.15 = (bf16[3,2,1024,128]{3,2,1,0:T(8,128)(2,1)}, bf16[3,2,1024,128]{3,2,1,0:T(8,128)(2,1)S(1)}, u32[]{:S(2)}) copy-start(bf16[3,2,1024,128]{3,2,1,0:T(8,128)(2,1)S(1)} %collective-permute-done.4.other) | copy-start | bytes 4718596
  97.0 25.6 %copy-start.27 = (bf16[2,1024,128]{2,1,0:T(8,128)(2,1)}, bf16[2,1024,128]{2,1,0:T(8,128)(2,1)S(1)}, u32[]{:S(2)}) copy-start(bf16[2,1024,128]{2,1,0:T(8,128)(2,1)S(1)} %get-tuple-element.133.refs_0_) | copy-start | bytes 1572868
  97.0 1.9 collective-permute-start.5
  97.1 14.7 %collective-permute-start.6 = (bf16[2,1024,128]{2,1,0:T(8,128)(2,1)S(1)}, bf16[2,1024,128]{2,1,0:T(8,128)(2,1)S(1)}, u32[]{:S(2)}, u32[]{:S(2)}) collective-permute-start(bf16[2,1024,128]{2,1,0:T(8,128)(2,1)S(1)} %get-tuple-element.133.refs_0_), channel_id=1, source_target_pairs={{0,1},{1,0},{2,3},{3,2},{4,5},{5,4},{6,7},{7,6},{8,9},{9,8},{10,11... | collective-permute-start | bytes 1572872 | tf_op jit(solution)/shard_map/ppermute | solution.py:935
  98.9 23.7 %copy-start.47 = (bf16[2,1024,128]{2,1,0:T(8,128)(2,1)}, bf16[2,1024,128]{2,1,0:T(8,128)(2,1)S(1)}, u32[]{:S(2)}) copy-start(bf16[2,1024,128]{2,1,0:T(8,128)(2,1)S(1)} %collective-permute-done.5.refs_1_) | copy-start | bytes 1572868
  98.9 23.7 %collective-permute-start.7 = (bf16[2,1024,128]{2,1,0:T(8,128)(2,1)S(1)}, bf16[2,1024,128]{2,1,0:T(8,128)(2,1)S(1)}, u32[]{:S(2)}, u32[]{:S(2)}) collective-permute-start(bf16[2,1024,128]{2,1,0:T(8,128)(2,1)S(1)} %collective-permute-done.5.refs_1_), channel_id=1, source_target_pairs={{0,1},{1,0},{2,3},{3,2},{4,5},{5,4},{6,7},{7,6},{8,9},{9,8},{10,11... | collective-permute-start | bytes 1572872 | tf_op jit(solution)/shard_map/ppermute | solution.py:935
  130.2 18.8 %slice-start = ((s8[10747904]{0:T(1024)(128)(4,1)}), s8[4194304]{0:T(1024)(128)(4,1)S(1)}, s32[]{:S(2)}) async-start(s8[10747904]{0:T(1024)(128)(4,1)} %bitcast.71), calls=%async_computation.3 | async-start | bytes 8388608
  130.2 18.9 %slice-start.1 = ((s8[10747904]{0:T(1024)(128)(4,1)}), s8[4194304]{0:T(1024)(128)(4,1)S(1)}, s32[]{:S(2)}) async-start(s8[10747904]{0:T(1024)(128)(4,1)} %bitcast.71), calls=%async_computation.4 | async-start | bytes 8388608
  135.8 13.3 %slice-start.2 = ((s8[10747904]{0:T(1024)(128)(4,1)}), s8[2359296]{0:T(1024)(128)(4,1)S(1)}, s32[]{:S(2)}) async-start(s8[10747904]{0:T(1024)(128)(4,1)} %bitcast.71), calls=%async_computation.5 | async-start | bytes 4718592
  141.3 22.7 %collective-permute-start.10 = (bf16[256,1024]{1,0:T(8,128)(2,1)S(1)}, bf16[256,1024]{1,0:T(8,128)(2,1)S(1)}, u32[]{:S(2)}, u32[]{:S(2)}) collective-permute-start(bf16[256,1024]{1,0:T(8,128)(2,1)S(1)} %get-tuple-element.142.back_own), channel_id=1, source_target_pairs={{0,1},{1,0},{2,3},{3,2},{4,5},{5,4},{6,7},{7,6},{8,9},{9,8},{10,11... | collective-permute-start | bytes 1572872 | tf_op jit(solution)/shard_map/ppermute | solution.py:935
  141.7 25.8 %collective-permute-start.9 = (bf16[256,1024]{1,0:T(8,128)(2,1)S(1)}, bf16[256,1024]{1,0:T(8,128)(2,1)S(1)}, u32[]{:S(2)}, u32[]{:S(2)}) collective-permute-start(bf16[256,1024]{1,0:T(8,128)(2,1)S(1)} %get-tuple-element.153.back_own), channel_id=1, source_target_pairs={{0,1},{1,0},{2,3},{3,2},{4,5},{5,4},{6,7},{7,6},{8,9},{9,8},{10,11... | collective-permute-start | bytes 1572872 | tf_op jit(solution)/shard_map/ppermute | solution.py:935
  155.4 29.5 %collective-permute-start.12 = (bf16[256,1024]{1,0:T(8,128)(2,1)}, bf16[256,1024]{1,0:T(8,128)(2,1)}, u32[]{:S(2)}, u32[]{:S(2)}) collective-permute-start(bf16[256,1024]{1,0:T(8,128)(2,1)} %get-tuple-element.162.back_own), channel_id=1, source_target_pairs={{0,1},{1,0},{2,3},{3,2},{4,5},{5,4},{6,7},{7,6},{8,9},{9,8},{10,11... | collective-permute-start | bytes 1572872 | tf_op jit(solution)/shard_map/ppermute | solution.py:935
  162.1 28.2 %collective-permute-start.11 = (bf16[256,1024]{1,0:T(8,128)(2,1)}, bf16[256,1024]{1,0:T(8,128)(2,1)}, u32[]{:S(2)}, u32[]{:S(2)}) collective-permute-start(bf16[256,1024]{1,0:T(8,128)(2,1)} %get-tuple-element.157.back_own), channel_id=1, source_target_pairs={{0,1},{1,0},{2,3},{3,2},{4,5},{5,4},{6,7},{7,6},{8,9},{9,8},{10,11... | collective-permute-start | bytes 1572872 | tf_op jit(solution)/shard_map/ppermute | solution.py:935
  163.8 75.2 %collective-permute-start.21 = (bf16[1024,1024]{1,0:T(8,128)(2,1)}, bf16[1024,1024]{1,0:T(8,128)(2,1)}, u32[]{:S(2)}, u32[]{:S(2)}) collective-permute-start(bf16[1024,1024]{1,0:T(8,128)(2,1)} %get-tuple-element.196), channel_id=1, source_target_pairs={{0,1},{1,0},{2,3},{3,2},{4,5},{5,4},{6,7},{7,6},{8,9},{9,8},{10,11... | collective-permute-start | bytes 6291464 | tf_op jit(solution)/shard_map/ppermute | solution.py:935
  164.1 20.8 %copy-start.34 = (bf16[256,1024]{1,0:T(8,128)(2,1)}, bf16[256,1024]{1,0:T(8,128)(2,1)S(1)}, u32[]{:S(2)}) copy-start(bf16[256,1024]{1,0:T(8,128)(2,1)S(1)} %collective-permute-done.10.back_other) | copy-start | bytes 1572868
  202.6 1.7 collective-permute-start.14
  202.6 10.5 %collective-permute-start.13 = (bf16[1,1024,128]{2,1,0:T(8,128)(2,1)S(1)}, bf16[1,1024,128]{2,1,0:T(8,128)(2,1)S(1)}, u32[]{:S(2)}, u32[]{:S(2)}) collective-permute-start(bf16[1,1024,128]{2,1,0:T(8,128)(2,1)S(1)} %get-tuple-element.180), channel_id=1, source_target_pairs={{0,2},{2,0},{4,6},{6,4},{8,10},{10,8},{12,14},{14,12},{16,18},{18,... | collective-permute-start | bytes 786440 | tf_op jit(solution)/shard_map/ppermute | solution.py:938
  213.0 12.0 %collective-permute-start.17 = (bf16[2,1,1024,128]{3,2,1,0:T(8,128)(2,1)S(1)}, bf16[2,1,1024,128]{3,2,1,0:T(8,128)(2,1)S(1)}, u32[]{:S(2)}, u32[]{:S(2)}) collective-permute-start(bf16[2,1,1024,128]{3,2,1,0:T(8,128)(2,1)S(1)} %get-tuple-element.188), channel_id=1, source_target_pairs={{0,2},{2,0},{4,6},{6,4},{8,10},{10,8},{12,14},{14,12},{16,18},{18,... | collective-permute-start | bytes 1572872 | tf_op jit(solution)/shard_map/ppermute | solution.py:938
  222.2 2.7 collective-permute-start.15
  222.7 1.9 collective-permute-start.18
  222.8 2.2 collective-permute-start.16
  238.6 4.2 %collective-permute-start.19 = (bf16[2,4,64,2048]{3,2,1,0:T(8,128)(2,1)S(1)}, bf16[2,4,64,2048]{3,2,1,0:T(8,128)(2,1)S(1)}, u32[]{:S(2)}, u32[]{:S(2)}) collective-permute-start(bf16[2,4,64,2048]{3,2,1,0:T(8,128)(2,1)S(1)} %get-tuple-element.194), channel_id=1, source_target_pairs={{0,2},{2,0},{4,6},{6,4},{8,10},{10,8},{12,14},{14,12},{16,18},{18,... | collective-permute-start | bytes 6291464 | tf_op jit(solution)/shard_map/ppermute | solution.py:791
  239.0 49.2 %collective-permute-start.27 = (bf16[1024,1024]{1,0:T(8,128)(2,1)}, bf16[1024,1024]{1,0:T(8,128)(2,1)}, u32[]{:S(2)}, u32[]{:S(2)}) collective-permute-start(bf16[1024,1024]{1,0:T(8,128)(2,1)} %back.1.back_own), channel_id=1, source_target_pairs={{0,1},{1,0},{2,3},{3,2},{4,5},{5,4},{6,7},{7,6},{8,9},{9,8},{10,11... | collective-permute-start | bytes 6291464 | tf_op jit(solution)/shard_map/ppermute | solution.py:935
  243.3 22.5 %collective-permute-start.20 = (bf16[2,64,2048]{2,1,0:T(8,128)(2,1)S(1)}, bf16[2,64,2048]{2,1,0:T(8,128)(2,1)S(1)}, u32[]{:S(2)}, u32[]{:S(2)}) collective-permute-start(bf16[2,64,2048]{2,1,0:T(8,128)(2,1)S(1)} %get-tuple-element.195), channel_id=1, source_target_pairs={{0,4},{2,6},{4,0},{6,2},{8,12},{10,14},{12,8},{14,10},{16,20},{18,... | collective-permute-start | bytes 1572872 | tf_op jit(solution)/shard_map/ppermute | solution.py:794
  245.8 35.3 %collective-permute-start.24 = (bf16[2,64,2048]{2,1,0:T(8,128)(2,1)S(1)}, bf16[2,64,2048]{2,1,0:T(8,128)(2,1)S(1)}, u32[]{:S(2)}, u32[]{:S(2)}) collective-permute-start(bf16[2,64,2048]{2,1,0:T(8,128)(2,1)S(1)} %get-tuple-element.203), channel_id=1, source_target_pairs={{0,4},{2,6},{4,0},{6,2},{8,12},{10,14},{12,8},{14,10},{16,20},{18,... | collective-permute-start | bytes 1572872 | tf_op jit(solution)/shard_map/ppermute | solution.py:796
  250.7 37.5 %copy-start.7 = (bf16[1024,1024]{1,0:T(8,128)(2,1)S(1)}, bf16[1024,1024]{1,0:T(8,128)(2,1)}, u32[]{:S(2)}) copy-start(bf16[1024,1024]{1,0:T(8,128)(2,1)} %tokens.3) | copy-start | bytes 6291460
  265.9 16.7 %copy-start.40 = (bf16[64,2048]{1,0:T(8,128)(2,1)}, bf16[64,2048]{1,0:T(8,128)(2,1)S(1)}, u32[]{:S(2)}) copy-start(bf16[64,2048]{1,0:T(8,128)(2,1)S(1)} %get-tuple-element.201.first) | copy-start | bytes 786436
  266.0 15.1 %collective-permute-start.23 = (bf16[64,2048]{1,0:T(8,128)(2,1)S(1)}, bf16[64,2048]{1,0:T(8,128)(2,1)S(1)}, u32[]{:S(2)}, u32[]{:S(2)}) collective-permute-start(bf16[64,2048]{1,0:T(8,128)(2,1)S(1)} %get-tuple-element.201.first), channel_id=1, source_target_pairs={{24,16},{26,18},{28,20},{30,22},{25,17},{27,19},{29,21},{31,23}} | collective-permute-start | bytes 786440 | tf_op jit(solution)/shard_map/ppermute | solution.py:825
  266.6 14.5 %collective-permute-start.22 = (bf16[64,2048]{1,0:T(8,128)(2,1)S(1)}, bf16[64,2048]{1,0:T(8,128)(2,1)S(1)}, u32[]{:S(2)}, u32[]{:S(2)}) collective-permute-start(bf16[64,2048]{1,0:T(8,128)(2,1)S(1)} %get-tuple-element.201.first), channel_id=1, source_target_pairs={{0,8},{2,10},{4,12},{6,14},{1,9},{3,11},{5,13},{7,15}} | collective-permute-start | bytes 786440 | tf_op jit(solution)/shard_map/ppermute | solution.py:824
  282.6 13.0 %collective-permute-start.26 = (bf16[64,2048]{1,0:T(8,128)(2,1)}, bf16[64,2048]{1,0:T(8,128)(2,1)}, u32[]{:S(2)}, u32[]{:S(2)}) collective-permute-start(bf16[64,2048]{1,0:T(8,128)(2,1)} %low_add.3), channel_id=1, source_target_pairs={{16,8},{18,10},{20,12},{22,14},{24,16},{26,18},{28,20},{30,22},{17... | collective-permute-start | bytes 786440 | tf_op jit(solution)/shard_map/ppermute | solution.py:825
  284.2 15.5 %collective-permute-start.25 = (bf16[64,2048]{1,0:T(8,128)(2,1)}, bf16[64,2048]{1,0:T(8,128)(2,1)}, u32[]{:S(2)}, u32[]{:S(2)}) collective-permute-start(bf16[64,2048]{1,0:T(8,128)(2,1)} %low_add.2), channel_id=1, source_target_pairs={{0,8},{2,10},{4,12},{6,14},{8,16},{10,18},{12,20},{14,22},{1,9},{3... | collective-permute-start | bytes 786440 | tf_op jit(solution)/shard_map/ppermute | solution.py:824
  295.6 16.7 %copy-start.53 = (f32[1408,64]{0,1:T(8,128)S(1)}, f32[1408,64]{0,1:T(8,128)}, u32[]{:S(2)}) copy-start(f32[1408,64]{0,1:T(8,128)} %param.26) | copy-start | bytes 1081348
  300.9 15.7 %collective-permute-start.28 = (bf16[64,2048]{1,0:T(8,128)(2,1)S(1)}, bf16[64,2048]{1,0:T(8,128)(2,1)}, u32[]{:S(2)}, u32[]{:S(2)}) collective-permute-start(bf16[64,2048]{1,0:T(8,128)(2,1)S(1)} %get-tuple-element.215), channel_id=1, source_target_pairs={{0,8},{2,10},{4,12},{6,14},{8,16},{10,18},{12,20},{14,22},{16,24},... | collective-permute-start | bytes 786440 | tf_op jit(solution)/shard_map/ppermute | solution.py:824
  308.4 9.6 %collective-permute-start.29 = (bf16[64,2048]{1,0:T(8,128)(2,1)S(1)}, bf16[64,2048]{1,0:T(8,128)(2,1)}, u32[]{:S(2)}, u32[]{:S(2)}) collective-permute-start(bf16[64,2048]{1,0:T(8,128)(2,1)S(1)} %get-tuple-element.216), channel_id=1, source_target_pairs={{8,0},{10,2},{12,4},{14,6},{16,8},{18,10},{20,12},{22,14},{24,16},... | collective-permute-start | bytes 786440 | tf_op jit(solution)/shard_map/ppermute | solution.py:825
  320.7 3.8 %collective-permute-start.30 = (f32[2,64]{1,0:T(2,128)S(1)}, f32[2,64]{1,0:T(2,128)S(1)}, u32[]{:S(2)}, u32[]{:S(2)}) collective-permute-start(f32[2,64]{1,0:T(2,128)S(1)} %pad_maximum_fusion.4.own), channel_id=1, source_target_pairs={{0,1},{1,0},{2,3},{3,2},{4,5},{5,4},{6,7},{7,6},{8,9},{9,8},{10,11... | collective-permute-start | bytes 1544 | tf_op jit(solution)/shard_map/ppermute | solution.py:935
  (50 other events, 265.7 us)
Sparse Core Ops, SparseCore 0:
  16.1 95.6 all-gather.1
  185.0 126.1 reduce-scatter.1

commit v4 on v3

--- a/solution.py
+++ b/solution.py
@@ -28,7 +28,6 @@
 F32 = jnp.float32
 MIB = 1024 * 1024
 TILE = 256
-PART = 512
 VMEM = 26
 WEIGH = 1.0
 
@@ -390,8 +389,8 @@
     pieces, (tokens, weight, gain, middle, normed, attended, joined) = refs[:4], refs[4:]
     rank, group = info[0], info[1]
     for index, piece in enumerate(pieces):
+        side = (group, 1 - group)[index // 2]
         pair = (rank, 1 - rank)[index % 2]
-        side = (group, 1 - group)[index // 2]
         for head in range(2):
             column = pl.multiple_of((side * 4 + pair * 2 + head) * HEAD_DIM, HEAD_DIM)
             joined[:, pl.ds(column, HEAD_DIM)] = piece[head]
@@ -403,28 +402,27 @@
     normed[...] = (value * inverse * gain[...]).astype(BF)
 
 
-def middle_call(info, pieces, tokens, weights, gain, chunk):
-    half = 4 * HEAD_DIM
-    first = chunk * (PART // TILE)
-    piece = pl.BlockSpec((2, TILE, HEAD_DIM), lambda i, info: (0, i + first, 0))
-    one = pl.BlockSpec((TILE, D), lambda i, info: (i, 0))
+def middle_call(info, pieces, tokens, weights, gain):
+    rows, half = tokens.shape[0], 4 * HEAD_DIM
+    piece = pl.BlockSpec((2, TILE, HEAD_DIM), lambda i, info: (0, i, 0))
+    wide = pl.BlockSpec((TILE, D), lambda i, info: (i, 0))
     return pl.pallas_call(
         middle_kernel,
         out_shape=(
-            pltpu.HBM((PART, D), F32),
-            jax.ShapeDtypeStruct((PART, D), BF),
-            jax.ShapeDtypeStruct((PART, half), BF),
+            pltpu.HBM((rows, D), F32),
+            jax.ShapeDtypeStruct((rows, D), BF),
+            jax.ShapeDtypeStruct((rows, half), BF),
         ),
         grid_spec=pltpu.PrefetchScalarGridSpec(
             num_scalar_prefetch=1,
-            grid=(PART // TILE,),
+            grid=(rows // TILE,),
             in_specs=[piece] * 4
             + [
-                pl.BlockSpec((TILE, D), lambda i, info: (i + first, 0)),
+                wide,
                 columns(D, lambda i, info: (0, OUT_AT)),
                 pl.BlockSpec((1, D), lambda i, info: (0, 0)),
             ],
-            out_specs=(one, one, pl.BlockSpec((TILE, half), lambda i, info: (i, 0))),
+            out_specs=(wide, wide, pl.BlockSpec((TILE, half), lambda i, info: (i, 0))),
             scratch_shapes=[pltpu.VMEM((TILE, D), BF)],
         ),
         compiler_params=params(VMEM),
@@ -458,10 +456,10 @@
     narrow = pl.BlockSpec((TILE, width), lambda i: (i + first // TILE, 0))
     return pl.pallas_call(
         feed_kernel,
-        out_shape=(pltpu.HBM((rows, width), BF),) * 3
+        out_shape=(pltpu.VMEM((rows, width), BF),) * 3
         + (jax.ShapeDtypeStruct((rows, D), BF), jax.ShapeDtypeStruct((count, D), BF)),
         grid=(count // TILE,),
-        in_specs=[pl.BlockSpec((TILE, D), lambda i: (first % PART // TILE, 0)), source, whole(0), whole(1), whole(2)]
+        in_specs=[source, source, whole(0), whole(1), whole(2)]
         + [pl.BlockSpec(memory_space=pl.ANY)] * len(earlier),
         out_specs=(narrow, narrow, narrow, source, pl.BlockSpec((TILE, D), lambda i: (i, 0))),
         input_output_aliases={5 + index: index for index in range(len(earlier))},
@@ -471,64 +469,29 @@
     )(normed, upstream, weights, weights, weights, *earlier)
 
 
-def feed_weight_kernel(upstream, hidden, gate_grad, up_grad, *refs):
-    normed, (out, held, left_s, sems, left_sem) = refs[:-5], refs[-5:]
-    part, tile = pl.program_id(0), pl.program_id(1)
-    copies = [
-        pltpu.make_async_copy(source, held.at[index], sems.at[index])
-        for index, source in enumerate((gate_grad, up_grad, hidden))
-    ]
-    chunks = [
-        pltpu.make_async_copy(chunk, left_s.at[0, pl.ds(index * PART, PART), :], left_sem.at[index])
-        for index, chunk in enumerate(normed)
-    ]
-    chunks.append(pltpu.make_async_copy(upstream, left_s.at[1], left_sem.at[len(normed)]))
-
-    @pl.when((part == 0) & (tile == 0))
-    def _():
-        for copy in chunks[:-1]:
-            copy.start()
-        copies[0].start()
-        copies[1].start()
-        chunks[-1].start()
-        copies[2].start()
-        for copy in chunks[:-1]:
-            copy.wait()
-        copies[0].wait()
-
-    @pl.when((part == 1) & (tile == 0))
-    def _():
-        copies[1].wait()
-
-    @pl.when((part == 2) & (tile == 0))
-    def _():
-        chunks[-1].wait()
-        copies[2].wait()
-
-    column = pl.multiple_of(tile * TILE, TILE)
-    left = left_s[part // 2, :, pl.ds(column, TILE)].astype(F32).T.astype(BF)
-    out[...] = dot(left, held[part]).astype(BF)
+def feed_weight_kernel(normed, upstream, hidden, gate_grad, up_grad, out):
+    width = hidden.shape[1]
+    left = normed[...].astype(F32).T.astype(BF)
+    out[:, :width] = dot(left, gate_grad[...]).astype(BF)
+    out[:, width : 2 * width] = dot(left, up_grad[...]).astype(BF)
+    left = upstream[...].astype(F32).T.astype(BF)
+    out[:, 2 * width :] = dot(left, hidden[...]).astype(BF)
 
 
 def feed_weight_call(normed, upstream, hidden, gate_grad, up_grad):
     rows, width = hidden.shape
-    anywhere = pl.BlockSpec(memory_space=pl.ANY)
+    left = pl.BlockSpec((rows, TILE), lambda i: (0, i))
+    whole = pl.BlockSpec((rows, width), lambda i: (0, 0), pipeline_mode=pl.Buffered(1))
     return pl.pallas_call(
         feed_weight_kernel,
         out_shape=pltpu.HBM((D, 3 * width), BF),
-        grid=(3, D // TILE),
-        in_specs=[anywhere] * (4 + len(normed)),
-        out_specs=pl.BlockSpec((TILE, width), lambda part, tile: (tile, part)),
-        scratch_shapes=[
-            pltpu.VMEM((3, rows, width), BF),
-            pltpu.VMEM((2, rows, D), BF),
-            pltpu.SemaphoreType.DMA((3,)),
-            pltpu.SemaphoreType.DMA((len(normed) + 1,)),
-        ],
-        compiler_params=params(VMEM, 2),
+        grid=(D // TILE,),
+        in_specs=[left, left, whole, whole, whole],
+        out_specs=pl.BlockSpec((TILE, 3 * width), lambda i: (i, 0)),
+        compiler_params=params(VMEM),
         cost_estimate=cost(5e7, 0),
         name="feed_weights",
-    )(*[in_hbm(value) for value in (upstream, hidden, gate_grad, up_grad, *normed)])
+    )(normed, in_hbm(upstream), hidden, gate_grad, up_grad)
 
 
 def residual_kernel(info, middle, back_own, back_other, upstream, gain, weight, *refs):
@@ -572,7 +535,7 @@
             num_scalar_prefetch=1,
             grid=(count // TILE,),
             in_specs=[
-                pl.BlockSpec((TILE, D), lambda i, info: (i + first % PART // TILE, 0)),
+                wide,
                 part,
                 part,
                 wide,
@@ -643,7 +606,7 @@
     left = normed[...].astype(F32).T.astype(BF)
     out[:, :width] = dot(left, joined[...]).astype(BF)
     left = low[...].astype(F32).T.astype(BF)
-    out[:, width:] = dot(left, jnp.concatenate([part[...] for part in attended])).astype(BF)
+    out[:, width:] = dot(left, attended[0][...]).astype(BF)
     count, size = keep.shape[1], keep.shape[2]
     for line in range(tile // (4 * size)):
         slot = count - 1 - ((step * (tile // (4 * size)) + line) ^ info[4])
@@ -655,7 +618,7 @@
 
 
 def attend_weight_call(info, normed, low, attended, pieces, size):
-    rows, half = normed.shape[0], attended[0].shape[1]
+    rows, half = normed.shape[0], attended.shape[1]
     width = 3 * half
     total = width + half
     left = pl.BlockSpec((rows, TILE), lambda i, info: (0, i))
@@ -672,14 +635,14 @@
             grid=(D // TILE,),
             in_specs=[left, left]
             + piece
-            + [pl.BlockSpec((PART, half), lambda i, info: (0, 0))] * len(attended),
+            + [pl.BlockSpec((rows, half), lambda i, info: (0, 0))],
             out_specs=(pl.BlockSpec((2, count, size, total), lambda i, info: (0, 0, 0, 0)),) * 2,
             scratch_shapes=[pltpu.VMEM((rows, width), BF), pltpu.VMEM((TILE, total), BF)],
         ),
         compiler_params=params(VMEM),
         cost_estimate=cost(0, 0),
         name="attend_weights",
-    )(info, normed, low, *pieces, *attended)
+    )(info, normed, low, *pieces, attended)
 
 
 def input_kernel(grad, back_own, back_other, tokens, gain, out):
@@ -981,20 +944,17 @@
     out_keep, out_send, turned, logs = attend_forward(info, own, other, mem_own, mem_other, bias)
     out_recv = beside(out_send)
     pieces = (out_keep, out_recv, across(out_keep), across(out_recv))
-    middles, normed_two, attended = [], [], []
-    for chunk in range(rows // PART):
-        middle, normed, own_out = middle_call(info, pieces, tokens, weights_two, gain_two, chunk)
-        middles.append(middle)
-        normed_two.append(normed)
-        attended.append(own_out)
+    middle, normed_two, attended = middle_call(info, pieces, tokens, weights_two, gain_two)
 
     earlier, backs, backs_other = (), [], []
     for chunk, first in enumerate(range(0, rows, TILE)):
-        *earlier, back = feed_call(normed_two[first // PART], cotangent, weights_two, first, TILE, earlier)
+        if first + TILE == rows:
+            earlier, backs_other[0] = pin((earlier, backs_other[0]))
+        *earlier, back = feed_call(normed_two, cotangent, weights_two, first, TILE, earlier)
         backs.append(back)
         backs_other.append(across(back))
     hidden, grad_gate, grad_up, feed_part = earlier
-    hidden, backs_other[:2] = pin((hidden, backs_other[:2]))
+    hidden, backs_other[1] = pin((hidden, backs_other[1]))
     feed_grads = feed_weight_call(normed_two, cotangent, hidden, grad_gate, grad_up)
     feed_other = across(feed_part)
     backs[2], _ = pin((backs[2], feed_grads))
@@ -1002,7 +962,7 @@
     for index in (2, 3, 0, 1):
         first = index * TILE
         earlier = residual_call(
-            info, middles[first // PART], backs[index], backs_other[index], cotangent, gain_two, weights_two,
+            info, middle, backs[index], backs_other[index], cotangent, gain_two, weights_two,
             first, earlier,
         )
     grad_middle, grad_low, grad_keep, *grad_sends = earlier
@@ -1024,7 +984,7 @@
     back_one_other = across(back_one)
     input_grad = input_call(grad_middle, back_one, back_one_other, tokens, gain_one)
     block_out = (
-        jnp.concatenate(middles) + (feed_part.astype(F32) + feed_other.astype(F32))
+        middle + (feed_part.astype(F32) + feed_other.astype(F32))
     ).astype(BF)
     total, below, above, block_out, input_grad = reduce_rows(
         attend_keep, attend_send, count, block_out, input_grad

time: 338 us -> 328 us (0.970)
  Pallas kernels: 134 us -> 128 us
  starting transfers between devices: 37.1 us -> 32.5 us
    ppermute x1, waiting for transfers between devices: 15.5 us -> 8.79 us  [body(): lax.ppermute(own_column, 'dp', [(i, i ^ 2) for i in range(count)])]
    ppermute x10, waiting for transfers between devices: 27.6 us -> 33.4 us  [across(): return lax.ppermute(value, 'mp', [(0, 1), (1, 0)])]
    pallas_call x6 -> x5, Pallas kernels: 35.5 us -> 33.1 us  [the longest x4 23.2 us: feed_call(): pl.pallas_call(feed_kernel, out_shape=(pltpu.VMEM((rows, width), BF),) *...]
    unnamed x134 -> x126, local copies, waits for them, and re-layouts: 9.08 us -> 9.22 us
  transfers between devices with their start and end apart: 33 -> 33, of which waited for: 15 -> 16; matrix products, arithmetic and copies ran while one was open for 7% -> 7% of each run, Pallas kernels for 35% -> 35%
where the time goes in v4:
time: 328 us; the launch traced here: 322 us
  Pallas kernels  128 us (39%)
  waiting for transfers between devices  82.1 us (25%)
  starting transfers between devices  32.5 us (10%)
  blocking collectives  26.8 us (8%)
  other arithmetic  25.6 us (8%)
  between operations  15.8 us (5%)
  local copies, waits for them, and re-layouts  10.8 us (3%)
    ppermute x10, waiting for transfers between devices, across(): return lax.ppermute(value, 'mp', [(0, 1), (1, 0)])  33.4 us
    all_gather x1, blocking collectives, body(): lax.all_gather(shard_one, 'dp', axis=0, tiled=True, axis_index_groups=lines)  26.8 us
    pallas_call x4, Pallas kernels, feed_call(): pl.pallas_call(feed_kernel, out_shape=(pltpu.VMEM((rows, width), BF),) *...  23.2 us
    ppermute x1, waiting for transfers between devices, reduce_rows(): lax.ppermute(theirs_one, 'dp', pairs)  18.1 us
    pallas_call x2, Pallas kernels, attend_backward(): pl.pallas_call(backward_kernel, out_shape=tuple((jax.ShapeDtypeStruct((pa...  17.6 us
    pallas_call x4, Pallas kernels, residual_call(): pl.pallas_call(residual_kernel, out_shape=(pltpu.HBM((rows, D), F32), jax...  15.8 us
    ppermute x3, starting transfers between devices, reduce_rows(): lax.ppermute(up, 'dp', [(i, i + 4) for i in range(count - 4) if i // 4 +...  14.8 us
    pallas_call x1, Pallas kernels, feed_weight_call(): pl.pallas_call(feed_weight_kernel, out_shape=pltpu.HBM((D, 3 * width), BF...  13.5 us
  transfers between devices with their start and end apart: 33, of which 16 were waited for; matrix products, arithmetic and copies ran while one was open for 7% of the time, Pallas kernels for 35%

profile of v4, /device:TPU:0, one launch (start us, length us, event | category | flops | bytes accessed | tf_op | source)
XLA Modules:
  0.0 321.6 jit_solution(6834579724048747018)
XLA Ops:
  8.4 3.0 collective-permute-start.8
  16.1 26.8 %all_gather.6 = bf16[256,1664]{1,0:T(8,128)(2,1)S(1)} all-gather(bf16[64,1664]{1,0:T(8,128)(2,1)S(1)} %shard.1), channel_id=1, replica_groups={{0,8,16,24},{2,10,18,26},{4,12,20,28},{6,14,22,30},{1,9,17,25},{3,11,19..., dimensions={0}, use_global_device_ids=true | all-gather | bytes 1064960 | tf_op jit(solution)/shard_map/all_gather | solution.py:918
  47.1 3.7 %fusion.3 = (f32[2048,64]{1,0:T(8,128)S(1)}, f32[2048,64]{1,0:T(8,128)S(1)}, f32[2048,64]{1,0:T(8,128)S(1)}) fusion(f32[64]{0:T(128)S(1)} %negate_power_fusion, f32[2048]{0:T(1024)S(1)} %iota_convert_fusion), kind=kLoop, calls=%fused_computation.27 | loop fusion | flops 262144 | bytes 1581312 | tf_op jit(solution)/shard_map/neg | solution.py:62
  50.8 8.8 %collective-permute-done = bf16[256,1664]{1,0:T(8,128)(2,1)} collective-permute-done((bf16[256,1664]{1,0:T(8,128)(2,1)S(1)}, bf16[256,1664]{1,0:T(8,128)(2,1)}, u32[]{:S(2)}, u32[]{:S(2)}) %collective-permute-start) | collective-permute-done | bytes 852000 | tf_op jit(solution)/shard_map/ppermute | solution.py:919
  60.0 2.0 pad_maximum_fusion
  63.7 1.7 interleave.1.gain_columns.weight.refs_6_
  65.5 7.6 %project_first.1 = (bf16[3,2,1024,128]{3,2,1,0:T(8,128)(2,1)S(1)}, bf16[1024,1024]{1,0:T(8,128)(2,1)S(1)}, f32[8,1024]{1,0:T(8,128)S(1)}) custom-call(s32[5]{0:T(128)S(1)} %stack.66.info, bf16[1024,1024]{1,0:T(8,128)(2,1)} %tokens.3, bf16[1024,1664]{1,0:T(8,128)(2,1)S(1)} %interleave.1.gain_columns.weight.refs_6_, ...), custom_call_target="tpu_custom_call" | custom-call | tf_op jit(solution)/shard_map/project_first/pallas_call | solution.py:111
  73.7 3.8 %project_second.1.own = bf16[3,2,1024,128]{3,2,1,0:T(8,128)(2,1)S(1)} custom-call(s32[5]{0:T(128)S(1)} %stack.66.info, bf16[1024,1024]{1,0:T(8,128)(2,1)S(1)} %get-tuple-element.129.normed, bf16[1024,1664]{1,0:T(8,128)(2,1)S(1)} %interleave.1.gain_columns.weight.refs_6_, f32[2048,128]{1,0:T(8,128)S(1)} %copy-done.9, f32[2048,128]{1,0:T(8,128)S(1)} %copy-done.11), custom_call_target="tpu_custom_call" | custom-call | tf_op jit(solution)/shard_map/project_second/pallas_call | solution.py:142
  77.5 12.0 %attend_forward.1 = (bf16[2,1024,128]{2,1,0:T(8,128)(2,1)S(1)}, bf16[2,1024,128]{2,1,0:T(8,128)(2,1)S(1)}, f32[2,128,2048]{2,1,0:T(8,128)}, f32[2,1,2048]{2,1,0:T(1,128)S(1)}) custom-call(s32[5]{0:T(128)S(1)} %stack.66.info, bf16[3,2,1024,128]{3,2,1,0:T(8,128)(2,1)S(1)} %project_second.1.own, bf16[3,2,1024,128]{3,2,1,0:T(8,128)(2,1)S(1)} %collective-permute-done.4.other, ...), custom_call_target="tpu_custom_call" | custom-call | tf_op jit(solution)/shard_map/attend_forward/pallas_call | solution.py:234
  90.7 1.9 collective-permute-done.5.refs_1_
  92.8 12.7 %collective-permute-done.6.refs_2_ = bf16[2,1024,128]{2,1,0:T(8,128)(2,1)S(1)} collective-permute-done((bf16[2,1024,128]{2,1,0:T(8,128)(2,1)S(1)}, bf16[2,1024,128]{2,1,0:T(8,128)(2,1)S(1)}, u32[]{:S(2)}, u32[]{:S(2)}) %collective-permute-start.6) | collective-permute-done | bytes 524320 | tf_op jit(solution)/shard_map/ppermute | solution.py:898
  105.5 10.9 %collective-permute-done.7.refs_3_ = bf16[2,1024,128]{2,1,0:T(8,128)(2,1)} collective-permute-done((bf16[2,1024,128]{2,1,0:T(8,128)(2,1)S(1)}, bf16[2,1024,128]{2,1,0:T(8,128)(2,1)}, u32[]{:S(2)}, u32[]{:S(2)}) %collective-permute-start.7) | collective-permute-done | bytes 524320 | tf_op jit(solution)/shard_map/ppermute | solution.py:898
  116.4 9.9 %middle.1 = (f32[1024,1024]{1,0:T(8,128)}, bf16[1024,1024]{1,0:T(8,128)(2,1)S(1)}, bf16[1024,512]{1,0:T(8,128)(2,1)S(1)}) custom-call(s32[5]{0:T(128)S(1)} %stack.66.info, bf16[2,1024,128]{2,1,0:T(8,128)(2,1)} %copy-done.39, bf16[2,1024,128]{2,1,0:T(8,128)(2,1)} %copy-done.53, bf16[2,1024,128]{2,1,0:T(8,128)(2,1)} %copy-done.54, ...), custom_call_target="tpu_custom_call" | custom-call | tf_op jit(solution)/shard_map/middle/pallas_call | solution.py:409
  127.3 5.5 %feed.4 = (bf16[1024,1408]{1,0:T(8,128)(2,1)S(1)}, bf16[1024,1408]{1,0:T(8,128)(2,1)S(1)}, bf16[1024,1408]{1,0:T(8,128)(2,1)S(1)}, bf16[1024,1024]{1,0:T(8,128)(2,1)}, bf16[256,1024]{1,0:T(8,128)(2,1)S(1)}) custom-call(bf16[1024,1024]{1,0:T(8,128)(2,1)S(1)} %get-tuple-element.138.normed, bf16[1024,1024]{1,0:T(8,128)(2,1)S(1)} %copy-done.3, ...), custom_call_target="tpu_custom_call" | custom-call | flops 50000000 | tf_op jit(solution)/shard_map/feed/pallas_call | solution.py:457
  133.3 5.5 %feed.5 = (bf16[1024,1408]{1,0:T(8,128)(2,1)S(1)}, bf16[1024,1408]{1,0:T(8,128)(2,1)S(1)}, bf16[1024,1408]{1,0:T(8,128)(2,1)S(1)}, bf16[1024,1024]{1,0:T(8,128)(2,1)}, bf16[256,1024]{1,0:T(8,128)(2,1)S(1)}) custom-call(bf16[1024,1024]{1,0:T(8,128)(2,1)S(1)} %get-tuple-element.138.normed, ...), custom_call_target="tpu_custom_call", output_to_operand_aliasing={{0}: (5, {}), {1}: (6, {}), {2}: (7, {}), {3}: (8, {})} | custom-call | flops 50000000 | tf_op jit(solution)/shard_map/feed/pallas_call | solution.py:457
  138.8 1.8 collective-permute-start.10
  140.6 5.7 %feed.6 = (bf16[1024,1408]{1,0:T(8,128)(2,1)S(1)}, bf16[1024,1408]{1,0:T(8,128)(2,1)S(1)}, bf16[1024,1408]{1,0:T(8,128)(2,1)S(1)}, bf16[1024,1024]{1,0:T(8,128)(2,1)}, bf16[256,1024]{1,0:T(8,128)(2,1)S(1)}) custom-call(bf16[1024,1024]{1,0:T(8,128)(2,1)S(1)} %get-tuple-element.138.normed, ...), custom_call_target="tpu_custom_call", output_to_operand_aliasing={{0}: (5, {}), {1}: (6, {}), {2}: (7, {}), {3}: (8, {})} | custom-call | flops 50000000 | tf_op jit(solution)/shard_map/feed/pallas_call | solution.py:457
  147.8 6.3 %feed.7 = (bf16[1024,1408]{1,0:T(8,128)(2,1)S(1)}, bf16[1024,1408]{1,0:T(8,128)(2,1)S(1)}, bf16[1024,1408]{1,0:T(8,128)(2,1)S(1)}, bf16[1024,1024]{1,0:T(8,128)(2,1)}, bf16[256,1024]{1,0:T(8,128)(2,1)}) custom-call(bf16[1024,1024]{1,0:T(8,128)(2,1)S(1)} %get-tuple-element.138.normed, ...), custom_call_target="tpu_custom_call", output_to_operand_aliasing={{0}: (5, {}), {1}: (6, {}), {2}: (7, {}), {3}: (8, {})} | custom-call | flops 50000000 | tf_op jit(solution)/shard_map/feed/pallas_call | solution.py:457
  154.8 4.2 %collective-permute-done.10.back_other = bf16[256,1024]{1,0:T(8,128)(2,1)S(1)} collective-permute-done((bf16[256,1024]{1,0:T(8,128)(2,1)S(1)}, bf16[256,1024]{1,0:T(8,128)(2,1)S(1)}, u32[]{:S(2)}, u32[]{:S(2)}) %collective-permute-start.10) | collective-permute-done | bytes 524320 | tf_op jit(solution)/shard_map/ppermute | solution.py:898
  159.8 13.5 %feed_weights.1 = bf16[1024,4224]{1,0:T(8,128)(2,1)} custom-call(bf16[1024,1024]{1,0:T(8,128)(2,1)S(1)} %get-tuple-element.138.normed, bf16[1024,1024]{1,0:T(8,128)(2,1)} %upstream.17, bf16[1024,1408]{1,0:T(8,128)(2,1)S(1)} %get-tuple-element.162.hidden, bf16[1024,1408]{1,0:T(8,128)(2,1)S(1)} %get-tuple-element.163.gate_grad, ...), custom_call_target="tpu_custom_call" | custom-call | flops 50000000 | tf_op jit(solution)/shard_map/feed_weights/pallas_call | solution.py:485
  173.7 2.2 copy-done.6
  175.9 3.7 %residual.4 = (f32[1024,1024]{1,0:T(8,128)}, bf16[1024,1024]{1,0:T(8,128)(2,1)S(1)}, bf16[2,1024,128]{2,1,0:T(8,128)(2,1)S(1)}, bf16[1,1024,128]{2,1,0:T(8,128)(2,1)S(1)}, bf16[1,1024,128]{2,1,0:T(8,128)(2,1)S(1)}) custom-call(s32[5]{0:T(128)S(1)} %stack.66.info, f32[1024,1024]{1,0:T(8,128)S(1)} %copy-done.6, ...), custom_call_target="tpu_custom_call" | custom-call | flops 50000000 | tf_op jit(solution)/shard_map/residual/pallas_call | solution.py:525
  179.6 1.9 collective-permute-done.11.back_other
  181.5 3.9 %residual.5 = (f32[1024,1024]{1,0:T(8,128)}, bf16[1024,1024]{1,0:T(8,128)(2,1)S(1)}, bf16[2,1024,128]{2,1,0:T(8,128)(2,1)S(1)}, bf16[1,1024,128]{2,1,0:T(8,128)(2,1)S(1)}, bf16[1,1024,128]{2,1,0:T(8,128)(2,1)S(1)}) custom-call(s32[5]{0:T(128)S(1)} %stack.66.info, ...), custom_call_target="tpu_custom_call", output_to_operand_aliasing={{0}: (7, {}), {1}: (8, {}), {2}: (9, {}), {3}: (10, {}), {4... | custom-call | flops 299999985664 | tf_op jit(solution)/shard_map/residual/pallas_call | solution.py:525
  185.5 3.8 %residual.6 = (f32[1024,1024]{1,0:T(8,128)}, bf16[1024,1024]{1,0:T(8,128)(2,1)S(1)}, bf16[2,1024,128]{2,1,0:T(8,128)(2,1)S(1)}, bf16[1,1024,128]{2,1,0:T(8,128)(2,1)S(1)}, bf16[1,1024,128]{2,1,0:T(8,128)(2,1)S(1)}) custom-call(s32[5]{0:T(128)S(1)} %stack.66.info, ...), custom_call_target="tpu_custom_call", output_to_operand_aliasing={{0}: (7, {}), {1}: (8, {}), {2}: (9, {}), {3}: (10, {}), {4... | custom-call | flops 50000000 | tf_op jit(solution)/shard_map/residual/pallas_call | solution.py:525
  189.4 4.3 %residual.7 = (f32[1024,1024]{1,0:T(8,128)}, bf16[1024,1024]{1,0:T(8,128)(2,1)S(1)}, bf16[2,1024,128]{2,1,0:T(8,128)(2,1)S(1)}, bf16[1,1024,128]{2,1,0:T(8,128)(2,1)S(1)}, bf16[1,1024,128]{2,1,0:T(8,128)(2,1)S(1)}) custom-call(s32[5]{0:T(128)S(1)} %stack.66.info, ...), custom_call_target="tpu_custom_call", output_to_operand_aliasing={{0}: (7, {}), {1}: (8, {}), {2}: (9, {}), {3}: (10, {}), {4... | custom-call | flops 50000000 | tf_op jit(solution)/shard_map/residual/pallas_call | solution.py:525
  195.3 8.6 %attend_backward.3 = (bf16[3,1,1024,128]{3,2,1,0:T(8,128)(2,1)S(1)}, bf16[2,1,1024,128]{3,2,1,0:T(8,128)(2,1)S(1)}, bf16[1,1,1024,128]{3,2,1,0:T(8,128)(2,1)S(1)}) custom-call(s32[5]{0:T(128)S(1)} %stack.66.info, bf16[3,2,1024,128]{3,2,1,0:T(8,128)(2,1)S(1)} %copy-done.14, bf16[3,2,1024,128]{3,2,1,0:T(8,128)(2,1)S(1)} %copy-done.17, ...), custom_call_target="tpu_custom_call" | custom-call | tf_op jit(solution)/shard_map/attend_backward/pallas_call | solution.py:335
  204.1 9.0 %attend_backward.2 = (bf16[3,1,1024,128]{3,2,1,0:T(8,128)(2,1)S(1)}, bf16[2,1,1024,128]{3,2,1,0:T(8,128)(2,1)S(1)}, bf16[1,1,1024,128]{3,2,1,0:T(8,128)(2,1)S(1)}) custom-call(s32[5]{0:T(128)S(1)} %stack.66.info, bf16[3,2,1024,128]{3,2,1,0:T(8,128)(2,1)S(1)} %copy-done.14, bf16[3,2,1024,128]{3,2,1,0:T(8,128)(2,1)S(1)} %copy-done.17, ...), custom_call_target="tpu_custom_call" | custom-call | tf_op jit(solution)/shard_map/attend_backward/pallas_call | solution.py:335
  214.1 1.4 collective-permute-done.18.refs_5_
  215.9 6.3 %back.1.back_own = bf16[1024,1024]{1,0:T(8,128)(2,1)} custom-call(s32[5]{0:T(128)S(1)} %stack.66.info, bf16[3,1,1024,128]{3,2,1,0:T(8,128)(2,1)S(1)} %get-tuple-element.193.refs_0_, bf16[3,1,1024,128]{3,2,1,0:T(8,128)(2,1)S(1)} %get-tuple-element.188.refs_1_, bf16[2,1,1024,128]{3,2,1,0:T(8,128)(2,1)S(1)} %collective-permute-done.15.refs_2_, ...), custom_call_target="tpu_custom_call" | custom-call | tf_op jit(solution)/shard_map/back/pallas_call | solution.py:580
  222.2 7.3 %attend_weights.1 = (bf16[2,4,64,2048]{3,2,1,0:T(8,128)(2,1)S(1)}, bf16[2,4,64,2048]{3,2,1,0:T(8,128)(2,1)S(1)}) custom-call(s32[5]{0:T(128)S(1)} %stack.66.info, bf16[1024,1024]{1,0:T(8,128)(2,1)S(1)} %copy-done.22, bf16[1024,1024]{1,0:T(8,128)(2,1)S(1)} %get-tuple-element.181.low, bf16[3,1,1024,128]{3,2,1,0:T(8,128)(2,1)S(1)} %get-tuple-element.193.refs_0_, ...), custom_call_target="tpu_custom_call" | custom-call | tf_op jit(solution)/shard_map/attend_weights/pallas_call | solution.py:630
  230.5 3.3 %collective-permute-done.19.core = bf16[2,4,64,2048]{3,2,1,0:T(8,128)(2,1)S(1)} collective-permute-done((bf16[2,4,64,2048]{3,2,1,0:T(8,128)(2,1)S(1)}, bf16[2,4,64,2048]{3,2,1,0:T(8,128)(2,1)S(1)}, u32[]{:S(2)}, u32[]{:S(2)}) %collective-permute-start.19) | collective-permute-done | bytes 2097184 | tf_op jit(solution)/shard_map/ppermute | solution.py:754
  234.3 1.3 collective-permute-start.20
  236.4 5.0 %add_convert_fusion = bf16[1024,1024]{1,0:T(8,128)(2,1)} fusion(f32[1024,1024]{1,0:T(8,128)S(1)} %copy-done.7, bf16[1024,1024]{1,0:T(8,128)(2,1)} %collective-permute-done.21, bf16[1024,1024]{1,0:T(8,128)(2,1)} %get-tuple-element.198), kind=kLoop, calls=%fused_computation.1 | loop fusion | flops 5242880 | bytes 10485760 | tf_op jit(solution)/shard_map/convert_element_type | solution.py:988
  241.3 18.1 %collective-permute-done.20.right = bf16[2,64,2048]{2,1,0:T(8,128)(2,1)S(1)} collective-permute-done((bf16[2,64,2048]{2,1,0:T(8,128)(2,1)S(1)}, bf16[2,64,2048]{2,1,0:T(8,128)(2,1)S(1)}, u32[]{:S(2)}, u32[]{:S(2)}) %collective-permute-start.20) | collective-permute-done | bytes 524320 | tf_op jit(solution)/shard_map/ppermute | solution.py:757
  259.5 3.7 %collective-permute-start.22 = (bf16[64,2048]{1,0:T(8,128)(2,1)S(1)}, bf16[64,2048]{1,0:T(8,128)(2,1)S(1)}, u32[]{:S(2)}, u32[]{:S(2)}) collective-permute-start(bf16[64,2048]{1,0:T(8,128)(2,1)S(1)} %get-tuple-element.203.first), channel_id=1, source_target_pairs={{0,8},{2,10},{4,12},{6,14},{1,9},{3,11},{5,13},{7,15}} | collective-permute-start | bytes 786440 | tf_op jit(solution)/shard_map/ppermute | solution.py:787
  263.9 7.4 %collective-permute-done.24.right = bf16[2,64,2048]{2,1,0:T(8,128)(2,1)S(1)} collective-permute-done((bf16[2,64,2048]{2,1,0:T(8,128)(2,1)S(1)}, bf16[2,64,2048]{2,1,0:T(8,128)(2,1)S(1)}, u32[]{:S(2)}, u32[]{:S(2)}) %collective-permute-start.24) | collective-permute-done | bytes 524320 | tf_op jit(solution)/shard_map/ppermute | solution.py:759
  272.1 1.5 collective-permute-start.26
  274.4 3.8 %collective-permute-start.25 = (bf16[64,2048]{1,0:T(8,128)(2,1)}, bf16[64,2048]{1,0:T(8,128)(2,1)}, u32[]{:S(2)}, u32[]{:S(2)}) collective-permute-start(bf16[64,2048]{1,0:T(8,128)(2,1)} %low_add.2), channel_id=1, source_target_pairs={{0,8},{2,10},{4,12},{6,14},{8,16},{10,18},{12,20},{14,22},{1,9},{3... | collective-permute-start | bytes 786440 | tf_op jit(solution)/shard_map/ppermute | solution.py:787
  278.3 2.2 copy-done.8
  280.5 5.1 %input_grad.1 = bf16[1024,1024]{1,0:T(8,128)(2,1)} custom-call(f32[1024,1024]{1,0:T(8,128)S(1)} %copy-done.8, bf16[1024,1024]{1,0:T(8,128)(2,1)} %back.1.back_own, bf16[1024,1024]{1,0:T(8,128)(2,1)} %collective-permute-done.27.back_other, bf16[1024,1024]{1,0:T(8,128)(2,1)S(1)} %copy-done.15, f32[1,1024]{1,0:T(1,128)S(1)} %get-tuple-element.248.gain), custom_call_target="tpu_custom_call" | custom-call | flops 12582912 | bytes 12582912 | tf_op jit(solution)/shard_map/input_grad/pallas_call | solution.py:660
  285.7 4.0 %collective-permute-done.25.up_in = bf16[64,2048]{1,0:T(8,128)(2,1)} collective-permute-done((bf16[64,2048]{1,0:T(8,128)(2,1)}, bf16[64,2048]{1,0:T(8,128)(2,1)}, u32[]{:S(2)}, u32[]{:S(2)}) %collective-permute-start.25) | collective-permute-done | bytes 262176 | tf_op jit(solution)/shard_map/ppermute | solution.py:787
  291.0 7.3 %collective-permute-start.28 = (bf16[64,2048]{1,0:T(8,128)(2,1)S(1)}, bf16[64,2048]{1,0:T(8,128)(2,1)}, u32[]{:S(2)}, u32[]{:S(2)}) collective-permute-start(bf16[64,2048]{1,0:T(8,128)(2,1)S(1)} %get-tuple-element.217), channel_id=1, source_target_pairs={{0,8},{2,10},{4,12},{6,14},{8,16},{10,18},{12,20},{14,22},{16,24},... | collective-permute-start | bytes 786440 | tf_op jit(solution)/shard_map/ppermute | solution.py:787
  300.9 2.4 multiply_subtract_fusion.2
  303.3 1.8 multiply_subtract_fusion
  305.1 2.4 collective-permute-done.29
  308.9 1.3 multiply_subtract_fusion.1
  311.3 2.6 collective-permute-done.30.other
  (206 shorter events, 32.5 us)
Async XLA Ops:
  7.2 37.0 %copy-start = (bf16[1024,2,512]{2,1,0:T(2,128)(2,1)S(1)}, bf16[1024,2,512]{2,1,0:T(2,128)(2,1)}, u32[]{:S(2)}) copy-start(bf16[1024,2,512]{2,1,0:T(2,128)(2,1)} %param.38) | copy-start | bytes 6291460
  7.3 109.1 %all-gather.2.cloned.1.call-start = ((), (), s32[]{:S(2)}) async-start(), calls=%async_computation.1 | async-start | bytes 11419648 | tf_op jit(solution)/shard_map/all_gather | solution.py:921
  8.4 6.3 %collective-permute-start.8 = (bf16[64,512]{1,0:T(8,128)(2,1)S(1)}, bf16[64,512]{1,0:T(8,128)(2,1)S(1)}, u32[]{:S(2)}, u32[]{:S(2)}) collective-permute-start(bf16[64,512]{1,0:T(8,128)(2,1)S(1)} %convert_bitcast_fusion), channel_id=1, source_target_pairs={{0,1},{1,0},{2,3},{3,2},{4,5},{5,4},{6,7},{7,6},{8,9},{9,8},{10,11... | collective-permute-start | bytes 196616 | tf_op jit(solution)/shard_map/ppermute | solution.py:898
  12.6 31.6 %copy-start.60 = (s32[1,128]{1,0:T(1,128)S(1)}, s32[1,128]{1,0:T(1,128)}, u32[]{:S(2)}) copy-start(s32[1,128]{1,0:T(1,128)} %param.41) | copy-start | bytes 1540
  16.0 283.7 %reduce-scatter.2.cloned.1.call-start = ((), (), s32[]{:S(2)}) async-start(), calls=%async_computation.2 | async-start | bytes 9191424 | tf_op jit(solution)/shard_map/reduce_scatter | solution.py:992
  42.9 16.7 %collective-permute-start = (bf16[256,1664]{1,0:T(8,128)(2,1)S(1)}, bf16[256,1664]{1,0:T(8,128)(2,1)}, u32[]{:S(2)}, u32[]{:S(2)}) collective-permute-start(bf16[256,1664]{1,0:T(8,128)(2,1)S(1)} %all_gather.6), channel_id=1, source_target_pairs={{0,4},{2,6},{4,0},{6,2},{8,12},{10,14},{12,8},{14,10},{16,20},{18,... | collective-permute-start | bytes 2555912 | tf_op jit(solution)/shard_map/ppermute | solution.py:919
  44.2 19.5 %collective-permute-start.1 = (bf16[256,1664]{1,0:T(8,128)(2,1)S(1)}, bf16[256,1664]{1,0:T(8,128)(2,1)}, u32[]{:S(2)}, u32[]{:S(2)}) collective-permute-start(bf16[256,1664]{1,0:T(8,128)(2,1)S(1)} %all_gather.6), channel_id=1, source_target_pairs={{0,2},{2,0},{4,6},{6,4},{8,10},{10,8},{12,14},{14,12},{16,18},{18,... | collective-permute-start | bytes 2555912 | tf_op jit(solution)/shard_map/ppermute | solution.py:901
  45.8 17.9 %collective-permute-start.3 = (bf16[2,2,128,128]{3,2,1,0:T(8,128)(2,1)S(1)}, bf16[2,2,128,128]{3,2,1,0:T(8,128)(2,1)S(1)}, u32[]{:S(2)}, u32[]{:S(2)}) collective-permute-start(bf16[2,2,128,128]{3,2,1,0:T(8,128)(2,1)S(1)} %bitcast.77), channel_id=1, source_target_pairs={{0,2},{2,0},{4,6},{6,4},{8,10},{10,8},{12,14},{14,12},{16,18},{18,... | collective-permute-start | bytes 393224 | tf_op jit(solution)/shard_map/ppermute | solution.py:901
  59.6 4.1 %collective-permute-start.2 = (bf16[256,1664]{1,0:T(8,128)(2,1)}, bf16[256,1664]{1,0:T(8,128)(2,1)S(1)}, u32[]{:S(2)}, u32[]{:S(2)}) collective-permute-start(bf16[256,1664]{1,0:T(8,128)(2,1)} %collective-permute-done), channel_id=1, source_target_pairs={{0,2},{2,0},{4,6},{6,4},{8,10},{10,8},{12,14},{14,12},{16,18},{18,... | collective-permute-start | bytes 2555912 | tf_op jit(solution)/shard_map/ppermute | solution.py:901
  59.9 17.6 %copy-start.19 = (bf16[2048,128]{1,0:T(8,128)(2,1)}, bf16[2048,128]{1,0:T(8,128)(2,1)S(1)}, u32[]{:S(2)}) copy-start(bf16[2048,128]{1,0:T(8,128)(2,1)S(1)} %select_convert_fusion.bias) | copy-start | bytes 1572868
  63.6 13.9 %copy-start.23 = (bf16[128,2,1,2,128]{4,0,3,1,2:T(8,128)(2,1)}, bf16[128,2,1,2,128]{4,0,3,1,2:T(8,128)(2,1)S(1)}, u32[]{:S(2)}) copy-start(bf16[128,2,1,2,128]{4,0,3,1,2:T(8,128)(2,1)S(1)} %copy.70) | copy-start | bytes 393220
  63.7 13.8 %copy-start.27 = (bf16[2,2,128,128]{3,2,1,0:T(8,128)(2,1)}, bf16[2,2,128,128]{3,2,1,0:T(8,128)(2,1)S(1)}, u32[]{:S(2)}) copy-start(bf16[2,2,128,128]{3,2,1,0:T(8,128)(2,1)S(1)} %collective-permute-done.3.mem_other) | copy-start | bytes 393220
  73.1 4.4 %collective-permute-start.4 = (bf16[3,2,1024,128]{3,2,1,0:T(8,128)(2,1)S(1)}, bf16[3,2,1024,128]{3,2,1,0:T(8,128)(2,1)S(1)}, u32[]{:S(2)}, u32[]{:S(2)}) collective-permute-start(bf16[3,2,1024,128]{3,2,1,0:T(8,128)(2,1)S(1)} %get-tuple-element.130), channel_id=1, source_target_pairs={{0,2},{2,0},{4,6},{6,4},{8,10},{10,8},{12,14},{14,12},{16,18},{18,... | collective-permute-start | bytes 4718600 | tf_op jit(solution)/shard_map/ppermute | solution.py:901
  77.5 12.0 %copy-start.16 = (bf16[3,2,1024,128]{3,2,1,0:T(8,128)(2,1)}, bf16[3,2,1024,128]{3,2,1,0:T(8,128)(2,1)S(1)}, u32[]{:S(2)}) copy-start(bf16[3,2,1024,128]{3,2,1,0:T(8,128)(2,1)S(1)} %collective-permute-done.4.other) | copy-start | bytes 4718596
  90.7 25.7 %copy-start.39 = (bf16[2,1024,128]{2,1,0:T(8,128)(2,1)}, bf16[2,1024,128]{2,1,0:T(8,128)(2,1)S(1)}, u32[]{:S(2)}) copy-start(bf16[2,1024,128]{2,1,0:T(8,128)(2,1)S(1)} %get-tuple-element.134.refs_0_) | copy-start | bytes 1572868
  90.7 1.9 collective-permute-start.5
  90.7 14.7 %collective-permute-start.6 = (bf16[2,1024,128]{2,1,0:T(8,128)(2,1)S(1)}, bf16[2,1024,128]{2,1,0:T(8,128)(2,1)S(1)}, u32[]{:S(2)}, u32[]{:S(2)}) collective-permute-start(bf16[2,1024,128]{2,1,0:T(8,128)(2,1)S(1)} %get-tuple-element.134.refs_0_), channel_id=1, source_target_pairs={{0,1},{1,0},{2,3},{3,2},{4,5},{5,4},{6,7},{7,6},{8,9},{9,8},{10,11... | collective-permute-start | bytes 1572872 | tf_op jit(solution)/shard_map/ppermute | solution.py:898
  92.6 23.8 %copy-start.53 = (bf16[2,1024,128]{2,1,0:T(8,128)(2,1)}, bf16[2,1024,128]{2,1,0:T(8,128)(2,1)S(1)}, u32[]{:S(2)}) copy-start(bf16[2,1024,128]{2,1,0:T(8,128)(2,1)S(1)} %collective-permute-done.5.refs_1_) | copy-start | bytes 1572868
  92.6 23.8 %collective-permute-start.7 = (bf16[2,1024,128]{2,1,0:T(8,128)(2,1)S(1)}, bf16[2,1024,128]{2,1,0:T(8,128)(2,1)}, u32[]{:S(2)}, u32[]{:S(2)}) collective-permute-start(bf16[2,1024,128]{2,1,0:T(8,128)(2,1)S(1)} %collective-permute-done.5.refs_1_), channel_id=1, source_target_pairs={{0,1},{1,0},{2,3},{3,2},{4,5},{5,4},{6,7},{7,6},{8,9},{9,8},{10,11... | collective-permute-start | bytes 1572872 | tf_op jit(solution)/shard_map/ppermute | solution.py:898
  105.5 10.9 %copy-start.54 = (bf16[2,1024,128]{2,1,0:T(8,128)(2,1)}, bf16[2,1024,128]{2,1,0:T(8,128)(2,1)S(1)}, u32[]{:S(2)}) copy-start(bf16[2,1024,128]{2,1,0:T(8,128)(2,1)S(1)} %collective-permute-done.6.refs_2_) | copy-start | bytes 1572868
  116.4 10.9 %copy-start.2 = (bf16[1024,5248]{1,0:T(8,128)(2,1)S(1)}, bf16[1024,5248]{1,0:T(8,128)(2,1)}, u32[]{:S(2)}) copy-start(bf16[1024,5248]{1,0:T(8,128)(2,1)} %all-gather.2.cloned.1.call-done.refs_5_.gate_w.up_w.down_w.weight) | copy-start | bytes 32243716
  116.4 10.9 %copy-start.3 = (bf16[1024,1024]{1,0:T(8,128)(2,1)S(1)}, bf16[1024,1024]{1,0:T(8,128)(2,1)}, u32[]{:S(2)}) copy-start(bf16[1024,1024]{1,0:T(8,128)(2,1)} %upstream.17) | copy-start | bytes 6291460
  132.9 14.9 %collective-permute-start.9 = (bf16[256,1024]{1,0:T(8,128)(2,1)S(1)}, bf16[256,1024]{1,0:T(8,128)(2,1)S(1)}, u32[]{:S(2)}, u32[]{:S(2)}) collective-permute-start(bf16[256,1024]{1,0:T(8,128)(2,1)S(1)} %get-tuple-element.152.back_own), channel_id=1, source_target_pairs={{0,1},{1,0},{2,3},{3,2},{4,5},{5,4},{6,7},{7,6},{8,9},{9,8},{10,11... | collective-permute-start | bytes 1572872 | tf_op jit(solution)/shard_map/ppermute | solution.py:898
  138.8 20.2 %collective-permute-start.10 = (bf16[256,1024]{1,0:T(8,128)(2,1)S(1)}, bf16[256,1024]{1,0:T(8,128)(2,1)S(1)}, u32[]{:S(2)}, u32[]{:S(2)}) collective-permute-start(bf16[256,1024]{1,0:T(8,128)(2,1)S(1)} %get-tuple-element.143.back_own), channel_id=1, source_target_pairs={{0,1},{1,0},{2,3},{3,2},{4,5},{5,4},{6,7},{7,6},{8,9},{9,8},{10,11... | collective-permute-start | bytes 1572872 | tf_op jit(solution)/shard_map/ppermute | solution.py:898
  146.4 27.3 %collective-permute-start.12 = (bf16[256,1024]{1,0:T(8,128)(2,1)S(1)}, bf16[256,1024]{1,0:T(8,128)(2,1)}, u32[]{:S(2)}, u32[]{:S(2)}) collective-permute-start(bf16[256,1024]{1,0:T(8,128)(2,1)S(1)} %get-tuple-element.165.back_own), channel_id=1, source_target_pairs={{0,1},{1,0},{2,3},{3,2},{4,5},{5,4},{6,7},{7,6},{8,9},{9,8},{10,11... | collective-permute-start | bytes 1572872 | tf_op jit(solution)/shard_map/ppermute | solution.py:898
  154.1 27.4 %collective-permute-start.11 = (bf16[256,1024]{1,0:T(8,128)(2,1)}, bf16[256,1024]{1,0:T(8,128)(2,1)S(1)}, u32[]{:S(2)}, u32[]{:S(2)}) collective-permute-start(bf16[256,1024]{1,0:T(8,128)(2,1)} %get-tuple-element.160.back_own), channel_id=1, source_target_pairs={{0,1},{1,0},{2,3},{3,2},{4,5},{5,4},{6,7},{7,6},{8,9},{9,8},{10,11... | collective-permute-start | bytes 1572872 | tf_op jit(solution)/shard_map/ppermute | solution.py:898
  173.4 56.6 %collective-permute-start.21 = (bf16[1024,1024]{1,0:T(8,128)(2,1)}, bf16[1024,1024]{1,0:T(8,128)(2,1)}, u32[]{:S(2)}, u32[]{:S(2)}) collective-permute-start(bf16[1024,1024]{1,0:T(8,128)(2,1)} %get-tuple-element.198), channel_id=1, source_target_pairs={{0,1},{1,0},{2,3},{3,2},{4,5},{5,4},{6,7},{7,6},{8,9},{9,8},{10,11... | collective-permute-start | bytes 6291464 | tf_op jit(solution)/shard_map/ppermute | solution.py:898
  193.7 1.5 collective-permute-start.14
  193.7 10.4 %collective-permute-start.13 = (bf16[1,1024,128]{2,1,0:T(8,128)(2,1)S(1)}, bf16[1,1024,128]{2,1,0:T(8,128)(2,1)S(1)}, u32[]{:S(2)}, u32[]{:S(2)}) collective-permute-start(bf16[1,1024,128]{2,1,0:T(8,128)(2,1)S(1)} %get-tuple-element.183), channel_id=1, source_target_pairs={{0,2},{2,0},{4,6},{6,4},{8,10},{10,8},{12,14},{14,12},{16,18},{18,... | collective-permute-start | bytes 786440 | tf_op jit(solution)/shard_map/ppermute | solution.py:901
  203.9 12.0 %collective-permute-start.17 = (bf16[2,1,1024,128]{3,2,1,0:T(8,128)(2,1)S(1)}, bf16[2,1,1024,128]{3,2,1,0:T(8,128)(2,1)S(1)}, u32[]{:S(2)}, u32[]{:S(2)}) collective-permute-start(bf16[2,1,1024,128]{3,2,1,0:T(8,128)(2,1)S(1)} %get-tuple-element.191), channel_id=1, source_target_pairs={{0,2},{2,0},{4,6},{6,4},{8,10},{10,8},{12,14},{14,12},{16,18},{18,... | collective-permute-start | bytes 1572872 | tf_op jit(solution)/shard_map/ppermute | solution.py:901
  204.1 11.8 %copy-start.5 = (bf16[1024,1664]{1,0:T(8,128)(2,1)S(1)}, bf16[1024,1664]{1,0:T(8,128)(2,1)}, u32[]{:S(2)}) copy-start(bf16[1024,1664]{1,0:T(8,128)(2,1)} %copy-done.4) | copy-start | bytes 10223620
  213.1 2.7 collective-permute-start.15
  213.6 1.9 collective-permute-start.18
  213.7 2.2 collective-permute-start.16
  229.5 4.2 %collective-permute-start.19 = (bf16[2,4,64,2048]{3,2,1,0:T(8,128)(2,1)S(1)}, bf16[2,4,64,2048]{3,2,1,0:T(8,128)(2,1)S(1)}, u32[]{:S(2)}, u32[]{:S(2)}) collective-permute-start(bf16[2,4,64,2048]{3,2,1,0:T(8,128)(2,1)S(1)} %get-tuple-element.196), channel_id=1, source_target_pairs={{0,2},{2,0},{4,6},{6,4},{8,10},{10,8},{12,14},{14,12},{16,18},{18,... | collective-permute-start | bytes 6291464 | tf_op jit(solution)/shard_map/ppermute | solution.py:754
  230.0 48.3 %collective-permute-start.27 = (bf16[1024,1024]{1,0:T(8,128)(2,1)}, bf16[1024,1024]{1,0:T(8,128)(2,1)}, u32[]{:S(2)}, u32[]{:S(2)}) collective-permute-start(bf16[1024,1024]{1,0:T(8,128)(2,1)} %back.1.back_own), channel_id=1, source_target_pairs={{0,1},{1,0},{2,3},{3,2},{4,5},{5,4},{6,7},{7,6},{8,9},{9,8},{10,11... | collective-permute-start | bytes 6291464 | tf_op jit(solution)/shard_map/ppermute | solution.py:898
  234.3 25.1 %collective-permute-start.20 = (bf16[2,64,2048]{2,1,0:T(8,128)(2,1)S(1)}, bf16[2,64,2048]{2,1,0:T(8,128)(2,1)S(1)}, u32[]{:S(2)}, u32[]{:S(2)}) collective-permute-start(bf16[2,64,2048]{2,1,0:T(8,128)(2,1)S(1)} %get-tuple-element.197), channel_id=1, source_target_pairs={{0,4},{2,6},{4,0},{6,2},{8,12},{10,14},{12,8},{14,10},{16,20},{18,... | collective-permute-start | bytes 1572872 | tf_op jit(solution)/shard_map/ppermute | solution.py:757
  235.6 35.8 %collective-permute-start.24 = (bf16[2,64,2048]{2,1,0:T(8,128)(2,1)S(1)}, bf16[2,64,2048]{2,1,0:T(8,128)(2,1)S(1)}, u32[]{:S(2)}, u32[]{:S(2)}) collective-permute-start(bf16[2,64,2048]{2,1,0:T(8,128)(2,1)S(1)} %get-tuple-element.205), channel_id=1, source_target_pairs={{0,4},{2,6},{4,0},{6,2},{8,12},{10,14},{12,8},{14,10},{16,20},{18,... | collective-permute-start | bytes 1572872 | tf_op jit(solution)/shard_map/ppermute | solution.py:759
  241.3 36.9 %copy-start.15 = (bf16[1024,1024]{1,0:T(8,128)(2,1)S(1)}, bf16[1024,1024]{1,0:T(8,128)(2,1)}, u32[]{:S(2)}) copy-start(bf16[1024,1024]{1,0:T(8,128)(2,1)} %tokens.3) | copy-start | bytes 6291460
  259.5 14.9 %copy-start.40 = (bf16[64,2048]{1,0:T(8,128)(2,1)}, bf16[64,2048]{1,0:T(8,128)(2,1)S(1)}, u32[]{:S(2)}) copy-start(bf16[64,2048]{1,0:T(8,128)(2,1)S(1)} %get-tuple-element.203.first) | copy-start | bytes 786436
  259.5 11.8 %collective-permute-start.22 = (bf16[64,2048]{1,0:T(8,128)(2,1)S(1)}, bf16[64,2048]{1,0:T(8,128)(2,1)S(1)}, u32[]{:S(2)}, u32[]{:S(2)}) collective-permute-start(bf16[64,2048]{1,0:T(8,128)(2,1)S(1)} %get-tuple-element.203.first), channel_id=1, source_target_pairs={{0,8},{2,10},{4,12},{6,14},{1,9},{3,11},{5,13},{7,15}} | collective-permute-start | bytes 786440 | tf_op jit(solution)/shard_map/ppermute | solution.py:787
  263.2 8.1 %collective-permute-start.23 = (bf16[64,2048]{1,0:T(8,128)(2,1)S(1)}, bf16[64,2048]{1,0:T(8,128)(2,1)S(1)}, u32[]{:S(2)}, u32[]{:S(2)}) collective-permute-start(bf16[64,2048]{1,0:T(8,128)(2,1)S(1)} %get-tuple-element.203.first), channel_id=1, source_target_pairs={{24,16},{26,18},{28,20},{30,22},{25,17},{27,19},{29,21},{31,23}} | collective-permute-start | bytes 786440 | tf_op jit(solution)/shard_map/ppermute | solution.py:788
  272.1 13.6 %collective-permute-start.26 = (bf16[64,2048]{1,0:T(8,128)(2,1)}, bf16[64,2048]{1,0:T(8,128)(2,1)}, u32[]{:S(2)}, u32[]{:S(2)}) collective-permute-start(bf16[64,2048]{1,0:T(8,128)(2,1)} %low_add.3), channel_id=1, source_target_pairs={{16,8},{18,10},{20,12},{22,14},{24,16},{26,18},{28,20},{30,22},{17... | collective-permute-start | bytes 786440 | tf_op jit(solution)/shard_map/ppermute | solution.py:788
  274.4 15.4 %collective-permute-start.25 = (bf16[64,2048]{1,0:T(8,128)(2,1)}, bf16[64,2048]{1,0:T(8,128)(2,1)}, u32[]{:S(2)}, u32[]{:S(2)}) collective-permute-start(bf16[64,2048]{1,0:T(8,128)(2,1)} %low_add.2), channel_id=1, source_target_pairs={{0,8},{2,10},{4,12},{6,14},{8,16},{10,18},{12,20},{14,22},{1,9},{3... | collective-permute-start | bytes 786440 | tf_op jit(solution)/shard_map/ppermute | solution.py:787
  285.7 15.2 %copy-start.50 = (f32[1408,64]{0,1:T(8,128)S(1)}, f32[1408,64]{0,1:T(8,128)}, u32[]{:S(2)}) copy-start(f32[1408,64]{0,1:T(8,128)} %param.26) | copy-start | bytes 1081348
  291.0 14.1 %collective-permute-start.28 = (bf16[64,2048]{1,0:T(8,128)(2,1)S(1)}, bf16[64,2048]{1,0:T(8,128)(2,1)}, u32[]{:S(2)}, u32[]{:S(2)}) collective-permute-start(bf16[64,2048]{1,0:T(8,128)(2,1)S(1)} %get-tuple-element.217), channel_id=1, source_target_pairs={{0,8},{2,10},{4,12},{6,14},{8,16},{10,18},{12,20},{14,22},{16,24},... | collective-permute-start | bytes 786440 | tf_op jit(solution)/shard_map/ppermute | solution.py:787
  298.3 9.2 %collective-permute-start.29 = (bf16[64,2048]{1,0:T(8,128)(2,1)S(1)}, bf16[64,2048]{1,0:T(8,128)(2,1)}, u32[]{:S(2)}, u32[]{:S(2)}) collective-permute-start(bf16[64,2048]{1,0:T(8,128)(2,1)S(1)} %get-tuple-element.218), channel_id=1, source_target_pairs={{8,0},{10,2},{12,4},{14,6},{16,8},{18,10},{20,12},{22,14},{24,16},... | collective-permute-start | bytes 786440 | tf_op jit(solution)/shard_map/ppermute | solution.py:788
  310.3 3.6 %collective-permute-start.30 = (f32[2,64]{1,0:T(2,128)S(1)}, f32[2,64]{1,0:T(2,128)S(1)}, u32[]{:S(2)}, u32[]{:S(2)}) collective-permute-start(f32[2,64]{1,0:T(2,128)S(1)} %pad_maximum_fusion.4.own), channel_id=1, source_target_pairs={{0,1},{1,0},{2,3},{3,2},{4,5},{5,4},{6,7},{7,6},{8,9},{9,8},{10,11... | collective-permute-start | bytes 1544 | tf_op jit(solution)/shard_map/ppermute | solution.py:898
  (46 other events, 223.8 us)
Sparse Core Ops, SparseCore 0:
  16.1 95.6 all-gather.1
  173.5 124.9 reduce-scatter.1

commit v5 on v4

--- a/solution.py
+++ b/solution.py
@@ -134,7 +134,7 @@
         compiler_params=params(VMEM),
         cost_estimate=cost(0, 0),
         name="project_first",
-    )(info, in_hbm(tokens), weights, weights, in_hbm(cosines), in_hbm(sines))
+    )(info, tokens, weights, weights, cosines, sines)
 
 
 def project_second(info, normed, weights, cosines, sines):
@@ -411,7 +411,7 @@
         out_shape=(
             pltpu.HBM((rows, D), F32),
             jax.ShapeDtypeStruct((rows, D), BF),
-            jax.ShapeDtypeStruct((rows, half), BF),
+            pltpu.HBM((rows, half), BF),
         ),
         grid_spec=pltpu.PrefetchScalarGridSpec(
             num_scalar_prefetch=1,
@@ -469,44 +469,76 @@
     )(normed, upstream, weights, weights, weights, *earlier)
 
 
-def feed_weight_kernel(normed, upstream, hidden, gate_grad, up_grad, out):
-    width = hidden.shape[1]
+DOWN_SPLIT = 768
+
+
+DOWN_SPLIT = 768
+
+
+def scatter(info, out, keep, send):
+    step, tile = pl.program_id(0), out.shape[0]
+    count, size = keep.shape[1], keep.shape[2]
+    for line in range(tile // (4 * size)):
+        slot = count - 1 - ((step * (tile // (4 * size)) + line) ^ info[4])
+        for column in range(2):
+            for target, core in ((keep, info[0]), (send, 1 - info[0])):
+                side = info[3] if column == 0 else 1 - info[3]
+                start = pl.multiple_of((line * 4 + side * 2 + core) * size, size)
+                target[column, slot] = out[pl.ds(start, size), :]
+
+
+def feed_weight_kernel(info, normed, upstream, hidden, gate_grad, up_grad, out, keep, send, last):
+    width = gate_grad.shape[1]
     left = normed[...].astype(F32).T.astype(BF)
     out[:, :width] = dot(left, gate_grad[...]).astype(BF)
     out[:, width : 2 * width] = dot(left, up_grad[...]).astype(BF)
     left = upstream[...].astype(F32).T.astype(BF)
-    out[:, 2 * width :] = dot(left, hidden[...]).astype(BF)
-
-
-def feed_weight_call(normed, upstream, hidden, gate_grad, up_grad):
-    rows, width = hidden.shape
-    left = pl.BlockSpec((rows, TILE), lambda i: (0, i))
-    whole = pl.BlockSpec((rows, width), lambda i: (0, 0), pipeline_mode=pl.Buffered(1))
+    result = dot(left, hidden[...]).astype(BF)
+    out[:, 2 * width :] = result[:, :DOWN_SPLIT]
+    last[...] = result[:, DOWN_SPLIT:]
+    scatter(info, last, keep, send)
+
+
+def feed_weight_call(info, normed, upstream, hidden, gate_grad, up_grad, size):
+    rows, width = gate_grad.shape
+    total, rest, count = 2 * width + DOWN_SPLIT, width - DOWN_SPLIT, D // (4 * size)
+    left = pl.BlockSpec((rows, TILE), lambda i, info: (0, i))
+    whole = pl.BlockSpec((rows, width), lambda i, info: (0, 0), pipeline_mode=pl.Buffered(1))
     return pl.pallas_call(
         feed_weight_kernel,
-        out_shape=pltpu.HBM((D, 3 * width), BF),
-        grid=(D // TILE,),
-        in_specs=[left, left, whole, whole, whole],
-        out_specs=pl.BlockSpec((TILE, 3 * width), lambda i: (i, 0)),
-        compiler_params=params(VMEM),
+        out_shape=(pltpu.HBM((D, total), BF),)
+        + (jax.ShapeDtypeStruct((2, count, size, rest), BF),) * 2,
+        grid_spec=pltpu.PrefetchScalarGridSpec(
+            num_scalar_prefetch=1,
+            grid=(D // TILE,),
+            in_specs=[left, left, whole, whole, whole],
+            out_specs=(pl.BlockSpec((TILE, total), lambda i, info: (i, 0)),)
+            + (pl.BlockSpec((2, count, size, rest), lambda i, info: (0, 0, 0, 0)),) * 2,
+            scratch_shapes=[pltpu.VMEM((TILE, rest), BF)],
+        ),
+        compiler_params=params(24),
         cost_estimate=cost(5e7, 0),
         name="feed_weights",
-    )(normed, in_hbm(upstream), hidden, gate_grad, up_grad)
-
-
-def residual_kernel(info, middle, back_own, back_other, upstream, gain, weight, *refs):
-    grad, low, keep, send_one, send_two = refs[-5:]
+    )(info, normed, in_hbm(upstream), hidden, gate_grad, up_grad)
+
+
+def residual_kernel(count, info, middle, upstream, gain, weight, *refs):
+    grad, low, keep, send_one, send_two, back_s = refs[-6:]
     rank = info[0]
+    for index in range(count):
+
+        @pl.when(pl.program_id(0) == index)
+        def _():
+            back_s[...] = refs[index][...].astype(F32) + refs[count + index][...].astype(F32)
+
     value = middle[...]
-    back = back_own[...].astype(F32) + back_other[...].astype(F32)
     inverse = lax.rsqrt(jnp.mean(value * value, axis=1, keepdims=True) + EPS)
-    scaled = gain[...] * back
+    scaled = gain[...] * back_s[...]
     inner = jnp.mean(scaled * value, axis=1, keepdims=True)
     total = upstream[...].astype(F32) + inverse * scaled - value * (inverse**3 * inner)
     grad[...] = total
     branch = total.astype(BF)
     low[...] = branch
-
     for outs, pair in (((keep.at[0], keep.at[1]), rank), ((send_one.at[0], send_two.at[0]), 1 - rank)):
         column = pl.multiple_of(pair * 2 * HEAD_DIM, 2 * HEAD_DIM)
         result = dot(branch, weight[:, pl.ds(column, 2 * HEAD_DIM)]).astype(BF)
@@ -514,16 +546,14 @@
             outs[head][...] = result[:, head * HEAD_DIM : (head + 1) * HEAD_DIM]
 
 
-def residual_call(info, middle, back_own, back_other, upstream, gain, weights, first, earlier):
-    rows, count = upstream.shape[0], back_own.shape[0]
-    start, half = first // TILE, 4 * HEAD_DIM
-    wide = pl.BlockSpec((TILE, D), lambda i, info: (i + start, 0))
-    part = pl.BlockSpec((TILE, D), lambda i, info: (i, 0))
-    row = pl.BlockSpec((1, D), lambda i, info: (0, 0))
-    piece = pl.BlockSpec((2, TILE, HEAD_DIM), lambda i, info: (0, i + start, 0))
-    single = pl.BlockSpec((1, TILE, HEAD_DIM), lambda i, info: (0, i + start, 0))
-    return pl.pallas_call(
-        residual_kernel,
+def residual_call(info, middle, owns, others, upstream, gain, weights, first, earlier):
+    rows, half, count = upstream.shape[0], 4 * HEAD_DIM, len(owns)
+    wide = pl.BlockSpec((TILE, D), lambda i, info: (i + first, 0))
+    part = pl.BlockSpec((TILE, D), lambda i, info: (0, 0), pipeline_mode=pl.Buffered(1))
+    piece = pl.BlockSpec((2, TILE, HEAD_DIM), lambda i, info: (0, i + first, 0))
+    single = pl.BlockSpec((1, TILE, HEAD_DIM), lambda i, info: (0, i + first, 0))
+    return pl.pallas_call(
+        functools.partial(residual_kernel, count),
         out_shape=(
             pltpu.HBM((rows, D), F32),
             jax.ShapeDtypeStruct((rows, D), BF),
@@ -533,23 +563,23 @@
         ),
         grid_spec=pltpu.PrefetchScalarGridSpec(
             num_scalar_prefetch=1,
-            grid=(count // TILE,),
+            grid=(count,),
             in_specs=[
                 wide,
-                part,
-                part,
                 wide,
-                row,
+                pl.BlockSpec((1, D), lambda i, info: (0, 0)),
                 columns(half, lambda i, info: (0, pl.multiple_of(OUT_AT + info[1] * half, HEAD_DIM))),
             ]
+            + [part] * (2 * count)
             + [pl.BlockSpec(memory_space=pl.ANY)] * len(earlier),
             out_specs=(wide, wide, piece, single, single),
-        ),
-        input_output_aliases={7 + index: index for index in range(len(earlier))},
-        compiler_params=params(VMEM),
-        cost_estimate=cost(3e11 if first + count == rows else 5e7, 0),
+            scratch_shapes=[pltpu.VMEM((TILE, D), F32)],
+        ),
+        input_output_aliases={5 + 2 * count + index: index for index in range(len(earlier))},
+        compiler_params=params(18),
+        cost_estimate=cost(3e11 if first + count == rows // TILE else 5e7, 0),
         name="residual",
-    )(info, middle, back_own, back_other, in_hbm(upstream), gain, in_hbm(weights), *earlier)
+    )(info, in_hbm(middle), in_hbm(upstream), gain, in_hbm(weights), *owns, *others, *earlier)
 
 
 def join(rank, pieces, joined):
@@ -607,14 +637,7 @@
     out[:, :width] = dot(left, joined[...]).astype(BF)
     left = low[...].astype(F32).T.astype(BF)
     out[:, width:] = dot(left, attended[0][...]).astype(BF)
-    count, size = keep.shape[1], keep.shape[2]
-    for line in range(tile // (4 * size)):
-        slot = count - 1 - ((step * (tile // (4 * size)) + line) ^ info[4])
-        for column in range(2):
-            for target, core in ((keep, info[0]), (send, 1 - info[0])):
-                side = info[3] if column == 0 else 1 - info[3]
-                start = pl.multiple_of((line * 4 + side * 2 + core) * size, size)
-                target[column, slot] = out[pl.ds(start, size), :]
+    scatter(info, out, keep, send)
 
 
 def attend_weight_call(info, normed, low, attended, pieces, size):
@@ -698,20 +721,23 @@
     )(keep, core)
 
 
-def split_kernel(left, right, *outs):
+def split_kernel(left_one, right_one, left_two, right_two, *outs):
+    width = left_one.shape[2]
     for index, out in enumerate(outs):
-        out[...] = (left[index].astype(F32) + right[index].astype(F32)).astype(BF)
-
-
-def split_add(left, right):
-    count, size, width = left.shape
+        out[:, :width] = (left_one[index].astype(F32) + right_one[index].astype(F32)).astype(BF)
+        out[:, width:] = (left_two[index].astype(F32) + right_two[index].astype(F32)).astype(BF)
+
+
+def split_add(one, two):
+    count, size, width = one[0].shape
+    total = width + two[0].shape[2]
     return pl.pallas_call(
         split_kernel,
-        out_shape=(jax.ShapeDtypeStruct((size, width), BF),) * count,
+        out_shape=(jax.ShapeDtypeStruct((size, total), BF),) * count,
         compiler_params=pltpu.CompilerParams(vmem_limit_bytes=VMEM * MIB),
         cost_estimate=cost(0, 0),
         name="split_add",
-    )(left, right)
+    )(*one, *two)
 
 
 def low_kernel(left, right, out):
@@ -748,15 +774,15 @@
     )(flags, first, second, up_in, down_in)
 
 
-def reduce_rows(keep, send, count, first_wait, last_wait):
+def reduce_rows(paired, count, first_wait, last_wait):
     length = count // 4
     line = lax.axis_index("dp") // 4
-    core = lax.ppermute(send, "dp", [(i, i ^ 1) for i in range(count)])
-    mine_one, theirs_one, mine_two, theirs_two = pair_add(keep, core)
     pairs = [(i, i ^ 2) for i in range(count)]
-    other_one, first_wait = pin((lax.ppermute(theirs_one, "dp", pairs), first_wait))
-    sums = list(split_add(mine_one, other_one))
-    other = lax.ppermute(theirs_two, "dp", pairs)
+    over = lambda value: lax.ppermute(value, "dp", pairs)
+    (mine_one, theirs_one, mine_two, theirs_two), (down_one, far_one, down_two, far_two) = paired
+    others, first_wait = pin(((over(theirs_one), over(far_one)), first_wait))
+    sums = list(split_add((mine_one, others[0]), (down_one, others[1])))
+    others = (over(theirs_two), over(far_two))
     above = below = None
     for step in range(1, length):
         gap = length - step
@@ -787,8 +813,8 @@
         below = lax.ppermute(up, "dp", [(i, i + 4) for i in range(count - 4) if i // 4 + gap < length])
         above = lax.ppermute(down, "dp", [(i, i - 4) for i in range(4, count) if i // 4 >= gap])
         if step == length // 2 - 1:
-            below, above, other = pin((below, above, other))
-            sums += split_add(mine_two, other)
+            below, above, others = pin((below, above, others))
+            sums += split_add((mine_two, others[0]), (down_two, others[1]))
     return sums[-1], below, above, first_wait, last_wait
 
 
@@ -954,16 +980,16 @@
         backs.append(back)
         backs_other.append(across(back))
     hidden, grad_gate, grad_up, feed_part = earlier
-    hidden, backs_other[1] = pin((hidden, backs_other[1]))
-    feed_grads = feed_weight_call(normed_two, cotangent, hidden, grad_gate, grad_up)
+    feed_grads, down_keep, down_send = feed_weight_call(
+        info, normed_two, cotangent, hidden, grad_gate, grad_up, shard
+    )
     feed_other = across(feed_part)
-    backs[2], _ = pin((backs[2], feed_grads))
+    backs[0], _ = pin((backs[0], feed_grads))
     earlier = ()
-    for index in (2, 3, 0, 1):
-        first = index * TILE
+    for chunks in ((0, 1), (2,), (3,)):
         earlier = residual_call(
-            info, middle, backs[index], backs_other[index], cotangent, gain_two, weights_two,
-            first, earlier,
+            info, middle, [backs[index] for index in chunks], [backs_other[index] for index in chunks],
+            cotangent, gain_two, weights_two, chunks[0], earlier,
         )
     grad_middle, grad_low, grad_keep, *grad_sends = earlier
     grad_others = [beside(value) for value in grad_sends]
@@ -986,20 +1012,22 @@
     block_out = (
         middle + (feed_part.astype(F32) + feed_other.astype(F32))
     ).astype(BF)
-    total, below, above, block_out, input_grad = reduce_rows(
-        attend_keep, attend_send, count, block_out, input_grad
-    )
+    paired = [
+        pair_add(keep, beside(send))
+        for keep, send in ((attend_keep, attend_send), (down_keep, down_send))
+    ]
+    total, below, above, block_out, input_grad = reduce_rows(paired, count, block_out, input_grad)
     feed_sum = lax.psum_scatter(feed_grads, "dp", scatter_dimension=0, tiled=True).astype(F32)
     gate_up_sum = jnp.stack([feed_sum[:, :hidden_here], feed_sum[:, hidden_here : 2 * hidden_here]])
-    down_sum = feed_sum[:, 2 * hidden_here :].T
     gate_up_first, gate_up_second, gate_up_new = adamw(
         proj_gate_up, gate_up_sum, first_gate_up, second_gate_up, 0.5 / math.sqrt(D)
     )
+    gate_up_new, total, below, above = pin((gate_up_new, total, below, above))
+    attend_sum = total.astype(F32) + (below.astype(F32) + above.astype(F32))
+    down_sum = jnp.concatenate([feed_sum[:, 2 * hidden_here :].T, attend_sum[:, 4 * local :].T])
     down_first, down_second, down_new = adamw(
         proj_down, down_sum, first_down, second_down, 0.5 / math.sqrt(FF)
     )
-    gate_up_new, down_new, total, below, above = pin((gate_up_new, down_new, total, below, above))
-    attend_sum = total.astype(F32) + (below.astype(F32) + above.astype(F32))
     qkv_sum = jnp.stack([attend_sum[:, part * local : (part + 1) * local] for part in range(3)])
     out_sum = attend_sum[:, 3 * local : 4 * local].T
     low_qkv, low_gate_up = proj_qkv.astype(BF).astype(F32), proj_gate_up.astype(BF).astype(F32)

time: 328 us -> 316 us (0.963)
  waiting for transfers between devices: 82.1 us -> 67.4 us
    ppermute x10, waiting for transfers between devices: 33.4 us -> 23.9 us  [across(): return lax.ppermute(value, 'mp', [(0, 1), (1, 0)])]
    ppermute x3 -> x4, waiting for transfers between devices: 28.8 us -> 22.3 us  [reduce_rows(): over = lambda value: lax.ppermute(value, 'dp', pairs)]
    ppermute x3, starting transfers between devices: 14.8 us -> 11 us  [reduce_rows(): lax.ppermute(up, 'dp', [(i, i + 4) for i in range(count - 4) if i // 4 +...]
    ppermute x11 -> x13, waiting for transfers between devices: 4.69 us -> 7.63 us  [beside(): return lax.ppermute(value, 'dp', core_pairs)]
    unnamed x126 -> x120, local copies, waits for them, and re-layouts: 9.22 us -> 10.6 us
    pallas_call x7 -> x6, Pallas kernels: 29.5 us -> 28.5 us  [the longest x3 14.6 us: residual_call(): pl.pallas_call(functools.partial(residual_kernel, count), out_shape=(pltp...]
  transfers between devices with their start and end apart: 33 -> 36, of which waited for: 16 -> 14; matrix products, arithmetic and copies ran while one was open for 7% -> 8% of each run, Pallas kernels for 35% -> 37%
where the time goes in v5:
time: 316 us; the launch traced here: 310 us
  Pallas kernels  130 us (41%)
  waiting for transfers between devices  67.4 us (21%)
  starting transfers between devices  34.1 us (11%)
  blocking collectives  26.8 us (8%)
  other arithmetic  22.9 us (7%)
  between operations  15.8 us (5%)
  local copies, waits for them, and re-layouts  12.9 us (4%)
    all_gather x1, blocking collectives, body(): lax.all_gather(shard_one, 'dp', axis=0, tiled=True, axis_index_groups=lines)  26.8 us
    pallas_call x4, Pallas kernels, feed_call(): pl.pallas_call(feed_kernel, out_shape=(pltpu.VMEM((rows, width), BF),) *...  24.8 us
    ppermute x10, waiting for transfers between devices, across(): return lax.ppermute(value, 'mp', [(0, 1), (1, 0)])  23.9 us
    ppermute x4, waiting for transfers between devices, reduce_rows(): over = lambda value: lax.ppermute(value, 'dp', pairs)  22.3 us
    pallas_call x2, Pallas kernels, attend_backward(): pl.pallas_call(backward_kernel, out_shape=tuple((jax.ShapeDtypeStruct((pa...  19.7 us
    pallas_call x3, Pallas kernels, residual_call(): pl.pallas_call(functools.partial(residual_kernel, count), out_shape=(pltp...  14.6 us
    pallas_call x1, Pallas kernels, feed_weight_call(): pl.pallas_call(feed_weight_kernel, out_shape=(pltpu.HBM((D, total), BF),)...  13.6 us
    pallas_call x1, Pallas kernels, attend_forward(): pl.pallas_call(forward_kernel, out_shape=(jax.ShapeDtypeStruct((2, rows,...  12.7 us
  transfers between devices with their start and end apart: 36, of which 14 were waited for; matrix products, arithmetic and copies ran while one was open for 8% of the time, Pallas kernels for 37%

profile of v5, /device:TPU:0, one launch (start us, length us, event | category | flops | bytes accessed | tf_op | source)
XLA Modules:
  0.0 309.6 jit_solution(15300700652527278743)
XLA Ops:
  8.4 3.0 collective-permute-start.8
  16.1 26.8 %all_gather.6 = bf16[256,1664]{1,0:T(8,128)(2,1)S(1)} all-gather(bf16[64,1664]{1,0:T(8,128)(2,1)S(1)} %shard.1), channel_id=1, replica_groups={{0,8,16,24},{2,10,18,26},{4,12,20,28},{6,14,22,30},{1,9,17,25},{3,11,19..., dimensions={0}, use_global_device_ids=true | all-gather | bytes 1064960 | tf_op jit(solution)/shard_map/all_gather | solution.py:944
  42.9 1.3 collective-permute-start
  48.3 3.7 %fusion.3 = (f32[2048,64]{1,0:T(8,128)S(1)}, f32[2048,64]{1,0:T(8,128)S(1)}, f32[2048,64]{1,0:T(8,128)S(1)}) fusion(f32[64]{0:T(128)S(1)} %negate_power_fusion, f32[2048]{0:T(1024)S(1)} %iota_convert_fusion), kind=kLoop, calls=%fused_computation.27 | loop fusion | flops 262144 | bytes 1581312 | tf_op jit(solution)/shard_map/neg | solution.py:62
  52.0 7.6 %collective-permute-done = bf16[256,1664]{1,0:T(8,128)(2,1)} collective-permute-done((bf16[256,1664]{1,0:T(8,128)(2,1)S(1)}, bf16[256,1664]{1,0:T(8,128)(2,1)}, u32[]{:S(2)}, u32[]{:S(2)}) %collective-permute-start) | collective-permute-done | bytes 852000 | tf_op jit(solution)/shard_map/ppermute | solution.py:945
  62.4 1.7 copy.65
  64.2 2.1 interleave.1.gain_columns.weight.refs_6_
  66.5 4.9 %project_first.1 = (bf16[3,2,1024,128]{3,2,1,0:T(8,128)(2,1)S(1)}, bf16[1024,1024]{1,0:T(8,128)(2,1)S(1)}, f32[8,1024]{1,0:T(8,128)S(1)}) custom-call(s32[5]{0:T(128)S(1)} %stack.66.info, bf16[1024,1024]{1,0:T(8,128)(2,1)S(1)} %copy-done.12, bf16[1024,1664]{1,0:T(8,128)(2,1)S(1)} %interleave.1.gain_columns.weight.refs_6_, ...), custom_call_target="tpu_custom_call" | custom-call | tf_op jit(solution)/shard_map/project_first/pallas_call | solution.py:111
  72.1 3.7 %project_second.1.own = bf16[3,2,1024,128]{3,2,1,0:T(8,128)(2,1)S(1)} custom-call(s32[5]{0:T(128)S(1)} %stack.66.info, bf16[1024,1024]{1,0:T(8,128)(2,1)S(1)} %get-tuple-element.130.normed, bf16[1024,1664]{1,0:T(8,128)(2,1)S(1)} %interleave.1.gain_columns.weight.refs_6_, f32[2048,128]{1,0:T(8,128)S(1)} %get-tuple-element.128.cosines, ...), custom_call_target="tpu_custom_call" | custom-call | tf_op jit(solution)/shard_map/project_second/pallas_call | solution.py:142
  75.9 12.7 %attend_forward.1 = (bf16[2,1024,128]{2,1,0:T(8,128)(2,1)S(1)}, bf16[2,1024,128]{2,1,0:T(8,128)(2,1)S(1)}, f32[2,128,2048]{2,1,0:T(8,128)}, f32[2,1,2048]{2,1,0:T(1,128)S(1)}) custom-call(s32[5]{0:T(128)S(1)} %stack.66.info, bf16[3,2,1024,128]{3,2,1,0:T(8,128)(2,1)S(1)} %project_second.1.own, bf16[3,2,1024,128]{3,2,1,0:T(8,128)(2,1)S(1)} %collective-permute-done.4.other, ...), custom_call_target="tpu_custom_call" | custom-call | tf_op jit(solution)/shard_map/attend_forward/pallas_call | solution.py:234
  89.8 1.9 collective-permute-done.5.refs_1_
  91.9 12.7 %collective-permute-done.6.refs_2_ = bf16[2,1024,128]{2,1,0:T(8,128)(2,1)S(1)} collective-permute-done((bf16[2,1024,128]{2,1,0:T(8,128)(2,1)S(1)}, bf16[2,1024,128]{2,1,0:T(8,128)(2,1)S(1)}, u32[]{:S(2)}, u32[]{:S(2)}) %collective-permute-start.6) | collective-permute-done | bytes 524320 | tf_op jit(solution)/shard_map/ppermute | solution.py:924
  105.4 10.1 %collective-permute-done.7.refs_3_ = bf16[2,1024,128]{2,1,0:T(8,128)(2,1)} collective-permute-done((bf16[2,1024,128]{2,1,0:T(8,128)(2,1)S(1)}, bf16[2,1024,128]{2,1,0:T(8,128)(2,1)}, u32[]{:S(2)}, u32[]{:S(2)}) %collective-permute-start.7) | collective-permute-done | bytes 524320 | tf_op jit(solution)/shard_map/ppermute | solution.py:924
  115.5 10.2 %middle.1 = (f32[1024,1024]{1,0:T(8,128)}, bf16[1024,1024]{1,0:T(8,128)(2,1)S(1)}, bf16[1024,512]{1,0:T(8,128)(2,1)}) custom-call(s32[5]{0:T(128)S(1)} %stack.66.info, bf16[2,1024,128]{2,1,0:T(8,128)(2,1)} %copy-done.29, bf16[2,1024,128]{2,1,0:T(8,128)(2,1)} %copy-done.48, bf16[2,1024,128]{2,1,0:T(8,128)(2,1)} %copy-done.49, ...), custom_call_target="tpu_custom_call" | custom-call | tf_op jit(solution)/shard_map/middle/pallas_call | solution.py:409
  125.7 5.5 %feed.4 = (bf16[1024,1408]{1,0:T(8,128)(2,1)S(1)}, bf16[1024,1408]{1,0:T(8,128)(2,1)S(1)}, bf16[1024,1408]{1,0:T(8,128)(2,1)S(1)}, bf16[1024,1024]{1,0:T(8,128)(2,1)}, bf16[256,1024]{1,0:T(8,128)(2,1)S(1)}) custom-call(bf16[1024,1024]{1,0:T(8,128)(2,1)S(1)} %get-tuple-element.139.normed, bf16[1024,1024]{1,0:T(8,128)(2,1)S(1)} %copy-done.3, ...), custom_call_target="tpu_custom_call" | custom-call | flops 50000000 | tf_op jit(solution)/shard_map/feed/pallas_call | solution.py:457
  131.6 6.3 %feed.5 = (bf16[1024,1408]{1,0:T(8,128)(2,1)S(1)}, bf16[1024,1408]{1,0:T(8,128)(2,1)S(1)}, bf16[1024,1408]{1,0:T(8,128)(2,1)S(1)}, bf16[1024,1024]{1,0:T(8,128)(2,1)}, bf16[256,1024]{1,0:T(8,128)(2,1)}) custom-call(bf16[1024,1024]{1,0:T(8,128)(2,1)S(1)} %get-tuple-element.139.normed, ...), custom_call_target="tpu_custom_call", output_to_operand_aliasing={{0}: (5, {}), {1}: (6, {}), {2}: (7, {}), {3}: (8, {})} | custom-call | flops 50000000 | tf_op jit(solution)/shard_map/feed/pallas_call | solution.py:457
  137.9 1.7 collective-permute-start.12
  139.7 6.5 %feed.6 = (bf16[1024,1408]{1,0:T(8,128)(2,1)S(1)}, bf16[1024,1408]{1,0:T(8,128)(2,1)S(1)}, bf16[1024,1408]{1,0:T(8,128)(2,1)S(1)}, bf16[1024,1024]{1,0:T(8,128)(2,1)}, bf16[256,1024]{1,0:T(8,128)(2,1)}) custom-call(bf16[1024,1024]{1,0:T(8,128)(2,1)S(1)} %get-tuple-element.139.normed, ...), custom_call_target="tpu_custom_call", output_to_operand_aliasing={{0}: (5, {}), {1}: (6, {}), {2}: (7, {}), {3}: (8, {})} | custom-call | flops 50000000 | tf_op jit(solution)/shard_map/feed/pallas_call | solution.py:457
  146.5 6.4 %feed.7 = (bf16[1024,1408]{1,0:T(8,128)(2,1)S(1)}, bf16[1024,1408]{1,0:T(8,128)(2,1)S(1)}, bf16[1024,1408]{1,0:T(8,128)(2,1)S(1)}, bf16[1024,1024]{1,0:T(8,128)(2,1)}, bf16[256,1024]{1,0:T(8,128)(2,1)}) custom-call(bf16[1024,1024]{1,0:T(8,128)(2,1)S(1)} %get-tuple-element.139.normed, ...), custom_call_target="tpu_custom_call", output_to_operand_aliasing={{0}: (5, {}), {1}: (6, {}), {2}: (7, {}), {3}: (8, {})} | custom-call | flops 50000000 | tf_op jit(solution)/shard_map/feed/pallas_call | solution.py:457
  152.9 1.7 collective-permute-start.10
  154.6 13.6 %feed_weights.1 = (bf16[1024,3584]{1,0:T(8,128)(2,1)}, bf16[2,4,64,640]{3,2,1,0:T(8,128)(2,1)S(1)}, bf16[2,4,64,640]{3,2,1,0:T(8,128)(2,1)S(1)}) custom-call(s32[5]{0:T(128)S(1)} %stack.66.info, bf16[1024,1024]{1,0:T(8,128)(2,1)S(1)} %get-tuple-element.139.normed, bf16[1024,1024]{1,0:T(8,128)(2,1)} %upstream.15, ...), custom_call_target="tpu_custom_call" | custom-call | flops 50000000 | tf_op jit(solution)/shard_map/feed_weights/pallas_call | solution.py:507
  170.0 5.3 %residual.3 = (f32[1024,1024]{1,0:T(8,128)}, bf16[1024,1024]{1,0:T(8,128)(2,1)S(1)}, bf16[2,1024,128]{2,1,0:T(8,128)(2,1)S(1)}, bf16[1,1024,128]{2,1,0:T(8,128)(2,1)S(1)}, bf16[1,1024,128]{2,1,0:T(8,128)(2,1)S(1)}) custom-call(s32[5]{0:T(128)S(1)} %stack.66.info, f32[1024,1024]{1,0:T(8,128)} %get-tuple-element.138.middle, bf16[1024,1024]{1,0:T(8,128)(2,1)} %upstream.15, ...), custom_call_target="tpu_custom_call" | custom-call | flops 50000000 | tf_op jit(solution)/shard_map/residual/pallas_call | solution.py:555
  175.3 4.5 %residual.4 = (f32[1024,1024]{1,0:T(8,128)}, bf16[1024,1024]{1,0:T(8,128)(2,1)S(1)}, bf16[2,1024,128]{2,1,0:T(8,128)(2,1)S(1)}, bf16[1,1024,128]{2,1,0:T(8,128)(2,1)S(1)}, bf16[1,1024,128]{2,1,0:T(8,128)(2,1)S(1)}) custom-call(s32[5]{0:T(128)S(1)} %stack.66.info, ...), custom_call_target="tpu_custom_call", output_to_operand_aliasing={{0}: (7, {}), {1}: (8, {}), {2}: (9, {}), {3}: (10, {}), {4... | custom-call | flops 50000000 | tf_op jit(solution)/shard_map/residual/pallas_call | solution.py:555
  179.9 4.8 %residual.5 = (f32[1024,1024]{1,0:T(8,128)}, bf16[1024,1024]{1,0:T(8,128)(2,1)S(1)}, bf16[2,1024,128]{2,1,0:T(8,128)(2,1)S(1)}, bf16[1,1024,128]{2,1,0:T(8,128)(2,1)S(1)}, bf16[1,1024,128]{2,1,0:T(8,128)(2,1)S(1)}) custom-call(s32[5]{0:T(128)S(1)} %stack.66.info, ...), custom_call_target="tpu_custom_call", output_to_operand_aliasing={{0}: (7, {}), {1}: (8, {}), {2}: (9, {}), {3}: (10, {}), {4... | custom-call | flops 299999985664 | tf_op jit(solution)/shard_map/residual/pallas_call | solution.py:555
  186.4 9.5 %attend_backward.3 = (bf16[3,1,1024,128]{3,2,1,0:T(8,128)(2,1)S(1)}, bf16[2,1,1024,128]{3,2,1,0:T(8,128)(2,1)S(1)}, bf16[1,1,1024,128]{3,2,1,0:T(8,128)(2,1)S(1)}) custom-call(s32[5]{0:T(128)S(1)} %stack.66.info, bf16[3,2,1024,128]{3,2,1,0:T(8,128)(2,1)S(1)} %copy-done.11, bf16[3,2,1024,128]{3,2,1,0:T(8,128)(2,1)S(1)} %copy-done.16, ...), custom_call_target="tpu_custom_call" | custom-call | tf_op jit(solution)/shard_map/attend_backward/pallas_call | solution.py:335
  196.0 10.2 %attend_backward.2 = (bf16[3,1,1024,128]{3,2,1,0:T(8,128)(2,1)S(1)}, bf16[2,1,1024,128]{3,2,1,0:T(8,128)(2,1)S(1)}, bf16[1,1,1024,128]{3,2,1,0:T(8,128)(2,1)S(1)}) custom-call(s32[5]{0:T(128)S(1)} %stack.66.info, bf16[3,2,1024,128]{3,2,1,0:T(8,128)(2,1)S(1)} %copy-done.11, bf16[3,2,1024,128]{3,2,1,0:T(8,128)(2,1)S(1)} %copy-done.16, ...), custom_call_target="tpu_custom_call" | custom-call | tf_op jit(solution)/shard_map/attend_backward/pallas_call | solution.py:335
  207.2 1.4 collective-permute-done.18.refs_5_
  209.0 6.3 %back.1.back_own = bf16[1024,1024]{1,0:T(8,128)(2,1)} custom-call(s32[5]{0:T(128)S(1)} %stack.66.info, bf16[3,1,1024,128]{3,2,1,0:T(8,128)(2,1)S(1)} %get-tuple-element.188.refs_0_, bf16[3,1,1024,128]{3,2,1,0:T(8,128)(2,1)S(1)} %get-tuple-element.183.refs_1_, bf16[2,1,1024,128]{3,2,1,0:T(8,128)(2,1)S(1)} %collective-permute-done.15.refs_2_, ...), custom_call_target="tpu_custom_call" | custom-call | tf_op jit(solution)/shard_map/back/pallas_call | solution.py:610
  215.4 7.3 %attend_weights.1 = (bf16[2,4,64,2048]{3,2,1,0:T(8,128)(2,1)S(1)}, bf16[2,4,64,2048]{3,2,1,0:T(8,128)(2,1)S(1)}) custom-call(s32[5]{0:T(128)S(1)} %stack.66.info, bf16[1024,1024]{1,0:T(8,128)(2,1)S(1)} %copy-done.21, bf16[1024,1024]{1,0:T(8,128)(2,1)S(1)} %get-tuple-element.176.low, bf16[3,1,1024,128]{3,2,1,0:T(8,128)(2,1)S(1)} %get-tuple-element.188.refs_0_, ...), custom_call_target="tpu_custom_call" | custom-call | tf_op jit(solution)/shard_map/attend_weights/pallas_call | solution.py:653
  224.1 2.9 collective-permute-done.19.core
  227.4 1.3 collective-permute-start.20
  230.4 1.2 collective-permute-start.26
  231.6 4.8 %add_convert_fusion = bf16[1024,1024]{1,0:T(8,128)(2,1)} fusion(f32[1024,1024]{1,0:T(8,128)S(1)} %copy-done.40, bf16[1024,1024]{1,0:T(8,128)(2,1)} %collective-permute-done.23, bf16[1024,1024]{1,0:T(8,128)(2,1)} %get-tuple-element.196), kind=kLoop, calls=%fused_computation.1 | loop fusion | flops 5242880 | bytes 10485760 | tf_op jit(solution)/shard_map/convert_element_type | solution.py:1014
  236.4 9.7 %collective-permute-done.22.right_two = bf16[2,64,640]{2,1,0:T(8,128)(2,1)S(1)} collective-permute-done((bf16[2,64,640]{2,1,0:T(8,128)(2,1)S(1)}, bf16[2,64,640]{2,1,0:T(8,128)(2,1)S(1)}, u32[]{:S(2)}, u32[]{:S(2)}) %collective-permute-start.22) | collective-permute-done | bytes 163872 | tf_op jit(solution)/shard_map/ppermute | solution.py:781
  246.3 2.8 collective-permute-start.24
  249.8 2.5 collective-permute-start.27
  252.3 12.6 %collective-permute-done.27.right_two = bf16[2,64,640]{2,1,0:T(8,128)(2,1)S(1)} collective-permute-done((bf16[2,64,640]{2,1,0:T(8,128)(2,1)S(1)}, bf16[2,64,640]{2,1,0:T(8,128)(2,1)S(1)}, u32[]{:S(2)}, u32[]{:S(2)}) %collective-permute-start.27) | collective-permute-done | bytes 163872 | tf_op jit(solution)/shard_map/ppermute | solution.py:781
  265.7 1.4 collective-permute-start.29
  267.9 3.7 %collective-permute-start.28 = (bf16[64,2688]{1,0:T(8,128)(2,1)}, bf16[64,2688]{1,0:T(8,128)(2,1)}, u32[]{:S(2)}, u32[]{:S(2)}) collective-permute-start(bf16[64,2688]{1,0:T(8,128)(2,1)} %low_add.2), channel_id=1, source_target_pairs={{0,8},{2,10},{4,12},{6,14},{8,16},{10,18},{12,20},{14,22},{1,9},{3... | collective-permute-start | bytes 1032200 | tf_op jit(solution)/shard_map/ppermute | solution.py:813
  271.7 2.2 copy-done.14
  273.9 5.2 %input_grad.1 = bf16[1024,1024]{1,0:T(8,128)(2,1)} custom-call(f32[1024,1024]{1,0:T(8,128)S(1)} %copy-done.14, bf16[1024,1024]{1,0:T(8,128)(2,1)} %back.1.back_own, bf16[1024,1024]{1,0:T(8,128)(2,1)} %collective-permute-done.30.back_other, bf16[1024,1024]{1,0:T(8,128)(2,1)S(1)} %copy-done.13, f32[1,1024]{1,0:T(1,128)S(1)} %get-tuple-element.250.gain), custom_call_target="tpu_custom_call" | custom-call | flops 12582912 | bytes 12582912 | tf_op jit(solution)/shard_map/input_grad/pallas_call | solution.py:683
  279.3 1.5 chosen_add.1
  280.8 4.4 %collective-permute-start.31 = (bf16[64,2688]{1,0:T(8,128)(2,1)S(1)}, bf16[64,2688]{1,0:T(8,128)(2,1)S(1)}, u32[]{:S(2)}, u32[]{:S(2)}) collective-permute-start(bf16[64,2688]{1,0:T(8,128)(2,1)S(1)} %get-tuple-element.220), channel_id=1, source_target_pairs={{0,8},{2,10},{4,12},{6,14},{8,16},{10,18},{12,20},{14,22},{16,24},... | collective-permute-start | bytes 1032200 | tf_op jit(solution)/shard_map/ppermute | solution.py:813
  285.3 1.3 collective-permute-start.32
  287.8 1.8 multiply_subtract_fusion
  289.6 1.8 collective-permute-done.31
  291.4 4.2 %collective-permute-done.32 = bf16[64,2688]{1,0:T(8,128)(2,1)} collective-permute-done((bf16[64,2688]{1,0:T(8,128)(2,1)S(1)}, bf16[64,2688]{1,0:T(8,128)(2,1)}, u32[]{:S(2)}, u32[]{:S(2)}) %collective-permute-start.32) | collective-permute-done | bytes 344096 | tf_op jit(solution)/shard_map/ppermute | solution.py:814
  296.9 1.3 multiply_subtract_fusion.1
  (208 shorter events, 33.7 us)
Async XLA Ops:
  7.2 37.0 %copy-start = (bf16[1024,2,512]{2,1,0:T(2,128)(2,1)S(1)}, bf16[1024,2,512]{2,1,0:T(2,128)(2,1)}, u32[]{:S(2)}) copy-start(bf16[1024,2,512]{2,1,0:T(2,128)(2,1)} %param.38) | copy-start | bytes 6291460
  7.3 108.2 %all-gather.2.cloned.1.call-start = ((), (), s32[]{:S(2)}) async-start(), calls=%async_computation.1 | async-start | bytes 11419648 | tf_op jit(solution)/shard_map/all_gather | solution.py:947
  8.4 6.3 %collective-permute-start.8 = (bf16[64,512]{1,0:T(8,128)(2,1)S(1)}, bf16[64,512]{1,0:T(8,128)(2,1)S(1)}, u32[]{:S(2)}, u32[]{:S(2)}) collective-permute-start(bf16[64,512]{1,0:T(8,128)(2,1)S(1)} %convert_bitcast_fusion), channel_id=1, source_target_pairs={{0,1},{1,0},{2,3},{3,2},{4,5},{5,4},{6,7},{7,6},{8,9},{9,8},{10,11... | collective-permute-start | bytes 196616 | tf_op jit(solution)/shard_map/ppermute | solution.py:924
  12.6 31.6 %copy-start.57 = (s32[1,128]{1,0:T(1,128)S(1)}, s32[1,128]{1,0:T(1,128)}, u32[]{:S(2)}) copy-start(s32[1,128]{1,0:T(1,128)} %param.41) | copy-start | bytes 1540
  16.0 270.6 %reduce-scatter.2.cloned.1.call-start = ((), (), s32[]{:S(2)}) async-start(), calls=%async_computation.2 | async-start | bytes 7798784 | tf_op jit(solution)/shard_map/reduce_scatter | solution.py:1020
  42.9 16.7 %collective-permute-start = (bf16[256,1664]{1,0:T(8,128)(2,1)S(1)}, bf16[256,1664]{1,0:T(8,128)(2,1)}, u32[]{:S(2)}, u32[]{:S(2)}) collective-permute-start(bf16[256,1664]{1,0:T(8,128)(2,1)S(1)} %all_gather.6), channel_id=1, source_target_pairs={{0,4},{2,6},{4,0},{6,2},{8,12},{10,14},{12,8},{14,10},{16,20},{18,... | collective-permute-start | bytes 2555912 | tf_op jit(solution)/shard_map/ppermute | solution.py:945
  44.2 20.0 %collective-permute-start.1 = (bf16[256,1664]{1,0:T(8,128)(2,1)S(1)}, bf16[256,1664]{1,0:T(8,128)(2,1)}, u32[]{:S(2)}, u32[]{:S(2)}) collective-permute-start(bf16[256,1664]{1,0:T(8,128)(2,1)S(1)} %all_gather.6), channel_id=1, source_target_pairs={{0,2},{2,0},{4,6},{6,4},{8,10},{10,8},{12,14},{14,12},{16,18},{18,... | collective-permute-start | bytes 2555912 | tf_op jit(solution)/shard_map/ppermute | solution.py:927
  47.1 17.1 %collective-permute-start.3 = (bf16[2,2,128,128]{3,2,1,0:T(8,128)(2,1)}, bf16[2,2,128,128]{3,2,1,0:T(8,128)(2,1)}, u32[]{:S(2)}, u32[]{:S(2)}) collective-permute-start(bf16[2,2,128,128]{3,2,1,0:T(8,128)(2,1)} %bitcast.6), channel_id=1, source_target_pairs={{0,2},{2,0},{4,6},{6,4},{8,10},{10,8},{12,14},{14,12},{16,18},{18,... | collective-permute-start | bytes 393224 | tf_op jit(solution)/shard_map/ppermute | solution.py:927
  59.6 4.6 %collective-permute-start.2 = (bf16[256,1664]{1,0:T(8,128)(2,1)}, bf16[256,1664]{1,0:T(8,128)(2,1)}, u32[]{:S(2)}, u32[]{:S(2)}) collective-permute-start(bf16[256,1664]{1,0:T(8,128)(2,1)} %collective-permute-done), channel_id=1, source_target_pairs={{0,2},{2,0},{4,6},{6,4},{8,10},{10,8},{12,14},{14,12},{16,18},{18,... | collective-permute-start | bytes 2555912 | tf_op jit(solution)/shard_map/ppermute | solution.py:927
  59.9 16.0 %copy-start.18 = (bf16[2048,128]{1,0:T(8,128)(2,1)}, bf16[2048,128]{1,0:T(8,128)(2,1)S(1)}, u32[]{:S(2)}) copy-start(bf16[2048,128]{1,0:T(8,128)(2,1)S(1)} %select_convert_fusion.bias) | copy-start | bytes 1572868
  60.6 11.6 %copy-start.6 = (f32[2048,128]{1,0:T(8,128)}, f32[2048,128]{1,0:T(8,128)S(1)}, u32[]{:S(2)}) copy-start(f32[2048,128]{1,0:T(8,128)S(1)} %get-tuple-element.128.cosines) | copy-start | bytes 3145732
  60.6 11.6 %copy-start.8 = (f32[2048,128]{1,0:T(8,128)}, f32[2048,128]{1,0:T(8,128)S(1)}, u32[]{:S(2)}) copy-start(f32[2048,128]{1,0:T(8,128)S(1)} %get-tuple-element.129.sines) | copy-start | bytes 3145732
  71.4 4.4 %collective-permute-start.4 = (bf16[3,2,1024,128]{3,2,1,0:T(8,128)(2,1)S(1)}, bf16[3,2,1024,128]{3,2,1,0:T(8,128)(2,1)S(1)}, u32[]{:S(2)}, u32[]{:S(2)}) collective-permute-start(bf16[3,2,1024,128]{3,2,1,0:T(8,128)(2,1)S(1)} %get-tuple-element.131), channel_id=1, source_target_pairs={{0,2},{2,0},{4,6},{6,4},{8,10},{10,8},{12,14},{14,12},{16,18},{18,... | collective-permute-start | bytes 4718600 | tf_op jit(solution)/shard_map/ppermute | solution.py:927
  75.9 12.7 %copy-start.15 = (bf16[3,2,1024,128]{3,2,1,0:T(8,128)(2,1)}, bf16[3,2,1024,128]{3,2,1,0:T(8,128)(2,1)S(1)}, u32[]{:S(2)}) copy-start(bf16[3,2,1024,128]{3,2,1,0:T(8,128)(2,1)S(1)} %collective-permute-done.4.other) | copy-start | bytes 4718596
  89.8 25.7 %copy-start.29 = (bf16[2,1024,128]{2,1,0:T(8,128)(2,1)}, bf16[2,1024,128]{2,1,0:T(8,128)(2,1)S(1)}, u32[]{:S(2)}) copy-start(bf16[2,1024,128]{2,1,0:T(8,128)(2,1)S(1)} %get-tuple-element.135.refs_0_) | copy-start | bytes 1572868
  89.8 1.9 collective-permute-start.5
  89.8 14.7 %collective-permute-start.6 = (bf16[2,1024,128]{2,1,0:T(8,128)(2,1)S(1)}, bf16[2,1024,128]{2,1,0:T(8,128)(2,1)S(1)}, u32[]{:S(2)}, u32[]{:S(2)}) collective-permute-start(bf16[2,1024,128]{2,1,0:T(8,128)(2,1)S(1)} %get-tuple-element.135.refs_0_), channel_id=1, source_target_pairs={{0,1},{1,0},{2,3},{3,2},{4,5},{5,4},{6,7},{7,6},{8,9},{9,8},{10,11... | collective-permute-start | bytes 1572872 | tf_op jit(solution)/shard_map/ppermute | solution.py:924
  91.7 12.9 %copy-start.48 = (bf16[2,1024,128]{2,1,0:T(8,128)(2,1)}, bf16[2,1024,128]{2,1,0:T(8,128)(2,1)S(1)}, u32[]{:S(2)}) copy-start(bf16[2,1024,128]{2,1,0:T(8,128)(2,1)S(1)} %collective-permute-done.5.refs_1_) | copy-start | bytes 1572868
  91.7 23.8 %collective-permute-start.7 = (bf16[2,1024,128]{2,1,0:T(8,128)(2,1)S(1)}, bf16[2,1024,128]{2,1,0:T(8,128)(2,1)}, u32[]{:S(2)}, u32[]{:S(2)}) collective-permute-start(bf16[2,1024,128]{2,1,0:T(8,128)(2,1)S(1)} %collective-permute-done.5.refs_1_), channel_id=1, source_target_pairs={{0,1},{1,0},{2,3},{3,2},{4,5},{5,4},{6,7},{7,6},{8,9},{9,8},{10,11... | collective-permute-start | bytes 1572872 | tf_op jit(solution)/shard_map/ppermute | solution.py:924
  115.5 10.2 %copy-start.2 = (bf16[1024,5248]{1,0:T(8,128)(2,1)S(1)}, bf16[1024,5248]{1,0:T(8,128)(2,1)}, u32[]{:S(2)}) copy-start(bf16[1024,5248]{1,0:T(8,128)(2,1)} %all-gather.2.cloned.1.call-done.refs_5_.gate_w.up_w.down_w.weight) | copy-start | bytes 32243716
  115.5 10.2 %copy-start.3 = (bf16[1024,1024]{1,0:T(8,128)(2,1)S(1)}, bf16[1024,1024]{1,0:T(8,128)(2,1)}, u32[]{:S(2)}) copy-start(bf16[1024,1024]{1,0:T(8,128)(2,1)} %upstream.15) | copy-start | bytes 6291460
  131.2 15.3 %collective-permute-start.9 = (bf16[256,1024]{1,0:T(8,128)(2,1)S(1)}, bf16[256,1024]{1,0:T(8,128)(2,1)S(1)}, u32[]{:S(2)}, u32[]{:S(2)}) collective-permute-start(bf16[256,1024]{1,0:T(8,128)(2,1)S(1)} %get-tuple-element.163.refs_0_), channel_id=1, source_target_pairs={{0,1},{1,0},{2,3},{3,2},{4,5},{5,4},{6,7},{7,6},{8,9},{9,8},{10,11... | collective-permute-start | bytes 1572872 | tf_op jit(solution)/shard_map/ppermute | solution.py:924
  137.9 31.5 %collective-permute-start.12 = (bf16[256,1024]{1,0:T(8,128)(2,1)}, bf16[256,1024]{1,0:T(8,128)(2,1)}, u32[]{:S(2)}, u32[]{:S(2)}) collective-permute-start(bf16[256,1024]{1,0:T(8,128)(2,1)} %get-tuple-element.164.refs_1_), channel_id=1, source_target_pairs={{0,1},{1,0},{2,3},{3,2},{4,5},{5,4},{6,7},{7,6},{8,9},{9,8},{10,11... | collective-permute-start | bytes 1572872 | tf_op jit(solution)/shard_map/ppermute | solution.py:924
  146.2 29.1 %collective-permute-start.11 = (bf16[256,1024]{1,0:T(8,128)(2,1)}, bf16[256,1024]{1,0:T(8,128)(2,1)}, u32[]{:S(2)}, u32[]{:S(2)}) collective-permute-start(bf16[256,1024]{1,0:T(8,128)(2,1)} %get-tuple-element.158.refs_0_), channel_id=1, source_target_pairs={{0,1},{1,0},{2,3},{3,2},{4,5},{5,4},{6,7},{7,6},{8,9},{9,8},{10,11... | collective-permute-start | bytes 1572872 | tf_op jit(solution)/shard_map/ppermute | solution.py:924
  152.9 27.0 %collective-permute-start.10 = (bf16[256,1024]{1,0:T(8,128)(2,1)}, bf16[256,1024]{1,0:T(8,128)(2,1)S(1)}, u32[]{:S(2)}, u32[]{:S(2)}) collective-permute-start(bf16[256,1024]{1,0:T(8,128)(2,1)} %get-tuple-element.157.refs_0_), channel_id=1, source_target_pairs={{0,1},{1,0},{2,3},{3,2},{4,5},{5,4},{6,7},{7,6},{8,9},{9,8},{10,11... | collective-permute-start | bytes 1572872 | tf_op jit(solution)/shard_map/ppermute | solution.py:924
  169.0 54.5 %collective-permute-start.23 = (bf16[1024,1024]{1,0:T(8,128)(2,1)}, bf16[1024,1024]{1,0:T(8,128)(2,1)}, u32[]{:S(2)}, u32[]{:S(2)}) collective-permute-start(bf16[1024,1024]{1,0:T(8,128)(2,1)} %get-tuple-element.196), channel_id=1, source_target_pairs={{0,1},{1,0},{2,3},{3,2},{4,5},{5,4},{6,7},{7,6},{8,9},{9,8},{10,11... | collective-permute-start | bytes 6291464 | tf_op jit(solution)/shard_map/ppermute | solution.py:924
  184.7 1.6 collective-permute-start.14
  184.7 11.3 %collective-permute-start.13 = (bf16[1,1024,128]{2,1,0:T(8,128)(2,1)S(1)}, bf16[1,1024,128]{2,1,0:T(8,128)(2,1)S(1)}, u32[]{:S(2)}, u32[]{:S(2)}) collective-permute-start(bf16[1,1024,128]{2,1,0:T(8,128)(2,1)S(1)} %get-tuple-element.178), channel_id=1, source_target_pairs={{0,2},{2,0},{4,6},{6,4},{8,10},{10,8},{12,14},{14,12},{16,18},{18,... | collective-permute-start | bytes 786440 | tf_op jit(solution)/shard_map/ppermute | solution.py:927
  195.8 13.2 %collective-permute-start.17 = (bf16[2,1,1024,128]{3,2,1,0:T(8,128)(2,1)S(1)}, bf16[2,1,1024,128]{3,2,1,0:T(8,128)(2,1)S(1)}, u32[]{:S(2)}, u32[]{:S(2)}) collective-permute-start(bf16[2,1,1024,128]{3,2,1,0:T(8,128)(2,1)S(1)} %get-tuple-element.186), channel_id=1, source_target_pairs={{0,2},{2,0},{4,6},{6,4},{8,10},{10,8},{12,14},{14,12},{16,18},{18,... | collective-permute-start | bytes 1572872 | tf_op jit(solution)/shard_map/ppermute | solution.py:927
  196.0 13.0 %copy-start.5 = (bf16[1024,1664]{1,0:T(8,128)(2,1)S(1)}, bf16[1024,1664]{1,0:T(8,128)(2,1)}, u32[]{:S(2)}) copy-start(bf16[1024,1664]{1,0:T(8,128)(2,1)} %copy-done.4) | copy-start | bytes 10223620
  206.3 2.8 collective-permute-start.15
  206.7 1.9 collective-permute-start.18
  206.8 2.2 collective-permute-start.16
  222.7 4.2 %collective-permute-start.19 = (bf16[2,4,64,2048]{3,2,1,0:T(8,128)(2,1)S(1)}, bf16[2,4,64,2048]{3,2,1,0:T(8,128)(2,1)S(1)}, u32[]{:S(2)}, u32[]{:S(2)}) collective-permute-start(bf16[2,4,64,2048]{3,2,1,0:T(8,128)(2,1)S(1)} %get-tuple-element.191), channel_id=1, source_target_pairs={{0,2},{2,0},{4,6},{6,4},{8,10},{10,8},{12,14},{14,12},{16,18},{18,... | collective-permute-start | bytes 6291464 | tf_op jit(solution)/shard_map/ppermute | solution.py:927
  223.6 48.2 %collective-permute-start.30 = (bf16[1024,1024]{1,0:T(8,128)(2,1)}, bf16[1024,1024]{1,0:T(8,128)(2,1)}, u32[]{:S(2)}, u32[]{:S(2)}) collective-permute-start(bf16[1024,1024]{1,0:T(8,128)(2,1)} %back.1.back_own), channel_id=1, source_target_pairs={{0,1},{1,0},{2,3},{3,2},{4,5},{5,4},{6,7},{7,6},{8,9},{9,8},{10,11... | collective-permute-start | bytes 6291464 | tf_op jit(solution)/shard_map/ppermute | solution.py:924
  224.1 4.7 %collective-permute-start.21 = (bf16[2,4,64,640]{3,2,1,0:T(8,128)(2,1)S(1)}, bf16[2,4,64,640]{3,2,1,0:T(8,128)(2,1)S(1)}, u32[]{:S(2)}, u32[]{:S(2)}) collective-permute-start(bf16[2,4,64,640]{3,2,1,0:T(8,128)(2,1)S(1)} %copy-done.39), channel_id=1, source_target_pairs={{0,2},{2,0},{4,6},{6,4},{8,10},{10,8},{12,14},{14,12},{16,18},{18,... | collective-permute-start | bytes 1966088 | tf_op jit(solution)/shard_map/ppermute | solution.py:927
  227.4 18.7 %collective-permute-start.20 = (bf16[2,64,2048]{2,1,0:T(8,128)(2,1)S(1)}, bf16[2,64,2048]{2,1,0:T(8,128)(2,1)S(1)}, u32[]{:S(2)}, u32[]{:S(2)}) collective-permute-start(bf16[2,64,2048]{2,1,0:T(8,128)(2,1)S(1)} %get-tuple-element.192), channel_id=1, source_target_pairs={{0,4},{2,6},{4,0},{6,2},{8,12},{10,14},{12,8},{14,10},{16,20},{18,... | collective-permute-start | bytes 1572872 | tf_op jit(solution)/shard_map/ppermute | solution.py:781
  229.6 16.6 %collective-permute-start.22 = (bf16[2,64,640]{2,1,0:T(8,128)(2,1)S(1)}, bf16[2,64,640]{2,1,0:T(8,128)(2,1)S(1)}, u32[]{:S(2)}, u32[]{:S(2)}) collective-permute-start(bf16[2,64,640]{2,1,0:T(8,128)(2,1)S(1)} %get-tuple-element.195), channel_id=1, source_target_pairs={{0,4},{2,6},{4,0},{6,2},{8,12},{10,14},{12,8},{14,10},{16,20},{18,... | collective-permute-start | bytes 491528 | tf_op jit(solution)/shard_map/ppermute | solution.py:781
  230.4 34.5 %collective-permute-start.26 = (bf16[2,64,2048]{2,1,0:T(8,128)(2,1)S(1)}, bf16[2,64,2048]{2,1,0:T(8,128)(2,1)S(1)}, u32[]{:S(2)}, u32[]{:S(2)}) collective-permute-start(bf16[2,64,2048]{2,1,0:T(8,128)(2,1)S(1)} %get-tuple-element.205), channel_id=1, source_target_pairs={{0,4},{2,6},{4,0},{6,2},{8,12},{10,14},{12,8},{14,10},{16,20},{18,... | collective-permute-start | bytes 1572872 | tf_op jit(solution)/shard_map/ppermute | solution.py:781
  236.4 35.3 %copy-start.13 = (bf16[1024,1024]{1,0:T(8,128)(2,1)S(1)}, bf16[1024,1024]{1,0:T(8,128)(2,1)}, u32[]{:S(2)}) copy-start(bf16[1024,1024]{1,0:T(8,128)(2,1)} %tokens.3) | copy-start | bytes 6291460
  246.3 18.6 %collective-permute-start.24 = (bf16[64,2688]{1,0:T(8,128)(2,1)S(1)}, bf16[64,2688]{1,0:T(8,128)(2,1)S(1)}, u32[]{:S(2)}, u32[]{:S(2)}) collective-permute-start(bf16[64,2688]{1,0:T(8,128)(2,1)S(1)} %get-tuple-element.203.first), channel_id=1, source_target_pairs={{0,8},{2,10},{4,12},{6,14},{1,9},{3,11},{5,13},{7,15}} | collective-permute-start | bytes 1032200 | tf_op jit(solution)/shard_map/ppermute | solution.py:813
  249.2 15.7 %collective-permute-start.25 = (bf16[64,2688]{1,0:T(8,128)(2,1)S(1)}, bf16[64,2688]{1,0:T(8,128)(2,1)S(1)}, u32[]{:S(2)}, u32[]{:S(2)}) collective-permute-start(bf16[64,2688]{1,0:T(8,128)(2,1)S(1)} %get-tuple-element.203.first), channel_id=1, source_target_pairs={{24,16},{26,18},{28,20},{30,22},{25,17},{27,19},{29,21},{31,23}} | collective-permute-start | bytes 1032200 | tf_op jit(solution)/shard_map/ppermute | solution.py:814
  249.8 15.0 %collective-permute-start.27 = (bf16[2,64,640]{2,1,0:T(8,128)(2,1)S(1)}, bf16[2,64,640]{2,1,0:T(8,128)(2,1)S(1)}, u32[]{:S(2)}, u32[]{:S(2)}) collective-permute-start(bf16[2,64,640]{2,1,0:T(8,128)(2,1)S(1)} %get-tuple-element.206), channel_id=1, source_target_pairs={{0,4},{2,6},{4,0},{6,2},{8,12},{10,14},{12,8},{14,10},{16,20},{18,... | collective-permute-start | bytes 491528 | tf_op jit(solution)/shard_map/ppermute | solution.py:781
  265.7 13.6 %collective-permute-start.29 = (bf16[64,2688]{1,0:T(8,128)(2,1)}, bf16[64,2688]{1,0:T(8,128)(2,1)}, u32[]{:S(2)}, u32[]{:S(2)}) collective-permute-start(bf16[64,2688]{1,0:T(8,128)(2,1)} %low_add.3), channel_id=1, source_target_pairs={{16,8},{18,10},{20,12},{22,14},{24,16},{26,18},{28,20},{30,22},{17... | collective-permute-start | bytes 1032200 | tf_op jit(solution)/shard_map/ppermute | solution.py:814
  267.9 11.4 %collective-permute-start.28 = (bf16[64,2688]{1,0:T(8,128)(2,1)}, bf16[64,2688]{1,0:T(8,128)(2,1)}, u32[]{:S(2)}, u32[]{:S(2)}) collective-permute-start(bf16[64,2688]{1,0:T(8,128)(2,1)} %low_add.2), channel_id=1, source_target_pairs={{0,8},{2,10},{4,12},{6,14},{8,16},{10,18},{12,20},{14,22},{1,9},{3... | collective-permute-start | bytes 1032200 | tf_op jit(solution)/shard_map/ppermute | solution.py:813
  280.8 10.5 %collective-permute-start.31 = (bf16[64,2688]{1,0:T(8,128)(2,1)S(1)}, bf16[64,2688]{1,0:T(8,128)(2,1)S(1)}, u32[]{:S(2)}, u32[]{:S(2)}) collective-permute-start(bf16[64,2688]{1,0:T(8,128)(2,1)S(1)} %get-tuple-element.220), channel_id=1, source_target_pairs={{0,8},{2,10},{4,12},{6,14},{8,16},{10,18},{12,20},{14,22},{16,24},... | collective-permute-start | bytes 1032200 | tf_op jit(solution)/shard_map/ppermute | solution.py:813
  285.3 10.4 %collective-permute-start.32 = (bf16[64,2688]{1,0:T(8,128)(2,1)S(1)}, bf16[64,2688]{1,0:T(8,128)(2,1)}, u32[]{:S(2)}, u32[]{:S(2)}) collective-permute-start(bf16[64,2688]{1,0:T(8,128)(2,1)S(1)} %get-tuple-element.221), channel_id=1, source_target_pairs={{8,0},{10,2},{12,4},{14,6},{16,8},{18,10},{20,12},{22,14},{24,16},... | collective-permute-start | bytes 1032200 | tf_op jit(solution)/shard_map/ppermute | solution.py:814
  298.3 3.6 %collective-permute-start.33 = (f32[2,64]{1,0:T(2,128)S(1)}, f32[2,64]{1,0:T(2,128)S(1)}, u32[]{:S(2)}, u32[]{:S(2)}) collective-permute-start(f32[2,64]{1,0:T(2,128)S(1)} %pad_maximum_fusion.5.own), channel_id=1, source_target_pairs={{0,1},{1,0},{2,3},{3,2},{4,5},{5,4},{6,7},{7,6},{8,9},{9,8},{10,11... | collective-permute-start | bytes 1544 | tf_op jit(solution)/shard_map/ppermute | solution.py:924
  (46 other events, 227.3 us)
Sparse Core Ops, SparseCore 0:
  16.1 95.6 all-gather.1
  169.2 97.6 reduce-scatter.1

commit v6 on v5

--- a/solution.py
+++ b/solution.py
@@ -141,7 +141,7 @@
     rows = normed.shape[0]
     return pl.pallas_call(
         second_kernel,
-        out_shape=jax.ShapeDtypeStruct((3, 2, rows, HEAD_DIM), BF),
+        out_shape=pltpu.HBM((3, 2, rows, HEAD_DIM), BF),
         grid_spec=pltpu.PrefetchScalarGridSpec(
             num_scalar_prefetch=1,
             grid=(3,),
@@ -469,10 +469,7 @@
     )(normed, upstream, weights, weights, weights, *earlier)
 
 
-DOWN_SPLIT = 768
-
-
-DOWN_SPLIT = 768
+DOWN_SPLIT = 1024
 
 
 def scatter(info, out, keep, send):
@@ -795,7 +792,8 @@
         if len(used) == 1 and step == 1:
             up = down = sums[used[0]]
         elif len(used) == 1:
-            up, down = low_add(sums[used[0]], below), low_add(sums[used[0]], above)
+            one = sums[used[0]]
+            up, down = chosen_add(jnp.ones((2,), jnp.int32), one, one, below, above)
         elif len(used) == 2:
             flags = jnp.stack(
                 [
@@ -808,13 +806,12 @@
             fill = lambda side: [sums[used[0] if slot is None else slot] for slot in side]
             up, down = choose(line, fill(ups)), choose(line, fill(downs))
             up, down = low_add(up, below), low_add(down, above)
-        if step == length - 1:
-            up, down, last_wait = pin((up, down, last_wait))
         below = lax.ppermute(up, "dp", [(i, i + 4) for i in range(count - 4) if i // 4 + gap < length])
         above = lax.ppermute(down, "dp", [(i, i - 4) for i in range(4, count) if i // 4 >= gap])
         if step == length // 2 - 1:
             below, above, others = pin((below, above, others))
             sums += split_add((mine_two, others[0]), (down_two, others[1]))
+    below, above, last_wait = pin((below, above, last_wait))
     return sums[-1], below, above, first_wait, last_wait
 
 
@@ -943,7 +940,6 @@
     lines = [[i for i in range(count) if i % 4 == lane] for lane in range(4)]
     own_column = lax.all_gather(shard_one, "dp", axis=0, tiled=True, axis_index_groups=lines)
     next_column = lax.ppermute(own_column, "dp", [(i, i ^ 2) for i in range(count)])
-    pieces = (own_column, next_column, beside(own_column), beside(next_column))
     weights_two = lax.all_gather(shard_two, "dp", axis=0, tiled=True)
 
     places = jnp.arange(SEG, dtype=jnp.int32)
@@ -958,9 +954,10 @@
     fetched = cache[retrieval[0]].reshape(RETR, 2, 2, 2, HEAD_DIM).transpose(2, 1, 3, 0, 4)
     mem_own = lax.dynamic_index_in_dim(fetched, rank, keepdims=False)
     mem_other = beside(lax.dynamic_index_in_dim(fetched, 1 - rank, keepdims=False))
-    pieces, mem_own, mem_other, bias, cosines, sines, info = pin(
-        (pieces, mem_own, mem_other, bias, cosines, sines, info)
-    )
+    next_column, mem_own, mem_other, bias, cosines, sines, info = pin(
+        (next_column, mem_own, mem_other, bias, cosines, sines, info)
+    )
+    pieces = (own_column, next_column, beside(own_column), beside(next_column))
     weights_one = interleave(info, pieces, shard)
 
     send, normed_one, gains = project_first(info, tokens, weights_one, cosines, sines)

time: 316 us -> 323 us (1.022)
  starting transfers between devices: 34.1 us -> 42.1 us
    ppermute x10, waiting for transfers between devices: 23.9 us -> 31.6 us  [across(): return lax.ppermute(value, 'mp', [(0, 1), (1, 0)])]
    ppermute x3, starting transfers between devices: 11 us -> 17.3 us  [reduce_rows(): lax.ppermute(up, 'dp', [(i, i + 4) for i in range(count - 4) if i // 4 +...]
    ppermute x1, waiting for transfers between devices: 7.57 us -> 3.06 us  [body(): lax.ppermute(own_column, 'dp', [(i, i ^ 2) for i in range(count)])]
    ppermute x3, waiting for transfers between devices: 4.25 us -> 0.01 us  [reduce_rows(): lax.ppermute(down, 'dp', [(i, i - 4) for i in range(4, count) if i // 4 >...]
    unnamed x120 -> x130, local copies, waits for them, and re-layouts: 10.6 us -> 12.1 us
  transfers between devices with their start and end apart: 36 -> 36, of which waited for: 14 -> 12; matrix products, arithmetic and copies ran while one was open for 8% -> 6% of each run, Pallas kernels for 37% -> 36%
where the time goes in v6:
time: 323 us; the launch traced here: 317 us
  Pallas kernels  129 us (40%)
  waiting for transfers between devices  67.1 us (21%)
  starting transfers between devices  42.1 us (13%)
  blocking collectives  26.8 us (8%)
  other arithmetic  20.7 us (6%)
  between operations  15.8 us (5%)
  local copies, waits for them, and re-layouts  15 us (5%)
    ppermute x10, waiting for transfers between devices, across(): return lax.ppermute(value, 'mp', [(0, 1), (1, 0)])  31.6 us
    all_gather x1, blocking collectives, body(): lax.all_gather(shard_one, 'dp', axis=0, tiled=True, axis_index_groups=lines)  26.8 us
    pallas_call x4, Pallas kernels, feed_call(): pl.pallas_call(feed_kernel, out_shape=(pltpu.VMEM((rows, width), BF),) *...  24.7 us
    ppermute x4, waiting for transfers between devices, reduce_rows(): over = lambda value: lax.ppermute(value, 'dp', pairs)  22 us
    pallas_call x2, Pallas kernels, attend_backward(): pl.pallas_call(backward_kernel, out_shape=tuple((jax.ShapeDtypeStruct((pa...  19.7 us
    ppermute x3, starting transfers between devices, reduce_rows(): lax.ppermute(up, 'dp', [(i, i + 4) for i in range(count - 4) if i // 4 +...  17.3 us
    pallas_call x3, Pallas kernels, residual_call(): pl.pallas_call(functools.partial(residual_kernel, count), out_shape=(pltp...  14.3 us
    pallas_call x1, Pallas kernels, feed_weight_call(): pl.pallas_call(feed_weight_kernel, out_shape=(pltpu.HBM((D, total), BF),)...  13.7 us
  transfers between devices with their start and end apart: 36, of which 12 were waited for; matrix products, arithmetic and copies ran while one was open for 6% of the time, Pallas kernels for 36%

profile of v6, /device:TPU:0, one launch (start us, length us, event | category | flops | bytes accessed | tf_op | source)
XLA Modules:
  0.0 316.9 jit_solution(9856166762834589437)
XLA Ops:
  8.4 3.0 collective-permute-start.8
  16.1 26.8 %all_gather.6 = bf16[256,1664]{1,0:T(8,128)(2,1)S(1)} all-gather(bf16[64,1664]{1,0:T(8,128)(2,1)S(1)} %shard.1), channel_id=1, replica_groups={{0,8,16,24},{2,10,18,26},{4,12,20,28},{6,14,22,30},{1,9,17,25},{3,11,19..., dimensions={0}, use_global_device_ids=true | all-gather | bytes 1064960 | tf_op jit(solution)/shard_map/all_gather | solution.py:941
  48.3 3.7 %fusion.3 = (f32[2048,64]{1,0:T(8,128)S(1)}, f32[2048,64]{1,0:T(8,128)S(1)}, f32[2048,64]{1,0:T(8,128)S(1)}) fusion(f32[64]{0:T(128)S(1)} %negate_power_fusion, f32[2048]{0:T(1024)S(1)} %iota_convert_fusion), kind=kLoop, calls=%fused_computation.27 | loop fusion | flops 262144 | bytes 1581312 | tf_op jit(solution)/shard_map/neg | solution.py:62
  54.8 1.7 copy.65
  56.5 3.1 collective-permute-done
  59.6 2.6 collective-permute-done.3
  62.2 1.8 interleave.1.gain_columns.weight.refs_6_
  64.3 4.9 %project_first.1 = (bf16[3,2,1024,128]{3,2,1,0:T(8,128)(2,1)S(1)}, bf16[1024,1024]{1,0:T(8,128)(2,1)S(1)}, f32[8,1024]{1,0:T(8,128)S(1)}) custom-call(s32[5]{0:T(128)S(1)} %stack.66.info, bf16[1024,1024]{1,0:T(8,128)(2,1)S(1)} %copy-done.14, bf16[1024,1664]{1,0:T(8,128)(2,1)S(1)} %interleave.1.gain_columns.weight.refs_6_, ...), custom_call_target="tpu_custom_call" | custom-call | tf_op jit(solution)/shard_map/project_first/pallas_call | solution.py:111
  69.4 4.5 %project_second.1.own = bf16[3,2,1024,128]{3,2,1,0:T(8,128)(2,1)} custom-call(s32[5]{0:T(128)S(1)} %stack.66.info, bf16[1024,1024]{1,0:T(8,128)(2,1)S(1)} %get-tuple-element.126.normed, bf16[1024,1664]{1,0:T(8,128)(2,1)S(1)} %interleave.1.gain_columns.weight.refs_6_, f32[2048,128]{1,0:T(8,128)S(1)} %get-tuple-element.124.cosines, ...), custom_call_target="tpu_custom_call" | custom-call | tf_op jit(solution)/shard_map/project_second/pallas_call | solution.py:142
  74.0 1.4 copy-done.12
  75.4 12.7 %attend_forward.1 = (bf16[2,1024,128]{2,1,0:T(8,128)(2,1)S(1)}, bf16[2,1024,128]{2,1,0:T(8,128)(2,1)S(1)}, f32[2,128,2048]{2,1,0:T(8,128)}, f32[2,1,2048]{2,1,0:T(1,128)S(1)}) custom-call(s32[5]{0:T(128)S(1)} %stack.66.info, bf16[3,2,1024,128]{3,2,1,0:T(8,128)(2,1)S(1)} %copy-done.12, bf16[3,2,1024,128]{3,2,1,0:T(8,128)(2,1)S(1)} %collective-permute-done.4.other, ...), custom_call_target="tpu_custom_call" | custom-call | tf_op jit(solution)/shard_map/attend_forward/pallas_call | solution.py:234
  88.5 1.5 collective-permute-done.5.refs_1_
  91.1 12.1 %collective-permute-done.6.refs_2_ = bf16[2,1024,128]{2,1,0:T(8,128)(2,1)S(1)} collective-permute-done((bf16[2,1024,128]{2,1,0:T(8,128)(2,1)S(1)}, bf16[2,1024,128]{2,1,0:T(8,128)(2,1)S(1)}, u32[]{:S(2)}, u32[]{:S(2)}) %collective-permute-start.6) | collective-permute-done | bytes 524320 | tf_op jit(solution)/shard_map/ppermute | solution.py:921
  104.0 9.7 %collective-permute-done.7.refs_3_ = bf16[2,1024,128]{2,1,0:T(8,128)(2,1)} collective-permute-done((bf16[2,1024,128]{2,1,0:T(8,128)(2,1)S(1)}, bf16[2,1024,128]{2,1,0:T(8,128)(2,1)}, u32[]{:S(2)}, u32[]{:S(2)}) %collective-permute-start.7) | collective-permute-done | bytes 524320 | tf_op jit(solution)/shard_map/ppermute | solution.py:921
  113.8 10.2 %middle.1 = (f32[1024,1024]{1,0:T(8,128)}, bf16[1024,1024]{1,0:T(8,128)(2,1)S(1)}, bf16[1024,512]{1,0:T(8,128)(2,1)}) custom-call(s32[5]{0:T(128)S(1)} %stack.66.info, bf16[2,1024,128]{2,1,0:T(8,128)(2,1)} %copy-done.31, bf16[2,1024,128]{2,1,0:T(8,128)(2,1)} %copy-done.51, bf16[2,1024,128]{2,1,0:T(8,128)(2,1)} %copy-done.52, ...), custom_call_target="tpu_custom_call" | custom-call | tf_op jit(solution)/shard_map/middle/pallas_call | solution.py:409
  124.0 5.5 %feed.4 = (bf16[1024,1408]{1,0:T(8,128)(2,1)S(1)}, bf16[1024,1408]{1,0:T(8,128)(2,1)S(1)}, bf16[1024,1408]{1,0:T(8,128)(2,1)S(1)}, bf16[1024,1024]{1,0:T(8,128)(2,1)S(1)}, bf16[256,1024]{1,0:T(8,128)(2,1)S(1)}) custom-call(bf16[1024,1024]{1,0:T(8,128)(2,1)S(1)} %get-tuple-element.135.normed, bf16[1024,1024]{1,0:T(8,128)(2,1)S(1)} %copy-done.3, ...), custom_call_target="tpu_custom_call" | custom-call | flops 50000000 | tf_op jit(solution)/shard_map/feed/pallas_call | solution.py:457
  129.8 6.3 %feed.5 = (bf16[1024,1408]{1,0:T(8,128)(2,1)S(1)}, bf16[1024,1408]{1,0:T(8,128)(2,1)S(1)}, bf16[1024,1408]{1,0:T(8,128)(2,1)S(1)}, bf16[1024,1024]{1,0:T(8,128)(2,1)S(1)}, bf16[256,1024]{1,0:T(8,128)(2,1)}) custom-call(bf16[1024,1024]{1,0:T(8,128)(2,1)S(1)} %get-tuple-element.135.normed, ...), custom_call_target="tpu_custom_call", output_to_operand_aliasing={{0}: (5, {}), {1}: (6, {}), {2}: (7, {}), {3}: (8, {})} | custom-call | flops 50000000 | tf_op jit(solution)/shard_map/feed/pallas_call | solution.py:457
  136.2 1.8 collective-permute-start.12
  137.9 6.5 %feed.6 = (bf16[1024,1408]{1,0:T(8,128)(2,1)S(1)}, bf16[1024,1408]{1,0:T(8,128)(2,1)S(1)}, bf16[1024,1408]{1,0:T(8,128)(2,1)S(1)}, bf16[1024,1024]{1,0:T(8,128)(2,1)S(1)}, bf16[256,1024]{1,0:T(8,128)(2,1)}) custom-call(bf16[1024,1024]{1,0:T(8,128)(2,1)S(1)} %get-tuple-element.135.normed, ...), custom_call_target="tpu_custom_call", output_to_operand_aliasing={{0}: (5, {}), {1}: (6, {}), {2}: (7, {}), {3}: (8, {})} | custom-call | flops 50000000 | tf_op jit(solution)/shard_map/feed/pallas_call | solution.py:457
  144.7 6.3 %feed.7 = (bf16[1024,1408]{1,0:T(8,128)(2,1)S(1)}, bf16[1024,1408]{1,0:T(8,128)(2,1)S(1)}, bf16[1024,1408]{1,0:T(8,128)(2,1)S(1)}, bf16[1024,1024]{1,0:T(8,128)(2,1)S(1)}, bf16[256,1024]{1,0:T(8,128)(2,1)}) custom-call(bf16[1024,1024]{1,0:T(8,128)(2,1)S(1)} %get-tuple-element.135.normed, ...), custom_call_target="tpu_custom_call", output_to_operand_aliasing={{0}: (5, {}), {1}: (6, {}), {2}: (7, {}), {3}: (8, {})} | custom-call | flops 50000000 | tf_op jit(solution)/shard_map/feed/pallas_call | solution.py:457
  151.1 1.8 collective-permute-start.10
  152.8 13.7 %feed_weights.1 = (bf16[1024,3840]{1,0:T(8,128)(2,1)}, bf16[2,4,64,384]{3,2,1,0:T(8,128)(2,1)S(1)}, bf16[2,4,64,384]{3,2,1,0:T(8,128)(2,1)S(1)}) custom-call(s32[5]{0:T(128)S(1)} %stack.66.info, bf16[1024,1024]{1,0:T(8,128)(2,1)S(1)} %get-tuple-element.135.normed, bf16[1024,1024]{1,0:T(8,128)(2,1)} %upstream.15, ...), custom_call_target="tpu_custom_call" | custom-call | flops 50000000 | tf_op jit(solution)/shard_map/feed_weights/pallas_call | solution.py:504
  168.3 5.2 %residual.3 = (f32[1024,1024]{1,0:T(8,128)}, bf16[1024,1024]{1,0:T(8,128)(2,1)S(1)}, bf16[2,1024,128]{2,1,0:T(8,128)(2,1)S(1)}, bf16[1,1024,128]{2,1,0:T(8,128)(2,1)S(1)}, bf16[1,1024,128]{2,1,0:T(8,128)(2,1)S(1)}) custom-call(s32[5]{0:T(128)S(1)} %stack.66.info, f32[1024,1024]{1,0:T(8,128)} %get-tuple-element.134.middle, bf16[1024,1024]{1,0:T(8,128)(2,1)} %upstream.15, ...), custom_call_target="tpu_custom_call" | custom-call | flops 50000000 | tf_op jit(solution)/shard_map/residual/pallas_call | solution.py:552
  173.6 4.2 %residual.4 = (f32[1024,1024]{1,0:T(8,128)}, bf16[1024,1024]{1,0:T(8,128)(2,1)S(1)}, bf16[2,1024,128]{2,1,0:T(8,128)(2,1)S(1)}, bf16[1,1024,128]{2,1,0:T(8,128)(2,1)S(1)}, bf16[1,1024,128]{2,1,0:T(8,128)(2,1)S(1)}) custom-call(s32[5]{0:T(128)S(1)} %stack.66.info, ...), custom_call_target="tpu_custom_call", output_to_operand_aliasing={{0}: (7, {}), {1}: (8, {}), {2}: (9, {}), {3}: (10, {}), {4... | custom-call | flops 50000000 | tf_op jit(solution)/shard_map/residual/pallas_call | solution.py:552
  177.9 4.8 %residual.5 = (f32[1024,1024]{1,0:T(8,128)}, bf16[1024,1024]{1,0:T(8,128)(2,1)S(1)}, bf16[2,1024,128]{2,1,0:T(8,128)(2,1)S(1)}, bf16[1,1024,128]{2,1,0:T(8,128)(2,1)S(1)}, bf16[1,1024,128]{2,1,0:T(8,128)(2,1)S(1)}) custom-call(s32[5]{0:T(128)S(1)} %stack.66.info, ...), custom_call_target="tpu_custom_call", output_to_operand_aliasing={{0}: (7, {}), {1}: (8, {}), {2}: (9, {}), {3}: (10, {}), {4... | custom-call | flops 299999985664 | tf_op jit(solution)/shard_map/residual/pallas_call | solution.py:552
  184.3 9.5 %attend_backward.3 = (bf16[3,1,1024,128]{3,2,1,0:T(8,128)(2,1)S(1)}, bf16[2,1,1024,128]{3,2,1,0:T(8,128)(2,1)S(1)}, bf16[1,1,1024,128]{3,2,1,0:T(8,128)(2,1)S(1)}) custom-call(s32[5]{0:T(128)S(1)} %stack.66.info, bf16[3,2,1024,128]{3,2,1,0:T(8,128)(2,1)S(1)} %copy-done.13, bf16[3,2,1024,128]{3,2,1,0:T(8,128)(2,1)S(1)} %copy-done.18, ...), custom_call_target="tpu_custom_call" | custom-call | tf_op jit(solution)/shard_map/attend_backward/pallas_call | solution.py:335
  194.0 10.2 %attend_backward.2 = (bf16[3,1,1024,128]{3,2,1,0:T(8,128)(2,1)S(1)}, bf16[2,1,1024,128]{3,2,1,0:T(8,128)(2,1)S(1)}, bf16[1,1,1024,128]{3,2,1,0:T(8,128)(2,1)S(1)}) custom-call(s32[5]{0:T(128)S(1)} %stack.66.info, bf16[3,2,1024,128]{3,2,1,0:T(8,128)(2,1)S(1)} %copy-done.13, bf16[3,2,1024,128]{3,2,1,0:T(8,128)(2,1)S(1)} %copy-done.18, ...), custom_call_target="tpu_custom_call" | custom-call | tf_op jit(solution)/shard_map/attend_backward/pallas_call | solution.py:335
  205.1 1.4 collective-permute-done.18.refs_5_
  206.9 6.3 %back.1.back_own = bf16[1024,1024]{1,0:T(8,128)(2,1)} custom-call(s32[5]{0:T(128)S(1)} %stack.66.info, bf16[3,1,1024,128]{3,2,1,0:T(8,128)(2,1)S(1)} %get-tuple-element.184.refs_0_, bf16[3,1,1024,128]{3,2,1,0:T(8,128)(2,1)S(1)} %get-tuple-element.179.refs_1_, bf16[2,1,1024,128]{3,2,1,0:T(8,128)(2,1)S(1)} %collective-permute-done.15.refs_2_, ...), custom_call_target="tpu_custom_call" | custom-call | tf_op jit(solution)/shard_map/back/pallas_call | solution.py:607
  213.2 7.3 %attend_weights.1 = (bf16[2,4,64,2048]{3,2,1,0:T(8,128)(2,1)S(1)}, bf16[2,4,64,2048]{3,2,1,0:T(8,128)(2,1)S(1)}) custom-call(s32[5]{0:T(128)S(1)} %stack.66.info, bf16[1024,1024]{1,0:T(8,128)(2,1)S(1)} %copy-done.23, bf16[1024,1024]{1,0:T(8,128)(2,1)S(1)} %get-tuple-element.172.low, bf16[3,1,1024,128]{3,2,1,0:T(8,128)(2,1)S(1)} %get-tuple-element.184.refs_0_, ...), custom_call_target="tpu_custom_call" | custom-call | tf_op jit(solution)/shard_map/attend_weights/pallas_call | solution.py:650
  221.0 9.7 %collective-permute-done.23 = bf16[1024,1024]{1,0:T(8,128)(2,1)S(1)} collective-permute-done((bf16[1024,1024]{1,0:T(8,128)(2,1)S(1)}, bf16[1024,1024]{1,0:T(8,128)(2,1)S(1)}, u32[]{:S(2)}, u32[]{:S(2)}) %collective-permute-start.23) | collective-permute-done | bytes 2097184 | tf_op jit(solution)/shard_map/ppermute | solution.py:921
  231.5 1.7 collective-permute-start.20
  235.4 2.5 add_convert_fusion
  238.0 11.9 %collective-permute-done.22.right_two = bf16[2,64,384]{2,1,0:T(8,128)(2,1)S(1)} collective-permute-done((bf16[2,64,384]{2,1,0:T(8,128)(2,1)S(1)}, bf16[2,64,384]{2,1,0:T(8,128)(2,1)S(1)}, u32[]{:S(2)}, u32[]{:S(2)}) %collective-permute-start.22) | collective-permute-done | bytes 98336 | tf_op jit(solution)/shard_map/ppermute | solution.py:778
  250.0 3.5 %collective-permute-start.24 = (bf16[64,2432]{1,0:T(8,128)(2,1)S(1)}, bf16[64,2432]{1,0:T(8,128)(2,1)S(1)}, u32[]{:S(2)}, u32[]{:S(2)}) collective-permute-start(bf16[64,2432]{1,0:T(8,128)(2,1)S(1)} %get-tuple-element.199.first), channel_id=1, source_target_pairs={{0,8},{2,10},{4,12},{6,14},{1,9},{3,11},{5,13},{7,15}} | collective-permute-start | bytes 933896 | tf_op jit(solution)/shard_map/ppermute | solution.py:809
  254.2 2.3 collective-permute-start.27
  256.5 10.1 %collective-permute-done.27.right_two = bf16[2,64,384]{2,1,0:T(8,128)(2,1)S(1)} collective-permute-done((bf16[2,64,384]{2,1,0:T(8,128)(2,1)S(1)}, bf16[2,64,384]{2,1,0:T(8,128)(2,1)S(1)}, u32[]{:S(2)}, u32[]{:S(2)}) %collective-permute-start.27) | collective-permute-done | bytes 98336 | tf_op jit(solution)/shard_map/ppermute | solution.py:778
  266.7 1.5 chosen_add.2
  268.2 4.3 %collective-permute-start.28 = (bf16[64,2432]{1,0:T(8,128)(2,1)}, bf16[64,2432]{1,0:T(8,128)(2,1)}, u32[]{:S(2)}, u32[]{:S(2)}) collective-permute-start(bf16[64,2432]{1,0:T(8,128)(2,1)} %get-tuple-element.210), channel_id=1, source_target_pairs={{0,8},{2,10},{4,12},{6,14},{8,16},{10,18},{12,20},{14,22},{1,9},{3... | collective-permute-start | bytes 933896 | tf_op jit(solution)/shard_map/ppermute | solution.py:809
  272.5 1.4 collective-permute-start.29
  275.0 3.7 %collective-permute-done.28.up_in = bf16[64,2432]{1,0:T(8,128)(2,1)} collective-permute-done((bf16[64,2432]{1,0:T(8,128)(2,1)}, bf16[64,2432]{1,0:T(8,128)(2,1)}, u32[]{:S(2)}, u32[]{:S(2)}) %collective-permute-start.28) | collective-permute-done | bytes 311328 | tf_op jit(solution)/shard_map/ppermute | solution.py:809
  280.0 9.5 %collective-permute-start.30 = (bf16[64,2432]{1,0:T(8,128)(2,1)S(1)}, bf16[64,2432]{1,0:T(8,128)(2,1)S(1)}, u32[]{:S(2)}, u32[]{:S(2)}) collective-permute-start(bf16[64,2432]{1,0:T(8,128)(2,1)S(1)} %get-tuple-element.212), channel_id=1, source_target_pairs={{0,8},{2,10},{4,12},{6,14},{8,16},{10,18},{12,20},{14,22},{16,24},... | collective-permute-start | bytes 933896 | tf_op jit(solution)/shard_map/ppermute | solution.py:809
  289.5 1.5 collective-permute-start.31
  291.0 2.2 copy-done.16
  293.2 5.0 %input_grad.1 = bf16[1024,1024]{1,0:T(8,128)(2,1)} custom-call(f32[1024,1024]{1,0:T(8,128)S(1)} %copy-done.16, bf16[1024,1024]{1,0:T(8,128)(2,1)} %back.1.back_own, bf16[1024,1024]{1,0:T(8,128)(2,1)} %collective-permute-done.32.back_other, bf16[1024,1024]{1,0:T(8,128)(2,1)S(1)} %copy-done.15, f32[1,1024]{1,0:T(1,128)S(1)} %copy-done.36), custom_call_target="tpu_custom_call" | custom-call | flops 12582912 | bytes 12582912 | tf_op jit(solution)/shard_map/input_grad/pallas_call | solution.py:680
  300.2 1.8 multiply_subtract_fusion
  303.5 1.3 multiply_subtract_fusion.1
  304.9 2.4 collective-permute-start.33
  (218 shorter events, 34.1 us)
Async XLA Ops:
  7.2 37.0 %copy-start = (bf16[1024,2,512]{2,1,0:T(2,128)(2,1)S(1)}, bf16[1024,2,512]{2,1,0:T(2,128)(2,1)}, u32[]{:S(2)}) copy-start(bf16[1024,2,512]{2,1,0:T(2,128)(2,1)} %param.38) | copy-start | bytes 6291460
  7.3 106.5 %all-gather.2.cloned.1.call-start = ((), (), s32[]{:S(2)}) async-start(), calls=%async_computation.1 | async-start | bytes 11419648 | tf_op jit(solution)/shard_map/all_gather | solution.py:943
  8.4 6.3 %collective-permute-start.8 = (bf16[64,512]{1,0:T(8,128)(2,1)S(1)}, bf16[64,512]{1,0:T(8,128)(2,1)S(1)}, u32[]{:S(2)}, u32[]{:S(2)}) collective-permute-start(bf16[64,512]{1,0:T(8,128)(2,1)S(1)} %convert_bitcast_fusion), channel_id=1, source_target_pairs={{0,1},{1,0},{2,3},{3,2},{4,5},{5,4},{6,7},{7,6},{8,9},{9,8},{10,11... | collective-permute-start | bytes 196616 | tf_op jit(solution)/shard_map/ppermute | solution.py:921
  12.6 31.6 %copy-start.62 = (s32[1,128]{1,0:T(1,128)S(1)}, s32[1,128]{1,0:T(1,128)}, u32[]{:S(2)}) copy-start(s32[1,128]{1,0:T(1,128)} %param.41) | copy-start | bytes 1540
  16.0 283.0 %reduce-scatter.2.cloned.1.call-start = ((), (), s32[]{:S(2)}) async-start(), calls=%async_computation.2 | async-start | bytes 8355840 | tf_op jit(solution)/shard_map/reduce_scatter | solution.py:1017
  42.9 16.7 %collective-permute-start = (bf16[256,1664]{1,0:T(8,128)(2,1)S(1)}, bf16[256,1664]{1,0:T(8,128)(2,1)}, u32[]{:S(2)}, u32[]{:S(2)}) collective-permute-start(bf16[256,1664]{1,0:T(8,128)(2,1)S(1)} %all_gather.6), channel_id=1, source_target_pairs={{0,4},{2,6},{4,0},{6,2},{8,12},{10,14},{12,8},{14,10},{16,20},{18,... | collective-permute-start | bytes 2555912 | tf_op jit(solution)/shard_map/ppermute | solution.py:942
  44.2 15.4 %collective-permute-start.2 = (bf16[256,1664]{1,0:T(8,128)(2,1)S(1)}, bf16[256,1664]{1,0:T(8,128)(2,1)}, u32[]{:S(2)}, u32[]{:S(2)}) collective-permute-start(bf16[256,1664]{1,0:T(8,128)(2,1)S(1)} %all_gather.6), channel_id=1, source_target_pairs={{0,2},{2,0},{4,6},{6,4},{8,10},{10,8},{12,14},{14,12},{16,18},{18,... | collective-permute-start | bytes 2555912 | tf_op jit(solution)/shard_map/ppermute | solution.py:924
  47.1 9.5 %collective-permute-start.1 = (bf16[2,2,128,128]{3,2,1,0:T(8,128)(2,1)}, bf16[2,2,128,128]{3,2,1,0:T(8,128)(2,1)}, u32[]{:S(2)}, u32[]{:S(2)}) collective-permute-start(bf16[2,2,128,128]{3,2,1,0:T(8,128)(2,1)} %bitcast.6), channel_id=1, source_target_pairs={{0,2},{2,0},{4,6},{6,4},{8,10},{10,8},{12,14},{14,12},{16,18},{18,... | collective-permute-start | bytes 393224 | tf_op jit(solution)/shard_map/ppermute | solution.py:924
  52.4 21.6 %copy-start.20 = (bf16[2048,128]{1,0:T(8,128)(2,1)}, bf16[2048,128]{1,0:T(8,128)(2,1)S(1)}, u32[]{:S(2)}) copy-start(bf16[2048,128]{1,0:T(8,128)(2,1)S(1)} %select_convert_fusion.bias) | copy-start | bytes 1572868
  53.0 16.4 %copy-start.8 = (f32[2048,128]{1,0:T(8,128)}, f32[2048,128]{1,0:T(8,128)S(1)}, u32[]{:S(2)}) copy-start(f32[2048,128]{1,0:T(8,128)S(1)} %get-tuple-element.124.cosines) | copy-start | bytes 3145732
  53.0 16.4 %copy-start.10 = (f32[2048,128]{1,0:T(8,128)}, f32[2048,128]{1,0:T(8,128)S(1)}, u32[]{:S(2)}) copy-start(f32[2048,128]{1,0:T(8,128)S(1)} %get-tuple-element.125.sines) | copy-start | bytes 3145732
  59.6 2.6 collective-permute-start.3
  69.2 4.7 %collective-permute-start.4 = (bf16[3,2,1024,128]{3,2,1,0:T(8,128)(2,1)S(1)}, bf16[3,2,1024,128]{3,2,1,0:T(8,128)(2,1)S(1)}, u32[]{:S(2)}, u32[]{:S(2)}) collective-permute-start(bf16[3,2,1024,128]{3,2,1,0:T(8,128)(2,1)S(1)} %get-tuple-element.127), channel_id=1, source_target_pairs={{0,2},{2,0},{4,6},{6,4},{8,10},{10,8},{12,14},{14,12},{16,18},{18,... | collective-permute-start | bytes 4718600 | tf_op jit(solution)/shard_map/ppermute | solution.py:924
  88.1 25.7 %copy-start.31 = (bf16[2,1024,128]{2,1,0:T(8,128)(2,1)}, bf16[2,1024,128]{2,1,0:T(8,128)(2,1)S(1)}, u32[]{:S(2)}) copy-start(bf16[2,1024,128]{2,1,0:T(8,128)(2,1)S(1)} %get-tuple-element.131.refs_0_) | copy-start | bytes 1572868
  88.1 1.9 collective-permute-start.5
  88.5 14.8 %collective-permute-start.6 = (bf16[2,1024,128]{2,1,0:T(8,128)(2,1)S(1)}, bf16[2,1024,128]{2,1,0:T(8,128)(2,1)S(1)}, u32[]{:S(2)}, u32[]{:S(2)}) collective-permute-start(bf16[2,1024,128]{2,1,0:T(8,128)(2,1)S(1)} %get-tuple-element.131.refs_0_), channel_id=1, source_target_pairs={{0,1},{1,0},{2,3},{3,2},{4,5},{5,4},{6,7},{7,6},{8,9},{9,8},{10,11... | collective-permute-start | bytes 1572872 | tf_op jit(solution)/shard_map/ppermute | solution.py:921
  90.0 13.2 %copy-start.51 = (bf16[2,1024,128]{2,1,0:T(8,128)(2,1)}, bf16[2,1024,128]{2,1,0:T(8,128)(2,1)S(1)}, u32[]{:S(2)}) copy-start(bf16[2,1024,128]{2,1,0:T(8,128)(2,1)S(1)} %collective-permute-done.5.refs_1_) | copy-start | bytes 1572868
  90.0 23.8 %collective-permute-start.7 = (bf16[2,1024,128]{2,1,0:T(8,128)(2,1)S(1)}, bf16[2,1024,128]{2,1,0:T(8,128)(2,1)}, u32[]{:S(2)}, u32[]{:S(2)}) collective-permute-start(bf16[2,1024,128]{2,1,0:T(8,128)(2,1)S(1)} %collective-permute-done.5.refs_1_), channel_id=1, source_target_pairs={{0,1},{1,0},{2,3},{3,2},{4,5},{5,4},{6,7},{7,6},{8,9},{9,8},{10,11... | collective-permute-start | bytes 1572872 | tf_op jit(solution)/shard_map/ppermute | solution.py:921
  129.5 15.2 %collective-permute-start.9 = (bf16[256,1024]{1,0:T(8,128)(2,1)S(1)}, bf16[256,1024]{1,0:T(8,128)(2,1)S(1)}, u32[]{:S(2)}, u32[]{:S(2)}) collective-permute-start(bf16[256,1024]{1,0:T(8,128)(2,1)S(1)} %get-tuple-element.159.refs_0_), channel_id=1, source_target_pairs={{0,1},{1,0},{2,3},{3,2},{4,5},{5,4},{6,7},{7,6},{8,9},{9,8},{10,11... | collective-permute-start | bytes 1572872 | tf_op jit(solution)/shard_map/ppermute | solution.py:921
  136.2 31.1 %collective-permute-start.12 = (bf16[256,1024]{1,0:T(8,128)(2,1)}, bf16[256,1024]{1,0:T(8,128)(2,1)}, u32[]{:S(2)}, u32[]{:S(2)}) collective-permute-start(bf16[256,1024]{1,0:T(8,128)(2,1)} %get-tuple-element.160.refs_1_), channel_id=1, source_target_pairs={{0,1},{1,0},{2,3},{3,2},{4,5},{5,4},{6,7},{7,6},{8,9},{9,8},{10,11... | collective-permute-start | bytes 1572872 | tf_op jit(solution)/shard_map/ppermute | solution.py:921
  144.4 29.1 %collective-permute-start.11 = (bf16[256,1024]{1,0:T(8,128)(2,1)}, bf16[256,1024]{1,0:T(8,128)(2,1)}, u32[]{:S(2)}, u32[]{:S(2)}) collective-permute-start(bf16[256,1024]{1,0:T(8,128)(2,1)} %get-tuple-element.154.refs_0_), channel_id=1, source_target_pairs={{0,1},{1,0},{2,3},{3,2},{4,5},{5,4},{6,7},{7,6},{8,9},{9,8},{10,11... | collective-permute-start | bytes 1572872 | tf_op jit(solution)/shard_map/ppermute | solution.py:921
  151.1 15.5 %copy-start.6 = (bf16[1024,1024]{1,0:T(8,128)(2,1)}, bf16[1024,1024]{1,0:T(8,128)(2,1)S(1)}, u32[]{:S(2)}) copy-start(bf16[1024,1024]{1,0:T(8,128)(2,1)S(1)} %get-tuple-element.192) | copy-start | bytes 6291460
  151.1 26.7 %collective-permute-start.10 = (bf16[256,1024]{1,0:T(8,128)(2,1)}, bf16[256,1024]{1,0:T(8,128)(2,1)S(1)}, u32[]{:S(2)}, u32[]{:S(2)}) collective-permute-start(bf16[256,1024]{1,0:T(8,128)(2,1)} %get-tuple-element.153.refs_0_), channel_id=1, source_target_pairs={{0,1},{1,0},{2,3},{3,2},{4,5},{5,4},{6,7},{7,6},{8,9},{9,8},{10,11... | collective-permute-start | bytes 1572872 | tf_op jit(solution)/shard_map/ppermute | solution.py:921
  182.7 1.5 collective-permute-start.14
  182.7 11.3 %collective-permute-start.13 = (bf16[1,1024,128]{2,1,0:T(8,128)(2,1)S(1)}, bf16[1,1024,128]{2,1,0:T(8,128)(2,1)S(1)}, u32[]{:S(2)}, u32[]{:S(2)}) collective-permute-start(bf16[1,1024,128]{2,1,0:T(8,128)(2,1)S(1)} %get-tuple-element.174), channel_id=1, source_target_pairs={{0,2},{2,0},{4,6},{6,4},{8,10},{10,8},{12,14},{14,12},{16,18},{18,... | collective-permute-start | bytes 786440 | tf_op jit(solution)/shard_map/ppermute | solution.py:924
  183.2 47.5 %collective-permute-start.23 = (bf16[1024,1024]{1,0:T(8,128)(2,1)S(1)}, bf16[1024,1024]{1,0:T(8,128)(2,1)S(1)}, u32[]{:S(2)}, u32[]{:S(2)}) collective-permute-start(bf16[1024,1024]{1,0:T(8,128)(2,1)S(1)} %copy-done.7), channel_id=1, source_target_pairs={{0,1},{1,0},{2,3},{3,2},{4,5},{5,4},{6,7},{7,6},{8,9},{9,8},{10,11... | collective-permute-start | bytes 6291464 | tf_op jit(solution)/shard_map/ppermute | solution.py:921
  193.8 13.2 %collective-permute-start.17 = (bf16[2,1,1024,128]{3,2,1,0:T(8,128)(2,1)S(1)}, bf16[2,1,1024,128]{3,2,1,0:T(8,128)(2,1)S(1)}, u32[]{:S(2)}, u32[]{:S(2)}) collective-permute-start(bf16[2,1,1024,128]{3,2,1,0:T(8,128)(2,1)S(1)} %get-tuple-element.182), channel_id=1, source_target_pairs={{0,2},{2,0},{4,6},{6,4},{8,10},{10,8},{12,14},{14,12},{16,18},{18,... | collective-permute-start | bytes 1572872 | tf_op jit(solution)/shard_map/ppermute | solution.py:924
  204.2 2.8 collective-permute-start.15
  204.6 1.9 collective-permute-start.18
  204.7 2.2 collective-permute-start.16
  213.2 17.8 %copy-start.42 = (bf16[2,4,64,384]{3,2,1,0:T(8,128)(2,1)S(1)}, bf16[2,4,64,384]{3,2,1,0:T(8,128)(2,1)}, u32[]{:S(2)}) copy-start(bf16[2,4,64,384]{3,2,1,0:T(8,128)(2,1)} %copy-done.41) | copy-start | bytes 1179652
  220.6 10.5 %collective-permute-start.19 = (bf16[2,4,64,2048]{3,2,1,0:T(8,128)(2,1)S(1)}, bf16[2,4,64,2048]{3,2,1,0:T(8,128)(2,1)S(1)}, u32[]{:S(2)}, u32[]{:S(2)}) collective-permute-start(bf16[2,4,64,2048]{3,2,1,0:T(8,128)(2,1)S(1)} %get-tuple-element.187), channel_id=1, source_target_pairs={{0,2},{2,0},{4,6},{6,4},{8,10},{10,8},{12,14},{14,12},{16,18},{18,... | collective-permute-start | bytes 6291464 | tf_op jit(solution)/shard_map/ppermute | solution.py:924
  230.8 60.2 %collective-permute-start.32 = (bf16[1024,1024]{1,0:T(8,128)(2,1)}, bf16[1024,1024]{1,0:T(8,128)(2,1)}, u32[]{:S(2)}, u32[]{:S(2)}) collective-permute-start(bf16[1024,1024]{1,0:T(8,128)(2,1)} %back.1.back_own), channel_id=1, source_target_pairs={{0,1},{1,0},{2,3},{3,2},{4,5},{5,4},{6,7},{7,6},{8,9},{9,8},{10,11... | collective-permute-start | bytes 6291464 | tf_op jit(solution)/shard_map/ppermute | solution.py:921
  231.0 2.2 collective-permute-start.21
  231.5 18.3 %collective-permute-start.20 = (bf16[2,64,2048]{2,1,0:T(8,128)(2,1)S(1)}, bf16[2,64,2048]{2,1,0:T(8,128)(2,1)S(1)}, u32[]{:S(2)}, u32[]{:S(2)}) collective-permute-start(bf16[2,64,2048]{2,1,0:T(8,128)(2,1)S(1)} %get-tuple-element.188), channel_id=1, source_target_pairs={{0,4},{2,6},{4,0},{6,2},{8,12},{10,14},{12,8},{14,10},{16,20},{18,... | collective-permute-start | bytes 1572872 | tf_op jit(solution)/shard_map/ppermute | solution.py:778
  233.4 16.5 %collective-permute-start.22 = (bf16[2,64,384]{2,1,0:T(8,128)(2,1)S(1)}, bf16[2,64,384]{2,1,0:T(8,128)(2,1)S(1)}, u32[]{:S(2)}, u32[]{:S(2)}) collective-permute-start(bf16[2,64,384]{2,1,0:T(8,128)(2,1)S(1)} %get-tuple-element.191), channel_id=1, source_target_pairs={{0,4},{2,6},{4,0},{6,2},{8,12},{10,14},{12,8},{14,10},{16,20},{18,... | collective-permute-start | bytes 294920 | tf_op jit(solution)/shard_map/ppermute | solution.py:778
  234.6 32.1 %collective-permute-start.26 = (bf16[2,64,2048]{2,1,0:T(8,128)(2,1)S(1)}, bf16[2,64,2048]{2,1,0:T(8,128)(2,1)S(1)}, u32[]{:S(2)}, u32[]{:S(2)}) collective-permute-start(bf16[2,64,2048]{2,1,0:T(8,128)(2,1)S(1)} %get-tuple-element.201), channel_id=1, source_target_pairs={{0,4},{2,6},{4,0},{6,2},{8,12},{10,14},{12,8},{14,10},{16,20},{18,... | collective-permute-start | bytes 1572872 | tf_op jit(solution)/shard_map/ppermute | solution.py:778
  250.0 41.0 %copy-start.15 = (bf16[1024,1024]{1,0:T(8,128)(2,1)S(1)}, bf16[1024,1024]{1,0:T(8,128)(2,1)}, u32[]{:S(2)}) copy-start(bf16[1024,1024]{1,0:T(8,128)(2,1)} %tokens.3) | copy-start | bytes 6291460
  250.0 16.6 %collective-permute-start.24 = (bf16[64,2432]{1,0:T(8,128)(2,1)S(1)}, bf16[64,2432]{1,0:T(8,128)(2,1)S(1)}, u32[]{:S(2)}, u32[]{:S(2)}) collective-permute-start(bf16[64,2432]{1,0:T(8,128)(2,1)S(1)} %get-tuple-element.199.first), channel_id=1, source_target_pairs={{0,8},{2,10},{4,12},{6,14},{1,9},{3,11},{5,13},{7,15}} | collective-permute-start | bytes 933896 | tf_op jit(solution)/shard_map/ppermute | solution.py:809
  253.5 13.2 %collective-permute-start.25 = (bf16[64,2432]{1,0:T(8,128)(2,1)S(1)}, bf16[64,2432]{1,0:T(8,128)(2,1)S(1)}, u32[]{:S(2)}, u32[]{:S(2)}) collective-permute-start(bf16[64,2432]{1,0:T(8,128)(2,1)S(1)} %get-tuple-element.199.first), channel_id=1, source_target_pairs={{24,16},{26,18},{28,20},{30,22},{25,17},{27,19},{29,21},{31,23}} | collective-permute-start | bytes 933896 | tf_op jit(solution)/shard_map/ppermute | solution.py:810
  254.2 12.5 %collective-permute-start.27 = (bf16[2,64,384]{2,1,0:T(8,128)(2,1)S(1)}, bf16[2,64,384]{2,1,0:T(8,128)(2,1)S(1)}, u32[]{:S(2)}, u32[]{:S(2)}) collective-permute-start(bf16[2,64,384]{2,1,0:T(8,128)(2,1)S(1)} %get-tuple-element.202), channel_id=1, source_target_pairs={{0,4},{2,6},{4,0},{6,2},{8,12},{10,14},{12,8},{14,10},{16,20},{18,... | collective-permute-start | bytes 294920 | tf_op jit(solution)/shard_map/ppermute | solution.py:778
  268.2 10.5 %collective-permute-start.28 = (bf16[64,2432]{1,0:T(8,128)(2,1)}, bf16[64,2432]{1,0:T(8,128)(2,1)}, u32[]{:S(2)}, u32[]{:S(2)}) collective-permute-start(bf16[64,2432]{1,0:T(8,128)(2,1)} %get-tuple-element.210), channel_id=1, source_target_pairs={{0,8},{2,10},{4,12},{6,14},{8,16},{10,18},{12,20},{14,22},{1,9},{3... | collective-permute-start | bytes 933896 | tf_op jit(solution)/shard_map/ppermute | solution.py:809
  272.5 6.2 %collective-permute-start.29 = (bf16[64,2432]{1,0:T(8,128)(2,1)}, bf16[64,2432]{1,0:T(8,128)(2,1)}, u32[]{:S(2)}, u32[]{:S(2)}) collective-permute-start(bf16[64,2432]{1,0:T(8,128)(2,1)} %get-tuple-element.211), channel_id=1, source_target_pairs={{16,8},{18,10},{20,12},{22,14},{24,16},{26,18},{28,20},{30,22},{17... | collective-permute-start | bytes 933896 | tf_op jit(solution)/shard_map/ppermute | solution.py:810
  274.8 16.2 %copy-start.36 = (f32[1,1024]{1,0:T(1,128)S(1)}, f32[1,1024]{1,0:T(1,128)}, u32[]{:S(2)}) copy-start(f32[1,1024]{1,0:T(1,128)} %get-tuple-element.248.gain) | copy-start | bytes 12292
  275.0 16.0 %copy-start.32 = (bf16[64,2432]{1,0:T(8,128)(2,1)}, bf16[64,2432]{1,0:T(8,128)(2,1)S(1)}, u32[]{:S(2)}) copy-start(bf16[64,2432]{1,0:T(8,128)(2,1)S(1)} %get-tuple-element.220) | copy-start | bytes 933892
  280.0 18.3 %collective-permute-start.30 = (bf16[64,2432]{1,0:T(8,128)(2,1)S(1)}, bf16[64,2432]{1,0:T(8,128)(2,1)S(1)}, u32[]{:S(2)}, u32[]{:S(2)}) collective-permute-start(bf16[64,2432]{1,0:T(8,128)(2,1)S(1)} %get-tuple-element.212), channel_id=1, source_target_pairs={{0,8},{2,10},{4,12},{6,14},{8,16},{10,18},{12,20},{14,22},{16,24},... | collective-permute-start | bytes 933896 | tf_op jit(solution)/shard_map/ppermute | solution.py:809
  289.5 9.5 %collective-permute-start.31 = (bf16[64,2432]{1,0:T(8,128)(2,1)S(1)}, bf16[64,2432]{1,0:T(8,128)(2,1)}, u32[]{:S(2)}, u32[]{:S(2)}) collective-permute-start(bf16[64,2432]{1,0:T(8,128)(2,1)S(1)} %get-tuple-element.213), channel_id=1, source_target_pairs={{8,0},{10,2},{12,4},{14,6},{16,8},{18,10},{20,12},{22,14},{24,16},... | collective-permute-start | bytes 933896 | tf_op jit(solution)/shard_map/ppermute | solution.py:810
  304.9 4.4 %collective-permute-start.33 = (f32[2,64]{1,0:T(2,128)S(1)}, f32[2,64]{1,0:T(2,128)S(1)}, u32[]{:S(2)}, u32[]{:S(2)}) collective-permute-start(f32[2,64]{1,0:T(2,128)S(1)} %pad_maximum_fusion.5.own), channel_id=1, source_target_pairs={{0,1},{1,0},{2,3},{3,2},{4,5},{5,4},{6,7},{7,6},{8,9},{9,8},{10,11... | collective-permute-start | bytes 1544 | tf_op jit(solution)/shard_map/ppermute | solution.py:921
  (51 other events, 238.7 us)
Sparse Core Ops, SparseCore 0:
  16.1 95.5 all-gather.1
  167.4 102.2 reduce-scatter.1
